TPU v7x, 32 devices: a whole 2x2x4 slice. The times are simulated.
32 devices in a mesh: row: 4 (over z), col: 8 (over y, x, core).
Axes of the slice: x: 2, y: 2, z: 4, core: 2. Of those that a mesh axis runs over, the one named last changes fastest.
Arguments:
- atom_feat: bfloat16 [4096, 128], P(('row', 'col')), may hold values from -12 to 12
- atom_token: int32 [4096], P(('row', 'col')), may hold values from 0 to 767, as said below
- window_start: int32 [128], P(('row', 'col')), may hold values from -64 to 4032, as said below
- token_cond: bfloat16 [768, 768], P('row'), may hold values from -6 to 6
- token_mask: int32 [768], replicated, may hold values from 0 to 1, as said below
- pair: bfloat16 [768, 768, 128], P('row', 'col'), may hold values from -300 to 300
- enc_in: bfloat16 [4, 128, 128], replicated, may hold values from -2 to 2
- enc_out: bfloat16 [128, 128], replicated, may hold values from -0.5 to 0.5
- pool_weight: bfloat16 [128, 768], replicated, may hold values from -0.5 to 0.5
- tok_in: bfloat16 [2, 4, 768, 768], replicated, may hold values from -0.21875 to 0.21875
- tok_out: bfloat16 [2, 768, 768], replicated, may hold values from -0.21875 to 0.21875
- pair_weight: bfloat16 [2, 128, 16], replicated, may hold values from -0.5 to 0.5
- trans_in: bfloat16 [2, 2, 768, 1536], P(None, None, None, 'col'), may hold values from -0.21875 to 0.21875
- trans_out: bfloat16 [2, 1536, 768], P(None, 'col'), may hold values from -0.15625 to 0.15625
- tok_atom: bfloat16 [768, 128], replicated, may hold values from -0.21875 to 0.21875
- dec_in: bfloat16 [4, 128, 128], replicated, may hold values from -2 to 2
- dec_out: bfloat16 [128, 128], replicated, may hold values from -0.5 to 0.5
- pos_out: bfloat16 [3, 128], replicated, may hold values from -0.5 to 0.5
Outputs:
- position_update: float32 [3, 4096], P(None, ('row', 'col'))
Inputs may be any that keep to these rules, and one draw needn't show every extreme that they name: `atom_token`: non-decreasing; every token number 0 to 767 occurs; for every r, the atoms r * 1024 to (r + 1) * 1024 - 1 belong to the tokens r * 192 to (r + 1) * 192 - 1. window_start[b] lies between 32 b - 64 and 32 b - 32. `token_mask`: ones on a leading run of 384 tokens or more, zeros after, at least one zero.
All inputs are finite; a program needn't handle non-finite values.
Results may differ from a plain program's by a relative error of at most 0.029.
Values may be sent and summed in bfloat16 or wider, within the bound.
No kernel may reach another device: no remote copies, remote signals or barrier semaphores. Data moves between devices by JAX's collectives and lax.ppermute only.
A program may use at most 128 MiB of HBM per device.

v0:
```python
import jax
import jax.numpy as jnp
from jax import lax
from jax.sharding import PartitionSpec as P

HA = 4
QB = 32
KW = 128
HALO = 64
BLOCKS = 2


def with_halo(block, sides, width):
    for axis, dim in sides:
        count = lax.axis_size(axis)
        forward = [(i, i + 1) for i in range(count - 1)]
        backward = [(target, source) for source, target in forward]
        low = lax.ppermute(
            lax.slice_in_dim(block, block.shape[dim] - width, None, axis=dim), axis, forward
        )
        high = lax.ppermute(lax.slice_in_dim(block, 0, width, axis=dim), axis, backward)
        block = jnp.concatenate([low, block, high], axis=dim)
    return block


def combined_all(part, axis, combine):
    gathered = jax.tree.map(lambda a: lax.all_gather(a, axis), part)

    def take(source):
        return jax.tree.map(lambda a: lax.dynamic_index_in_dim(a, source, 0, False), gathered)

    return lax.fori_loop(
        1, lax.axis_size(axis), lambda source, state: combine(state, take(source)), take(0)
    )


def normed(x):
    x = x.astype(jnp.float32)
    cent = x - jnp.mean(x, -1, keepdims=True)
    var = jnp.mean(cent * cent, -1, keepdims=True)
    return cent * lax.rsqrt(var + 1e-05)


def atom_layer(x, starts, w_in, w_out):
    rows, width = x.shape
    hsize = width // HA
    nblk = rows // QB
    xn = normed(x).astype(jnp.bfloat16)
    query = jnp.dot(xn, w_in[0], preferred_element_type=jnp.float32).astype(jnp.bfloat16)
    keys = jnp.dot(xn, w_in[1], preferred_element_type=jnp.float32).astype(jnp.bfloat16)
    vals = jnp.dot(xn, w_in[2], preferred_element_type=jnp.float32).astype(jnp.bfloat16)
    gate = jnp.dot(xn, w_in[3], preferred_element_type=jnp.float32)
    both = jnp.concatenate([keys, vals], 1)
    padded = with_halo(both, ((("row", "col"), 0),), HALO)
    natom = lax.axis_size(("row", "col")) * rows
    offset = lax.axis_index(("row", "col")) * rows
    local = starts - offset + HALO
    windows = jax.vmap(lambda s: lax.dynamic_slice_in_dim(padded, s, KW, 0))(local)
    glob = starts[:, None] + jnp.arange(KW, dtype=jnp.int32)[None, :]
    valid = (glob >= 0) & (glob < natom)
    qblk = query.reshape(nblk, QB, HA, hsize)
    kblk = windows[:, :, :width].reshape(nblk, KW, HA, hsize)
    vblk = windows[:, :, width:].reshape(nblk, KW, HA, hsize)
    scores = jnp.einsum(
        "bqhd,bkhd->bhqk", qblk, kblk, preferred_element_type=jnp.float32
    ) / jnp.sqrt(jnp.float32(hsize))
    scores = jnp.where(valid[:, None, None, :], scores, -1000000000.0)
    top = jnp.max(scores, -1, keepdims=True)
    expd = jnp.exp(scores - top)
    total = jnp.sum(expd, -1)
    outs = jnp.einsum(
        "bhqk,bkhd->bqhd", expd.astype(jnp.bfloat16), vblk, preferred_element_type=jnp.float32
    )
    outs = outs / jnp.transpose(total, (0, 2, 1))[:, :, :, None]
    outs = outs.reshape(rows, width)
    gated = (jax.nn.sigmoid(gate) * outs).astype(jnp.bfloat16)
    return (
        x.astype(jnp.float32) + jnp.dot(gated, w_out, preferred_element_type=jnp.float32)
    ).astype(jnp.bfloat16)


def spread_heads(factor, hsize):
    return jnp.repeat(jnp.transpose(factor), hsize, axis=1)


def token_block(act, pair_tile, token_mask, w_in, w_out, w_pair, t_in, t_out):
    rows, width = act.shape
    cols = pair_tile.shape[1]
    heads = w_pair.shape[1]
    hsize = width // heads
    col_start = lax.axis_index("col") * cols
    key_valid = lax.dynamic_slice_in_dim(token_mask, col_start, cols, 0) == 1
    xn = normed(act).astype(jnp.bfloat16)
    query = jnp.dot(xn, w_in[0], preferred_element_type=jnp.float32).astype(jnp.bfloat16)
    gate = jnp.dot(xn, w_in[3], preferred_element_type=jnp.float32)
    keys_own = jnp.dot(xn, w_in[1], preferred_element_type=jnp.float32).astype(jnp.bfloat16)
    vals_own = jnp.dot(xn, w_in[2], preferred_element_type=jnp.float32).astype(jnp.bfloat16)
    whole = lax.all_gather(jnp.concatenate([keys_own, vals_own], 1), "row", axis=0, tiled=True)
    mine = lax.dynamic_slice_in_dim(whole, col_start, cols, 0)
    keys = mine[:, :width]
    vals = mine[:, width:]
    bias = jnp.einsum("qkc,ch->hqk", pair_tile, w_pair, preferred_element_type=jnp.float32)
    qh = query.reshape(rows, heads, hsize)
    kh = keys.reshape(cols, heads, hsize)
    vh = vals.reshape(cols, heads, hsize)
    scores = (
        jnp.einsum("qhd,khd->hqk", qh, kh, preferred_element_type=jnp.float32)
        / jnp.sqrt(jnp.float32(hsize))
        + bias
    )
    scores = jnp.where(key_valid[None, None, :], scores, -1000000000.0)
    top = jnp.max(scores, -1)
    expd = jnp.exp(scores - top[:, :, None])
    total = jnp.sum(expd, -1)
    partial_value = jnp.einsum(
        "hqk,khd->qhd", expd.astype(jnp.bfloat16), vh, preferred_element_type=jnp.float32
    ).reshape(rows, width)

    def combine(first, second):
        joint = jnp.maximum(first[0], second[0])
        scale_one = jnp.exp(first[0] - joint)
        scale_two = jnp.exp(second[0] - joint)
        summed = first[1] * scale_one + second[1] * scale_two
        outs = first[2] * spread_heads(scale_one, hsize) + second[2] * spread_heads(
            scale_two, hsize
        )
        return (joint, summed, outs)

    top, total, partial_value = combined_all((top, total, partial_value), "col", combine)
    attn = partial_value / spread_heads(total, hsize)
    gated = (jax.nn.sigmoid(gate) * attn).astype(jnp.bfloat16)
    act = act + jnp.dot(gated, w_out, preferred_element_type=jnp.float32)
    xn2 = normed(act).astype(jnp.bfloat16)
    swish = jax.nn.silu(jnp.dot(xn2, t_in[0], preferred_element_type=jnp.float32))
    hidden = (swish * jnp.dot(xn2, t_in[1], preferred_element_type=jnp.float32)).astype(
        jnp.bfloat16
    )
    return act + lax.psum(
        jnp.dot(hidden, t_out, preferred_element_type=jnp.float32).astype(jnp.bfloat16), "col"
    ).astype(jnp.float32)


def body(
    atom_feat,
    atom_token,
    window_start,
    token_cond,
    token_mask,
    pair,
    enc_in,
    enc_out,
    pool_weight,
    tok_in,
    tok_out,
    pair_weight,
    trans_in,
    trans_out,
    tok_atom,
    dec_in,
    dec_out,
    pos_out,
):
    row_tokens = token_cond.shape[0]
    row_start = lax.axis_index("row") * row_tokens
    first = atom_layer(atom_feat, window_start, enc_in, enc_out)
    feats = jax.nn.relu(jnp.dot(first, pool_weight, preferred_element_type=jnp.float32)).astype(
        jnp.bfloat16
    )
    local_token = atom_token - row_start
    onehot = local_token[None, :] == jnp.arange(row_tokens, dtype=jnp.int32)[:, None]
    own_sums = jnp.dot(onehot.astype(jnp.bfloat16), feats, preferred_element_type=jnp.float32)
    own_counts = jnp.sum(onehot.astype(jnp.float32), 1)
    sums, counts = (
        lax.psum(own_sums.astype(jnp.bfloat16), "col").astype(jnp.float32),
        lax.psum(own_counts.astype(jnp.bfloat16), "col").astype(jnp.float32),
    )
    act = sums / counts[:, None] + token_cond.astype(jnp.float32)
    for layer in range(BLOCKS):
        act = token_block(
            act,
            pair,
            token_mask,
            tok_in[layer],
            tok_out[layer],
            pair_weight[layer],
            trans_in[layer],
            trans_out[layer],
        )
    proj = jnp.dot(
        normed(act).astype(jnp.bfloat16), tok_atom, preferred_element_type=jnp.float32
    ).astype(jnp.bfloat16)
    spread = jnp.take(proj, local_token, axis=0)
    second = (first.astype(jnp.float32) + spread.astype(jnp.float32)).astype(jnp.bfloat16)
    third = atom_layer(second, window_start, dec_in, dec_out)
    return jnp.dot(
        pos_out,
        jnp.transpose(normed(third).astype(jnp.bfloat16)),
        preferred_element_type=jnp.float32,
    )


def solution(mesh):
    in_specs = (
        P(("row", "col"), None),
        P(("row", "col")),
        P(("row", "col")),
        P("row", None),
        P(),
        P("row", "col", None),
        P(),
        P(),
        P(),
        P(),
        P(),
        P(),
        P(None, None, None, "col"),
        P(None, "col", None),
        P(),
        P(),
        P(),
        P(),
    )
    out_specs = P(None, ("row", "col"))
    return jax.shard_map(body, mesh=mesh, in_specs=in_specs, out_specs=out_specs, check_vma=False)
```

profile of v0, /device:TPU:24, one launch (start us, length us, event | category | flops | bytes accessed | tf_op | source)
XLA Modules:
  0.0 469.3 jit_solution(4262686826890324669)
XLA Ops:
  9.6 3.7 collective-permute-start.1
  13.3 1.9 collective-permute-start
  16.9 1.2 compare_and_fusion
  18.9 1.8 collective-permute-done
  20.8 6.4 %while.42 = (s32[]{:T(128)}, bf16[256,256]{0,1:T(8,128)(2,1)S(1)}, s32[4,2]{0,1:T(2,128)S(1)}, bf16[4,128,256]{2,1,0:T(8,128)(2,1)S(1)}, s32[]{:T(128)}) while((s32[]{:T(128)}, bf16[256,256]{0,1:T(8,128)(2,1)S(1)}, s32[4,2]{0,1:T(2,128)S(1)}, bf16[4,128,256]{2,1,0:T(8,128)(2,1)S(1)}, s32[]{:T(128)}) %tuple.128), condition=%wide.while_cond, body=%wide.while_body.sunk | while | flops 2 | bytes 393321 | solution.py:58
  30.0 1.1 convolution_convert_fusion.8
  31.3 11.8 %psum.29 = bf16[192]{0:T(256)(128)(2,1)S(1)} all-reduce(bf16[192]{0:T(256)(128)(2,1)S(1)} %convert_reduce_fusion.1), channel_id=1, replica_groups=mesh['row'=4,'col'=8] {'col'}, use_global_device_ids=true, to_apply=%region_6.7 | all-reduce | flops 192 | bytes 768 | tf_op jit(solution)/shard_map/psum | solution.py:175
  43.1 40.6 %all-reduce.5.cloned.1.call-done = bf16[192,768]{1,0:T(8,128)(2,1)} async-done(((bf16[192,768]{1,0:T(8,128)(2,1)}), bf16[192,768]{1,0:T(8,128)(2,1)}) %all-reduce.5.cloned.1.call-update) | async-done | bytes 294928 | tf_op jit(solution)/shard_map/psum | solution.py:174
  83.7 1.2 fusion.183
  85.0 1.3 multiply_reduce_fusion.4
  86.3 1.9 convolution_convert_fusion.5
  88.2 1.7 convolution_convert_fusion.6
  90.9 5.3 %fusion.168 = f32[16,192,96]{2,0,1:T(8,128)S(1)} fusion(bf16[192,96,128]{2,1,0:T(8,128)(2,1)} %param.27, bf16[2,128,16]{1,2,0:T(8,128)(2,1)S(1)} %copy-done.17), kind=kOutput, calls=%fused_computation.234 | convolution fusion | flops 75497472 | bytes 5902336 | tf_op jit(solution)/shard_map/qkc,ch->hqk/dot_general | solution.py:102
  97.0 1.4 dynamic-slice_compare_fusion
  98.3 2.1 convolution_convert_fusion.7
  101.3 37.9 %all-gather.9.cloned.1.call-done = bf16[768,1536]{1,0:T(8,128)(2,1)} async-done(((bf16[192,1536]{1,0:T(8,128)(2,1)}), bf16[768,1536]{1,0:T(8,128)(2,1)}) %all-gather.9.cloned.1.call-update) | async-done | bytes 2359312 | tf_op jit(solution)/shard_map/all_gather | solution.py:98
  140.5 1.5 fusion.189
  143.7 9.4 %all-gather = f32[128,192]{1,0:T(8,128)S(1)} all-gather(f32[16,192]{1,0:T(8,128)S(1)} %get-tuple-element.509), channel_id=2, replica_groups=mesh['row'=4,'col'=8] {'col'}, dimensions={0}, use_global_device_ids=true | all-gather | bytes 110592 | tf_op jit(solution)/shard_map/all_gather | solution.py:27
  153.4 9.7 %all-gather.1 = f32[128,192]{1,0:T(8,128)S(1)} all-gather(f32[16,192]{1,0:T(8,128)S(1)} %fusion.11), channel_id=3, replica_groups=mesh['row'=4,'col'=8] {'col'}, dimensions={0}, use_global_device_ids=true | all-gather | bytes 110592 | tf_op jit(solution)/shard_map/all_gather | solution.py:27
  163.0 21.4 %all-gather.11.cloned.1.call-done = f32[8,192,768]{2,1,0:T(8,128)} async-done(((f32[1,192,768]{2,1,0:T(8,128)}), f32[8,192,768]{2,1,0:T(8,128)}) %all-gather.11.cloned.1.call-update) | async-done | bytes 4718608 | tf_op jit(solution)/shard_map/all_gather | solution.py:27
  185.8 12.5 %while.40 = (s32[]{:T(128)}, f32[16,192]{1,0:T(8,128)S(1)}, f32[16,192]{1,0:T(8,128)S(1)}, f32[192,768]{0,1:T(8,128)S(1)}, f32[8,16,192]{2,1,0:T(8,128)S(1)}, /*...) while((s32[]{:T(128)}, f32[16,192]{1,0:T(8,128)S(1)}, ...), condition=%wide.region_12.13_spmd, body=%wide.region_11.12_spmd.sunk | while | flops 463877 | bytes 4313243 | solution.py:32
  199.4 2.6 fusion.190
  202.3 1.3 fusion.84
  203.5 2.2 convolution_convert_fusion.4
  205.9 53.1 %all-reduce.7.cloned.1.call-done = bf16[192,768]{1,0:T(8,128)(2,1)} async-done(((bf16[192,768]{1,0:T(8,128)(2,1)}), bf16[192,768]{1,0:T(8,128)(2,1)}) %all-reduce.7.cloned.1.call-update) | async-done | bytes 294928 | tf_op jit(solution)/shard_map/psum | solution.py:138
  259.0 1.2 fusion.131
  260.2 1.2 multiply_reduce_fusion.2
  261.5 1.8 convolution_convert_fusion.1
  263.3 1.7 convolution_convert_fusion.2
  266.0 5.3 %fusion.166 = f32[16,192,96]{2,0,1:T(8,128)S(1)} fusion(bf16[192,96,128]{2,1,0:T(8,128)(2,1)} %param.27, bf16[2,128,16]{1,2,0:T(8,128)(2,1)S(1)} %copy-done.18), kind=kOutput, calls=%fused_computation.232 | convolution fusion | flops 75497472 | bytes 5902336 | tf_op jit(solution)/shard_map/qkc,ch->hqk/dot_general | solution.py:102
  271.2 1.9 copy.119
  273.2 1.8 convolution_convert_fusion.3
  275.1 39.1 %all-gather.13.cloned.1.call-done = bf16[768,1536]{1,0:T(8,128)(2,1)} async-done(((bf16[192,1536]{1,0:T(8,128)(2,1)}), bf16[768,1536]{1,0:T(8,128)(2,1)}) %all-gather.13.cloned.1.call-update) | async-done | bytes 2359312 | tf_op jit(solution)/shard_map/all_gather | solution.py:98
  316.3 2.0 fusion.193
  319.8 9.4 %all-gather.2 = f32[128,192]{1,0:T(8,128)S(1)} all-gather(f32[16,192]{1,0:T(8,128)S(1)} %get-tuple-element.513), channel_id=4, replica_groups=mesh['row'=4,'col'=8] {'col'}, dimensions={0}, use_global_device_ids=true | all-gather | bytes 110592 | tf_op jit(solution)/shard_map/all_gather | solution.py:27
  329.5 10.4 %all-gather.3 = f32[128,192]{1,0:T(8,128)} all-gather(f32[16,192]{1,0:T(8,128)S(1)} %fusion.13), channel_id=5, replica_groups=mesh['row'=4,'col'=8] {'col'}, dimensions={0}, use_global_device_ids=true | all-gather | bytes 110592 | tf_op jit(solution)/shard_map/all_gather | solution.py:27
  340.7 20.0 %all-gather.15.cloned.1.call-done = f32[8,192,768]{2,1,0:T(8,128)} async-done(((f32[1,192,768]{2,1,0:T(8,128)}), f32[8,192,768]{2,1,0:T(8,128)}) %all-gather.15.cloned.1.call-update) | async-done | bytes 4718608 | tf_op jit(solution)/shard_map/all_gather | solution.py:27
  362.0 17.5 %while.41 = (s32[]{:T(128)}, f32[16,192]{1,0:T(8,128)S(1)}, f32[16,192]{1,0:T(8,128)S(1)}, f32[192,768]{0,1:T(8,128)S(1)}, f32[8,16,192]{2,1,0:T(8,128)S(1)}, /*...) while((s32[]{:T(128)}, f32[16,192]{1,0:T(8,128)S(1)}, ...), condition=%wide.region_21.22_spmd, body=%wide.region_20.21_spmd.sunk | while | flops 463877 | bytes 4313243 | solution.py:32
  380.5 2.5 fusion.194
  383.3 1.2 fusion.79
  384.5 2.2 convolution_convert_fusion
  386.9 53.2 %all-reduce.9.cloned.1.call-done = bf16[192,768]{1,0:T(8,128)(2,1)} async-done(((bf16[192,768]{1,0:T(8,128)(2,1)}), bf16[192,768]{1,0:T(8,128)(2,1)}) %all-reduce.9.cloned.1.call-update) | async-done | bytes 294928 | tf_op jit(solution)/shard_map/psum | solution.py:138
  440.1 1.2 fusion.102
  441.2 1.2 multiply_reduce_fusion
  444.2 2.0 collective-permute-start.3
  446.3 2.3 collective-permute-start.2
  448.9 4.7 %collective-permute-done.2 = bf16[64,256]{0,1:T(8,128)(2,1)S(1)} collective-permute-done((bf16[64,256]{0,1:T(8,128)(2,1)S(1)}, bf16[64,256]{0,1:T(8,128)(2,1)S(1)}, u32[]{:S(2)}, u32[]{:S(2)}) %collective-permute-start.2) | collective-permute-done | bytes 32800 | tf_op jit(solution)/shard_map/ppermute | solution.py:18
  453.8 5.9 %while.43 = (s32[]{:T(128)}, bf16[256,256]{0,1:T(8,128)(2,1)S(1)}, s32[4,2]{0,1:T(2,128)S(1)}, bf16[4,128,256]{2,1,0:T(8,128)(2,1)S(1)}, s32[]{:T(128)}) while((s32[]{:T(128)}, bf16[256,256]{0,1:T(8,128)(2,1)S(1)}, s32[4,2]{0,1:T(2,128)S(1)}, bf16[4,128,256]{2,1,0:T(8,128)(2,1)S(1)}, s32[]{:T(128)}) %tuple.157), condition=%wide.while_cond.1, body=%wide.while_body.1.sunk | while | flops 2 | bytes 393321 | solution.py:58
  (311 shorter events, 71.4 us)
Async XLA Ops:
  6.5 23.4 %copy-start = (bf16[128,768]{1,0:T(8,128)(2,1)S(1)}, bf16[128,768]{1,0:T(8,128)(2,1)}, u32[]{:S(2)}) copy-start(bf16[128,768]{1,0:T(8,128)(2,1)} %param.30) | copy-start | bytes 589828
  6.5 77.2 %all-reduce.5.cloned.1.call-start = ((), (), s32[]{:S(2)}) async-start(), calls=%async_computation | async-start | bytes 589824 | tf_op jit(solution)/shard_map/psum | solution.py:174
  9.6 9.3 %collective-permute-start.1 = (bf16[64,256]{0,1:T(8,128)(2,1)S(1)}, bf16[64,256]{0,1:T(8,128)(2,1)S(1)}, u32[]{:S(2)}, u32[]{:S(2)}) collective-permute-start(bf16[64,256]{0,1:T(8,128)(2,1)S(1)} %get-tuple-element.506), channel_id=1, source_target_pairs={{1,0},{2,1},{3,2},{4,3},{5,4},{6,5},{7,6},{8,7},{9,8},{10,9},{11,1... | collective-permute-start | bytes 98312 | tf_op jit(solution)/shard_map/ppermute | solution.py:21
  13.3 7.4 %collective-permute-start = (bf16[64,256]{0,1:T(8,128)(2,1)S(1)}, bf16[64,256]{0,1:T(8,128)(2,1)S(1)}, u32[]{:S(2)}, u32[]{:S(2)}) collective-permute-start(bf16[64,256]{0,1:T(8,128)(2,1)S(1)} %get-tuple-element.505), channel_id=1, source_target_pairs={{0,1},{1,2},{2,3},{3,4},{4,5},{5,6},{6,7},{7,8},{8,9},{9,10},{10,1... | collective-permute-start | bytes 98312 | tf_op jit(solution)/shard_map/ppermute | solution.py:18
  16.9 10.7 %copy-start.23 = (pred[4,128]{1,0:T(4,128)(4,1)}, pred[4,128]{1,0:T(4,128)(4,1)S(1)}, u32[]{:S(2)}) copy-start(pred[4,128]{1,0:T(4,128)(4,1)S(1)} %fusion.174) | copy-start | bytes 1540
  18.1 13.1 %copy-start.26 = (s32[128]{0:T(128)}, s32[128]{0:T(128)S(1)}, u32[]{:S(2)}) copy-start(s32[128]{0:T(128)S(1)} %get-tuple-element.490) | copy-start | bytes 1540
  27.3 0.9 copy-start.14
  27.5 1.3 copy-start.34
  28.2 55.6 %copy-start.4 = (bf16[192,768]{1,0:T(8,128)(2,1)S(1)}, bf16[192,768]{1,0:T(8,128)(2,1)}, u32[]{:S(2)}) copy-start(bf16[192,768]{1,0:T(8,128)(2,1)} %param.25) | copy-start | bytes 884740
  29.9 58.2 %copy-start.12 = (bf16[128,128]{0,1:T(8,128)(2,1)}, bf16[128,128]{0,1:T(8,128)(2,1)S(1)}, u32[]{:S(2)}) copy-start(bf16[128,128]{0,1:T(8,128)(2,1)S(1)} %fusion.60) | copy-start | bytes 98308
  31.1 108.1 %all-gather.9.cloned.1.call-start = ((), (), s32[]{:S(2)}) async-start(), calls=%async_computation.1 | async-start | bytes 2949120 | tf_op jit(solution)/shard_map/all_gather | solution.py:98
  43.1 55.2 %copy-start.19 = (f32[192]{0:T(256)}, f32[192]{0:T(256)S(1)}, u32[]{:S(2)}) copy-start(f32[192]{0:T(256)S(1)} %convert_element_type.167) | copy-start | bytes 2308
  85.0 13.4 %copy-start.21 = (f32[192]{0:T(256)}, f32[192]{0:T(256)S(1)}, u32[]{:S(2)}) copy-start(f32[192]{0:T(256)S(1)} %broadcast_multiply_fusion.4) | copy-start | bytes 2308
  86.3 12.1 %copy-start.30 = (f32[192]{0:T(256)}, f32[192]{0:T(256)S(1)}, u32[]{:S(2)}) copy-start(f32[192]{0:T(256)S(1)} %add_rsqrt_fusion.4) | copy-start | bytes 2308
  86.3 1.9 copy-start.6
  89.9 1.0 copy-start.17
  90.8 93.6 %all-gather.11.cloned.1.call-start = ((), (), s32[]{:S(2)}) async-start(), calls=%async_computation.2 | async-start | bytes 5308416 | tf_op jit(solution)/shard_map/all_gather | solution.py:27
  143.6 115.4 %all-reduce.7.cloned.1.call-start = ((), (), s32[]{:S(2)}) async-start(), calls=%async_computation.3 | async-start | bytes 589824 | tf_op jit(solution)/shard_map/psum | solution.py:138
  198.4 1.0 copy-start.5
  198.4 1.0 copy-start.7
  198.4 1.0 copy-start.20
  198.4 1.0 copy-start.22
  198.4 1.0 copy-start.31
  202.0 1.5 copy-start.32
  205.8 108.5 %all-gather.13.cloned.1.call-start = ((), (), s32[]{:S(2)}) async-start(), calls=%async_computation.4 | async-start | bytes 2949120 | tf_op jit(solution)/shard_map/all_gather | solution.py:98
  259.0 2.4 copy-start.2
  261.5 11.7 %copy-start.9 = (bf16[192,768]{1,0:T(8,128)(2,1)}, bf16[192,768]{1,0:T(8,128)(2,1)S(1)}, u32[]{:S(2)}) copy-start(bf16[192,768]{1,0:T(8,128)(2,1)S(1)} %multiply_convert_fusion.2) | copy-start | bytes 884740
  263.3 2.6 copy-start.18
  265.9 94.7 %all-gather.15.cloned.1.call-start = ((), (), s32[]{:S(2)}) async-start(), calls=%async_computation.5 | async-start | bytes 5308416 | tf_op jit(solution)/shard_map/all_gather | solution.py:27
  273.2 43.1 %copy-start.28 = (pred[96]{0:T(512)(128)(4,1)S(1)}, pred[96]{0:T(512)(128)(4,1)}, u32[]{:S(2)}) copy-start(pred[96]{0:T(512)(128)(4,1)} %dynamic-slice_compare_fusion) | copy-start | bytes 292
  316.3 2.0 copy-start.8
  319.8 120.3 %all-reduce.9.cloned.1.call-start = ((), (), s32[]{:S(2)}) async-start(), calls=%async_computation.6 | async-start | bytes 589824 | tf_op jit(solution)/shard_map/psum | solution.py:138
  379.5 1.0 copy-start.10
  383.0 1.5 copy-start.33
  383.3 3.5 copy-start.27
  386.8 55.7 %copy-start.11 = (bf16[768,128]{1,0:T(8,128)(2,1)S(1)}, bf16[768,128]{1,0:T(8,128)(2,1)}, u32[]{:S(2)}) copy-start(bf16[768,128]{1,0:T(8,128)(2,1)} %param.36) | copy-start | bytes 589828
  386.8 56.8 %copy-start.13 = (bf16[128,128]{0,1:T(8,128)(2,1)S(1)}, bf16[128,128]{0,1:T(8,128)(2,1)}, u32[]{:S(2)}) copy-start(bf16[128,128]{0,1:T(8,128)(2,1)} %copy-done.12) | copy-start | bytes 98308
  386.8 56.8 %copy-start.25 = (pred[128]{0:T(512)(128)(4,1)S(1)}, pred[128]{0:T(512)(128)(4,1)}, u32[]{:S(2)}) copy-start(pred[128]{0:T(512)(128)(4,1)} %get-tuple-element.489) | copy-start | bytes 388
  386.9 56.9 %copy-start.16 = (bf16[4,128,128]{2,1,0:T(8,128)(2,1)S(1)}, bf16[4,128,128]{2,1,0:T(8,128)(2,1)}, u32[]{:S(2)}) copy-start(bf16[4,128,128]{2,1,0:T(8,128)(2,1)} %param.37) | copy-start | bytes 393220
  440.1 2.4 copy-start.3
  442.4 11.4 %copy-start.15 = (s32[4,2]{0,1:T(2,128)S(1)}, s32[4,2]{0,1:T(2,128)}, u32[]{:S(2)}) copy-start(s32[4,2]{0,1:T(2,128)} %copy-done.14) | copy-start | bytes 100
  444.2 4.7 collective-permute-start.3
  446.3 7.4 %collective-permute-start.2 = (bf16[64,256]{0,1:T(8,128)(2,1)S(1)}, bf16[64,256]{0,1:T(8,128)(2,1)S(1)}, u32[]{:S(2)}, u32[]{:S(2)}) collective-permute-start(bf16[64,256]{0,1:T(8,128)(2,1)S(1)} %get-tuple-element.503), channel_id=1, source_target_pairs={{0,1},{1,2},{2,3},{3,4},{4,5},{5,6},{6,7},{7,8},{8,9},{9,10},{10,1... | collective-permute-start | bytes 98312 | tf_op jit(solution)/shard_map/ppermute | solution.py:18
  453.8 6.3 %copy-start.24 = (pred[4,128]{1,0:T(4,128)(4,1)S(1)}, pred[4,128]{1,0:T(4,128)(4,1)}, u32[]{:S(2)}) copy-start(pred[4,128]{1,0:T(4,128)(4,1)} %copy-done.23) | copy-start | bytes 1540
  460.0 1.4 copy-start.35
  460.1 1.6 copy-start.29
  460.1 2.3 copy-start.1
Sparse Core Ops, SparseCore 0:
  31.3 52.4 all-reduce.4
  91.0 48.1 all-gather.8
  143.7 40.6 all-gather.10
  205.9 53.0 all-reduce.6
  266.0 48.2 all-gather.12
  319.9 40.6 all-gather.14
  386.9 53.0 all-reduce.8
where the time goes:
time: 472 us; the launch traced here: 469 us
  waiting for transfers between devices  272 us (58%)
  blocking collectives  50.8 us (11%)
  local copies, waits for them, and re-layouts  49.4 us (10%)
  matrix products  46.1 us (10%)
  other arithmetic  25.3 us (5%)
  between operations  14.5 us (3%)
  starting transfers between devices  10.2 us (2%)
    psum x2, waiting for transfers between devices, token_block(): lax.psum(jnp.dot(hidden, t_out, preferred_element_type=jnp.float32).astyp...  106 us
    all_gather x2, waiting for transfers between devices, token_block(): lax.all_gather(jnp.concatenate([keys_own, vals_own], 1), 'row', axis=0, t...  77 us
    all_gather x2, waiting for transfers between devices, combined_all(): gathered = jax.tree.map(lambda a: lax.all_gather(a, axis), part)  41.4 us
    psum x1, waiting for transfers between devices, body(): lax.psum(own_sums.astype(jnp.bfloat16), 'col').astype(jnp.float32)  40.6 us
    all_gather x4, blocking collectives, combined_all(): gathered = jax.tree.map(lambda a: lax.all_gather(a, axis), part)  39 us
    dynamic_slice x32, local copies, waits for them, and re-layouts, take(): lax.dynamic_index_in_dim(a, source, 0, False)  19.9 us
    gather x40, local copies, waits for them, and re-layouts  12.1 us
    psum x1, blocking collectives, body(): lax.psum(own_counts.astype(jnp.bfloat16), 'col').astype(jnp.float32)  11.8 us
  transfers between devices with their start and end apart: 11, of which 9 were waited for; matrix products, arithmetic and copies ran while one was open for 5% of the time, Pallas kernels for 0%

commit v1 on v0

v1 whole, which is shorter than its diff:
```python
import functools
import math

import jax
import jax.numpy as jnp
from jax import lax
from jax.experimental import pallas as pl
from jax.experimental.pallas import tpu as pltpu
from jax.sharding import PartitionSpec as P

HA = 4
QB = 32
KW = 128
HALO = 64
BLOCKS = 2
EXTRA = 16
MIB = 1 << 20
F32 = jnp.float32
BF16 = jnp.bfloat16


def call(kernel, outs, *args, scalars=(), far=(), scratch=(), grant=8, flops=0, moved=0):
    smem = pl.BlockSpec(memory_space=pltpu.SMEM)
    vmem = pl.BlockSpec(memory_space=pltpu.VMEM)
    hbm = pl.BlockSpec(memory_space=pltpu.HBM)
    return pl.pallas_call(
        kernel,
        out_shape=outs,
        in_specs=[smem] * len(scalars) + [vmem] * len(args) + [hbm] * len(far),
        out_specs=jax.tree.map(lambda _: vmem, outs),
        scratch_shapes=list(scratch),
        compiler_params=pltpu.CompilerParams(vmem_limit_bytes=grant * MIB),
        cost_estimate=pl.CostEstimate(flops=flops, bytes_accessed=moved, transcendentals=0),
    )(*scalars, *args, *far)


def dot(a, b):
    return jnp.dot(a, b, preferred_element_type=F32)


def dot_nt(a, b):
    return lax.dot_general(a, b, (((1,), (1,)), ((), ())), preferred_element_type=F32)


def dot_tn(a, b):
    return lax.dot_general(a, b, (((0,), (0,)), ((), ())), preferred_element_type=F32)


def normed(x):
    x = x.astype(F32)
    cent = x - jnp.mean(x, -1, keepdims=True)
    var = jnp.mean(cent * cent, -1, keepdims=True)
    return cent * lax.rsqrt(var + 1e-05)


def iota(shape, dim):
    return lax.broadcasted_iota(jnp.int32, shape, dim)


def window_mask(shifts, first, natom, nkeys):
    shape = (len(shifts) * QB, nkeys)
    block = iota(shape, 0) // QB
    low = jnp.zeros(shape, jnp.int32)
    for i, shift in enumerate(shifts):
        low = jnp.where(block == i, shift + QB * i, low)
    key = iota(shape, 1)
    atom = key + first
    return (key >= low) & (key < low + KW) & (atom >= 0) & (atom < natom)


def attend(x, xn, gate, query, keys, vals, mask, w_out):
    width = x.shape[1]
    hsize = width // HA
    lane = iota((1, width), 1) // hsize
    outs = jnp.zeros(x.shape, F32)
    for h in range(HA):
        pick = (lane == h).astype(BF16)
        scores = dot_nt(query, keys * pick) * (1.0 / math.sqrt(hsize))
        scores = jnp.where(mask, scores, -1000000000.0)
        top = jnp.max(scores, -1, keepdims=True)
        expd = jnp.exp(scores - top)
        total = jnp.sum(expd, -1, keepdims=True)
        outs = outs + dot(expd.astype(BF16), vals * pick) / total
    gated = (jax.nn.sigmoid(gate) * outs).astype(BF16)
    return (x.astype(F32) + dot(gated, w_out)).astype(BF16)


def shifts_of(tail_ref, lanes):
    tail = tail_ref[tail_ref.shape[0] - EXTRA :, :].astype(F32)
    return [tail[1:2, k : k + 1].astype(jnp.int32) for k in lanes]


def encoder_kernel(natom, place, own_ref, prev_ref, next_ref, w_in, w_out, ext_ref, all_ref):
    rows = own_ref.shape[0] - EXTRA
    nblk = rows // QB
    half = HALO // QB
    x = jnp.concatenate([prev_ref[:rows], own_ref[:rows], next_ref[:rows]], 0)
    xn = normed(x).astype(BF16)
    keys = dot(xn, w_in[1]).astype(BF16)
    vals = dot(xn, w_in[2]).astype(BF16)
    qx, qn = x[HALO : 3 * rows - HALO], xn[HALO : 3 * rows - HALO]
    query = dot(qn, w_in[0]).astype(BF16)
    gate = dot(qn, w_in[3])
    shifts = (
        shifts_of(prev_ref, range(nblk - half, nblk))
        + shifts_of(own_ref, range(nblk))
        + shifts_of(next_ref, range(half))
    )
    first = place[0] * rows - rows
    for part in range(2):
        mine = slice(part * rows, (part + 1) * rows)
        seen = slice(part * rows, (part + 2) * rows)
        mask = window_mask(
            shifts[part * nblk : (part + 1) * nblk], first + part * rows, natom, 2 * rows
        )
        ext_ref[mine] = attend(
            qx[mine], qn[mine], gate[mine], query[mine], keys[seen], vals[seen], mask, w_out[...]
        )
    new = ext_ref[HALO : HALO + rows]
    tail = own_ref[rows:]
    for j in range(all_ref.shape[0]):
        all_ref[j, :rows] = new
        all_ref[j, rows:] = tail


def pool_kernel(place, both_ref, weight, cond, act_ref, xn_ref, send_ref):
    count, rows = both_ref.shape[0], both_ref.shape[1] - EXTRA
    tokens = cond.shape[0]
    sums = jnp.zeros(cond.shape, F32)
    counts = jnp.zeros((tokens, 1), F32)
    step = 4 if count % 4 == 0 else 1
    for j in range(0, count, step):
        atoms = jnp.concatenate([both_ref[j + k, :rows] for k in range(step)], 0)
        feats = jnp.maximum(dot(atoms, weight[...]), 0.0).astype(BF16)
        spot = jnp.concatenate(
            [both_ref[j + k, rows:].astype(F32)[0:1] for k in range(step)], 1
        ).astype(jnp.int32)
        onehot = (iota((tokens, step * rows), 0) == spot).astype(F32)
        sums = sums + dot(onehot.astype(BF16), feats)
        counts = counts + jnp.sum(onehot, -1, keepdims=True)
    act = sums / counts + cond[...].astype(F32)
    xn = normed(act)
    xn_ref[...] = xn.astype(BF16)
    cols = send_ref.shape[0]
    part = xn[:cols]
    for k in range(1, tokens // cols):
        part = jnp.where(place[2] == k, xn[k * cols : (k + 1) * cols], part)
    send_ref[...] = part.astype(BF16)
    own = act_ref.shape[0]
    mine = act[:own]
    for c in range(1, tokens // own):
        mine = jnp.where(place[1] == c, act[c * own : (c + 1) * own], mine)
    act_ref[...] = mine


def decoder_kernel(natom, place, x1_ref, own_ref, prev_ref, next_ref, proj, w_in, w_out, pos, out):
    rows = own_ref.shape[0] - EXTRA
    tokens = proj.shape[0]
    spread = []
    for k, ref in enumerate((prev_ref, own_ref, next_ref)):
        spot = ref[rows:].astype(F32)[0:1].astype(jnp.int32) + place[7 + k]
        onehot = (iota((tokens, rows), 0) == spot).astype(F32).astype(BF16)
        spread.append(dot_tn(onehot, proj[...]))
    spread = jnp.concatenate([spread[0][rows - HALO :], spread[1], spread[2][:HALO]], 0)
    x = (x1_ref[...].astype(F32) + spread).astype(BF16)
    xn = normed(x).astype(BF16)
    keys = dot(xn, w_in[1]).astype(BF16)
    vals = dot(xn, w_in[2]).astype(BF16)
    qx, qn = x[HALO : HALO + rows], xn[HALO : HALO + rows]
    query = dot(qn, w_in[0]).astype(BF16)
    gate = dot(qn, w_in[3])
    shifts = shifts_of(own_ref, range(rows // QB))
    mask = window_mask(shifts, place[0] * rows - HALO, natom, 2 * rows)
    third = attend(qx, qn, gate, query, keys, vals, mask, w_out[...])
    out[...] = dot_nt(pos[...], normed(third).astype(BF16))


def pack_kernel(first, second, *outs):
    hid = second.shape[1]
    for layer, out in enumerate(outs):
        out[:hid] = first[layer, 0]
        out[hid : 2 * hid] = first[layer, 1]
        out[2 * hid :] = second[layer]


def bias_kernel(pair_ref, weight, out_ref):
    rows, cols, _ = pair_ref.shape
    pad = out_ref.shape[2] - cols

    for q in range(rows):
        bias = dot_nt(weight[...], pair_ref[q])
        out_ref[q] = jnp.concatenate([bias, jnp.zeros((bias.shape[0], pad), F32)], 1)


def prepare(sources, targets, sems):
    return [
        pltpu.make_async_copy(source, target, sems.at[i])
        for i, (source, target) in enumerate(zip(sources, targets))
    ]


def attention_kernel(
    layer,
    place,
    xn_ref,
    here_ref,
    came_ref,
    bias_ref,
    w_in,
    out_ref,
    w_query,
    w_key,
    w_val,
    sems,
):
    fetches = prepare([w_in.at[layer, k] for k in range(3)], [w_query, w_key, w_val], sems)
    fetches[0].start()
    fetches[1].start()
    rows, width = xn_ref.shape
    cols = here_ref.shape[0]
    heads = bias_ref.shape[1] // BLOCKS
    hsize = width // heads
    span = bias_ref.shape[2]
    key_xn = jnp.where(place[3] == place[4], here_ref[...].astype(F32), came_ref[...].astype(F32))
    key_xn = jnp.concatenate([key_xn, jnp.zeros((span - cols, width), F32)], 0).astype(BF16)
    fetches[0].wait()
    fetches[2].start()
    query = dot(xn_ref[...], w_query[...]).astype(BF16)
    fetches[1].wait()
    keys = dot(key_xn, w_key[...]).astype(BF16)
    fetches[2].wait()
    vals = dot(key_xn, w_val[...]).astype(BF16)
    valid = iota((1, span), 1) + place[5] < place[6]
    valid = valid & (iota((1, span), 1) < cols)
    group = heads // 2
    part = group * hsize
    lane = iota((1, part), 1) // hsize
    spot = iota((1, span), 1)
    levels = jnp.zeros((rows, span), F32)
    for g in range(2):
        wide = slice(g * part, (g + 1) * part)
        kg, vg = keys[:, wide], vals[:, wide]
        picks = [(lane == h).astype(BF16) for h in range(group)]
        stacked = jnp.concatenate([kg * p for p in picks], 0)
        scores = dot_nt(query[:, wide], stacked) * (1.0 / math.sqrt(hsize))
        probs = []
        for h in range(group):
            head = g * group + h
            score = scores[:, h * span : (h + 1) * span] + bias_ref[:, layer * heads + head, :]
            score = jnp.where(valid, score, -1000000000.0)
            top = jnp.max(score, -1, keepdims=True)
            expd = jnp.exp(score - top)
            total = jnp.sum(expd, -1, keepdims=True)
            probs.append((expd / total).astype(BF16))
            levels = jnp.where(spot % heads == head, top + jnp.log(total), levels)
        stacked = jnp.concatenate([vg * p for p in picks], 0)
        out_ref[:, wide] = dot(jnp.concatenate(probs, 1), stacked).astype(BF16)
    high = levels.astype(BF16).astype(F32)
    rest = levels - high
    middle = rest.astype(BF16).astype(F32)
    low = rest - middle
    packed = jnp.where(spot < heads, high, jnp.where(spot < 2 * heads, middle, low))
    out_ref[:, width:] = jnp.where(spot < 3 * heads, packed, 0.0).astype(BF16)


def finish_kernel(
    layer,
    heads,
    project,
    message,
    act_ref,
    *refs,
):
    if project:
        tok_atom, *refs = refs
    w_in, w_out, trans, act_out, all_ref, w_gate, w_mix, w_first, w_second, sems = refs
    blocks, hid = w_second.shape[:2]
    fetches = prepare(
        [w_in.at[layer, 3], w_out.at[layer]]
        + [trans.at[j, pl.ds(0, 2 * hid)] for j in range(blocks)]
        + [trans.at[j, pl.ds(2 * hid, hid)] for j in range(blocks)],
        [w_gate, w_mix]
        + [w_first.at[j] for j in range(blocks)]
        + [w_second.at[j] for j in range(blocks)],
        sems,
    )
    firsts, seconds = fetches[2 : 2 + blocks], fetches[2 + blocks :]
    for copy in fetches[:2]:
        copy.start()
    width = act_ref.shape[1]
    hsize = width // heads
    parts = [message[j, :, width:].astype(F32) for j in range(message.shape[0])]
    span = parts[0].shape[1]
    levels = [
        p + pltpu.roll(p, span - heads, 1) + pltpu.roll(p, span - 2 * heads, 1) for p in parts
    ]
    top = functools.reduce(jnp.maximum, levels)
    weights = [jnp.exp(level - top) for level in levels]
    whole = functools.reduce(jnp.add, weights)
    lane = iota((1, span), 1)
    row = iota((span, width), 0)
    expand = (row % heads == iota((span, width), 1) // hsize) & (row < 2 * heads)
    expand = expand.astype(F32).astype(BF16)
    attn = jnp.zeros(act_ref.shape, F32)
    for j, weight in enumerate(weights):
        weight = weight / whole
        high = weight.astype(BF16).astype(F32)
        packed = jnp.where(lane < heads, high, pltpu.roll(weight - high, heads, 1))
        packed = jnp.where(lane < 2 * heads, packed, 0.0).astype(BF16)
        attn = attn + dot(packed, expand) * message[j, :, :width].astype(F32)
    fetches[0].wait()
    for copy in firsts:
        copy.start()
    gate = dot(normed(act_ref[...]).astype(BF16), w_gate[...])
    gated = (jax.nn.sigmoid(gate) * attn).astype(BF16)
    fetches[1].wait()
    for copy in seconds:
        copy.start()
    act = act_ref[...] + dot(gated, w_mix[...])
    xn2 = normed(act).astype(BF16)
    hidden = []
    for j in range(blocks):
        firsts[j].wait()
        both = dot_nt(xn2, w_first[j])
        left, right = both[:, :hid], both[:, hid:]
        hidden.append((left * jax.nn.sigmoid(left) * right).astype(BF16))
    for j in range(blocks):
        seconds[j].wait()
        act = act + dot(hidden[j], w_second[j])
    act_out[...] = act
    normal = normed(act).astype(BF16)
    if project:
        normal = dot(normal, tok_atom[...]).astype(BF16)
    for j in range(all_ref.shape[0]):
        all_ref[j] = normal


def finish(layer, message, act, w_in, w_out, trans, heads, copies, tok_atom=None):
    own, width = act.shape
    last = width if tok_atom is None else tok_atom.shape[1]
    blocks, packed, _ = trans.shape
    hid = packed // 3
    return call(
        functools.partial(finish_kernel, layer, heads, tok_atom is not None),
        [
            jax.ShapeDtypeStruct((own, width), F32),
            jax.ShapeDtypeStruct((copies, own, last), BF16),
        ],
        message,
        act,
        *(() if tok_atom is None else (tok_atom,)),
        far=(w_in, w_out, trans),
        scratch=[
            pltpu.VMEM((width, width), BF16),
            pltpu.VMEM((width, width), BF16),
            pltpu.VMEM((blocks, 2 * hid, width), BF16),
            pltpu.VMEM((blocks, hid, width), BF16),
            pltpu.SemaphoreType.DMA((2 + 2 * blocks,)),
        ],
        grant=59,
        flops=2 * own * trans.size,
        moved=2 * trans.size,
    )


def key_source(rows, cols):
    nrow, ncol = lax.axis_size("row"), lax.axis_size("col")
    shares = rows // cols
    pairs = []
    for owner in range(nrow):
        free = [list(range(share, ncol, shares)) for share in range(shares)]
        for r in range(nrow):
            for share in range(shares):
                if r != owner:
                    spot = (2 * ((r + owner) % 2) + share) % (ncol // shares) * shares + share
                    source = spot if spot in free[share] else free[share][0]
                    free[share].remove(source)
                    pairs.append((owner * ncol + source, r * ncol + owner * shares + share))
    return pairs


def body(
    atom_feat,
    atom_token,
    window_start,
    token_cond,
    token_mask,
    pair,
    enc_in,
    enc_out,
    pool_weight,
    tok_in,
    tok_out,
    pair_weight,
    trans_in,
    trans_out,
    tok_atom,
    dec_in,
    dec_out,
    pos_out,
):
    nrow, ncol = lax.axis_size("row"), lax.axis_size("col")
    everyone = ("row", "col")
    count = nrow * ncol
    me_row, me_col = lax.axis_index("row"), lax.axis_index("col")
    me = me_row * ncol + me_col
    rows, width = token_cond.shape
    cols = pair.shape[1]
    heads = pair_weight.shape[2]
    own = rows // ncol
    atoms, afeat = atom_feat.shape
    natom = atoms * count
    nblk = atoms // QB

    hid = trans_out.shape[1]
    packed = call(
        pack_kernel,
        [jax.ShapeDtypeStruct((3 * hid, width), BF16)] * BLOCKS,
        jnp.swapaxes(trans_in, 2, 3),
        trans_out,
        grant=60,
        moved=12 * trans_out.size,
    )
    trans = [lax.all_gather(part, "col") for part in packed]

    share = me_col % (rows // cols)
    start = me_col * cols
    place = jnp.stack(
        [me, me_col, share, start // rows, me_row, start, jnp.sum(token_mask)]
        + [(me + step) // ncol * rows for step in (-1, 0, 1)]
    )

    local_token = atom_token - me_row * rows
    first_block = me * nblk
    shift = window_start - QB * (first_block + jnp.arange(nblk, dtype=jnp.int32)) + HALO
    tail = jnp.stack([local_token, jnp.pad(shift, (0, atoms - nblk))])
    tail = jnp.pad(tail, ((0, EXTRA - 2), (0, afeat - atoms))).astype(BF16)
    feat = jnp.concatenate([atom_feat, tail], 0)
    up = [(i, i + 1) for i in range(count - 1)]
    prev = lax.ppermute(feat, everyone, up)
    after = lax.ppermute(feat, everyone, [(b, a) for a, b in up])

    ext, copies = call(
        functools.partial(encoder_kernel, natom),
        [
            jax.ShapeDtypeStruct((atoms + 2 * HALO, afeat), BF16),
            jax.ShapeDtypeStruct((ncol, atoms + EXTRA, afeat), BF16),
        ],
        feat,
        prev,
        after,
        enc_in,
        enc_out,
        scalars=(place,),
        flops=10**8,
        moved=10**6,
    )
    both = lax.all_to_all(copies, "col", 0, 0)

    span = -(-cols // 128) * 128
    weights = jnp.swapaxes(pair_weight, 1, 2).reshape(BLOCKS * heads, -1)
    step = 24
    bias = pl.pallas_call(
        bias_kernel,
        grid=(rows // step,),
        out_shape=jax.ShapeDtypeStruct((rows, BLOCKS * heads, span), F32),
        in_specs=[
            pl.BlockSpec((step, cols, pair.shape[2]), lambda i: (i, 0, 0)),
            pl.BlockSpec(weights.shape, lambda i: (0, 0)),
        ],
        out_specs=pl.BlockSpec((step, BLOCKS * heads, span), lambda i: (i, 0, 0)),
        compiler_params=pltpu.CompilerParams(vmem_limit_bytes=56 * MIB),
        cost_estimate=pl.CostEstimate(flops=4 * 10**9, bytes_accessed=8 * 10**6, transcendentals=0),
    )(pair, weights)

    act, xn, send = call(
        pool_kernel,
        [
            jax.ShapeDtypeStruct((own, width), F32),
            jax.ShapeDtypeStruct((rows, width), BF16),
            jax.ShapeDtypeStruct((cols, width), BF16),
        ],
        both,
        pool_weight,
        token_cond,
        scalars=(place,),
        flops=10**9,
        moved=10**6,
    )

    pairs = key_source(rows, cols)
    for layer in range(BLOCKS):
        if layer:
            send = lax.dynamic_slice_in_dim(xn, share * cols, cols, 0)
        came = lax.ppermute(send, everyone, pairs)
        message = call(
            functools.partial(attention_kernel, layer),
            jax.ShapeDtypeStruct((rows, width + span), BF16),
            xn,
            send,
            came,
            bias,
            scalars=(place,),
            far=(tok_in,),
            scratch=[pltpu.VMEM((width, width), BF16)] * 3 + [pltpu.SemaphoreType.DMA((3,))],
            grant=54,
            flops=10**9,
            moved=8 * 10**6,
        )
        message = lax.all_to_all(message.reshape(ncol, own, -1), "col", 0, 0)
        last = layer == BLOCKS - 1
        act, copies = finish(
            layer,
            message,
            act,
            tok_in,
            tok_out,
            trans[layer],
            heads,
            count if last else ncol,
            tok_atom if last else None,
        )
        if not last:
            xn = lax.all_to_all(copies, "col", 0, 0).reshape(rows, width)
    proj = lax.all_to_all(copies, everyone, 0, 0).reshape(count * own, afeat)

    return call(
        functools.partial(decoder_kernel, natom),
        jax.ShapeDtypeStruct((pos_out.shape[0], atoms), F32),
        ext,
        feat,
        prev,
        after,
        proj,
        dec_in,
        dec_out,
        pos_out,
        scalars=(place,),
        flops=10**8,
        moved=10**6,
    )


def solution(mesh):
    in_specs = (
        P(("row", "col"), None),
        P(("row", "col")),
        P(("row", "col")),
        P("row", None),
        P(),
        P("row", "col", None),
        P(),
        P(),
        P(),
        P(),
        P(),
        P(),
        P(None, None, None, "col"),
        P(None, "col", None),
        P(),
        P(),
        P(),
        P(),
    )
    out_specs = P(None, ("row", "col"))
    return jax.shard_map(body, mesh=mesh, in_specs=in_specs, out_specs=out_specs, check_vma=False)
```

time: 472 us -> 157 us (0.33)
  the two profiles are of different devices: /device:TPU:24 before, /device:TPU:1 now
where the time goes in v1:
time: 157 us; the launch traced here: 155 us
  Pallas kernels  49.9 us (32%)
  blocking collectives  40.3 us (26%)
  starting transfers between devices  25.8 us (16%)
  waiting for transfers between devices  16.6 us (11%)
  between operations  13.6 us (9%)
  local copies, waits for them, and re-layouts  5.85 us (4%)
  other arithmetic  3.49 us (2%)
    pallas_call x8, Pallas kernels, call(): pl.pallas_call(kernel, out_shape=outs, in_specs=[smem] * len(scalars) + [...  42 us
    all_to_all x1, blocking collectives, body(): proj = lax.all_to_all(copies, everyone, 0, 0).reshape(count * own, afeat)  15.5 us
    all_to_all x1, blocking collectives, body(): message = lax.all_to_all(message.reshape(ncol, own, -1), 'col', 0, 0)  12.6 us
    all_to_all x1, blocking collectives, body(): both = lax.all_to_all(copies, 'col', 0, 0)  12.2 us
    all_to_all x1, starting transfers between devices, body(): message = lax.all_to_all(message.reshape(ncol, own, -1), 'col', 0, 0)  8.39 us
    pallas_call x1, Pallas kernels, body(): pl.pallas_call(bias_kernel, grid=(rows // step,), out_shape=jax.ShapeDtyp...  7.92 us
    ppermute x2, starting transfers between devices, body(): came = lax.ppermute(send, everyone, pairs)  6.73 us
    all_to_all x1, waiting for transfers between devices, body(): xn = lax.all_to_all(copies, 'col', 0, 0).reshape(rows, width)  5.82 us
  transfers between devices with their start and end apart: 8, of which 5 were waited for; matrix products, arithmetic and copies ran while one was open for 3% of the time, Pallas kernels for 23%

profile of v1, /device:TPU:1, one launch (start us, length us, event | category | flops | bytes accessed | tf_op | source)
XLA Modules:
  0.0 155.5 jit_solution(11685459397010431036)
XLA Ops:
  6.5 0.0 all-gather.5.cloned.1.call-start
  6.5 2.8 %shard_map.176 = (bf16[576,768]{1,0:T(8,128)(2,1)}, bf16[576,768]{1,0:T(8,128)(2,1)}) custom-call(bf16[2,2,192,768]{3,2,1,0:T(8,128)(2,1)} %bitcast.31, bf16[2,192,768]{2,1,0:T(8,128)(2,1)} %second.1), custom_call_target="tpu_custom_call" | custom-call | bytes 3538944 | tf_op jit(solution)/shard_map/pallas_call | solution.py:26
  9.3 0.0 all-gather.5.cloned.1.call-update
  9.3 0.0 all-gather.7.cloned.1.call-start
  9.4 0.7 all-gather.7.cloned.1.call-update
  10.1 0.7 add_convert_fusion
  10.8 0.7 convert_bitcast_fusion
  11.4 0.8 pad_maximum_fusion.own_ref
  12.2 4.5 %collective-permute-start = (bf16[144,128]{1,0:T(8,128)(2,1)S(1)}, bf16[144,128]{1,0:T(8,128)(2,1)S(1)}, u32[]{:S(2)}, u32[]{:S(2)}) collective-permute-start(bf16[144,128]{1,0:T(8,128)(2,1)S(1)} %pad_maximum_fusion.own_ref), channel_id=1, source_target_pairs={{0,1},{1,2},{2,3},{3,4},{4,5},{5,6},{6,7},{7,8},{8,9},{9,10},{10,1... | collective-permute-start | bytes 110600 | tf_op jit(solution)/shard_map/ppermute | solution.py:440
  16.7 1.9 %collective-permute-start.1 = (bf16[144,128]{1,0:T(8,128)(2,1)S(1)}, bf16[144,128]{1,0:T(8,128)(2,1)S(1)}, u32[]{:S(2)}, u32[]{:S(2)}) collective-permute-start(bf16[144,128]{1,0:T(8,128)(2,1)S(1)} %pad_maximum_fusion.own_ref), channel_id=1, source_target_pairs={{1,0},{2,1},{3,2},{4,3},{5,4},{6,5},{7,6},{8,7},{9,8},{10,9},{11,1... | collective-permute-start | bytes 110600 | tf_op jit(solution)/shard_map/ppermute | solution.py:441
  18.7 1.4 reduce_sum.9
  20.1 0.8 stack.55.place
  20.8 0.0 collective-permute-done.prev_ref
  20.8 1.2 collective-permute-done.1.next_ref
  22.1 0.9 copy-done.10
  23.0 0.8 copy-done.11
  23.8 1.8 %shard_map.172 = (bf16[256,128]{1,0:T(8,128)(2,1)S(1)}, bf16[8,144,128]{2,1,0:T(8,128)(2,1)S(1)}) custom-call(s32[10]{0:T(128)S(1)} %stack.55.place, bf16[144,128]{1,0:T(8,128)(2,1)S(1)} %pad_maximum_fusion.own_ref, bf16[144,128]{1,0:T(8,128)(2,1)S(1)} %collective-permute-done.prev_ref, bf16[144,128]{1,0:T(8,128)(2,1)S(1)} %collective-permute-done.1.next_ref, ...), custom_call_target="tpu_custom_call" | custom-call | flops 100000000 | bytes 1000000 | tf_op jit(solution)/shard_map/pallas_call | solution.py:26
  25.6 12.2 %all_to_all.25.both_ref = bf16[8,144,128]{2,1,0:T(8,128)(2,1)S(1)} all-to-all(bf16[8,144,128]{2,1,0:T(8,128)(2,1)S(1)} %get-tuple-element.16), channel_id=1, replica_groups=mesh['row'=4,'col'=8] {'col'}, dimensions={0} | all-to-all | bytes 589824 | tf_op jit(solution)/shard_map/all_to_all | solution.py:458
  37.8 0.0 copy-done.9
  37.8 0.0 copy-done.8
  37.8 1.8 %shard_map.173 = (f32[24,768]{1,0:T(8,128)S(1)}, bf16[192,768]{1,0:T(8,128)(2,1)S(1)}, bf16[96,768]{1,0:T(8,128)(2,1)S(1)}) custom-call(s32[10]{0:T(128)S(1)} %stack.55.place, bf16[8,144,128]{2,1,0:T(8,128)(2,1)S(1)} %all_to_all.25.both_ref, bf16[128,768]{1,0:T(8,128)(2,1)S(1)} %copy-done.9, bf16[192,768]{1,0:T(8,128)(2,1)S(1)} %copy-done.8), custom_call_target="tpu_custom_call" | custom-call | flops 1000000000 | bytes 1000000 | tf_op jit(solution)/shard_map/pallas_call | solution.py:26
  39.6 0.0 copy-start
  39.7 0.7 copy-done
  40.4 0.6 copy-done.3
  41.0 3.7 %collective-permute-start.2 = (bf16[96,768]{1,0:T(8,128)(2,1)S(1)}, bf16[96,768]{1,0:T(8,128)(2,1)S(1)}, u32[]{:S(2)}, u32[]{:S(2)}) collective-permute-start(bf16[96,768]{1,0:T(8,128)(2,1)S(1)} %get-tuple-element.18.here_ref), channel_id=1, source_target_pairs={{4,8},{7,9},{0,16},{3,17},{2,24},{1,25},{12,2},{15,3},{8,18},{9,19... | collective-permute-start | bytes 442376 | tf_op jit(solution)/shard_map/ppermute | solution.py:495
  44.7 7.9 %shard_map.174.bias_ref = f32[192,32,128]{2,1,0:T(8,128)} custom-call(bf16[192,96,128]{2,1,0:T(8,128)(2,1)} %pair_ref.1, bf16[32,128]{1,0:T(8,128)(2,1)} %bitcast.32), custom_call_target="tpu_custom_call" | custom-call | flops 4000000000 | bytes 8000000 | tf_op jit(solution)/shard_map/pallas_call | solution.py:463
  52.6 0.0 copy-done.5
  52.6 0.0 copy-done.1
  52.6 0.0 collective-permute-done.2.came_ref
  52.6 0.0 copy-start.15
  52.7 0.6 copy-done.15
  53.3 8.1 %shard_map.175 = bf16[192,896]{1,0:T(8,128)(2,1)} custom-call(s32[10]{0:T(128)} %copy-done.5, bf16[192,768]{1,0:T(8,128)(2,1)} %copy-done, bf16[96,768]{1,0:T(8,128)(2,1)} %copy-done.1, bf16[96,768]{1,0:T(8,128)(2,1)} %copy-done.15, f32[192,32,128]{2,1,0:T(8,128)} %shard_map.174.bias_ref, bf16[2,4,768,768]{3,2,1,0:T(8,128)(2,1)} %refs_1_.3), custom_call_target="tpu_custom_call" | custom-call | flops 1000000000 | bytes 8000000 | tf_op jit(solution)/shard_map/pallas_call | solution.py:26
  61.4 12.6 %all_to_all.26.message = bf16[8,24,896]{2,1,0:T(8,128)(2,1)} all-to-all(bf16[8,24,896]{2,1,0:T(8,128)(2,1)} %bitcast.30), channel_id=1, replica_groups=mesh['row'=4,'col'=8] {'col'}, dimensions={0} | all-to-all | bytes 688128 | tf_op jit(solution)/shard_map/all_to_all | solution.py:510
  73.9 8.3 %shard_map.177 = (f32[24,768]{1,0:T(8,128)}, bf16[8,24,768]{2,1,0:T(8,128)(2,1)}) custom-call(bf16[8,24,896]{2,1,0:T(8,128)(2,1)} %all_to_all.26.message, f32[24,768]{1,0:T(8,128)} %copy-done.3, bf16[2,4,768,768]{3,2,1,0:T(8,128)(2,1)} %refs_1_.3, bf16[2,768,768]{2,1,0:T(8,128)(2,1)} %refs_2_.1, bf16[8,576,768]{2,1,0:T(8,128)(2,1)} %bitcast.26), custom_call_target="tpu_custom_call" | custom-call | flops 169869312 | bytes 7077888 | tf_op jit(solution)/shard_map/pallas_call | solution.py:26
  82.2 4.2 %all-to-all-start.2 = ((bf16[8,24,768]{2,1,0:T(8,128)(2,1)}), bf16[8,24,768]{2,1,0:T(8,128)(2,1)S(1)}, u32[]{:S(2)}, u32[]{:S(2)}) async-start(bf16[8,24,768]{2,1,0:T(8,128)(2,1)} %get-tuple-element.21), calls=%async_computation.2 | async-start | bytes 589824 | tf_op jit(solution)/shard_map/all_to_all | solution.py:524
  86.4 5.8 %all-to-all-done.2 = bf16[8,24,768]{2,1,0:T(8,128)(2,1)S(1)} async-done(((bf16[8,24,768]{2,1,0:T(8,128)(2,1)}), bf16[8,24,768]{2,1,0:T(8,128)(2,1)S(1)}, u32[]{:S(2)}, u32[]{:S(2)}) %all-to-all-start.2) | async-done | bytes 294944 | tf_op jit(solution)/shard_map/all_to_all | solution.py:524
  92.3 3.0 %collective-permute-start.3 = (bf16[96,768]{1,0:T(8,128)(2,1)S(1)}, bf16[96,768]{1,0:T(8,128)(2,1)S(1)}, u32[]{:S(2)}, u32[]{:S(2)}) collective-permute-start(bf16[96,768]{1,0:T(8,128)(2,1)S(1)} %constant_dynamic-slice_fusion.here_ref), channel_id=1, source_target_pairs={{4,8},{7,9},{0,16},{3,17},{2,24},{1,25},{12,2},{15,3},{8,18},{9,19... | collective-permute-start | bytes 442376 | tf_op jit(solution)/shard_map/ppermute | solution.py:495
  95.3 2.7 %collective-permute-done.3.came_ref = bf16[96,768]{1,0:T(8,128)(2,1)S(1)} collective-permute-done((bf16[96,768]{1,0:T(8,128)(2,1)S(1)}, bf16[96,768]{1,0:T(8,128)(2,1)S(1)}, u32[]{:S(2)}, u32[]{:S(2)}) %collective-permute-start.3) | collective-permute-done | bytes 147488 | tf_op jit(solution)/shard_map/ppermute | solution.py:495
  98.0 0.7 copy-done.16
  98.7 8.1 %shard_map.178 = bf16[192,896]{1,0:T(8,128)(2,1)} custom-call(s32[10]{0:T(128)} %copy-done.5, bf16[192,768]{1,0:T(8,128)(2,1)} %bitcast.28, bf16[96,768]{1,0:T(8,128)(2,1)} %copy-done.14, bf16[96,768]{1,0:T(8,128)(2,1)} %copy-done.16, f32[192,32,128]{2,1,0:T(8,128)} %shard_map.174.bias_ref, bf16[2,4,768,768]{3,2,1,0:T(8,128)(2,1)} %refs_1_.3), custom_call_target="tpu_custom_call" | custom-call | flops 1000000000 | bytes 8000000 | tf_op jit(solution)/shard_map/pallas_call | solution.py:26
  106.8 8.4 %all-to-all-start.3 = ((bf16[8,24,896]{2,1,0:T(8,128)(2,1)}), bf16[8,24,896]{2,1,0:T(8,128)(2,1)S(1)}, u32[]{:S(2)}, u32[]{:S(2)}) async-start(bf16[8,24,896]{2,1,0:T(8,128)(2,1)} %bitcast.29), calls=%async_computation.3 | async-start | bytes 688128 | tf_op jit(solution)/shard_map/all_to_all | solution.py:510
  115.2 0.8 all-gather.7.cloned.1.call-done
  115.9 5.3 %all-to-all-done.3.message = bf16[8,24,896]{2,1,0:T(8,128)(2,1)S(1)} async-done(((bf16[8,24,896]{2,1,0:T(8,128)(2,1)}), bf16[8,24,896]{2,1,0:T(8,128)(2,1)S(1)}, u32[]{:S(2)}, u32[]{:S(2)}) %all-to-all-start.3) | async-done | bytes 344096 | tf_op jit(solution)/shard_map/all_to_all | solution.py:510
  121.2 0.7 copy-done.13
  122.0 8.5 %shard_map.179 = (f32[24,768]{1,0:T(8,128)}, bf16[32,24,128]{2,1,0:T(8,128)(2,1)}) custom-call(bf16[8,24,896]{2,1,0:T(8,128)(2,1)} %copy-done.13, f32[24,768]{1,0:T(8,128)} %get-tuple-element.22.act_ref, bf16[768,128]{1,0:T(8,128)(2,1)} %refs_0_.3, bf16[2,4,768,768]{3,2,1,0:T(8,128)(2,1)} %refs_1_.3, bf16[2,768,768]{2,1,0:T(8,128)(2,1)} %refs_2_.1, ...), custom_call_target="tpu_custom_call" | custom-call | flops 169869312 | bytes 7077888 | tf_op jit(solution)/shard_map/pallas_call | solution.py:26
  130.5 15.5 %all_to_all.27 = bf16[32,24,128]{2,1,0:T(8,128)(2,1)S(1)} all-to-all(bf16[32,24,128]{2,1,0:T(8,128)(2,1)} %get-tuple-element.24), channel_id=1, replica_groups=mesh['row'=4,'col'=8] {'row','col'}, dimensions={0} | all-to-all | bytes 393216 | tf_op jit(solution)/shard_map/all_to_all | solution.py:525
  146.0 0.0 copy-done.4
  146.0 2.6 %shard_map.180 = f32[3,128]{1,0:T(4,128)} custom-call(s32[10]{0:T(128)S(1)} %copy-done.6, bf16[256,128]{1,0:T(8,128)(2,1)S(1)} %get-tuple-element.15.x1_ref, bf16[144,128]{1,0:T(8,128)(2,1)S(1)} %pad_maximum_fusion.own_ref, bf16[144,128]{1,0:T(8,128)(2,1)S(1)} %collective-permute-done.prev_ref, bf16[144,128]{1,0:T(8,128)(2,1)S(1)} %collective-permute-done.1.next_ref, ...), custom_call_target="tpu_custom_call" | custom-call | flops 100000000 | bytes 1000000 | tf_op jit(solution)/shard_map/pallas_call | solution.py:26
  (24 shorter events, 0.1 us)
Async XLA Ops:
  6.5 31.3 %copy-start.9 = (bf16[128,768]{1,0:T(8,128)(2,1)S(1)}, bf16[128,768]{1,0:T(8,128)(2,1)}, u32[]{:S(2)}) copy-start(bf16[128,768]{1,0:T(8,128)(2,1)} %weight.1) | copy-start | bytes 589828
  6.5 31.3 %copy-start.8 = (bf16[192,768]{1,0:T(8,128)(2,1)S(1)}, bf16[192,768]{1,0:T(8,128)(2,1)}, u32[]{:S(2)}) copy-start(bf16[192,768]{1,0:T(8,128)(2,1)} %cond.1) | copy-start | bytes 884740
  6.5 67.4 %all-gather.5.cloned.1.call-start = ((), (), s32[]{:S(2)}) async-start(), calls=%async_computation.5 | async-start | bytes 7962624 | tf_op jit(solution)/shard_map/all_gather | solution.py:424
  9.3 106.6 %all-gather.7.cloned.1.call-start = ((), (), s32[]{:S(2)}) async-start(), calls=%async_computation.6 | async-start | bytes 7962624 | tf_op jit(solution)/shard_map/all_gather | solution.py:424
  12.2 8.6 %collective-permute-start = (bf16[144,128]{1,0:T(8,128)(2,1)S(1)}, bf16[144,128]{1,0:T(8,128)(2,1)S(1)}, u32[]{:S(2)}, u32[]{:S(2)}) collective-permute-start(bf16[144,128]{1,0:T(8,128)(2,1)S(1)} %pad_maximum_fusion.own_ref), channel_id=1, source_target_pairs={{0,1},{1,2},{2,3},{3,4},{4,5},{5,6},{6,7},{7,8},{8,9},{9,10},{10,1... | collective-permute-start | bytes 110600 | tf_op jit(solution)/shard_map/ppermute | solution.py:440
  16.7 5.4 %collective-permute-start.1 = (bf16[144,128]{1,0:T(8,128)(2,1)S(1)}, bf16[144,128]{1,0:T(8,128)(2,1)S(1)}, u32[]{:S(2)}, u32[]{:S(2)}) collective-permute-start(bf16[144,128]{1,0:T(8,128)(2,1)S(1)} %pad_maximum_fusion.own_ref), channel_id=1, source_target_pairs={{1,0},{2,1},{3,2},{4,3},{5,4},{6,5},{7,6},{8,7},{9,8},{10,9},{11,1... | collective-permute-start | bytes 110600 | tf_op jit(solution)/shard_map/ppermute | solution.py:441
  20.8 31.8 %copy-start.5 = (s32[10]{0:T(128)}, s32[10]{0:T(128)S(1)}, u32[]{:S(2)}) copy-start(s32[10]{0:T(128)S(1)} %stack.55.place) | copy-start | bytes 124
  22.1 0.9 copy-start.10
  23.0 0.8 copy-start.11
  39.6 0.7 copy-start
  40.4 0.6 copy-start.3
  41.0 11.6 %copy-start.1 = (bf16[96,768]{1,0:T(8,128)(2,1)}, bf16[96,768]{1,0:T(8,128)(2,1)S(1)}, u32[]{:S(2)}) copy-start(bf16[96,768]{1,0:T(8,128)(2,1)S(1)} %get-tuple-element.18.here_ref) | copy-start | bytes 442372
  41.0 11.6 %collective-permute-start.2 = (bf16[96,768]{1,0:T(8,128)(2,1)S(1)}, bf16[96,768]{1,0:T(8,128)(2,1)S(1)}, u32[]{:S(2)}, u32[]{:S(2)}) collective-permute-start(bf16[96,768]{1,0:T(8,128)(2,1)S(1)} %get-tuple-element.18.here_ref), channel_id=1, source_target_pairs={{4,8},{7,9},{0,16},{3,17},{2,24},{1,25},{12,2},{15,3},{8,18},{9,19... | collective-permute-start | bytes 442376 | tf_op jit(solution)/shard_map/ppermute | solution.py:495
  52.6 0.7 copy-start.15
  82.2 10.0 %all-to-all-start.2 = ((bf16[8,24,768]{2,1,0:T(8,128)(2,1)}), bf16[8,24,768]{2,1,0:T(8,128)(2,1)S(1)}, u32[]{:S(2)}, u32[]{:S(2)}) async-start(bf16[8,24,768]{2,1,0:T(8,128)(2,1)} %get-tuple-element.21), calls=%async_computation.2 | async-start | bytes 589824 | tf_op jit(solution)/shard_map/all_to_all | solution.py:524
  92.3 5.8 %copy-start.12 = (bf16[8,24,768]{2,1,0:T(8,128)(2,1)}, bf16[8,24,768]{2,1,0:T(8,128)(2,1)S(1)}, u32[]{:S(2)}) copy-start(bf16[8,24,768]{2,1,0:T(8,128)(2,1)S(1)} %all-to-all-done.2) | copy-start | bytes 884740
  92.3 5.8 %copy-start.14 = (bf16[96,768]{1,0:T(8,128)(2,1)}, bf16[96,768]{1,0:T(8,128)(2,1)S(1)}, u32[]{:S(2)}) copy-start(bf16[96,768]{1,0:T(8,128)(2,1)S(1)} %constant_dynamic-slice_fusion.here_ref) | copy-start | bytes 442372
  92.3 5.8 %collective-permute-start.3 = (bf16[96,768]{1,0:T(8,128)(2,1)S(1)}, bf16[96,768]{1,0:T(8,128)(2,1)S(1)}, u32[]{:S(2)}, u32[]{:S(2)}) collective-permute-start(bf16[96,768]{1,0:T(8,128)(2,1)S(1)} %constant_dynamic-slice_fusion.here_ref), channel_id=1, source_target_pairs={{4,8},{7,9},{0,16},{3,17},{2,24},{1,25},{12,2},{15,3},{8,18},{9,19... | collective-permute-start | bytes 442376 | tf_op jit(solution)/shard_map/ppermute | solution.py:495
  98.0 0.7 copy-start.16
  106.8 14.4 %all-to-all-start.3 = ((bf16[8,24,896]{2,1,0:T(8,128)(2,1)}), bf16[8,24,896]{2,1,0:T(8,128)(2,1)S(1)}, u32[]{:S(2)}, u32[]{:S(2)}) async-start(bf16[8,24,896]{2,1,0:T(8,128)(2,1)} %bitcast.29), calls=%async_computation.3 | async-start | bytes 688128 | tf_op jit(solution)/shard_map/all_to_all | solution.py:510
  121.2 0.7 copy-start.13
  121.9 24.0 %copy-start.2 = (bf16[4,128,128]{2,1,0:T(8,128)(2,1)S(1)}, bf16[4,128,128]{2,1,0:T(8,128)(2,1)}, u32[]{:S(2)}) copy-start(bf16[4,128,128]{2,1,0:T(8,128)(2,1)} %w_in.7) | copy-start | bytes 393220
  122.0 24.0 %copy-start.4 = (bf16[128,128]{1,0:T(8,128)(2,1)S(1)}, bf16[128,128]{1,0:T(8,128)(2,1)}, u32[]{:S(2)}) copy-start(bf16[128,128]{1,0:T(8,128)(2,1)} %w_out.3) | copy-start | bytes 98308
  122.0 24.0 %copy-start.6 = (s32[10]{0:T(128)S(1)}, s32[10]{0:T(128)}, u32[]{:S(2)}) copy-start(s32[10]{0:T(128)} %copy-done.5) | copy-start | bytes 124
  122.0 24.0 %copy-start.7 = (bf16[3,128]{1,0:T(4,128)(2,1)S(1)}, bf16[3,128]{1,0:T(4,128)(2,1)}, u32[]{:S(2)}) copy-start(bf16[3,128]{1,0:T(4,128)(2,1)} %pos.1) | copy-start | bytes 2308
Sparse Core Ops, SparseCore 0:
  9.5 53.0 all-gather.4
  64.4 51.4 all-gather.6

commit v2 on v1

--- a/solution.py
+++ b/solution.py
@@ -55,6 +55,11 @@
 
 def iota(shape, dim):
     return lax.broadcasted_iota(jnp.int32, shape, dim)
+
+
+def device():
+    row, col = lax.axis_index("row"), lax.axis_index("col")
+    return row, col, row * lax.axis_size("col") + col
 
 
 def window_mask(shifts, first, natom, nkeys):
@@ -90,7 +95,7 @@
     return [tail[1:2, k : k + 1].astype(jnp.int32) for k in lanes]
 
 
-def encoder_kernel(natom, place, own_ref, prev_ref, next_ref, w_in, w_out, ext_ref, all_ref):
+def encoder_kernel(natom, own_ref, prev_ref, next_ref, w_in, w_out, ext_ref, all_ref):
     rows = own_ref.shape[0] - EXTRA
     nblk = rows // QB
     half = HALO // QB
@@ -106,7 +111,7 @@
         + shifts_of(own_ref, range(nblk))
         + shifts_of(next_ref, range(half))
     )
-    first = place[0] * rows - rows
+    first = device()[2] * rows - rows
     for part in range(2):
         mine = slice(part * rows, (part + 1) * rows)
         seen = slice(part * rows, (part + 2) * rows)
@@ -123,7 +128,7 @@
         all_ref[j, rows:] = tail
 
 
-def pool_kernel(place, both_ref, weight, cond, act_ref, xn_ref, send_ref):
+def pool_kernel(both_ref, weight, cond, act_ref, xn_ref, send_ref):
     count, rows = both_ref.shape[0], both_ref.shape[1] - EXTRA
     tokens = cond.shape[0]
     sums = jnp.zeros(cond.shape, F32)
@@ -144,21 +149,24 @@
     cols = send_ref.shape[0]
     part = xn[:cols]
     for k in range(1, tokens // cols):
-        part = jnp.where(place[2] == k, xn[k * cols : (k + 1) * cols], part)
+        part = jnp.where(device()[1] % (tokens // cols) == k, xn[k * cols : (k + 1) * cols], part)
     send_ref[...] = part.astype(BF16)
     own = act_ref.shape[0]
+    col = device()[1]
     mine = act[:own]
     for c in range(1, tokens // own):
-        mine = jnp.where(place[1] == c, act[c * own : (c + 1) * own], mine)
+        mine = jnp.where(col == c, act[c * own : (c + 1) * own], mine)
     act_ref[...] = mine
 
 
-def decoder_kernel(natom, place, x1_ref, own_ref, prev_ref, next_ref, proj, w_in, w_out, pos, out):
+def decoder_kernel(natom, row_tokens, x1_ref, own_ref, prev_ref, next_ref, proj, w_in, w_out, pos, out):
     rows = own_ref.shape[0] - EXTRA
     tokens = proj.shape[0]
+    me = device()[2]
     spread = []
     for k, ref in enumerate((prev_ref, own_ref, next_ref)):
-        spot = ref[rows:].astype(F32)[0:1].astype(jnp.int32) + place[7 + k]
+        spot = ref[rows:].astype(F32)[0:1].astype(jnp.int32)
+        spot = spot + (me + k - 1) // lax.axis_size("col") * row_tokens
         onehot = (iota((tokens, rows), 0) == spot).astype(F32).astype(BF16)
         spread.append(dot_tn(onehot, proj[...]))
     spread = jnp.concatenate([spread[0][rows - HALO :], spread[1], spread[2][:HALO]], 0)
@@ -170,26 +178,41 @@
     query = dot(qn, w_in[0]).astype(BF16)
     gate = dot(qn, w_in[3])
     shifts = shifts_of(own_ref, range(rows // QB))
-    mask = window_mask(shifts, place[0] * rows - HALO, natom, 2 * rows)
+    mask = window_mask(shifts, me * rows - HALO, natom, 2 * rows)
     third = attend(qx, qn, gate, query, keys, vals, mask, w_out[...])
     out[...] = dot_nt(pos[...], normed(third).astype(BF16))
 
 
-def pack_kernel(first, second, *outs):
+def pack_kernel(row_tokens, starts, first, second, feat, token, *outs):
+    out, own = outs
     hid = second.shape[1]
-    for layer, out in enumerate(outs):
-        out[:hid] = first[layer, 0]
-        out[hid : 2 * hid] = first[layer, 1]
-        out[2 * hid :] = second[layer]
-
-
-def bias_kernel(pair_ref, weight, out_ref):
+    for layer in range(BLOCKS):
+        out[layer, :hid] = first[layer, 0]
+        out[layer, hid : 2 * hid] = first[layer, 1]
+        out[layer, 2 * hid :] = second[layer]
+    rows, width = feat.shape
+    row, _, me = device()
+    nblk = starts.shape[0]
+    lane = iota((EXTRA, width), 1)
+    line = iota((EXTRA, width), 0)
+    tail = jnp.where(line == 0, token[...] - row * row_tokens, 0)
+    for k in range(nblk):
+        shift = starts[k] - QB * (me * nblk + k) + HALO
+        tail = jnp.where((line == 1) & (lane == k), shift, tail)
+    own[:rows] = feat[...]
+    own[rows:] = tail.astype(F32).astype(BF16)
+
+
+def bias_kernel(pair_ref, weight, *outs):
     rows, cols, _ = pair_ref.shape
-    pad = out_ref.shape[2] - cols
+    _, heads, pad = outs[0].shape
+    pad = pad - cols
 
     for q in range(rows):
         bias = dot_nt(weight[...], pair_ref[q])
-        out_ref[q] = jnp.concatenate([bias, jnp.zeros((bias.shape[0], pad), F32)], 1)
+        bias = jnp.concatenate([bias, jnp.zeros((bias.shape[0], pad), F32)], 1)
+        for layer, out in enumerate(outs):
+            out[q] = bias[layer * heads : (layer + 1) * heads]
 
 
 def prepare(sources, targets, sems):
@@ -199,39 +222,46 @@
     ]
 
 
-def attention_kernel(
-    layer,
-    place,
-    xn_ref,
-    here_ref,
-    came_ref,
-    bias_ref,
-    w_in,
-    out_ref,
-    w_query,
-    w_key,
-    w_val,
-    sems,
-):
-    fetches = prepare([w_in.at[layer, k] for k in range(3)], [w_query, w_key, w_val], sems)
-    fetches[0].start()
-    fetches[1].start()
-    rows, width = xn_ref.shape
+def query_kernel(layer, xn_ref, w_in, query, w_query, sems):
+    (copy,) = prepare([w_in.at[layer, 0]], [w_query], sems)
+    copy.start()
+    copy.wait()
+    query[...] = dot(xn_ref[...], w_query[...]).astype(BF16)
+
+
+def attention_kernel(layer, mask_ref, *refs):
+    far, out_ref, near, sems = refs[:5], refs[5], refs[6:-1], refs[-1]
+    query, here, came, bias, w_in = far
+    fetches = prepare([here, came, w_in.at[layer, 1], w_in.at[layer, 2], query, bias], near, sems)
+    here_ref, came_ref, w_key, w_val, query, bias_ref = near
+    for copy in fetches:
+        copy.start()
+    rows, width = query.shape
     cols = here_ref.shape[0]
-    heads = bias_ref.shape[1] // BLOCKS
+    heads = bias_ref.shape[1]
     hsize = width // heads
     span = bias_ref.shape[2]
-    key_xn = jnp.where(place[3] == place[4], here_ref[...].astype(F32), came_ref[...].astype(F32))
+    row, col, _ = device()
+    mine = col * cols // rows == row
+    fetches[0].wait()
+    fetches[1].wait()
+    key_xn = jnp.where(mine, here_ref[...].astype(F32), came_ref[...].astype(F32))
     key_xn = jnp.concatenate([key_xn, jnp.zeros((span - cols, width), F32)], 0).astype(BF16)
-    fetches[0].wait()
-    fetches[2].start()
-    query = dot(xn_ref[...], w_query[...]).astype(BF16)
-    fetches[1].wait()
+    fetches[2].wait()
     keys = dot(key_xn, w_key[...]).astype(BF16)
-    fetches[2].wait()
+    fetches[3].wait()
     vals = dot(key_xn, w_val[...]).astype(BF16)
-    valid = iota((1, span), 1) + place[5] < place[6]
+    tokens = mask_ref.shape[0]
+    count = jnp.int32(0)
+    for bit in range(tokens.bit_length() - 1, -1, -1):
+        longer = count + (1 << bit)
+        inside = longer <= tokens
+        last = mask_ref[jnp.where(inside, longer - 1, 0)]
+        count = jnp.where(inside & (last == 1), longer, count)
+    valid = iota((1, span), 1) + col * cols < count
     valid = valid & (iota((1, span), 1) < cols)
+    fetches[4].wait()
+    fetches[5].wait()
     group = heads // 2
     part = group * hsize
     lane = iota((1, part), 1) // hsize
@@ -246,7 +276,7 @@
         probs = []
         for h in range(group):
             head = g * group + h
-            score = scores[:, h * span : (h + 1) * span] + bias_ref[:, layer * heads + head, :]
+            score = scores[:, h * span : (h + 1) * span] + bias_ref[:, head, :]
             score = jnp.where(valid, score, -1000000000.0)
             top = jnp.max(score, -1, keepdims=True)
             expd = jnp.exp(score - top)
@@ -263,29 +293,9 @@
     out_ref[:, width:] = jnp.where(spot < 3 * heads, packed, 0.0).astype(BF16)
 
 
-def finish_kernel(
-    layer,
-    heads,
-    project,
-    message,
-    act_ref,
-    *refs,
-):
-    if project:
-        tok_atom, *refs = refs
-    w_in, w_out, trans, act_out, all_ref, w_gate, w_mix, w_first, w_second, sems = refs
-    blocks, hid = w_second.shape[:2]
-    fetches = prepare(
-        [w_in.at[layer, 3], w_out.at[layer]]
-        + [trans.at[j, pl.ds(0, 2 * hid)] for j in range(blocks)]
-        + [trans.at[j, pl.ds(2 * hid, hid)] for j in range(blocks)],
-        [w_gate, w_mix]
-        + [w_first.at[j] for j in range(blocks)]
-        + [w_second.at[j] for j in range(blocks)],
-        sems,
-    )
-    firsts, seconds = fetches[2 : 2 + blocks], fetches[2 + blocks :]
-    for copy in fetches[:2]:
+def mix_kernel(layer, heads, message, act_ref, w_in, w_out, act_out, xn2_out, w_gate, w_mix, sems):
+    fetches = prepare([w_in.at[layer, 3], w_out.at[layer]], [w_gate, w_mix], sems)
+    for copy in fetches:
         copy.start()
     width = act_ref.shape[1]
     hsize = width // heads
@@ -301,32 +311,101 @@
     row = iota((span, width), 0)
     expand = (row % heads == iota((span, width), 1) // hsize) & (row < 2 * heads)
     expand = expand.astype(F32).astype(BF16)
-    attn = jnp.zeros(act_ref.shape, F32)
-    for j, weight in enumerate(weights):
+    packed = []
+    for weight in weights:
         weight = weight / whole
         high = weight.astype(BF16).astype(F32)
-        packed = jnp.where(lane < heads, high, pltpu.roll(weight - high, heads, 1))
-        packed = jnp.where(lane < 2 * heads, packed, 0.0).astype(BF16)
-        attn = attn + dot(packed, expand) * message[j, :, :width].astype(F32)
+        both = jnp.where(lane < heads, high, pltpu.roll(weight - high, heads, 1))
+        packed.append(jnp.where(lane < 2 * heads, both, 0.0))
+    spread = dot(jnp.concatenate(packed, 0).astype(BF16), expand)
+    own = act_ref.shape[0]
+    attn = jnp.zeros(act_ref.shape, F32)
+    for j in range(message.shape[0]):
+        attn = attn + spread[j * own : (j + 1) * own] * message[j, :, :width].astype(F32)
+    normal = normed(act_ref[...]).astype(BF16)
     fetches[0].wait()
-    for copy in firsts:
+    gated = (jax.nn.sigmoid(dot(normal, w_gate[...])) * attn).astype(BF16)
+    fetches[1].wait()
+    act = act_ref[...] + dot(gated, w_mix[...])
+    act_out[...] = act
+    xn2_out[...] = normed(act).astype(BF16)
+
+
+def mix(layer, message, act, w_in, w_out, heads):
+    own, width = act.shape
+    return call(
+        functools.partial(mix_kernel, layer, heads),
+        [jax.ShapeDtypeStruct((own, width), F32), jax.ShapeDtypeStruct((own, width), BF16)],
+        message,
+        act,
+        far=(w_in, w_out),
+        scratch=[pltpu.VMEM((width, width), BF16)] * 2 + [pltpu.SemaphoreType.DMA((2,))],
+        grant=60,
+        flops=4 * own * width * width,
+        moved=4 * width * width,
+    )
+
+
+def transition_kernel(layer, act_ref, xn2, *refs):
+    groups = len(refs) // 2 - 3
+    others, blocks = refs[: groups - 1], refs[groups - 1 : groups + 3]
+    outs, (w_first, w_second, sems) = refs[groups + 3 : -3], refs[-3:]
+    count, hid = w_second.shape[:2]
+    fetches = prepare(
+        [ref.at[layer, pl.ds(0, 2 * hid)] for ref in blocks]
+        + [ref.at[layer, pl.ds(2 * hid, hid)] for ref in blocks],
+        [w_first.at[j] for j in range(count)] + [w_second.at[j] for j in range(count)],
+        sems,
+    )
+    for copy in fetches:
         copy.start()
-    gate = dot(normed(act_ref[...]).astype(BF16), w_gate[...])
-    gated = (jax.nn.sigmoid(gate) * attn).astype(BF16)
-    fetches[1].wait()
-    for copy in seconds:
-        copy.start()
-    act = act_ref[...] + dot(gated, w_mix[...])
-    xn2 = normed(act).astype(BF16)
+    own = act_ref.shape[0]
+    rows = jnp.concatenate([ref[...].astype(F32) for ref in (xn2, *others)], 0).astype(BF16)
+    total = jnp.zeros((rows.shape[0], rows.shape[1]), F32)
     hidden = []
-    for j in range(blocks):
-        firsts[j].wait()
-        both = dot_nt(xn2, w_first[j])
+    for j in range(count):
+        fetches[j].wait()
+        both = dot_nt(rows, w_first[j])
         left, right = both[:, :hid], both[:, hid:]
         hidden.append((left * jax.nn.sigmoid(left) * right).astype(BF16))
-    for j in range(blocks):
-        seconds[j].wait()
-        act = act + dot(hidden[j], w_second[j])
+    for j in range(count):
+        fetches[count + j].wait()
+        total = total + dot(hidden[j], w_second[j])
+    outs[0][...] = act_ref[...] + total[:own]
+    for k, out in enumerate(outs[1:], 1):
+        out[...] = total[k * own : (k + 1) * own].astype(BF16)
+
+
+def transition(layer, act, xn2, others, weights):
+    own, width = act.shape
+    blocks = len(weights)
+    hid = weights[0].shape[1] // 3
+    return call(
+        functools.partial(transition_kernel, layer),
+        [jax.ShapeDtypeStruct((own, width), F32)]
+        + [jax.ShapeDtypeStruct((own, width), BF16)] * len(others),
+        act,
+        xn2,
+        *others,
+        far=weights,
+        scratch=[
+            pltpu.VMEM((blocks, 2 * hid, width), BF16),
+            pltpu.VMEM((blocks, hid, width), BF16),
+            pltpu.SemaphoreType.DMA((2 * blocks,)),
+        ],
+        grant=60,
+        flops=12 * own * hid * width * blocks,
+        moved=6 * hid * width * blocks,
+    )
+
+
+def close_kernel(project, act_ref, *refs):
+    *refs, act_out, all_ref = refs
+    if project:
+        *refs, tok_atom = refs
+    act = act_ref[...]
+    for ref in refs:
+        act = act + ref[...].astype(F32)
     act_out[...] = act
     normal = normed(act).astype(BF16)
     if project:
@@ -335,31 +414,21 @@
         all_ref[j] = normal
 
 
-def finish(layer, message, act, w_in, w_out, trans, heads, copies, tok_atom=None):
+def close(act, parts, copies, tok_atom):
     own, width = act.shape
-    last = width if tok_atom is None else tok_atom.shape[1]
-    blocks, packed, _ = trans.shape
-    hid = packed // 3
+    project = tok_atom is not None
+    last = tok_atom.shape[1] if project else width
     return call(
-        functools.partial(finish_kernel, layer, heads, tok_atom is not None),
+        functools.partial(close_kernel, project),
         [
             jax.ShapeDtypeStruct((own, width), F32),
             jax.ShapeDtypeStruct((copies, own, last), BF16),
         ],
-        message,
         act,
-        *(() if tok_atom is None else (tok_atom,)),
-        far=(w_in, w_out, trans),
-        scratch=[
-            pltpu.VMEM((width, width), BF16),
-            pltpu.VMEM((width, width), BF16),
-            pltpu.VMEM((blocks, 2 * hid, width), BF16),
-            pltpu.VMEM((blocks, hid, width), BF16),
-            pltpu.SemaphoreType.DMA((2 + 2 * blocks,)),
-        ],
-        grant=59,
-        flops=2 * own * trans.size,
-        moved=2 * trans.size,
+        *parts,
+        *([tok_atom] if project else []),
+        flops=10**7,
+        moved=10**6,
     )
 
 
@@ -402,8 +471,7 @@
     nrow, ncol = lax.axis_size("row"), lax.axis_size("col")
     everyone = ("row", "col")
     count = nrow * ncol
-    me_row, me_col = lax.axis_index("row"), lax.axis_index("col")
-    me = me_row * ncol + me_col
+    me_col = lax.axis_index("col")
     rows, width = token_cond.shape
     cols = pair.shape[1]
     heads = pair_weight.shape[2]
@@ -413,32 +481,27 @@
     nblk = atoms // QB
 
     hid = trans_out.shape[1]
-    packed = call(
-        pack_kernel,
-        [jax.ShapeDtypeStruct((3 * hid, width), BF16)] * BLOCKS,
+    packed, feat = call(
+        functools.partial(pack_kernel, rows),
+        [
+            jax.ShapeDtypeStruct((BLOCKS, 3 * hid, width), BF16),
+            jax.ShapeDtypeStruct((atoms + EXTRA, afeat), BF16),
+        ],
         jnp.swapaxes(trans_in, 2, 3),
         trans_out,
+        atom_feat,
+        atom_token[None],
+        scalars=(window_start,),
         grant=60,
         moved=12 * trans_out.size,
     )
-    trans = [lax.all_gather(part, "col") for part in packed]
-
-    share = me_col % (rows // cols)
-    start = me_col * cols
-    place = jnp.stack(
-        [me, me_col, share, start // rows, me_row, start, jnp.sum(token_mask)]
-        + [(me + step) // ncol * rows for step in (-1, 0, 1)]
-    )
-
-    local_token = atom_token - me_row * rows
-    first_block = me * nblk
-    shift = window_start - QB * (first_block + jnp.arange(nblk, dtype=jnp.int32)) + HALO
-    tail = jnp.stack([local_token, jnp.pad(shift, (0, atoms - nblk))])
-    tail = jnp.pad(tail, ((0, EXTRA - 2), (0, afeat - atoms))).astype(BF16)
-    feat = jnp.concatenate([atom_feat, tail], 0)
+
     up = [(i, i + 1) for i in range(count - 1)]
     prev = lax.ppermute(feat, everyone, up)
     after = lax.ppermute(feat, everyone, [(b, a) for a, b in up])
+
+    across = lax.ppermute(packed, everyone, [(i, i ^ 2) for i in range(count)])
+    sibling = lax.ppermute(packed, everyone, [(i, i ^ 1) for i in range(count)])
 
     ext, copies = call(
         functools.partial(encoder_kernel, natom),
@@ -451,7 +514,6 @@
         after,
         enc_in,
         enc_out,
-        scalars=(place,),
         flops=10**8,
         moved=10**6,
     )
@@ -463,12 +525,12 @@
     bias = pl.pallas_call(
         bias_kernel,
         grid=(rows // step,),
-        out_shape=jax.ShapeDtypeStruct((rows, BLOCKS * heads, span), F32),
+        out_shape=[jax.ShapeDtypeStruct((rows, heads, span), F32)] * BLOCKS,
         in_specs=[
             pl.BlockSpec((step, cols, pair.shape[2]), lambda i: (i, 0, 0)),
             pl.BlockSpec(weights.shape, lambda i: (0, 0)),
         ],
-        out_specs=pl.BlockSpec((step, BLOCKS * heads, span), lambda i: (i, 0, 0)),
+        out_specs=[pl.BlockSpec((step, heads, span), lambda i: (i, 0, 0))] * BLOCKS,
         compiler_params=pltpu.CompilerParams(vmem_limit_bytes=56 * MIB),
         cost_estimate=pl.CostEstimate(flops=4 * 10**9, bytes_accessed=8 * 10**6, transcendentals=0),
     )(pair, weights)
@@ -483,49 +545,65 @@
         both,
         pool_weight,
         token_cond,
-        scalars=(place,),
         flops=10**9,
         moved=10**6,
     )
 
     pairs = key_source(rows, cols)
+    share = me_col % (rows // cols)
     for layer in range(BLOCKS):
         if layer:
             send = lax.dynamic_slice_in_dim(xn, share * cols, cols, 0)
         came = lax.ppermute(send, everyone, pairs)
+        query = call(
+            functools.partial(query_kernel, layer),
+            jax.ShapeDtypeStruct((rows, width), BF16),
+            xn,
+            far=(tok_in,),
+            scratch=[pltpu.VMEM((width, width), BF16), pltpu.SemaphoreType.DMA((1,))],
+            grant=60,
+            flops=2 * rows * width * width,
+            moved=2 * width * width,
+        )
         message = call(
             functools.partial(attention_kernel, layer),
             jax.ShapeDtypeStruct((rows, width + span), BF16),
-            xn,
-            send,
-            came,
-            bias,
-            scalars=(place,),
-            far=(tok_in,),
-            scratch=[pltpu.VMEM((width, width), BF16)] * 3 + [pltpu.SemaphoreType.DMA((3,))],
-            grant=54,
+            scalars=(token_mask,),
+            far=(query, send, came, bias[layer], tok_in),
+            scratch=[pltpu.VMEM((cols, width), BF16)] * 2
+            + [pltpu.VMEM((width, width), BF16)] * 2
+            + [
+                pltpu.VMEM((rows, width), BF16),
+                pltpu.VMEM((rows, heads, span), F32),
+                pltpu.SemaphoreType.DMA((6,)),
+            ],
+            grant=60,
             flops=10**9,
             moved=8 * 10**6,
         )
+        if not layer:
+            message, across = lax.optimization_barrier((message, across))
+            beyond = lax.ppermute(across, everyone, [(i, i ^ 1) for i in range(count)])
+            weights = (packed, sibling, across, beyond)
         message = lax.all_to_all(message.reshape(ncol, own, -1), "col", 0, 0)
         last = layer == BLOCKS - 1
-        act, copies = finish(
-            layer,
-            message,
-            act,
-            tok_in,
-            tok_out,
-            trans[layer],
-            heads,
-            count if last else ncol,
-            tok_atom if last else None,
-        )
+        act, xn2 = mix(layer, message, act, tok_in, tok_out, heads)
+        peers = ncol // 4
+        shifts = [
+            [(r * ncol + c, r * ncol + (c + 4 * d) % ncol) for r in range(nrow) for c in range(ncol)]
+            for d in range(peers)
+        ]
+        back = [[(b, a) for a, b in pairs_of] for pairs_of in shifts]
+        came_rows = [lax.ppermute(xn2, everyone, shifts[d]) for d in range(1, peers)]
+        act, *parts = transition(layer, act, xn2, came_rows, weights)
+        parts = [lax.ppermute(part, everyone, back[d]) for d, part in enumerate(parts, 1)]
+        act, copies = close(act, parts, count if last else ncol, tok_atom if last else None)
         if not last:
             xn = lax.all_to_all(copies, "col", 0, 0).reshape(rows, width)
     proj = lax.all_to_all(copies, everyone, 0, 0).reshape(count * own, afeat)
 
     return call(
-        functools.partial(decoder_kernel, natom),
+        functools.partial(decoder_kernel, natom, rows),
         jax.ShapeDtypeStruct((pos_out.shape[0], atoms), F32),
         ext,
         feat,
@@ -535,7 +613,6 @@
         dec_in,
         dec_out,
         pos_out,
-        scalars=(place,),
         flops=10**8,
         moved=10**6,
     )

time: 157 us -> 190 us (1.21)
  waiting for transfers between devices: 16.6 us -> 54.7 us
  between operations: 13.6 us -> 0.27 us
  starting transfers between devices: 25.8 us -> 30.7 us
  Pallas kernels: 49.9 us -> 54.2 us
  other arithmetic: 3.49 us -> 0 us
    ppermute x1, waiting for transfers between devices: 1.24 us -> 34.3 us  [body(): after = lax.ppermute(feat, everyone, [(b, a) for a, b in up])]
    all_to_all x1 -> x2, blocking collectives: 12.6 us -> 25.8 us  [body(): message = lax.all_to_all(message.reshape(ncol, own, -1), 'col', 0, 0)]
    all_to_all x1 -> x0, blocking collectives: 12.2 us -> none  [body(): both = lax.all_to_all(copies, 'col', 0, 0)]
    ppermute x0 -> x7, waiting for transfers between devices: none -> 8.76 us  [the longest x2 4.38 us: body(): lax.ppermute(part, everyone, back[d])]
    ppermute x0 -> x7, starting transfers between devices: none -> 6.45 us  [the longest x1 2.04 us: body(): across = lax.ppermute(packed, everyone, [(i, i ^ 2) for i in range(count)])]
    all_to_all x1, starting transfers between devices: 8.39 us -> 4.08 us  [body(): both = lax.all_to_all(copies, 'col', 0, 0)]
    pallas_call x8 -> x14, Pallas kernels: 42 us -> 46.3 us  [call(): pl.pallas_call(kernel, out_shape=outs, in_specs=[smem] * len(scalars) + [...]
    ppermute x2, waiting for transfers between devices: 2.73 us -> 0.01 us  [body(): came = lax.ppermute(send, everyone, pairs)]
  transfers between devices with their start and end apart: 8 -> 13, of which waited for: 5 -> 7; matrix products, arithmetic and copies ran while one was open for 3% -> 0% of each run, Pallas kernels for 23% -> 15%
where the time goes in v2:
time: 190 us; the launch traced here: 189 us
  waiting for transfers between devices  54.7 us (29%)
  Pallas kernels  54.2 us (29%)
  blocking collectives  42 us (22%)
  starting transfers between devices  30.7 us (16%)
  local copies, waits for them, and re-layouts  7.09 us (4%)
    pallas_call x14, Pallas kernels, call(): pl.pallas_call(kernel, out_shape=outs, in_specs=[smem] * len(scalars) + [...  46.3 us
    ppermute x1, waiting for transfers between devices, body(): after = lax.ppermute(feat, everyone, [(b, a) for a, b in up])  34.3 us
    all_to_all x2, blocking collectives, body(): message = lax.all_to_all(message.reshape(ncol, own, -1), 'col', 0, 0)  25.8 us
    all_to_all x1, blocking collectives, body(): proj = lax.all_to_all(copies, everyone, 0, 0).reshape(count * own, afeat)  16.2 us
    ppermute x2, starting transfers between devices, body(): came = lax.ppermute(send, everyone, pairs)  8.21 us
    pallas_call x1, Pallas kernels, body(): pl.pallas_call(bias_kernel, grid=(rows // step,), out_shape=[jax.ShapeDty...  7.89 us
    unnamed x46, local copies, waits for them, and re-layouts  7.08 us
    all_to_all x1, starting transfers between devices, body(): xn = lax.all_to_all(copies, 'col', 0, 0).reshape(rows, width)  6.45 us
  transfers between devices with their start and end apart: 13, of which 7 were waited for; matrix products, arithmetic and copies ran while one was open for 0% of the time, Pallas kernels for 15%

profile of v2, /device:TPU:1, one launch (start us, length us, event | category | flops | bytes accessed | tf_op | source)
XLA Modules:
  0.0 188.9 jit_solution(572993493621791235)
XLA Ops:
  0.0 2.9 %shard_map.172 = (bf16[2,576,768]{2,1,0:T(8,128)(2,1)}, bf16[144,128]{1,0:T(8,128)(2,1)}) custom-call(s32[4]{0:T(128)} %starts.1, bf16[2,2,192,768]{3,2,1,0:T(8,128)(2,1)} %bitcast.14, bf16[2,192,768]{2,1,0:T(8,128)(2,1)} %second.1, bf16[128,128]{1,0:T(8,128)(2,1)} %feat.1, s32[1,128]{1,0:T(1,128)} %bitcast.15), custom_call_target="tpu_custom_call" | custom-call | bytes 3538944 | tf_op jit(solution)/shard_map/pallas_call | solution.py:26
  2.9 2.0 %collective-permute-start.3 = (bf16[2,576,768]{2,1,0:T(8,128)(2,1)}, bf16[2,576,768]{2,1,0:T(8,128)(2,1)S(1)}, u32[]{:S(2)}, u32[]{:S(2)}) collective-permute-start(bf16[2,576,768]{2,1,0:T(8,128)(2,1)} %get-tuple-element.33.refs_1_), channel_id=1, source_target_pairs={{0,2},{1,3},{2,0},{3,1},{4,6},{5,7},{6,4},{7,5},{8,10},{9,11},{10,... | collective-permute-start | bytes 5308424 | tf_op jit(solution)/shard_map/ppermute | solution.py:503
  4.9 2.9 %collective-permute-start.1 = (bf16[144,128]{1,0:T(8,128)(2,1)}, bf16[144,128]{1,0:T(8,128)(2,1)S(1)}, u32[]{:S(2)}, u32[]{:S(2)}) collective-permute-start(bf16[144,128]{1,0:T(8,128)(2,1)} %get-tuple-element.27.own_ref), channel_id=1, source_target_pairs={{1,0},{2,1},{3,2},{4,3},{5,4},{6,5},{7,6},{8,7},{9,8},{10,9},{11,1... | collective-permute-start | bytes 110600 | tf_op jit(solution)/shard_map/ppermute | solution.py:501
  7.8 2.7 %collective-permute-start = (bf16[144,128]{1,0:T(8,128)(2,1)}, bf16[144,128]{1,0:T(8,128)(2,1)S(1)}, u32[]{:S(2)}, u32[]{:S(2)}) collective-permute-start(bf16[144,128]{1,0:T(8,128)(2,1)} %get-tuple-element.27.own_ref), channel_id=1, source_target_pairs={{0,1},{1,2},{2,3},{3,4},{4,5},{5,6},{6,7},{7,8},{8,9},{9,10},{10,1... | collective-permute-start | bytes 110600 | tf_op jit(solution)/shard_map/ppermute | solution.py:500
  10.5 34.3 %collective-permute-done.1.next_ref = bf16[144,128]{1,0:T(8,128)(2,1)S(1)} collective-permute-done((bf16[144,128]{1,0:T(8,128)(2,1)}, bf16[144,128]{1,0:T(8,128)(2,1)S(1)}, u32[]{:S(2)}, u32[]{:S(2)}) %collective-permute-start.1) | collective-permute-done | bytes 36896 | tf_op jit(solution)/shard_map/ppermute | solution.py:501
  44.8 0.8 copy-done.8
  45.6 2.0 %shard_map.173 = (bf16[256,128]{1,0:T(8,128)(2,1)S(1)}, bf16[8,144,128]{2,1,0:T(8,128)(2,1)}) custom-call(bf16[144,128]{1,0:T(8,128)(2,1)S(1)} %copy-done.8, bf16[144,128]{1,0:T(8,128)(2,1)S(1)} %collective-permute-done.prev_ref, bf16[144,128]{1,0:T(8,128)(2,1)S(1)} %collective-permute-done.1.next_ref, bf16[4,128,128]{2,1,0:T(8,128)(2,1)S(1)} %copy-done.14, ...), custom_call_target="tpu_custom_call" | custom-call | flops 100000000 | bytes 1000000 | tf_op jit(solution)/shard_map/pallas_call | solution.py:26
  47.6 4.1 %all-to-all-start = ((bf16[8,144,128]{2,1,0:T(8,128)(2,1)}), bf16[8,144,128]{2,1,0:T(8,128)(2,1)S(1)}, u32[]{:S(2)}, u32[]{:S(2)}) async-start(bf16[8,144,128]{2,1,0:T(8,128)(2,1)} %get-tuple-element.29), calls=%async_computation | async-start | bytes 589824 | tf_op jit(solution)/shard_map/all_to_all | solution.py:520
  51.7 0.0 collective-permute-start.5
  51.7 5.8 %all-to-all-done.both_ref = bf16[8,144,128]{2,1,0:T(8,128)(2,1)S(1)} async-done(((bf16[8,144,128]{2,1,0:T(8,128)(2,1)}), bf16[8,144,128]{2,1,0:T(8,128)(2,1)S(1)}, u32[]{:S(2)}, u32[]{:S(2)}) %all-to-all-start) | async-done | bytes 294944 | tf_op jit(solution)/shard_map/all_to_all | solution.py:520
  57.5 1.3 shard_map.174
  58.8 0.7 copy-done
  59.5 0.6 copy-done.7
  60.1 5.2 %collective-permute-start.2 = (bf16[96,768]{1,0:T(8,128)(2,1)S(1)}, bf16[96,768]{1,0:T(8,128)(2,1)S(1)}, u32[]{:S(2)}, u32[]{:S(2)}) collective-permute-start(bf16[96,768]{1,0:T(8,128)(2,1)S(1)} %get-tuple-element.31.refs_1_), channel_id=1, source_target_pairs={{4,8},{7,9},{0,16},{3,17},{2,24},{1,25},{12,2},{15,3},{8,18},{9,19... | collective-permute-start | bytes 442376 | tf_op jit(solution)/shard_map/ppermute | solution.py:557
  65.4 7.9 %shard_map.176 = (f32[192,16,128]{2,1,0:T(8,128)}, f32[192,16,128]{2,1,0:T(8,128)}) custom-call(bf16[192,96,128]{2,1,0:T(8,128)(2,1)} %pair_ref.1, bf16[32,128]{1,0:T(8,128)(2,1)} %bitcast.16), custom_call_target="tpu_custom_call" | custom-call | flops 4000000000 | bytes 8000000 | tf_op jit(solution)/shard_map/pallas_call | solution.py:525
  73.3 3.4 %shard_map.175.refs_0_ = bf16[192,768]{1,0:T(8,128)(2,1)} custom-call(bf16[192,768]{1,0:T(8,128)(2,1)} %copy-done, bf16[2,4,768,768]{3,2,1,0:T(8,128)(2,1)} %w_in.10), custom_call_target="tpu_custom_call" | custom-call | flops 226492416 | bytes 1179648 | tf_op jit(solution)/shard_map/pallas_call | solution.py:26
  76.6 0.7 copy-done.19
  77.3 6.3 %shard_map.177 = bf16[192,896]{1,0:T(8,128)(2,1)} custom-call(s32[768]{0:T(1024)} %mask_ref.3, bf16[192,768]{1,0:T(8,128)(2,1)} %shard_map.175.refs_0_, bf16[96,768]{1,0:T(8,128)(2,1)} %copy-done.2, bf16[96,768]{1,0:T(8,128)(2,1)} %copy-done.19, f32[192,16,128]{2,1,0:T(8,128)} %get-tuple-element.32.refs_3_, bf16[2,4,768,768]{3,2,1,0:T(8,128)(2,1)} %w_in.10), custom_call_target="tpu_custom_call" | custom-call | flops 1000000000 | bytes 8000000 | tf_op jit(solution)/shard_map/pallas_call | solution.py:26
  83.6 0.8 collective-permute-start.6
  84.4 11.1 %all_to_all.25.message = bf16[8,24,896]{2,1,0:T(8,128)(2,1)} all-to-all(bf16[8,24,896]{2,1,0:T(8,128)(2,1)} %bitcast.12), channel_id=1, replica_groups=mesh['row'=4,'col'=8] {'col'}, dimensions={0} | all-to-all | bytes 688128 | tf_op jit(solution)/shard_map/all_to_all | solution.py:588
  95.5 3.8 %shard_map.178 = (f32[24,768]{1,0:T(8,128)}, bf16[24,768]{1,0:T(8,128)(2,1)}) custom-call(bf16[8,24,896]{2,1,0:T(8,128)(2,1)} %all_to_all.25.message, f32[24,768]{1,0:T(8,128)} %copy-done.7, bf16[2,4,768,768]{3,2,1,0:T(8,128)(2,1)} %w_in.10, bf16[2,768,768]{2,1,0:T(8,128)(2,1)} %w_out.6), custom_call_target="tpu_custom_call" | custom-call | flops 56623104 | bytes 2359296 | tf_op jit(solution)/shard_map/pallas_call | solution.py:26
  99.3 1.3 collective-permute-start.4
  100.6 1.7 collective-permute-done.4.refs_0_
  102.4 0.6 copy-done.21
  103.0 4.7 %shard_map.179 = (f32[24,768]{1,0:T(8,128)}, bf16[24,768]{1,0:T(8,128)(2,1)}) custom-call(f32[24,768]{1,0:T(8,128)} %get-tuple-element.36.act_ref, bf16[24,768]{1,0:T(8,128)(2,1)} %get-tuple-element.37.xn2, bf16[24,768]{1,0:T(8,128)(2,1)} %copy-done.21, bf16[2,576,768]{2,1,0:T(8,128)(2,1)} %get-tuple-element.33.refs_1_, ...), custom_call_target="tpu_custom_call" | custom-call | flops 169869312 | bytes 3538944 | tf_op jit(solution)/shard_map/pallas_call | solution.py:26
  107.7 1.3 collective-permute-start.7
  109.0 1.8 collective-permute-done.7.refs_0_
  110.8 0.9 copy-done.4
  111.7 0.9 shard_map.180
  112.6 0.6 copy-done.6
  113.2 6.5 %all-to-all-start.2 = ((bf16[8,24,768]{2,1,0:T(8,128)(2,1)}), bf16[8,24,768]{2,1,0:T(8,128)(2,1)S(1)}, u32[]{:S(2)}, u32[]{:S(2)}) async-start(bf16[8,24,768]{2,1,0:T(8,128)(2,1)} %get-tuple-element.41), calls=%async_computation.2 | async-start | bytes 589824 | tf_op jit(solution)/shard_map/all_to_all | solution.py:602
  119.7 5.8 %all-to-all-done.2 = bf16[8,24,768]{2,1,0:T(8,128)(2,1)S(1)} async-done(((bf16[8,24,768]{2,1,0:T(8,128)(2,1)}), bf16[8,24,768]{2,1,0:T(8,128)(2,1)S(1)}, u32[]{:S(2)}, u32[]{:S(2)}) %all-to-all-start.2) | async-done | bytes 294944 | tf_op jit(solution)/shard_map/all_to_all | solution.py:602
  125.5 3.0 %collective-permute-start.8 = (bf16[96,768]{1,0:T(8,128)(2,1)S(1)}, bf16[96,768]{1,0:T(8,128)(2,1)S(1)}, u32[]{:S(2)}, u32[]{:S(2)}) collective-permute-start(bf16[96,768]{1,0:T(8,128)(2,1)S(1)} %constant_dynamic-slice_fusion.refs_1_), channel_id=1, source_target_pairs={{4,8},{7,9},{0,16},{3,17},{2,24},{1,25},{12,2},{15,3},{8,18},{9,19... | collective-permute-start | bytes 442376 | tf_op jit(solution)/shard_map/ppermute | solution.py:557
  128.5 3.3 %shard_map.181.refs_0_ = bf16[192,768]{1,0:T(8,128)(2,1)} custom-call(bf16[192,768]{1,0:T(8,128)(2,1)} %bitcast.11, bf16[2,4,768,768]{3,2,1,0:T(8,128)(2,1)} %w_in.10), custom_call_target="tpu_custom_call" | custom-call | flops 226492416 | bytes 1179648 | tf_op jit(solution)/shard_map/pallas_call | solution.py:26
  131.9 0.7 copy-done.20
  132.6 6.3 %shard_map.182 = bf16[192,896]{1,0:T(8,128)(2,1)} custom-call(s32[768]{0:T(1024)} %mask_ref.3, bf16[192,768]{1,0:T(8,128)(2,1)} %shard_map.181.refs_0_, bf16[96,768]{1,0:T(8,128)(2,1)} %copy-done.18, bf16[96,768]{1,0:T(8,128)(2,1)} %copy-done.20, f32[192,16,128]{2,1,0:T(8,128)} %get-tuple-element.42.refs_3_, bf16[2,4,768,768]{3,2,1,0:T(8,128)(2,1)} %w_in.10), custom_call_target="tpu_custom_call" | custom-call | flops 1000000000 | bytes 8000000 | tf_op jit(solution)/shard_map/pallas_call | solution.py:26
  138.8 14.7 %all_to_all.26.message = bf16[8,24,896]{2,1,0:T(8,128)(2,1)} all-to-all(bf16[8,24,896]{2,1,0:T(8,128)(2,1)} %bitcast.13), channel_id=1, replica_groups=mesh['row'=4,'col'=8] {'col'}, dimensions={0} | all-to-all | bytes 688128 | tf_op jit(solution)/shard_map/all_to_all | solution.py:588
  153.5 3.8 %shard_map.183 = (f32[24,768]{1,0:T(8,128)}, bf16[24,768]{1,0:T(8,128)(2,1)}) custom-call(bf16[8,24,896]{2,1,0:T(8,128)(2,1)} %all_to_all.26.message, f32[24,768]{1,0:T(8,128)} %copy-done.6, bf16[2,4,768,768]{3,2,1,0:T(8,128)(2,1)} %w_in.10, bf16[2,768,768]{2,1,0:T(8,128)(2,1)} %w_out.6), custom_call_target="tpu_custom_call" | custom-call | flops 56623104 | bytes 2359296 | tf_op jit(solution)/shard_map/pallas_call | solution.py:26
  157.3 0.5 collective-permute-start.9
  157.8 2.6 %collective-permute-done.9.refs_0_ = bf16[24,768]{1,0:T(8,128)(2,1)S(1)} collective-permute-done((bf16[24,768]{1,0:T(8,128)(2,1)}, bf16[24,768]{1,0:T(8,128)(2,1)S(1)}, u32[]{:S(2)}, u32[]{:S(2)}) %collective-permute-start.9) | collective-permute-done | bytes 36896 | tf_op jit(solution)/shard_map/ppermute | solution.py:597
  160.4 0.6 copy-done.22
  161.0 4.8 %shard_map.184 = (f32[24,768]{1,0:T(8,128)}, bf16[24,768]{1,0:T(8,128)(2,1)}) custom-call(f32[24,768]{1,0:T(8,128)} %get-tuple-element.44.act_ref, bf16[24,768]{1,0:T(8,128)(2,1)} %get-tuple-element.45.xn2, bf16[24,768]{1,0:T(8,128)(2,1)} %copy-done.22, bf16[2,576,768]{2,1,0:T(8,128)(2,1)} %get-tuple-element.33.refs_1_, ...), custom_call_target="tpu_custom_call" | custom-call | flops 169869312 | bytes 3538944 | tf_op jit(solution)/shard_map/pallas_call | solution.py:26
  165.8 0.5 collective-permute-start.10
  166.3 2.6 %collective-permute-done.10.refs_0_ = bf16[24,768]{1,0:T(8,128)(2,1)S(1)} collective-permute-done((bf16[24,768]{1,0:T(8,128)(2,1)}, bf16[24,768]{1,0:T(8,128)(2,1)S(1)}, u32[]{:S(2)}, u32[]{:S(2)}) %collective-permute-start.10) | collective-permute-done | bytes 36896 | tf_op jit(solution)/shard_map/ppermute | solution.py:599
  168.9 0.9 copy-done.5
  169.8 0.8 shard_map.185
  170.6 16.2 %all_to_all.27 = bf16[32,24,128]{2,1,0:T(8,128)(2,1)S(1)} all-to-all(bf16[32,24,128]{2,1,0:T(8,128)(2,1)S(1)} %get-tuple-element.48), channel_id=1, replica_groups=mesh['row'=4,'col'=8] {'row','col'}, dimensions={0} | all-to-all | bytes 393216 | tf_op jit(solution)/shard_map/all_to_all | solution.py:603
  186.8 2.1 %shard_map.186 = f32[3,128]{1,0:T(4,128)} custom-call(bf16[256,128]{1,0:T(8,128)(2,1)S(1)} %get-tuple-element.28.x1_ref, bf16[144,128]{1,0:T(8,128)(2,1)S(1)} %copy-done.9, bf16[144,128]{1,0:T(8,128)(2,1)S(1)} %collective-permute-done.prev_ref, bf16[144,128]{1,0:T(8,128)(2,1)S(1)} %collective-permute-done.1.next_ref, bf16[768,128]{1,0:T(8,128)(2,1)S(1)} %bitcast.9, ...), custom_call_target="tpu_custom_call" | custom-call | flops 100000000 | bytes 1000000 | tf_op jit(solution)/shard_map/pallas_call | solution.py:26
  (43 shorter events, 0.1 us)
Async XLA Ops:
  0.0 44.8 %copy-start.15 = (bf16[128,128]{1,0:T(8,128)(2,1)S(1)}, bf16[128,128]{1,0:T(8,128)(2,1)}, u32[]{:S(2)}) copy-start(bf16[128,128]{1,0:T(8,128)(2,1)} %w_out.4) | copy-start | bytes 98308
  0.0 44.8 %copy-start.14 = (bf16[4,128,128]{2,1,0:T(8,128)(2,1)S(1)}, bf16[4,128,128]{2,1,0:T(8,128)(2,1)}, u32[]{:S(2)}) copy-start(bf16[4,128,128]{2,1,0:T(8,128)(2,1)} %w_in.6) | copy-start | bytes 393220
  0.0 57.5 %copy-start.13 = (bf16[128,768]{1,0:T(8,128)(2,1)S(1)}, bf16[128,768]{1,0:T(8,128)(2,1)}, u32[]{:S(2)}) copy-start(bf16[128,768]{1,0:T(8,128)(2,1)} %weight.1) | copy-start | bytes 589828
  0.0 57.5 %copy-start.12 = (bf16[192,768]{1,0:T(8,128)(2,1)S(1)}, bf16[192,768]{1,0:T(8,128)(2,1)}, u32[]{:S(2)}) copy-start(bf16[192,768]{1,0:T(8,128)(2,1)} %cond.1) | copy-start | bytes 884740
  2.9 80.7 %collective-permute-start.3 = (bf16[2,576,768]{2,1,0:T(8,128)(2,1)}, bf16[2,576,768]{2,1,0:T(8,128)(2,1)S(1)}, u32[]{:S(2)}, u32[]{:S(2)}) collective-permute-start(bf16[2,576,768]{2,1,0:T(8,128)(2,1)} %get-tuple-element.33.refs_1_), channel_id=1, source_target_pairs={{0,2},{1,3},{2,0},{3,1},{4,6},{5,7},{6,4},{7,5},{8,10},{9,11},{10,... | collective-permute-start | bytes 5308424 | tf_op jit(solution)/shard_map/ppermute | solution.py:503
  4.9 39.9 %collective-permute-start.1 = (bf16[144,128]{1,0:T(8,128)(2,1)}, bf16[144,128]{1,0:T(8,128)(2,1)S(1)}, u32[]{:S(2)}, u32[]{:S(2)}) collective-permute-start(bf16[144,128]{1,0:T(8,128)(2,1)} %get-tuple-element.27.own_ref), channel_id=1, source_target_pairs={{1,0},{2,1},{3,2},{4,3},{5,4},{6,5},{7,6},{8,7},{9,8},{10,9},{11,1... | collective-permute-start | bytes 110600 | tf_op jit(solution)/shard_map/ppermute | solution.py:501
  7.8 37.0 %collective-permute-start = (bf16[144,128]{1,0:T(8,128)(2,1)}, bf16[144,128]{1,0:T(8,128)(2,1)S(1)}, u32[]{:S(2)}, u32[]{:S(2)}) collective-permute-start(bf16[144,128]{1,0:T(8,128)(2,1)} %get-tuple-element.27.own_ref), channel_id=1, source_target_pairs={{0,1},{1,2},{2,3},{3,4},{4,5},{5,6},{6,7},{7,8},{8,9},{9,10},{10,1... | collective-permute-start | bytes 110600 | tf_op jit(solution)/shard_map/ppermute | solution.py:500
  44.8 0.8 copy-start.8
  47.6 9.9 %all-to-all-start = ((bf16[8,144,128]{2,1,0:T(8,128)(2,1)}), bf16[8,144,128]{2,1,0:T(8,128)(2,1)S(1)}, u32[]{:S(2)}, u32[]{:S(2)}) async-start(bf16[8,144,128]{2,1,0:T(8,128)(2,1)} %get-tuple-element.29), calls=%async_computation | async-start | bytes 589824 | tf_op jit(solution)/shard_map/all_to_all | solution.py:520
  51.7 48.9 %collective-permute-start.5 = (bf16[2,576,768]{2,1,0:T(8,128)(2,1)}, bf16[2,576,768]{2,1,0:T(8,128)(2,1)}, u32[]{:S(2)}, u32[]{:S(2)}) collective-permute-start(bf16[2,576,768]{2,1,0:T(8,128)(2,1)} %get-tuple-element.33.refs_1_), channel_id=1, source_target_pairs={{0,1},{1,0},{2,3},{3,2},{4,5},{5,4},{6,7},{7,6},{8,9},{9,8},{10,11... | collective-permute-start | bytes 5308424 | tf_op jit(solution)/shard_map/ppermute | solution.py:504
  58.8 0.7 copy-start
  59.5 0.6 copy-start.7
  60.1 13.1 %copy-start.2 = (bf16[96,768]{1,0:T(8,128)(2,1)}, bf16[96,768]{1,0:T(8,128)(2,1)S(1)}, u32[]{:S(2)}) copy-start(bf16[96,768]{1,0:T(8,128)(2,1)S(1)} %get-tuple-element.31.refs_1_) | copy-start | bytes 442372
  60.1 16.5 %collective-permute-start.2 = (bf16[96,768]{1,0:T(8,128)(2,1)S(1)}, bf16[96,768]{1,0:T(8,128)(2,1)S(1)}, u32[]{:S(2)}, u32[]{:S(2)}) collective-permute-start(bf16[96,768]{1,0:T(8,128)(2,1)S(1)} %get-tuple-element.31.refs_1_), channel_id=1, source_target_pairs={{4,8},{7,9},{0,16},{3,17},{2,24},{1,25},{12,2},{15,3},{8,18},{9,19... | collective-permute-start | bytes 442376 | tf_op jit(solution)/shard_map/ppermute | solution.py:557
  76.6 0.7 copy-start.19
  83.6 15.7 %copy-start.16 = (bf16[2,576,768]{2,1,0:T(8,128)(2,1)}, bf16[2,576,768]{2,1,0:T(8,128)(2,1)S(1)}, u32[]{:S(2)}) copy-start(bf16[2,576,768]{2,1,0:T(8,128)(2,1)S(1)} %collective-permute-done.3.refs_3_) | copy-start | bytes 5308420
  83.6 18.8 %collective-permute-start.6 = (bf16[2,576,768]{2,1,0:T(8,128)(2,1)S(1)}, bf16[2,576,768]{2,1,0:T(8,128)(2,1)}, u32[]{:S(2)}, u32[]{:S(2)}) collective-permute-start(bf16[2,576,768]{2,1,0:T(8,128)(2,1)S(1)} %collective-permute-done.3.refs_3_), channel_id=1, source_target_pairs={{0,1},{1,0},{2,3},{3,2},{4,5},{5,4},{6,7},{7,6},{8,9},{9,8},{10,11... | collective-permute-start | bytes 5308424 | tf_op jit(solution)/shard_map/ppermute | solution.py:586
  99.3 3.1 %collective-permute-start.4 = (bf16[24,768]{1,0:T(8,128)(2,1)}, bf16[24,768]{1,0:T(8,128)(2,1)S(1)}, u32[]{:S(2)}, u32[]{:S(2)}) collective-permute-start(bf16[24,768]{1,0:T(8,128)(2,1)} %get-tuple-element.37.xn2), channel_id=1, source_target_pairs={{0,4},{1,5},{2,6},{3,7},{4,0},{5,1},{6,2},{7,3},{8,12},{9,13},{10,... | collective-permute-start | bytes 110600 | tf_op jit(solution)/shard_map/ppermute | solution.py:597
  102.4 0.6 copy-start.21
  107.7 3.1 %collective-permute-start.7 = (bf16[24,768]{1,0:T(8,128)(2,1)}, bf16[24,768]{1,0:T(8,128)(2,1)S(1)}, u32[]{:S(2)}, u32[]{:S(2)}) collective-permute-start(bf16[24,768]{1,0:T(8,128)(2,1)} %get-tuple-element.40), channel_id=1, source_target_pairs={{4,0},{5,1},{6,2},{7,3},{0,4},{1,5},{2,6},{3,7},{12,8},{13,9},{14,... | collective-permute-start | bytes 110600 | tf_op jit(solution)/shard_map/ppermute | solution.py:599
  110.8 0.9 copy-start.4
  112.6 0.6 copy-start.6
  113.2 12.3 %all-to-all-start.2 = ((bf16[8,24,768]{2,1,0:T(8,128)(2,1)}), bf16[8,24,768]{2,1,0:T(8,128)(2,1)S(1)}, u32[]{:S(2)}, u32[]{:S(2)}) async-start(bf16[8,24,768]{2,1,0:T(8,128)(2,1)} %get-tuple-element.41), calls=%async_computation.2 | async-start | bytes 589824 | tf_op jit(solution)/shard_map/all_to_all | solution.py:602
  125.5 3.0 %copy-start.17 = (bf16[8,24,768]{2,1,0:T(8,128)(2,1)}, bf16[8,24,768]{2,1,0:T(8,128)(2,1)S(1)}, u32[]{:S(2)}) copy-start(bf16[8,24,768]{2,1,0:T(8,128)(2,1)S(1)} %all-to-all-done.2) | copy-start | bytes 884740
  125.5 6.4 %copy-start.18 = (bf16[96,768]{1,0:T(8,128)(2,1)}, bf16[96,768]{1,0:T(8,128)(2,1)S(1)}, u32[]{:S(2)}) copy-start(bf16[96,768]{1,0:T(8,128)(2,1)S(1)} %constant_dynamic-slice_fusion.refs_1_) | copy-start | bytes 442372
  125.5 6.4 %collective-permute-start.8 = (bf16[96,768]{1,0:T(8,128)(2,1)S(1)}, bf16[96,768]{1,0:T(8,128)(2,1)S(1)}, u32[]{:S(2)}, u32[]{:S(2)}) collective-permute-start(bf16[96,768]{1,0:T(8,128)(2,1)S(1)} %constant_dynamic-slice_fusion.refs_1_), channel_id=1, source_target_pairs={{4,8},{7,9},{0,16},{3,17},{2,24},{1,25},{12,2},{15,3},{8,18},{9,19... | collective-permute-start | bytes 442376 | tf_op jit(solution)/shard_map/ppermute | solution.py:557
  131.9 0.7 copy-start.20
  157.3 3.1 %collective-permute-start.9 = (bf16[24,768]{1,0:T(8,128)(2,1)}, bf16[24,768]{1,0:T(8,128)(2,1)S(1)}, u32[]{:S(2)}, u32[]{:S(2)}) collective-permute-start(bf16[24,768]{1,0:T(8,128)(2,1)} %get-tuple-element.45.xn2), channel_id=1, source_target_pairs={{0,4},{1,5},{2,6},{3,7},{4,0},{5,1},{6,2},{7,3},{8,12},{9,13},{10,... | collective-permute-start | bytes 110600 | tf_op jit(solution)/shard_map/ppermute | solution.py:597
  160.4 0.6 copy-start.22
  161.0 7.9 %copy-start.1 = (bf16[768,128]{1,0:T(8,128)(2,1)S(1)}, bf16[768,128]{1,0:T(8,128)(2,1)}, u32[]{:S(2)}) copy-start(bf16[768,128]{1,0:T(8,128)(2,1)} %refs_1_.1) | copy-start | bytes 589828
  161.0 25.8 %copy-start.3 = (bf16[4,128,128]{2,1,0:T(8,128)(2,1)S(1)}, bf16[4,128,128]{2,1,0:T(8,128)(2,1)}, u32[]{:S(2)}) copy-start(bf16[4,128,128]{2,1,0:T(8,128)(2,1)} %w_in.11) | copy-start | bytes 393220
  161.0 25.8 %copy-start.9 = (bf16[144,128]{1,0:T(8,128)(2,1)S(1)}, bf16[144,128]{1,0:T(8,128)(2,1)}, u32[]{:S(2)}) copy-start(bf16[144,128]{1,0:T(8,128)(2,1)} %get-tuple-element.27.own_ref) | copy-start | bytes 110596
  161.0 25.8 %copy-start.10 = (bf16[128,128]{1,0:T(8,128)(2,1)S(1)}, bf16[128,128]{1,0:T(8,128)(2,1)}, u32[]{:S(2)}) copy-start(bf16[128,128]{1,0:T(8,128)(2,1)} %w_out.7) | copy-start | bytes 98308
  161.0 25.8 %copy-start.11 = (bf16[3,128]{1,0:T(4,128)(2,1)S(1)}, bf16[3,128]{1,0:T(4,128)(2,1)}, u32[]{:S(2)}) copy-start(bf16[3,128]{1,0:T(4,128)(2,1)} %pos.1) | copy-start | bytes 2308
  165.8 3.1 %collective-permute-start.10 = (bf16[24,768]{1,0:T(8,128)(2,1)}, bf16[24,768]{1,0:T(8,128)(2,1)S(1)}, u32[]{:S(2)}, u32[]{:S(2)}) collective-permute-start(bf16[24,768]{1,0:T(8,128)(2,1)} %get-tuple-element.47), channel_id=1, source_target_pairs={{4,0},{5,1},{6,2},{7,3},{0,4},{1,5},{2,6},{3,7},{12,8},{13,9},{14,... | collective-permute-start | bytes 110600 | tf_op jit(solution)/shard_map/ppermute | solution.py:599
  168.9 0.9 copy-start.5

commit v3 on v2

--- a/solution.py
+++ b/solution.py
@@ -159,16 +159,31 @@
     act_ref[...] = mine
 
 
-def decoder_kernel(natom, row_tokens, x1_ref, own_ref, prev_ref, next_ref, proj, w_in, w_out, pos, out):
+def decoder_kernel(
+    natom, x1_ref, own_ref, prev_ref, next_ref, proj_ref, *refs
+):
+    *edges, w_in, w_out, pos, out = refs
     rows = own_ref.shape[0] - EXTRA
+    proj = proj_ref[...].astype(F32)
     tokens = proj.shape[0]
-    me = device()[2]
+    _, col, me = device()
+    edges = [edge[...].astype(F32) for edge in edges]
+    reach = len(edges) * edges[0].shape[0]
+    rest = tokens - reach
+    edge_low = jnp.where(col == 0, jnp.concatenate(edges[::-1], 0), proj[rest:])
+    edge_high = jnp.where(
+        col == lax.axis_size("col") - 1, jnp.concatenate(edges, 0), proj[:reach]
+    )
+    tables = (
+        jnp.concatenate([proj[:rest], edge_low], 0),
+        proj,
+        jnp.concatenate([edge_high, proj[reach:]], 0),
+    )
     spread = []
-    for k, ref in enumerate((prev_ref, own_ref, next_ref)):
+    for table, ref in zip(tables, (prev_ref, own_ref, next_ref)):
         spot = ref[rows:].astype(F32)[0:1].astype(jnp.int32)
-        spot = spot + (me + k - 1) // lax.axis_size("col") * row_tokens
         onehot = (iota((tokens, rows), 0) == spot).astype(F32).astype(BF16)
-        spread.append(dot_tn(onehot, proj[...]))
+        spread.append(dot_tn(onehot, table.astype(BF16)))
     spread = jnp.concatenate([spread[0][rows - HALO :], spread[1], spread[2][:HALO]], 0)
     x = (x1_ref[...].astype(F32) + spread).astype(BF16)
     xn = normed(x).astype(BF16)
@@ -183,13 +198,7 @@
     out[...] = dot_nt(pos[...], normed(third).astype(BF16))
 
 
-def pack_kernel(row_tokens, starts, first, second, feat, token, *outs):
-    out, own = outs
-    hid = second.shape[1]
-    for layer in range(BLOCKS):
-        out[layer, :hid] = first[layer, 0]
-        out[layer, hid : 2 * hid] = first[layer, 1]
-        out[layer, 2 * hid :] = second[layer]
+def feat_kernel(row_tokens, starts, feat, token, own):
     rows, width = feat.shape
     row, _, me = device()
     nblk = starts.shape[0]
@@ -203,6 +212,17 @@
     own[rows:] = tail.astype(F32).astype(BF16)
 
 
+def pack_kernel(first, second, upper, lower, *outs):
+    hid = second.shape[1]
+    half = upper.shape[0]
+    for layer, out in enumerate(outs):
+        out[:hid] = first[layer, 0]
+        out[hid : 2 * hid] = first[layer, 1]
+        out[2 * hid :] = second[layer]
+    upper[...] = outs[0][:half]
+    lower[...] = outs[0][half:]
+
+
 def bias_kernel(pair_ref, weight, *outs):
     rows, cols, _ = pair_ref.shape
     _, heads, pad = outs[0].shape
@@ -222,34 +242,33 @@
     ]
 
 
-def query_kernel(layer, xn_ref, w_in, query, w_query, sems):
-    (copy,) = prepare([w_in.at[layer, 0]], [w_query], sems)
-    copy.start()
-    copy.wait()
+def query_kernel(
+    layer, xn_ref, act_ref, w_in, query, w_key, w_val, gate, w_query, w_gate, sems
+):
+    fetches = prepare(
+        [w_in.at[layer, k] for k in range(4)], [w_query, w_key, w_val, w_gate], sems
+    )
+    for k in (0, 3, 1, 2):
+        fetches[k].start()
+    fetches[0].wait()
     query[...] = dot(xn_ref[...], w_query[...]).astype(BF16)
-
-
-def attention_kernel(layer, mask_ref, *refs):
-    far, out_ref, near, sems = refs[:5], refs[5], refs[6:-1], refs[-1]
-    query, here, came, bias, w_in = far
-    fetches = prepare([here, came, w_in.at[layer, 1], w_in.at[layer, 2], query, bias], near, sems)
-    here_ref, came_ref, w_key, w_val, query, bias_ref = near
-    for copy in fetches:
-        copy.start()
+    fetches[3].wait()
+    gate[...] = jax.nn.sigmoid(dot(normed(act_ref[...]).astype(BF16), w_gate[...]))
+    fetches[1].wait()
+    fetches[2].wait()
+
+
+def attention_kernel(mask_ref, query, here_ref, came_ref, low, high, w_key, w_val, out_ref):
     rows, width = query.shape
     cols = here_ref.shape[0]
-    heads = bias_ref.shape[1]
+    heads = low.shape[1]
     hsize = width // heads
-    span = bias_ref.shape[2]
+    span = low.shape[2]
     row, col, _ = device()
     mine = col * cols // rows == row
-    fetches[0].wait()
-    fetches[1].wait()
     key_xn = jnp.where(mine, here_ref[...].astype(F32), came_ref[...].astype(F32))
     key_xn = jnp.concatenate([key_xn, jnp.zeros((span - cols, width), F32)], 0).astype(BF16)
-    fetches[2].wait()
     keys = dot(key_xn, w_key[...]).astype(BF16)
-    fetches[3].wait()
     vals = dot(key_xn, w_val[...]).astype(BF16)
     tokens = mask_ref.shape[0]
     count = jnp.int32(0)
@@ -260,8 +279,6 @@
         count = jnp.where(inside & (last == 1), longer, count)
     valid = iota((1, span), 1) + col * cols < count
     valid = valid & (iota((1, span), 1) < cols)
-    fetches[4].wait()
-    fetches[5].wait()
     group = heads // 2
     part = group * hsize
     lane = iota((1, part), 1) // hsize
@@ -276,7 +293,8 @@
         probs = []
         for h in range(group):
             head = g * group + h
-            score = scores[:, h * span : (h + 1) * span] + bias_ref[:, head, :]
+            bias = jnp.concatenate([low[:, head, :], high[:, head, :]], 0)
+            score = scores[:, h * span : (h + 1) * span] + bias
             score = jnp.where(valid, score, -1000000000.0)
             top = jnp.max(score, -1, keepdims=True)
             expd = jnp.exp(score - top)
@@ -293,10 +311,9 @@
     out_ref[:, width:] = jnp.where(spot < 3 * heads, packed, 0.0).astype(BF16)
 
 
-def mix_kernel(layer, heads, message, act_ref, w_in, w_out, act_out, xn2_out, w_gate, w_mix, sems):
-    fetches = prepare([w_in.at[layer, 3], w_out.at[layer]], [w_gate, w_mix], sems)
-    for copy in fetches:
-        copy.start()
+def mix_kernel(layer, heads, message, act_ref, gate, w_out, act_out, xn2_out, w_mix, sems):
+    (copy,) = prepare([w_out.at[layer]], [w_mix], sems)
+    copy.start()
     width = act_ref.shape[1]
     hsize = width // heads
     parts = [message[j, :, width:].astype(F32) for j in range(message.shape[0])]
@@ -322,78 +339,93 @@
     attn = jnp.zeros(act_ref.shape, F32)
     for j in range(message.shape[0]):
         attn = attn + spread[j * own : (j + 1) * own] * message[j, :, :width].astype(F32)
-    normal = normed(act_ref[...]).astype(BF16)
-    fetches[0].wait()
-    gated = (jax.nn.sigmoid(dot(normal, w_gate[...])) * attn).astype(BF16)
-    fetches[1].wait()
+    gated = (gate[...] * attn).astype(BF16)
+    copy.wait()
     act = act_ref[...] + dot(gated, w_mix[...])
     act_out[...] = act
     xn2_out[...] = normed(act).astype(BF16)
 
 
-def mix(layer, message, act, w_in, w_out, heads):
+def mix(layer, message, act, gate, w_out, heads):
     own, width = act.shape
     return call(
         functools.partial(mix_kernel, layer, heads),
         [jax.ShapeDtypeStruct((own, width), F32), jax.ShapeDtypeStruct((own, width), BF16)],
         message,
         act,
-        far=(w_in, w_out),
-        scratch=[pltpu.VMEM((width, width), BF16)] * 2 + [pltpu.SemaphoreType.DMA((2,))],
-        grant=60,
+        gate,
+        far=(w_out,),
+        scratch=[pltpu.VMEM((width, width), BF16), pltpu.SemaphoreType.DMA((1,))],
+        grant=48,
         flops=4 * own * width * width,
         moved=4 * width * width,
     )
 
 
-def transition_kernel(layer, act_ref, xn2, *refs):
-    groups = len(refs) // 2 - 3
-    others, blocks = refs[: groups - 1], refs[groups - 1 : groups + 3]
-    outs, (w_first, w_second, sems) = refs[groups + 3 : -3], refs[-3:]
+def transition_kernel(groups, pieces, act_ref, xn2, *refs):
+    others, refs = refs[: groups - 1], refs[groups - 1 :]
+    sources = []
+    for number in pieces:
+        sources.append(refs[:number])
+        refs = refs[number:]
+    outs, (w_first, w_second, sems) = refs[:groups], refs[groups:]
     count, hid = w_second.shape[:2]
-    fetches = prepare(
-        [ref.at[layer, pl.ds(0, 2 * hid)] for ref in blocks]
-        + [ref.at[layer, pl.ds(2 * hid, hid)] for ref in blocks],
-        [w_first.at[j] for j in range(count)] + [w_second.at[j] for j in range(count)],
-        sems,
-    )
+    plan = []
+    for wanted, target in (((0, 2 * hid), w_first), ((2 * hid, 3 * hid), w_second)):
+        for j, source in enumerate(sources):
+            begin = 0
+            for ref in source:
+                end = begin + ref.shape[0]
+                low, high = max(begin, wanted[0]), min(end, wanted[1])
+                if low < high:
+                    near = target.at[j, pl.ds(low - wanted[0], high - low)]
+                    plan.append((target is w_first, j, ref.at[pl.ds(low - begin, high - low)], near))
+                begin = end
+    fetches = prepare([item[2] for item in plan], [item[3] for item in plan], sems)
     for copy in fetches:
         copy.start()
+
+    def arrived(first, j):
+        for item, copy in zip(plan, fetches):
+            if item[:2] == (first, j):
+                copy.wait()
+
     own = act_ref.shape[0]
     rows = jnp.concatenate([ref[...].astype(F32) for ref in (xn2, *others)], 0).astype(BF16)
     total = jnp.zeros((rows.shape[0], rows.shape[1]), F32)
     hidden = []
     for j in range(count):
-        fetches[j].wait()
+        arrived(True, j)
         both = dot_nt(rows, w_first[j])
         left, right = both[:, :hid], both[:, hid:]
         hidden.append((left * jax.nn.sigmoid(left) * right).astype(BF16))
     for j in range(count):
-        fetches[count + j].wait()
+        arrived(False, j)
         total = total + dot(hidden[j], w_second[j])
     outs[0][...] = act_ref[...] + total[:own]
     for k, out in enumerate(outs[1:], 1):
         out[...] = total[k * own : (k + 1) * own].astype(BF16)
 
 
-def transition(layer, act, xn2, others, weights):
+def transition(act, xn2, others, weights):
     own, width = act.shape
     blocks = len(weights)
-    hid = weights[0].shape[1] // 3
+    hid = sum(part.shape[0] for part in weights[0]) // 3
+    parts = [part for source in weights for part in source]
     return call(
-        functools.partial(transition_kernel, layer),
+        functools.partial(transition_kernel, len(others) + 1, [len(source) for source in weights]),
         [jax.ShapeDtypeStruct((own, width), F32)]
         + [jax.ShapeDtypeStruct((own, width), BF16)] * len(others),
         act,
         xn2,
         *others,
-        far=weights,
+        far=parts,
         scratch=[
             pltpu.VMEM((blocks, 2 * hid, width), BF16),
             pltpu.VMEM((blocks, hid, width), BF16),
-            pltpu.SemaphoreType.DMA((2 * blocks,)),
+            pltpu.SemaphoreType.DMA((2 * len(parts),)),
         ],
-        grant=60,
+        grant=48,
         flops=12 * own * hid * width * blocks,
         moved=6 * hid * width * blocks,
     )
@@ -481,27 +513,35 @@
     nblk = atoms // QB
 
     hid = trans_out.shape[1]
-    packed, feat = call(
-        functools.partial(pack_kernel, rows),
-        [
-            jax.ShapeDtypeStruct((BLOCKS, 3 * hid, width), BF16),
-            jax.ShapeDtypeStruct((atoms + EXTRA, afeat), BF16),
-        ],
-        jnp.swapaxes(trans_in, 2, 3),
-        trans_out,
+    feat = call(
+        functools.partial(feat_kernel, rows),
+        jax.ShapeDtypeStruct((atoms + EXTRA, afeat), BF16),
         atom_feat,
         atom_token[None],
         scalars=(window_start,),
-        grant=60,
-        moved=12 * trans_out.size,
-    )
-
+        grant=48,
+        moved=10**5,
+    )
     up = [(i, i + 1) for i in range(count - 1)]
     prev = lax.ppermute(feat, everyone, up)
     after = lax.ppermute(feat, everyone, [(b, a) for a, b in up])
-
-    across = lax.ppermute(packed, everyone, [(i, i ^ 2) for i in range(count)])
-    sibling = lax.ppermute(packed, everyone, [(i, i ^ 1) for i in range(count)])
+    _, first_part, second_part = lax.optimization_barrier(
+        (feat, jnp.swapaxes(trans_in, 2, 3), trans_out)
+    )
+    matrix = jax.ShapeDtypeStruct((3 * hid, width), BF16)
+    piece = jax.ShapeDtypeStruct((3 * hid // 2, width), BF16)
+    upper, lower, *packed = call(
+        pack_kernel,
+        [piece, piece] + [matrix] * BLOCKS,
+        first_part,
+        second_part,
+        grant=48,
+        moved=12 * trans_out.size,
+    )
+    prev, after, upper = lax.optimization_barrier((prev, after, upper))
+    neighbour = [(i, i ^ 2) for i in range(count)]
+    sibling = [(i, i ^ 1) for i in range(count)]
+    across = [[lax.ppermute(upper, everyone, neighbour)], []]
 
     ext, copies = call(
         functools.partial(encoder_kernel, natom),
@@ -517,23 +557,33 @@
         flops=10**8,
         moved=10**6,
     )
+    span = -(-cols // 128) * 128
+    half = rows // 2
+    step = 24
+
+    def bias_of(part, weights):
+        return pl.pallas_call(
+            bias_kernel,
+            grid=(half // step,),
+            out_shape=[jax.ShapeDtypeStruct((half, heads, span), F32)] * BLOCKS,
+            in_specs=[
+                pl.BlockSpec(
+                    (step, cols, pair.shape[2]), lambda i: (i + part * (half // step), 0, 0)
+                ),
+                pl.BlockSpec(weights.shape, lambda i: (0, 0)),
+            ],
+            out_specs=[pl.BlockSpec((step, heads, span), lambda i: (i, 0, 0))] * BLOCKS,
+            compiler_params=pltpu.CompilerParams(vmem_limit_bytes=(52 if part else 60) * MIB),
+            cost_estimate=pl.CostEstimate(
+                flops=2 * 10**9, bytes_accessed=4 * 10**6, transcendentals=0
+            ),
+        )(pair, weights)
+
+    weights = jnp.swapaxes(pair_weight, 1, 2).reshape(BLOCKS * heads, -1)
+    copies, first_weights = lax.optimization_barrier((copies, weights))
+    low = bias_of(0, first_weights)
     both = lax.all_to_all(copies, "col", 0, 0)
-
-    span = -(-cols // 128) * 128
-    weights = jnp.swapaxes(pair_weight, 1, 2).reshape(BLOCKS * heads, -1)
-    step = 24
-    bias = pl.pallas_call(
-        bias_kernel,
-        grid=(rows // step,),
-        out_shape=[jax.ShapeDtypeStruct((rows, heads, span), F32)] * BLOCKS,
-        in_specs=[
-            pl.BlockSpec((step, cols, pair.shape[2]), lambda i: (i, 0, 0)),
-            pl.BlockSpec(weights.shape, lambda i: (0, 0)),
-        ],
-        out_specs=[pl.BlockSpec((step, heads, span), lambda i: (i, 0, 0))] * BLOCKS,
-        compiler_params=pltpu.CompilerParams(vmem_limit_bytes=56 * MIB),
-        cost_estimate=pl.CostEstimate(flops=4 * 10**9, bytes_accessed=8 * 10**6, transcendentals=0),
-    )(pair, weights)
+    both, low, across[0][0] = lax.optimization_barrier((both, low, across[0][0]))
 
     act, xn, send = call(
         pool_kernel,
@@ -551,65 +601,96 @@
 
     pairs = key_source(rows, cols)
     share = me_col % (rows // cols)
+    peers = ncol // 4
+    shifts = [
+        [(r * ncol + c, r * ncol + (c + 4 * d) % ncol) for r in range(nrow) for c in range(ncol)]
+        for d in range(peers)
+    ]
+    back = [[(b, a) for a, b in pairs_of] for pairs_of in shifts]
+    xn, weights = lax.optimization_barrier((xn, weights))
+    beside, beyond = [], [[], []]
     for layer in range(BLOCKS):
+        last = layer == BLOCKS - 1
         if layer:
             send = lax.dynamic_slice_in_dim(xn, share * cols, cols, 0)
+            send, xn, ready = lax.optimization_barrier((send, xn, across[1][0]))
         came = lax.ppermute(send, everyone, pairs)
-        query = call(
+        matrix = jax.ShapeDtypeStruct((width, width), BF16)
+        query, w_key, w_val, gate = call(
             functools.partial(query_kernel, layer),
-            jax.ShapeDtypeStruct((rows, width), BF16),
+            [
+                jax.ShapeDtypeStruct((rows, width), BF16),
+                matrix,
+                matrix,
+                jax.ShapeDtypeStruct((own, width), F32),
+            ],
             xn,
+            act,
             far=(tok_in,),
-            scratch=[pltpu.VMEM((width, width), BF16), pltpu.SemaphoreType.DMA((1,))],
-            grant=60,
+            scratch=[pltpu.VMEM((width, width), BF16)] * 2 + [pltpu.SemaphoreType.DMA((4,))],
+            grant=48,
             flops=2 * rows * width * width,
-            moved=2 * width * width,
+            moved=8 * width * width,
         )
+        if not layer:
+            high = list(bias_of(1, weights))
+            high[0], lower, *ready = lax.optimization_barrier(
+                (high[0], lower, across[0][0], *packed)
+            )
+            across[0].append(lax.ppermute(lower, everyone, neighbour))
+            beyond[0].append(lax.ppermute(ready[0], everyone, sibling))
+            beside = [lax.ppermute(part, everyone, sibling) for part in ready[1:]]
+        else:
+            beyond[1].append(lax.ppermute(ready, everyone, sibling))
         message = call(
-            functools.partial(attention_kernel, layer),
+            attention_kernel,
             jax.ShapeDtypeStruct((rows, width + span), BF16),
+            query,
+            send,
+            came,
+            low[layer],
+            high[layer],
+            w_key,
+            w_val,
             scalars=(token_mask,),
-            far=(query, send, came, bias[layer], tok_in),
-            scratch=[pltpu.VMEM((cols, width), BF16)] * 2
-            + [pltpu.VMEM((width, width), BF16)] * 2
-            + [
-                pltpu.VMEM((rows, width), BF16),
-                pltpu.VMEM((rows, heads, span), F32),
-                pltpu.SemaphoreType.DMA((6,)),
-            ],
-            grant=60,
+            grant=16,
             flops=10**9,
             moved=8 * 10**6,
         )
+        message = lax.all_to_all(message.reshape(ncol, own, -1), "col", 0, 0)
         if not layer:
-            message, across = lax.optimization_barrier((message, across))
-            beyond = lax.ppermute(across, everyone, [(i, i ^ 1) for i in range(count)])
-            weights = (packed, sibling, across, beyond)
-        message = lax.all_to_all(message.reshape(ncol, own, -1), "col", 0, 0)
-        last = layer == BLOCKS - 1
-        act, xn2 = mix(layer, message, act, tok_in, tok_out, heads)
-        peers = ncol // 4
-        shifts = [
-            [(r * ncol + c, r * ncol + (c + 4 * d) % ncol) for r in range(nrow) for c in range(ncol)]
-            for d in range(peers)
-        ]
-        back = [[(b, a) for a, b in pairs_of] for pairs_of in shifts]
+            message, ready = lax.optimization_barrier((message, packed[1]))
+            across[1].append(lax.ppermute(ready, everyone, neighbour))
+        act, xn2 = mix(layer, message, act, gate, tok_out, heads)
         came_rows = [lax.ppermute(xn2, everyone, shifts[d]) for d in range(1, peers)]
-        act, *parts = transition(layer, act, xn2, came_rows, weights)
+        if not layer:
+            xn2, ready = lax.optimization_barrier((xn2, across[0][1]))
+            beyond[0].append(lax.ppermute(ready, everyone, sibling))
+        act, *parts = transition(
+            act, xn2, came_rows, ([packed[layer]], [beside[layer]], across[layer], beyond[layer])
+        )
         parts = [lax.ppermute(part, everyone, back[d]) for d, part in enumerate(parts, 1)]
-        act, copies = close(act, parts, count if last else ncol, tok_atom if last else None)
+        act, copies = close(act, parts, ncol, tok_atom if last else None)
+        if last:
+            reach = -(-HALO // own)
+            edges = []
+            for d in range(reach):
+                edge = [(r * ncol + ncol - 1 - d, (r + 1) * ncol) for r in range(nrow - 1)]
+                edge += [(r * ncol + d, r * ncol - 1) for r in range(1, nrow)]
+                edges.append(lax.ppermute(copies[0], everyone, edge))
+        gathered = lax.all_to_all(copies, "col", 0, 0).reshape(rows, -1)
         if not last:
-            xn = lax.all_to_all(copies, "col", 0, 0).reshape(rows, width)
-    proj = lax.all_to_all(copies, everyone, 0, 0).reshape(count * own, afeat)
+            xn = gathered
 
     return call(
-        functools.partial(decoder_kernel, natom, rows),
+        functools.partial(decoder_kernel, natom),
         jax.ShapeDtypeStruct((pos_out.shape[0], atoms), F32),
         ext,
         feat,
         prev,
         after,
-        proj,
+        gathered,
+        *edges,
         dec_in,
         dec_out,
         pos_out,

time: 190 us -> 139 us (0.73)
  the two profiles are of different devices: /device:TPU:1 before, /device:TPU:24 now
where the time goes in v3:
time: 139 us; the launch traced here: 137 us
  starting transfers between devices  37.1 us (27%)
  Pallas kernels  36.8 us (26%)
  waiting for transfers between devices  32.1 us (23%)
  blocking collectives  22 us (16%)
  local copies, waits for them, and re-layouts  9.03 us (6%)
    pallas_call x15, Pallas kernels, call(): pl.pallas_call(kernel, out_shape=outs, in_specs=[smem] * len(scalars) + [...  28.8 us
    all_to_all x2, blocking collectives, body(): message = lax.all_to_all(message.reshape(ncol, own, -1), 'col', 0, 0)  22 us
    unnamed x68, local copies, waits for them, and re-layouts  8.33 us
    pallas_call x2, Pallas kernels, bias_of(): pl.pallas_call(bias_kernel, grid=(half // step,), out_shape=[jax.ShapeDty...  8.02 us
    ppermute x2, starting transfers between devices, body(): came = lax.ppermute(send, everyone, pairs)  7.46 us
    ppermute x3, starting transfers between devices, body(): edges.append(lax.ppermute(copies[0], everyone, edge))  7.26 us
    all_to_all x2, waiting for transfers between devices, body(): gathered = lax.all_to_all(copies, 'col', 0, 0).reshape(rows, -1)  6.82 us
    ppermute x2, waiting for transfers between devices, body(): lax.ppermute(part, everyone, back[d])  6.79 us
  transfers between devices with their start and end apart: 22, of which 8 were waited for; matrix products, arithmetic and copies ran while one was open for 1% of the time, Pallas kernels for 21%

profile of v3, /device:TPU:24, one launch (start us, length us, event | category | flops | bytes accessed | tf_op | source)
XLA Modules:
  0.0 137.4 jit_solution(11601554947541050493)
XLA Ops:
  0.0 0.8 copy-done.24
  0.8 0.7 copy-done.27
  1.4 0.7 copy-done.28
  2.6 1.9 %collective-permute-start = (bf16[144,128]{1,0:T(8,128)(2,1)S(1)}, bf16[144,128]{1,0:T(8,128)(2,1)S(1)}, u32[]{:S(2)}, u32[]{:S(2)}) collective-permute-start(bf16[144,128]{1,0:T(8,128)(2,1)S(1)} %shard_map.172.own_ref), channel_id=1, source_target_pairs={{0,1},{1,2},{2,3},{3,4},{4,5},{5,6},{6,7},{7,8},{8,9},{9,10},{10,1... | collective-permute-start | bytes 110600 | tf_op jit(solution)/shard_map/ppermute | solution.py:526
  4.6 5.4 %collective-permute-start.1 = (bf16[144,128]{1,0:T(8,128)(2,1)S(1)}, bf16[144,128]{1,0:T(8,128)(2,1)S(1)}, u32[]{:S(2)}, u32[]{:S(2)}) collective-permute-start(bf16[144,128]{1,0:T(8,128)(2,1)S(1)} %shard_map.172.own_ref), channel_id=1, source_target_pairs={{1,0},{2,1},{3,2},{4,3},{5,4},{6,5},{7,6},{8,7},{9,8},{10,9},{11,1... | collective-permute-start | bytes 110600 | tf_op jit(solution)/shard_map/ppermute | solution.py:527
  10.0 1.3 copy-done.1
  11.3 1.1 copy-done.6
  12.4 1.3 shard_map.173
  13.8 2.0 %shard_map.174 = (bf16[256,128]{1,0:T(8,128)(2,1)S(1)}, bf16[8,144,128]{2,1,0:T(8,128)(2,1)}) custom-call(bf16[144,128]{1,0:T(8,128)(2,1)S(1)} %shard_map.172.own_ref, bf16[144,128]{1,0:T(8,128)(2,1)S(1)} %collective-permute-done.prev_ref, bf16[144,128]{1,0:T(8,128)(2,1)S(1)} %collective-permute-done.1.next_ref, bf16[4,128,128]{2,1,0:T(8,128)(2,1)S(1)} %copy-done.31, ...), custom_call_target="tpu_custom_call" | custom-call | flops 100000000 | bytes 1000000 | tf_op jit(solution)/shard_map/pallas_call | solution.py:26
  16.4 3.4 %all-to-all-start = ((bf16[8,144,128]{2,1,0:T(8,128)(2,1)}), bf16[8,144,128]{2,1,0:T(8,128)(2,1)S(1)}, u32[]{:S(2)}, u32[]{:S(2)}) async-start(bf16[8,144,128]{2,1,0:T(8,128)(2,1)} %get-tuple-element.69), calls=%async_computation | async-start | bytes 589824 | tf_op jit(solution)/shard_map/all_to_all | solution.py:585
  19.9 4.6 %shard_map.175 = (f32[96,16,128]{2,1,0:T(8,128)}, f32[96,16,128]{2,1,0:T(8,128)}) custom-call(bf16[192,96,128]{2,1,0:T(8,128)(2,1)} %pair_ref.3, bf16[32,128]{1,0:T(8,128)(2,1)} %bitcast.18), custom_call_target="tpu_custom_call" | custom-call | flops 2000000000 | bytes 4000000 | tf_op jit(solution)/shard_map/pallas_call | solution.py:565
  24.5 3.5 %all-to-all-done.both_ref = bf16[8,144,128]{2,1,0:T(8,128)(2,1)S(1)} async-done(((bf16[8,144,128]{2,1,0:T(8,128)(2,1)}), bf16[8,144,128]{2,1,0:T(8,128)(2,1)S(1)}, u32[]{:S(2)}, u32[]{:S(2)}) %all-to-all-start) | async-done | bytes 294944 | tf_op jit(solution)/shard_map/all_to_all | solution.py:585
  28.0 1.3 shard_map.176
  29.4 4.3 %collective-permute-start.3 = (bf16[96,768]{1,0:T(8,128)(2,1)S(1)}, bf16[96,768]{1,0:T(8,128)(2,1)S(1)}, u32[]{:S(2)}, u32[]{:S(2)}) collective-permute-start(bf16[96,768]{1,0:T(8,128)(2,1)S(1)} %get-tuple-element.79.here_ref), channel_id=1, source_target_pairs={{4,8},{7,9},{0,16},{3,17},{2,24},{1,25},{12,2},{15,3},{8,18},{9,19... | collective-permute-start | bytes 442376 | tf_op jit(solution)/shard_map/ppermute | solution.py:617
  33.6 3.4 %shard_map.178 = (f32[96,16,128]{2,1,0:T(8,128)S(1)}, f32[96,16,128]{2,1,0:T(8,128)S(1)}) custom-call(bf16[192,96,128]{2,1,0:T(8,128)(2,1)} %pair_ref.3, bf16[32,128]{1,0:T(8,128)(2,1)S(1)} %bitcast.19), custom_call_target="tpu_custom_call" | custom-call | flops 2000000000 | bytes 4000000 | tf_op jit(solution)/shard_map/pallas_call | solution.py:565
  37.1 0.9 copy-done.3
  38.0 0.7 collective-permute-start.4
  38.7 2.4 %shard_map.177 = (bf16[192,768]{1,0:T(8,128)(2,1)S(1)}, bf16[768,768]{1,0:T(8,128)(2,1)S(1)}, bf16[768,768]{1,0:T(8,128)(2,1)S(1)}, f32[24,768]{1,0:T(8,128)S(1)}) custom-call(bf16[192,768]{1,0:T(8,128)(2,1)S(1)} %get-tuple-element.76.xn_ref, f32[24,768]{1,0:T(8,128)S(1)} %get-tuple-element.77.act_ref, bf16[2,4,768,768]{3,2,1,0:T(8,128)(2,1)} %w_in.5), custom_call_target="tpu_custom_call" | custom-call | flops 226492416 | bytes 4718592 | tf_op jit(solution)/shard_map/pallas_call | solution.py:26
  41.2 3.4 %shard_map.179 = bf16[192,896]{1,0:T(8,128)(2,1)S(1)} custom-call(s32[768]{0:T(1024)S(1)} %copy-done.25, bf16[192,768]{1,0:T(8,128)(2,1)S(1)} %get-tuple-element.78.query, bf16[96,768]{1,0:T(8,128)(2,1)S(1)} %get-tuple-element.79.here_ref, bf16[96,768]{1,0:T(8,128)(2,1)S(1)} %collective-permute-done.3.came_ref, f32[96,16,128]{2,1,0:T(8,128)S(1)} %copy-done.5, ...), custom_call_target="tpu_custom_call" | custom-call | flops 1000000000 | bytes 8000000 | tf_op jit(solution)/shard_map/pallas_call | solution.py:26
  44.6 10.3 %all_to_all.25.message = bf16[8,24,896]{2,1,0:T(8,128)(2,1)S(1)} all-to-all(bf16[8,24,896]{2,1,0:T(8,128)(2,1)S(1)} %bitcast.13), channel_id=1, replica_groups=mesh['row'=4,'col'=8] {'col'}, dimensions={0} | all-to-all | bytes 688128 | tf_op jit(solution)/shard_map/all_to_all | solution.py:660
  55.5 1.2 shard_map.180
  57.9 3.4 %collective-permute-done.5.refs_0_ = bf16[24,768]{1,0:T(8,128)(2,1)S(1)} collective-permute-done((bf16[24,768]{1,0:T(8,128)(2,1)S(1)}, bf16[24,768]{1,0:T(8,128)(2,1)S(1)}, u32[]{:S(2)}, u32[]{:S(2)}) %collective-permute-start.5) | collective-permute-done | bytes 36896 | tf_op jit(solution)/shard_map/ppermute | solution.py:665
  61.3 3.3 %shard_map.181 = (f32[24,768]{1,0:T(8,128)S(1)}, bf16[24,768]{1,0:T(8,128)(2,1)S(1)}) custom-call(f32[24,768]{1,0:T(8,128)S(1)} %get-tuple-element.92.act_ref, bf16[24,768]{1,0:T(8,128)(2,1)S(1)} %get-tuple-element.95.xn2, bf16[24,768]{1,0:T(8,128)(2,1)S(1)} %collective-permute-done.5.refs_0_, bf16[576,768]{1,0:T(8,128)(2,1)} %get-tuple-element.96.refs_1_, ...), custom_call_target="tpu_custom_call" | custom-call | flops 169869312 | bytes 3538944 | tf_op jit(solution)/shard_map/pallas_call | solution.py:26
  65.2 3.4 %collective-permute-done.9.refs_0_ = bf16[24,768]{1,0:T(8,128)(2,1)S(1)} collective-permute-done((bf16[24,768]{1,0:T(8,128)(2,1)S(1)}, bf16[24,768]{1,0:T(8,128)(2,1)S(1)}, u32[]{:S(2)}, u32[]{:S(2)}) %collective-permute-start.9) | collective-permute-done | bytes 36896 | tf_op jit(solution)/shard_map/ppermute | solution.py:672
  68.9 0.7 copy-done.9
  69.6 0.6 copy-done.10
  70.2 3.4 %all-to-all-start.2 = ((bf16[8,24,768]{2,1,0:T(8,128)(2,1)}), bf16[8,24,768]{2,1,0:T(8,128)(2,1)S(1)}, u32[]{:S(2)}, u32[]{:S(2)}) async-start(bf16[8,24,768]{2,1,0:T(8,128)(2,1)} %copy-done.9), calls=%async_computation.2 | async-start | bytes 589824 | tf_op jit(solution)/shard_map/all_to_all | solution.py:681
  74.0 6.8 %all-to-all-done.2 = bf16[8,24,768]{2,1,0:T(8,128)(2,1)S(1)} async-done(((bf16[8,24,768]{2,1,0:T(8,128)(2,1)}), bf16[8,24,768]{2,1,0:T(8,128)(2,1)S(1)}, u32[]{:S(2)}, u32[]{:S(2)}) %all-to-all-start.2) | async-done | bytes 294944 | tf_op jit(solution)/shard_map/all_to_all | solution.py:681
  81.0 3.2 %collective-permute-start.11 = (bf16[96,768]{1,0:T(8,128)(2,1)S(1)}, bf16[96,768]{1,0:T(8,128)(2,1)S(1)}, u32[]{:S(2)}, u32[]{:S(2)}) collective-permute-start(bf16[96,768]{1,0:T(8,128)(2,1)S(1)} %constant_dynamic-slice_fusion.here_ref), channel_id=1, source_target_pairs={{4,8},{7,9},{0,16},{3,17},{2,24},{1,25},{12,2},{15,3},{8,18},{9,19... | collective-permute-start | bytes 442376 | tf_op jit(solution)/shard_map/ppermute | solution.py:617
  84.2 0.9 copy-done.11
  85.0 2.5 %shard_map.183 = (bf16[192,768]{1,0:T(8,128)(2,1)S(1)}, bf16[768,768]{1,0:T(8,128)(2,1)S(1)}, bf16[768,768]{1,0:T(8,128)(2,1)S(1)}, f32[24,768]{1,0:T(8,128)S(1)}) custom-call(bf16[192,768]{1,0:T(8,128)(2,1)S(1)} %bitcast.12, f32[24,768]{1,0:T(8,128)S(1)} %copy-done.11, bf16[2,4,768,768]{3,2,1,0:T(8,128)(2,1)} %w_in.5), custom_call_target="tpu_custom_call" | custom-call | flops 226492416 | bytes 4718592 | tf_op jit(solution)/shard_map/pallas_call | solution.py:26
  87.5 3.4 %collective-permute-done.11.came_ref = bf16[96,768]{1,0:T(8,128)(2,1)S(1)} collective-permute-done((bf16[96,768]{1,0:T(8,128)(2,1)S(1)}, bf16[96,768]{1,0:T(8,128)(2,1)S(1)}, u32[]{:S(2)}, u32[]{:S(2)}) %collective-permute-start.11) | collective-permute-done | bytes 147488 | tf_op jit(solution)/shard_map/ppermute | solution.py:617
  90.9 3.4 %shard_map.184 = bf16[192,896]{1,0:T(8,128)(2,1)S(1)} custom-call(s32[768]{0:T(1024)S(1)} %copy-done.25, bf16[192,768]{1,0:T(8,128)(2,1)S(1)} %get-tuple-element.105.query, bf16[96,768]{1,0:T(8,128)(2,1)S(1)} %constant_dynamic-slice_fusion.here_ref, bf16[96,768]{1,0:T(8,128)(2,1)S(1)} %collective-permute-done.11.came_ref, f32[96,16,128]{2,1,0:T(8,128)S(1)} %copy-done.2, ...), custom_call_target="tpu_custom_call" | custom-call | flops 1000000000 | bytes 8000000 | tf_op jit(solution)/shard_map/pallas_call | solution.py:26
  94.3 11.6 %all_to_all.26.message = bf16[8,24,896]{2,1,0:T(8,128)(2,1)S(1)} all-to-all(bf16[8,24,896]{2,1,0:T(8,128)(2,1)S(1)} %bitcast.14), channel_id=1, replica_groups=mesh['row'=4,'col'=8] {'col'}, dimensions={0} | all-to-all | bytes 688128 | tf_op jit(solution)/shard_map/all_to_all | solution.py:660
  106.0 1.2 shard_map.185
  107.2 0.6 collective-permute-start.12
  107.8 3.4 %collective-permute-done.12.refs_0_ = bf16[24,768]{1,0:T(8,128)(2,1)S(1)} collective-permute-done((bf16[24,768]{1,0:T(8,128)(2,1)S(1)}, bf16[24,768]{1,0:T(8,128)(2,1)S(1)}, u32[]{:S(2)}, u32[]{:S(2)}) %collective-permute-start.12) | collective-permute-done | bytes 36896 | tf_op jit(solution)/shard_map/ppermute | solution.py:665
  111.3 3.0 %shard_map.186 = (f32[24,768]{1,0:T(8,128)S(1)}, bf16[24,768]{1,0:T(8,128)(2,1)S(1)}) custom-call(f32[24,768]{1,0:T(8,128)S(1)} %get-tuple-element.112.act_ref, bf16[24,768]{1,0:T(8,128)(2,1)S(1)} %get-tuple-element.113.xn2, bf16[24,768]{1,0:T(8,128)(2,1)S(1)} %collective-permute-done.12.refs_0_, bf16[576,768]{1,0:T(8,128)(2,1)S(1)} %get-tuple-element.114.refs_1_, ...), custom_call_target="tpu_custom_call" | custom-call | flops 169869312 | bytes 3538944 | tf_op jit(solution)/shard_map/pallas_call | solution.py:26
  114.3 0.6 collective-permute-start.15
  114.9 3.4 %collective-permute-done.15.refs_0_ = bf16[24,768]{1,0:T(8,128)(2,1)S(1)} collective-permute-done((bf16[24,768]{1,0:T(8,128)(2,1)S(1)}, bf16[24,768]{1,0:T(8,128)(2,1)S(1)}, u32[]{:S(2)}, u32[]{:S(2)}) %collective-permute-start.15) | collective-permute-done | bytes 36896 | tf_op jit(solution)/shard_map/ppermute | solution.py:672
  118.3 0.9 shard_map.187
  119.3 3.3 %all-to-all-start.4 = ((bf16[8,24,128]{2,1,0:T(8,128)(2,1)}), bf16[8,24,128]{2,1,0:T(8,128)(2,1)S(1)}, u32[]{:S(2)}, u32[]{:S(2)}) async-start(bf16[8,24,128]{2,1,0:T(8,128)(2,1)} %get-tuple-element.118), calls=%async_computation.4 | async-start | bytes 98304 | tf_op jit(solution)/shard_map/all_to_all | solution.py:681
  122.6 0.7 slice_bitcast_fusion
  123.3 4.7 %collective-permute-start.16 = (bf16[24,128]{1,0:T(8,128)(2,1)S(1)}, bf16[24,128]{1,0:T(8,128)(2,1)S(1)}, u32[]{:S(2)}, u32[]{:S(2)}) collective-permute-start(bf16[24,128]{1,0:T(8,128)(2,1)S(1)} %slice_bitcast_fusion), channel_id=1, source_target_pairs={{7,8},{15,16},{23,24},{8,7},{16,15},{24,23}} | collective-permute-start | bytes 18440 | tf_op jit(solution)/shard_map/ppermute | solution.py:680
  128.0 1.3 collective-permute-start.17
  129.3 1.3 collective-permute-start.18
  130.6 4.7 %collective-permute-done.17.refs_1_ = bf16[24,128]{1,0:T(8,128)(2,1)S(1)} collective-permute-done((bf16[24,128]{1,0:T(8,128)(2,1)S(1)}, bf16[24,128]{1,0:T(8,128)(2,1)S(1)}, u32[]{:S(2)}, u32[]{:S(2)}) %collective-permute-start.17) | collective-permute-done | bytes 6176 | tf_op jit(solution)/shard_map/ppermute | solution.py:680
  135.4 2.0 %shard_map.188 = f32[3,128]{1,0:T(4,128)} custom-call(bf16[256,128]{1,0:T(8,128)(2,1)S(1)} %copy-done.18, bf16[144,128]{1,0:T(8,128)(2,1)S(1)} %copy-done.15, bf16[144,128]{1,0:T(8,128)(2,1)S(1)} %copy-done.20, bf16[144,128]{1,0:T(8,128)(2,1)S(1)} %copy-done.22, bf16[192,128]{1,0:T(8,128)(2,1)S(1)} %bitcast.16, ...), custom_call_target="tpu_custom_call" | custom-call | flops 100000000 | bytes 1000000 | tf_op jit(solution)/shard_map/pallas_call | solution.py:26
  (85 shorter events, 4.5 us)
Async XLA Ops:
  2.1 11.7 %copy-start.32 = (bf16[128,128]{1,0:T(8,128)(2,1)S(1)}, bf16[128,128]{1,0:T(8,128)(2,1)}, u32[]{:S(2)}) copy-start(bf16[128,128]{1,0:T(8,128)(2,1)} %w_out.3) | copy-start | bytes 98308
  2.6 11.1 %copy-start.14 = (bf16[144,128]{1,0:T(8,128)(2,1)}, bf16[144,128]{1,0:T(8,128)(2,1)S(1)}, u32[]{:S(2)}) copy-start(bf16[144,128]{1,0:T(8,128)(2,1)S(1)} %shard_map.172.own_ref) | copy-start | bytes 110596
  2.6 11.0 %collective-permute-start = (bf16[144,128]{1,0:T(8,128)(2,1)S(1)}, bf16[144,128]{1,0:T(8,128)(2,1)S(1)}, u32[]{:S(2)}, u32[]{:S(2)}) collective-permute-start(bf16[144,128]{1,0:T(8,128)(2,1)S(1)} %shard_map.172.own_ref), channel_id=1, source_target_pairs={{0,1},{1,2},{2,3},{3,4},{4,5},{5,6},{6,7},{7,8},{8,9},{9,10},{10,1... | collective-permute-start | bytes 110600 | tf_op jit(solution)/shard_map/ppermute | solution.py:526
  4.6 9.1 %collective-permute-start.1 = (bf16[144,128]{1,0:T(8,128)(2,1)S(1)}, bf16[144,128]{1,0:T(8,128)(2,1)S(1)}, u32[]{:S(2)}, u32[]{:S(2)}) collective-permute-start(bf16[144,128]{1,0:T(8,128)(2,1)S(1)} %shard_map.172.own_ref), channel_id=1, source_target_pairs={{1,0},{2,1},{3,2},{4,3},{5,4},{6,5},{7,6},{8,7},{9,8},{10,9},{11,1... | collective-permute-start | bytes 110600 | tf_op jit(solution)/shard_map/ppermute | solution.py:527
  10.0 1.3 copy-start.1
  11.3 1.1 copy-start.6
  12.4 1.4 %copy-start.31 = (bf16[4,128,128]{2,1,0:T(8,128)(2,1)S(1)}, bf16[4,128,128]{2,1,0:T(8,128)(2,1)}, u32[]{:S(2)}) copy-start(bf16[4,128,128]{2,1,0:T(8,128)(2,1)} %w_in.3) | copy-start | bytes 393220
  13.7 2.1 %copy-start.19 = (bf16[144,128]{1,0:T(8,128)(2,1)}, bf16[144,128]{1,0:T(8,128)(2,1)S(1)}, u32[]{:S(2)}) copy-start(bf16[144,128]{1,0:T(8,128)(2,1)S(1)} %collective-permute-done.prev_ref) | copy-start | bytes 110596
  13.7 2.7 %copy-start.21 = (bf16[144,128]{1,0:T(8,128)(2,1)}, bf16[144,128]{1,0:T(8,128)(2,1)S(1)}, u32[]{:S(2)}) copy-start(bf16[144,128]{1,0:T(8,128)(2,1)S(1)} %collective-permute-done.1.next_ref) | copy-start | bytes 110596
  13.7 14.3 %collective-permute-start.2 = (bf16[288,768]{1,0:T(8,128)(2,1)S(1)}, bf16[288,768]{1,0:T(8,128)(2,1)S(1)}, u32[]{:S(2)}, u32[]{:S(2)}) collective-permute-start(bf16[288,768]{1,0:T(8,128)(2,1)S(1)} %get-tuple-element.73), channel_id=1, source_target_pairs={{0,2},{1,3},{2,0},{3,1},{4,6},{5,7},{6,4},{7,5},{8,10},{9,11},{10,... | collective-permute-start | bytes 1327112 | tf_op jit(solution)/shard_map/ppermute | solution.py:544
  16.4 11.6 %all-to-all-start = ((bf16[8,144,128]{2,1,0:T(8,128)(2,1)}), bf16[8,144,128]{2,1,0:T(8,128)(2,1)S(1)}, u32[]{:S(2)}, u32[]{:S(2)}) async-start(bf16[8,144,128]{2,1,0:T(8,128)(2,1)} %get-tuple-element.69), calls=%async_computation | async-start | bytes 589824 | tf_op jit(solution)/shard_map/all_to_all | solution.py:585
  19.9 8.2 %copy-start.29 = (bf16[192,768]{1,0:T(8,128)(2,1)S(1)}, bf16[192,768]{1,0:T(8,128)(2,1)}, u32[]{:S(2)}) copy-start(bf16[192,768]{1,0:T(8,128)(2,1)} %cond.1) | copy-start | bytes 884740
  19.9 8.2 %copy-start.30 = (bf16[128,768]{1,0:T(8,128)(2,1)S(1)}, bf16[128,768]{1,0:T(8,128)(2,1)}, u32[]{:S(2)}) copy-start(bf16[128,768]{1,0:T(8,128)(2,1)} %weight.1) | copy-start | bytes 589828
  28.0 1.3 copy-start.7
  28.0 5.6 %copy-start.33 = (bf16[2,128,16]{1,2,0:T(8,128)(2,1)S(1)}, bf16[2,128,16]{1,2,0:T(8,128)(2,1)}, u32[]{:S(2)}) copy-start(bf16[2,128,16]{1,2,0:T(8,128)(2,1)} %param.29) | copy-start | bytes 24580
  29.4 11.8 %collective-permute-start.3 = (bf16[96,768]{1,0:T(8,128)(2,1)S(1)}, bf16[96,768]{1,0:T(8,128)(2,1)S(1)}, u32[]{:S(2)}, u32[]{:S(2)}) collective-permute-start(bf16[96,768]{1,0:T(8,128)(2,1)S(1)} %get-tuple-element.79.here_ref), channel_id=1, source_target_pairs={{4,8},{7,9},{0,16},{3,17},{2,24},{1,25},{12,2},{15,3},{8,18},{9,19... | collective-permute-start | bytes 442376 | tf_op jit(solution)/shard_map/ppermute | solution.py:617
  38.0 18.8 %collective-permute-start.4 = (bf16[288,768]{1,0:T(8,128)(2,1)}, bf16[288,768]{1,0:T(8,128)(2,1)S(1)}, u32[]{:S(2)}, u32[]{:S(2)}) collective-permute-start(bf16[288,768]{1,0:T(8,128)(2,1)} %get-tuple-element.94), channel_id=1, source_target_pairs={{0,2},{1,3},{2,0},{3,1},{4,6},{5,7},{6,4},{7,5},{8,10},{9,11},{10,... | collective-permute-start | bytes 1327112 | tf_op jit(solution)/shard_map/ppermute | solution.py:640
  38.7 22.6 %collective-permute-start.6 = (bf16[576,768]{1,0:T(8,128)(2,1)}, bf16[576,768]{1,0:T(8,128)(2,1)S(1)}, u32[]{:S(2)}, u32[]{:S(2)}) collective-permute-start(bf16[576,768]{1,0:T(8,128)(2,1)} %get-tuple-element.96.refs_1_), channel_id=1, source_target_pairs={{0,1},{1,0},{2,3},{3,2},{4,5},{5,4},{6,7},{7,6},{8,9},{9,8},{10,11... | collective-permute-start | bytes 2654216 | tf_op jit(solution)/shard_map/ppermute | solution.py:642
  38.7 2.6 %copy-start.5 = (f32[96,16,128]{2,1,0:T(8,128)S(1)}, f32[96,16,128]{2,1,0:T(8,128)}, u32[]{:S(2)}) copy-start(f32[96,16,128]{2,1,0:T(8,128)} %get-tuple-element.80.low) | copy-start | bytes 2359300
  38.7 2.6 %copy-start.25 = (s32[768]{0:T(1024)S(1)}, s32[768]{0:T(1024)}, u32[]{:S(2)}) copy-start(s32[768]{0:T(1024)} %mask_ref.3) | copy-start | bytes 9220
  41.2 14.3 %copy-start.8 = (bf16[288,768]{1,0:T(8,128)(2,1)S(1)}, bf16[288,768]{1,0:T(8,128)(2,1)}, u32[]{:S(2)}) copy-start(bf16[288,768]{1,0:T(8,128)(2,1)} %copy-done.7) | copy-start | bytes 1327108
  41.2 14.3 %copy-start = (bf16[2,768,768]{2,1,0:T(8,128)(2,1)S(1)}, bf16[2,768,768]{2,1,0:T(8,128)(2,1)}, u32[]{:S(2)}) copy-start(bf16[2,768,768]{2,1,0:T(8,128)(2,1)} %w_out.5) | copy-start | bytes 7077892
  54.9 25.9 %collective-permute-start.10 = (bf16[576,768]{1,0:T(8,128)(2,1)S(1)}, bf16[576,768]{1,0:T(8,128)(2,1)}, u32[]{:S(2)}, u32[]{:S(2)}) collective-permute-start(bf16[576,768]{1,0:T(8,128)(2,1)S(1)} %get-tuple-element.114.refs_1_), channel_id=1, source_target_pairs={{0,2},{1,3},{2,0},{3,1},{4,6},{5,7},{6,4},{7,5},{8,10},{9,11},{10,... | collective-permute-start | bytes 2654216 | tf_op jit(solution)/shard_map/ppermute | solution.py:663
  55.5 2.4 %collective-permute-start.7 = (bf16[288,768]{1,0:T(8,128)(2,1)S(1)}, bf16[288,768]{1,0:T(8,128)(2,1)S(1)}, u32[]{:S(2)}, u32[]{:S(2)}) collective-permute-start(bf16[288,768]{1,0:T(8,128)(2,1)S(1)} %copy-done.8), channel_id=1, source_target_pairs={{0,1},{1,0},{2,3},{3,2},{4,5},{5,4},{6,7},{7,6},{8,9},{9,8},{10,11... | collective-permute-start | bytes 1327112 | tf_op jit(solution)/shard_map/ppermute | solution.py:641
  56.8 4.5 %collective-permute-start.8 = (bf16[288,768]{1,0:T(8,128)(2,1)S(1)}, bf16[288,768]{1,0:T(8,128)(2,1)S(1)}, u32[]{:S(2)}, u32[]{:S(2)}) collective-permute-start(bf16[288,768]{1,0:T(8,128)(2,1)S(1)} %collective-permute-done.4.refs_4_), channel_id=1, source_target_pairs={{0,1},{1,0},{2,3},{3,2},{4,5},{5,4},{6,7},{7,6},{8,9},{9,8},{10,11... | collective-permute-start | bytes 1327112 | tf_op jit(solution)/shard_map/ppermute | solution.py:668
  57.3 4.0 %collective-permute-start.5 = (bf16[24,768]{1,0:T(8,128)(2,1)S(1)}, bf16[24,768]{1,0:T(8,128)(2,1)S(1)}, u32[]{:S(2)}, u32[]{:S(2)}) collective-permute-start(bf16[24,768]{1,0:T(8,128)(2,1)S(1)} %get-tuple-element.95.xn2), channel_id=1, source_target_pairs={{0,4},{1,5},{2,6},{3,7},{4,0},{5,1},{6,2},{7,3},{8,12},{9,13},{10,... | collective-permute-start | bytes 110600 | tf_op jit(solution)/shard_map/ppermute | solution.py:665
  64.6 4.0 %collective-permute-start.9 = (bf16[24,768]{1,0:T(8,128)(2,1)S(1)}, bf16[24,768]{1,0:T(8,128)(2,1)S(1)}, u32[]{:S(2)}, u32[]{:S(2)}) collective-permute-start(bf16[24,768]{1,0:T(8,128)(2,1)S(1)} %get-tuple-element.100), channel_id=1, source_target_pairs={{4,0},{5,1},{6,2},{7,3},{0,4},{1,5},{2,6},{3,7},{12,8},{13,9},{14,... | collective-permute-start | bytes 110600 | tf_op jit(solution)/shard_map/ppermute | solution.py:672
  70.2 10.6 %all-to-all-start.2 = ((bf16[8,24,768]{2,1,0:T(8,128)(2,1)}), bf16[8,24,768]{2,1,0:T(8,128)(2,1)S(1)}, u32[]{:S(2)}, u32[]{:S(2)}) async-start(bf16[8,24,768]{2,1,0:T(8,128)(2,1)} %copy-done.9), calls=%async_computation.2 | async-start | bytes 589824 | tf_op jit(solution)/shard_map/all_to_all | solution.py:681
  73.7 34.2 %collective-permute-start.13 = (bf16[576,768]{1,0:T(8,128)(2,1)S(1)}, bf16[576,768]{1,0:T(8,128)(2,1)}, u32[]{:S(2)}, u32[]{:S(2)}) collective-permute-start(bf16[576,768]{1,0:T(8,128)(2,1)S(1)} %get-tuple-element.114.refs_1_), channel_id=1, source_target_pairs={{0,1},{1,0},{2,3},{3,2},{4,5},{5,4},{6,7},{7,6},{8,9},{9,8},{10,11... | collective-permute-start | bytes 2654216 | tf_op jit(solution)/shard_map/ppermute | solution.py:642
  80.9 30.3 %collective-permute-start.14 = (bf16[576,768]{1,0:T(8,128)(2,1)}, bf16[576,768]{1,0:T(8,128)(2,1)S(1)}, u32[]{:S(2)}, u32[]{:S(2)}) collective-permute-start(bf16[576,768]{1,0:T(8,128)(2,1)} %collective-permute-done.10.refs_3_), channel_id=1, source_target_pairs={{0,1},{1,0},{2,3},{3,2},{4,5},{5,4},{6,7},{7,6},{8,9},{9,8},{10,11... | collective-permute-start | bytes 2654216 | tf_op jit(solution)/shard_map/ppermute | solution.py:644
  81.0 10.0 %collective-permute-start.11 = (bf16[96,768]{1,0:T(8,128)(2,1)S(1)}, bf16[96,768]{1,0:T(8,128)(2,1)S(1)}, u32[]{:S(2)}, u32[]{:S(2)}) collective-permute-start(bf16[96,768]{1,0:T(8,128)(2,1)S(1)} %constant_dynamic-slice_fusion.here_ref), channel_id=1, source_target_pairs={{4,8},{7,9},{0,16},{3,17},{2,24},{1,25},{12,2},{15,3},{8,18},{9,19... | collective-permute-start | bytes 442376 | tf_op jit(solution)/shard_map/ppermute | solution.py:617
  85.0 5.9 %copy-start.2 = (f32[96,16,128]{2,1,0:T(8,128)S(1)}, f32[96,16,128]{2,1,0:T(8,128)}, u32[]{:S(2)}) copy-start(f32[96,16,128]{2,1,0:T(8,128)} %get-tuple-element.107.low) | copy-start | bytes 2359300
  85.0 5.9 %copy-start.4 = (f32[96,16,128]{2,1,0:T(8,128)S(1)}, f32[96,16,128]{2,1,0:T(8,128)}, u32[]{:S(2)}) copy-start(f32[96,16,128]{2,1,0:T(8,128)} %copy-done.3) | copy-start | bytes 2359300
  90.9 15.0 %copy-start.12 = (f32[24,768]{1,0:T(8,128)S(1)}, f32[24,768]{1,0:T(8,128)}, u32[]{:S(2)}) copy-start(f32[24,768]{1,0:T(8,128)} %copy-done.10) | copy-start | bytes 221188
  107.2 4.0 %collective-permute-start.12 = (bf16[24,768]{1,0:T(8,128)(2,1)S(1)}, bf16[24,768]{1,0:T(8,128)(2,1)S(1)}, u32[]{:S(2)}, u32[]{:S(2)}) collective-permute-start(bf16[24,768]{1,0:T(8,128)(2,1)S(1)} %get-tuple-element.113.xn2), channel_id=1, source_target_pairs={{0,4},{1,5},{2,6},{3,7},{4,0},{5,1},{6,2},{7,3},{8,12},{9,13},{10,... | collective-permute-start | bytes 110600 | tf_op jit(solution)/shard_map/ppermute | solution.py:665
  111.2 7.1 %copy-start.13 = (bf16[768,128]{1,0:T(8,128)(2,1)S(1)}, bf16[768,128]{1,0:T(8,128)(2,1)}, u32[]{:S(2)}) copy-start(bf16[768,128]{1,0:T(8,128)(2,1)} %refs_1_.1) | copy-start | bytes 589828
  111.2 24.1 %copy-start.15 = (bf16[144,128]{1,0:T(8,128)(2,1)S(1)}, bf16[144,128]{1,0:T(8,128)(2,1)}, u32[]{:S(2)}) copy-start(bf16[144,128]{1,0:T(8,128)(2,1)} %copy-done.14) | copy-start | bytes 110596
  111.2 24.1 %copy-start.16 = (bf16[4,128,128]{2,1,0:T(8,128)(2,1)S(1)}, bf16[4,128,128]{2,1,0:T(8,128)(2,1)}, u32[]{:S(2)}) copy-start(bf16[4,128,128]{2,1,0:T(8,128)(2,1)} %refs_3_.1) | copy-start | bytes 393220
  111.2 24.1 %copy-start.18 = (bf16[256,128]{1,0:T(8,128)(2,1)S(1)}, bf16[256,128]{1,0:T(8,128)(2,1)}, u32[]{:S(2)}) copy-start(bf16[256,128]{1,0:T(8,128)(2,1)} %copy-done.17) | copy-start | bytes 196612
  111.2 24.1 %copy-start.20 = (bf16[144,128]{1,0:T(8,128)(2,1)S(1)}, bf16[144,128]{1,0:T(8,128)(2,1)}, u32[]{:S(2)}) copy-start(bf16[144,128]{1,0:T(8,128)(2,1)} %copy-done.19) | copy-start | bytes 110596
  111.2 24.1 %copy-start.22 = (bf16[144,128]{1,0:T(8,128)(2,1)S(1)}, bf16[144,128]{1,0:T(8,128)(2,1)}, u32[]{:S(2)}) copy-start(bf16[144,128]{1,0:T(8,128)(2,1)} %copy-done.21) | copy-start | bytes 110596
  111.3 24.1 %copy-start.23 = (bf16[128,128]{1,0:T(8,128)(2,1)S(1)}, bf16[128,128]{1,0:T(8,128)(2,1)}, u32[]{:S(2)}) copy-start(bf16[128,128]{1,0:T(8,128)(2,1)} %refs_4_.1) | copy-start | bytes 98308
  111.3 24.1 %copy-start.26 = (bf16[3,128]{1,0:T(4,128)(2,1)S(1)}, bf16[3,128]{1,0:T(4,128)(2,1)}, u32[]{:S(2)}) copy-start(bf16[3,128]{1,0:T(4,128)(2,1)} %refs_5_.1) | copy-start | bytes 2308
  114.3 4.0 %collective-permute-start.15 = (bf16[24,768]{1,0:T(8,128)(2,1)S(1)}, bf16[24,768]{1,0:T(8,128)(2,1)S(1)}, u32[]{:S(2)}, u32[]{:S(2)}) collective-permute-start(bf16[24,768]{1,0:T(8,128)(2,1)S(1)} %get-tuple-element.117), channel_id=1, source_target_pairs={{4,0},{5,1},{6,2},{7,3},{0,4},{1,5},{2,6},{3,7},{12,8},{13,9},{14,... | collective-permute-start | bytes 110600 | tf_op jit(solution)/shard_map/ppermute | solution.py:672
  119.3 16.1 %all-to-all-start.4 = ((bf16[8,24,128]{2,1,0:T(8,128)(2,1)}), bf16[8,24,128]{2,1,0:T(8,128)(2,1)S(1)}, u32[]{:S(2)}, u32[]{:S(2)}) async-start(bf16[8,24,128]{2,1,0:T(8,128)(2,1)} %get-tuple-element.118), calls=%async_computation.4 | async-start | bytes 98304 | tf_op jit(solution)/shard_map/all_to_all | solution.py:681
  123.3 7.3 %collective-permute-start.16 = (bf16[24,128]{1,0:T(8,128)(2,1)S(1)}, bf16[24,128]{1,0:T(8,128)(2,1)S(1)}, u32[]{:S(2)}, u32[]{:S(2)}) collective-permute-start(bf16[24,128]{1,0:T(8,128)(2,1)S(1)} %slice_bitcast_fusion), channel_id=1, source_target_pairs={{7,8},{15,16},{23,24},{8,7},{16,15},{24,23}} | collective-permute-start | bytes 18440 | tf_op jit(solution)/shard_map/ppermute | solution.py:680
  128.0 7.3 %collective-permute-start.17 = (bf16[24,128]{1,0:T(8,128)(2,1)S(1)}, bf16[24,128]{1,0:T(8,128)(2,1)S(1)}, u32[]{:S(2)}, u32[]{:S(2)}) collective-permute-start(bf16[24,128]{1,0:T(8,128)(2,1)S(1)} %slice_bitcast_fusion), channel_id=1, source_target_pairs={{6,8},{14,16},{22,24},{9,7},{17,15},{25,23}} | collective-permute-start | bytes 18440 | tf_op jit(solution)/shard_map/ppermute | solution.py:680
  129.3 6.0 %collective-permute-start.18 = (bf16[24,128]{1,0:T(8,128)(2,1)S(1)}, bf16[24,128]{1,0:T(8,128)(2,1)S(1)}, u32[]{:S(2)}, u32[]{:S(2)}) collective-permute-start(bf16[24,128]{1,0:T(8,128)(2,1)S(1)} %slice_bitcast_fusion), channel_id=1, source_target_pairs={{5,8},{13,16},{21,24},{10,7},{18,15},{26,23}} | collective-permute-start | bytes 18440 | tf_op jit(solution)/shard_map/ppermute | solution.py:680
  (8 other events, 5.8 us)

commit v4 on v3

--- a/solution.py
+++ b/solution.py
@@ -160,30 +160,17 @@
 
 
 def decoder_kernel(
-    natom, x1_ref, own_ref, prev_ref, next_ref, proj_ref, *refs
+    natom, row_tokens, x1_ref, own_ref, prev_ref, next_ref, proj, w_in, w_out, pos, out
 ):
-    *edges, w_in, w_out, pos, out = refs
     rows = own_ref.shape[0] - EXTRA
-    proj = proj_ref[...].astype(F32)
     tokens = proj.shape[0]
-    _, col, me = device()
-    edges = [edge[...].astype(F32) for edge in edges]
-    reach = len(edges) * edges[0].shape[0]
-    rest = tokens - reach
-    edge_low = jnp.where(col == 0, jnp.concatenate(edges[::-1], 0), proj[rest:])
-    edge_high = jnp.where(
-        col == lax.axis_size("col") - 1, jnp.concatenate(edges, 0), proj[:reach]
-    )
-    tables = (
-        jnp.concatenate([proj[:rest], edge_low], 0),
-        proj,
-        jnp.concatenate([edge_high, proj[reach:]], 0),
-    )
+    me = device()[2]
     spread = []
-    for table, ref in zip(tables, (prev_ref, own_ref, next_ref)):
+    for k, ref in enumerate((prev_ref, own_ref, next_ref)):
         spot = ref[rows:].astype(F32)[0:1].astype(jnp.int32)
+        spot = spot + (me + k - 1) // lax.axis_size("col") * row_tokens
         onehot = (iota((tokens, rows), 0) == spot).astype(F32).astype(BF16)
-        spread.append(dot_tn(onehot, table.astype(BF16)))
+        spread.append(dot_tn(onehot, proj[...]))
     spread = jnp.concatenate([spread[0][rows - HALO :], spread[1], spread[2][:HALO]], 0)
     x = (x1_ref[...].astype(F32) + spread).astype(BF16)
     xn = normed(x).astype(BF16)
@@ -214,13 +201,13 @@
 
 def pack_kernel(first, second, upper, lower, *outs):
     hid = second.shape[1]
-    half = upper.shape[0]
+    part = upper.shape[0]
     for layer, out in enumerate(outs):
         out[:hid] = first[layer, 0]
         out[hid : 2 * hid] = first[layer, 1]
         out[2 * hid :] = second[layer]
-    upper[...] = outs[0][:half]
-    lower[...] = outs[0][half:]
+    upper[...] = outs[0][:part]
+    lower[...] = outs[0][part:]
 
 
 def bias_kernel(pair_ref, weight, *outs):
@@ -529,10 +516,10 @@
         (feat, jnp.swapaxes(trans_in, 2, 3), trans_out)
     )
     matrix = jax.ShapeDtypeStruct((3 * hid, width), BF16)
-    piece = jax.ShapeDtypeStruct((3 * hid // 2, width), BF16)
     upper, lower, *packed = call(
         pack_kernel,
-        [piece, piece] + [matrix] * BLOCKS,
+        [jax.ShapeDtypeStruct((rows_of * hid, width), BF16) for rows_of in (1, 2)]
+        + [matrix] * BLOCKS,
         first_part,
         second_part,
         grant=48,
@@ -670,27 +657,20 @@
             act, xn2, came_rows, ([packed[layer]], [beside[layer]], across[layer], beyond[layer])
         )
         parts = [lax.ppermute(part, everyone, back[d]) for d, part in enumerate(parts, 1)]
-        act, copies = close(act, parts, ncol, tok_atom if last else None)
-        if last:
-            reach = -(-HALO // own)
-            edges = []
-            for d in range(reach):
-                edge = [(r * ncol + ncol - 1 - d, (r + 1) * ncol) for r in range(nrow - 1)]
-                edge += [(r * ncol + d, r * ncol - 1) for r in range(1, nrow)]
-                edges.append(lax.ppermute(copies[0], everyone, edge))
-        gathered = lax.all_to_all(copies, "col", 0, 0).reshape(rows, -1)
+        act, copies = close(act, parts, count if last else ncol, tok_atom if last else None)
+        axes = everyone if last else "col"
+        gathered = lax.all_to_all(copies, axes, 0, 0).reshape(copies.shape[0] * own, -1)
         if not last:
             xn = gathered
 
     return call(
-        functools.partial(decoder_kernel, natom),
+        functools.partial(decoder_kernel, natom, rows),
         jax.ShapeDtypeStruct((pos_out.shape[0], atoms), F32),
         ext,
         feat,
         prev,
         after,
         gathered,
-        *edges,
         dec_in,
         dec_out,
         pos_out,

time: 139 us -> 146 us (1.050)
  the two profiles are of different devices: /device:TPU:24 before, /device:TPU:1 now
where the time goes in v4:
time: 146 us; the launch traced here: 145 us
  starting transfers between devices  42 us (29%)
  Pallas kernels  37.4 us (26%)
  blocking collectives  29.8 us (20%)
  waiting for transfers between devices  25.7 us (18%)
  local copies, waits for them, and re-layouts  9.48 us (6%)
    pallas_call x15, Pallas kernels, call(): pl.pallas_call(kernel, out_shape=outs, in_specs=[smem] * len(scalars) + [...  29.3 us
    all_to_all x1, blocking collectives, body(): lax.all_to_all(copies, axes, 0, 0).reshape(copies.shape[0] * own, -1)  19.8 us
    ppermute x2, starting transfers between devices, body(): came = lax.ppermute(send, everyone, pairs)  12.1 us
    all_to_all x1, blocking collectives, body(): message = lax.all_to_all(message.reshape(ncol, own, -1), 'col', 0, 0)  9.97 us
    unnamed x72, local copies, waits for them, and re-layouts  9.47 us
    pallas_call x2, Pallas kernels, bias_of(): pl.pallas_call(bias_kernel, grid=(half // step,), out_shape=[jax.ShapeDty...  8.03 us
    all_to_all x1, waiting for transfers between devices, body(): lax.all_to_all(copies, axes, 0, 0).reshape(copies.shape[0] * own, -1)  7.07 us
    all_to_all x1, waiting for transfers between devices, body(): message = lax.all_to_all(message.reshape(ncol, own, -1), 'col', 0, 0)  6.05 us
  transfers between devices with their start and end apart: 19, of which 9 were waited for; matrix products, arithmetic and copies ran while one was open for 0% of the time, Pallas kernels for 18%

profile of v4, /device:TPU:1, one launch (start us, length us, event | category | flops | bytes accessed | tf_op | source)
XLA Modules:
  0.0 144.7 jit_solution(13031993443258752344)
XLA Ops:
  0.0 0.8 copy-done.26
  0.8 0.7 copy-done.29
  1.4 0.7 copy-done.30
  2.6 4.5 %collective-permute-start = (bf16[144,128]{1,0:T(8,128)(2,1)S(1)}, bf16[144,128]{1,0:T(8,128)(2,1)S(1)}, u32[]{:S(2)}, u32[]{:S(2)}) collective-permute-start(bf16[144,128]{1,0:T(8,128)(2,1)S(1)} %shard_map.172.own_ref), channel_id=1, source_target_pairs={{0,1},{1,2},{2,3},{3,4},{4,5},{5,6},{6,7},{7,8},{8,9},{9,10},{10,1... | collective-permute-start | bytes 110600 | tf_op jit(solution)/shard_map/ppermute | solution.py:513
  7.2 1.9 %collective-permute-start.1 = (bf16[144,128]{1,0:T(8,128)(2,1)S(1)}, bf16[144,128]{1,0:T(8,128)(2,1)S(1)}, u32[]{:S(2)}, u32[]{:S(2)}) collective-permute-start(bf16[144,128]{1,0:T(8,128)(2,1)S(1)} %shard_map.172.own_ref), channel_id=1, source_target_pairs={{1,0},{2,1},{3,2},{4,3},{5,4},{6,5},{7,6},{8,7},{9,8},{10,9},{11,1... | collective-permute-start | bytes 110600 | tf_op jit(solution)/shard_map/ppermute | solution.py:514
  9.1 1.3 copy-done.1
  10.4 1.1 copy-done.8
  11.4 1.3 shard_map.173
  12.7 0.9 copy-done.2
  13.7 1.3 collective-permute-start.2
  15.0 2.0 %shard_map.174 = (bf16[256,128]{1,0:T(8,128)(2,1)S(1)}, bf16[8,144,128]{2,1,0:T(8,128)(2,1)}) custom-call(bf16[144,128]{1,0:T(8,128)(2,1)S(1)} %shard_map.172.own_ref, bf16[144,128]{1,0:T(8,128)(2,1)S(1)} %collective-permute-done.prev_ref, bf16[144,128]{1,0:T(8,128)(2,1)S(1)} %collective-permute-done.1.next_ref, bf16[4,128,128]{2,1,0:T(8,128)(2,1)S(1)} %copy-done.33, ...), custom_call_target="tpu_custom_call" | custom-call | flops 100000000 | bytes 1000000 | tf_op jit(solution)/shard_map/pallas_call | solution.py:26
  17.0 0.6 copy-done.19
  17.6 4.6 %all-to-all-start = ((bf16[8,144,128]{2,1,0:T(8,128)(2,1)}), bf16[8,144,128]{2,1,0:T(8,128)(2,1)S(1)}, u32[]{:S(2)}, u32[]{:S(2)}) async-start(bf16[8,144,128]{2,1,0:T(8,128)(2,1)} %get-tuple-element.69), calls=%async_computation | async-start | bytes 589824 | tf_op jit(solution)/shard_map/all_to_all | solution.py:572
  22.2 4.6 %shard_map.175 = (f32[96,16,128]{2,1,0:T(8,128)}, f32[96,16,128]{2,1,0:T(8,128)}) custom-call(bf16[192,96,128]{2,1,0:T(8,128)(2,1)} %pair_ref.3, bf16[32,128]{1,0:T(8,128)(2,1)} %bitcast.15), custom_call_target="tpu_custom_call" | custom-call | flops 2000000000 | bytes 4000000 | tf_op jit(solution)/shard_map/pallas_call | solution.py:552
  26.8 1.2 all-to-all-done.both_ref
  28.0 1.3 shard_map.176
  29.3 3.4 %shard_map.178 = (f32[96,16,128]{2,1,0:T(8,128)S(1)}, f32[96,16,128]{2,1,0:T(8,128)S(1)}) custom-call(bf16[192,96,128]{2,1,0:T(8,128)(2,1)} %pair_ref.3, bf16[32,128]{1,0:T(8,128)(2,1)S(1)} %bitcast.16), custom_call_target="tpu_custom_call" | custom-call | flops 2000000000 | bytes 4000000 | tf_op jit(solution)/shard_map/pallas_call | solution.py:552
  32.8 1.3 collective-permute-start.4
  34.1 5.2 %collective-permute-start.3 = (bf16[96,768]{1,0:T(8,128)(2,1)S(1)}, bf16[96,768]{1,0:T(8,128)(2,1)S(1)}, u32[]{:S(2)}, u32[]{:S(2)}) collective-permute-start(bf16[96,768]{1,0:T(8,128)(2,1)S(1)} %get-tuple-element.79.here_ref), channel_id=1, source_target_pairs={{4,8},{7,9},{0,16},{3,17},{2,24},{1,25},{12,2},{15,3},{8,18},{9,19... | collective-permute-start | bytes 442376 | tf_op jit(solution)/shard_map/ppermute | solution.py:604
  39.4 2.4 %shard_map.177 = (bf16[192,768]{1,0:T(8,128)(2,1)S(1)}, bf16[768,768]{1,0:T(8,128)(2,1)S(1)}, bf16[768,768]{1,0:T(8,128)(2,1)S(1)}, f32[24,768]{1,0:T(8,128)S(1)}) custom-call(bf16[192,768]{1,0:T(8,128)(2,1)S(1)} %get-tuple-element.76.xn_ref, f32[24,768]{1,0:T(8,128)S(1)} %get-tuple-element.77.act_ref, bf16[2,4,768,768]{3,2,1,0:T(8,128)(2,1)} %w_in.6), custom_call_target="tpu_custom_call" | custom-call | flops 226492416 | bytes 4718592 | tf_op jit(solution)/shard_map/pallas_call | solution.py:26
  41.8 0.9 collective-permute-done.3.came_ref
  42.7 4.1 %shard_map.179 = bf16[192,896]{1,0:T(8,128)(2,1)} custom-call(s32[768]{0:T(1024)S(1)} %copy-done.27, bf16[192,768]{1,0:T(8,128)(2,1)S(1)} %get-tuple-element.78.query, bf16[96,768]{1,0:T(8,128)(2,1)S(1)} %get-tuple-element.79.here_ref, bf16[96,768]{1,0:T(8,128)(2,1)S(1)} %collective-permute-done.3.came_ref, f32[96,16,128]{2,1,0:T(8,128)S(1)} %copy-done.7, ...), custom_call_target="tpu_custom_call" | custom-call | flops 1000000000 | bytes 8000000 | tf_op jit(solution)/shard_map/pallas_call | solution.py:26
  46.9 5.4 %all-to-all-start.1 = ((bf16[8,24,896]{2,1,0:T(8,128)(2,1)}), bf16[8,24,896]{2,1,0:T(8,128)(2,1)S(1)}, u32[]{:S(2)}, u32[]{:S(2)}) async-start(bf16[8,24,896]{2,1,0:T(8,128)(2,1)} %bitcast.4), calls=%async_computation.1 | async-start | bytes 688128 | tf_op jit(solution)/shard_map/all_to_all | solution.py:647
  52.3 6.0 %all-to-all-done.1.message = bf16[8,24,896]{2,1,0:T(8,128)(2,1)S(1)} async-done(((bf16[8,24,896]{2,1,0:T(8,128)(2,1)}), bf16[8,24,896]{2,1,0:T(8,128)(2,1)S(1)}, u32[]{:S(2)}, u32[]{:S(2)}) %all-to-all-start.1) | async-done | bytes 344096 | tf_op jit(solution)/shard_map/all_to_all | solution.py:647
  58.3 0.9 copy-done.18
  59.2 1.2 shard_map.180
  60.4 1.8 %collective-permute-start.8 = (bf16[384,768]{1,0:T(8,128)(2,1)}, bf16[384,768]{1,0:T(8,128)(2,1)S(1)}, u32[]{:S(2)}, u32[]{:S(2)}) collective-permute-start(bf16[384,768]{1,0:T(8,128)(2,1)} %collective-permute-done.4.refs_4_), channel_id=1, source_target_pairs={{0,1},{1,0},{2,3},{3,2},{4,5},{5,4},{6,7},{7,6},{8,9},{9,8},{10,11... | collective-permute-start | bytes 1769480 | tf_op jit(solution)/shard_map/ppermute | solution.py:655
  63.2 1.1 collective-permute-done.7.refs_5_
  64.3 1.7 %collective-permute-done.5.refs_0_ = bf16[24,768]{1,0:T(8,128)(2,1)S(1)} collective-permute-done((bf16[24,768]{1,0:T(8,128)(2,1)S(1)}, bf16[24,768]{1,0:T(8,128)(2,1)S(1)}, u32[]{:S(2)}, u32[]{:S(2)}) %collective-permute-start.5) | collective-permute-done | bytes 36896 | tf_op jit(solution)/shard_map/ppermute | solution.py:652
  66.0 3.0 %shard_map.181 = (f32[24,768]{1,0:T(8,128)S(1)}, bf16[24,768]{1,0:T(8,128)(2,1)S(1)}) custom-call(f32[24,768]{1,0:T(8,128)S(1)} %get-tuple-element.92.act_ref, bf16[24,768]{1,0:T(8,128)(2,1)S(1)} %get-tuple-element.95.xn2, bf16[24,768]{1,0:T(8,128)(2,1)S(1)} %collective-permute-done.5.refs_0_, bf16[576,768]{1,0:T(8,128)(2,1)S(1)} %copy-done.3, ...), custom_call_target="tpu_custom_call" | custom-call | flops 169869312 | bytes 3538944 | tf_op jit(solution)/shard_map/pallas_call | solution.py:26
  69.3 2.8 %collective-permute-done.9.refs_0_ = bf16[24,768]{1,0:T(8,128)(2,1)S(1)} collective-permute-done((bf16[24,768]{1,0:T(8,128)(2,1)S(1)}, bf16[24,768]{1,0:T(8,128)(2,1)S(1)}, u32[]{:S(2)}, u32[]{:S(2)}) %collective-permute-start.9) | collective-permute-done | bytes 36896 | tf_op jit(solution)/shard_map/ppermute | solution.py:659
  72.4 0.7 copy-done.9
  73.1 0.6 copy-done.10
  73.7 5.2 %all-to-all-start.2 = ((bf16[8,24,768]{2,1,0:T(8,128)(2,1)}), bf16[8,24,768]{2,1,0:T(8,128)(2,1)S(1)}, u32[]{:S(2)}, u32[]{:S(2)}) async-start(bf16[8,24,768]{2,1,0:T(8,128)(2,1)} %copy-done.9), calls=%async_computation.2 | async-start | bytes 589824 | tf_op jit(solution)/shard_map/all_to_all | solution.py:662
  79.1 7.1 %all-to-all-done.2 = bf16[8,24,768]{2,1,0:T(8,128)(2,1)S(1)} async-done(((bf16[8,24,768]{2,1,0:T(8,128)(2,1)}), bf16[8,24,768]{2,1,0:T(8,128)(2,1)S(1)}, u32[]{:S(2)}, u32[]{:S(2)}) %all-to-all-start.2) | async-done | bytes 294944 | tf_op jit(solution)/shard_map/all_to_all | solution.py:662
  86.2 1.6 %collective-permute-start.14 = (bf16[576,768]{1,0:T(8,128)(2,1)S(1)}, bf16[576,768]{1,0:T(8,128)(2,1)S(1)}, u32[]{:S(2)}, u32[]{:S(2)}) collective-permute-start(bf16[576,768]{1,0:T(8,128)(2,1)S(1)} %collective-permute-done.10.refs_3_), channel_id=1, source_target_pairs={{0,1},{1,0},{2,3},{3,2},{4,5},{5,4},{6,7},{7,6},{8,9},{9,8},{10,11... | collective-permute-start | bytes 2654216 | tf_op jit(solution)/shard_map/ppermute | solution.py:631
  87.8 6.8 %collective-permute-start.11 = (bf16[96,768]{1,0:T(8,128)(2,1)S(1)}, bf16[96,768]{1,0:T(8,128)(2,1)S(1)}, u32[]{:S(2)}, u32[]{:S(2)}) collective-permute-start(bf16[96,768]{1,0:T(8,128)(2,1)S(1)} %constant_dynamic-slice_fusion.here_ref), channel_id=1, source_target_pairs={{4,8},{7,9},{0,16},{3,17},{2,24},{1,25},{12,2},{15,3},{8,18},{9,19... | collective-permute-start | bytes 442376 | tf_op jit(solution)/shard_map/ppermute | solution.py:604
  94.6 0.9 copy-done.11
  95.5 2.5 %shard_map.183 = (bf16[192,768]{1,0:T(8,128)(2,1)S(1)}, bf16[768,768]{1,0:T(8,128)(2,1)S(1)}, bf16[768,768]{1,0:T(8,128)(2,1)S(1)}, f32[24,768]{1,0:T(8,128)S(1)}) custom-call(bf16[192,768]{1,0:T(8,128)(2,1)S(1)} %bitcast.10, f32[24,768]{1,0:T(8,128)S(1)} %copy-done.11, bf16[2,4,768,768]{3,2,1,0:T(8,128)(2,1)} %w_in.6), custom_call_target="tpu_custom_call" | custom-call | flops 226492416 | bytes 4718592 | tf_op jit(solution)/shard_map/pallas_call | solution.py:26
  98.3 3.4 %shard_map.184 = bf16[192,896]{1,0:T(8,128)(2,1)S(1)} custom-call(s32[768]{0:T(1024)S(1)} %copy-done.27, bf16[192,768]{1,0:T(8,128)(2,1)S(1)} %get-tuple-element.105.query, bf16[96,768]{1,0:T(8,128)(2,1)S(1)} %constant_dynamic-slice_fusion.here_ref, bf16[96,768]{1,0:T(8,128)(2,1)S(1)} %collective-permute-done.11.came_ref, f32[96,16,128]{2,1,0:T(8,128)S(1)} %copy-done.4, ...), custom_call_target="tpu_custom_call" | custom-call | flops 1000000000 | bytes 8000000 | tf_op jit(solution)/shard_map/pallas_call | solution.py:26
  101.7 10.0 %all_to_all.25.message = bf16[8,24,896]{2,1,0:T(8,128)(2,1)S(1)} all-to-all(bf16[8,24,896]{2,1,0:T(8,128)(2,1)S(1)} %bitcast.11), channel_id=1, replica_groups=mesh['row'=4,'col'=8] {'col'}, dimensions={0} | all-to-all | bytes 688128 | tf_op jit(solution)/shard_map/all_to_all | solution.py:647
  111.6 1.2 shard_map.185
  113.3 2.4 %collective-permute-done.12.refs_0_ = bf16[24,768]{1,0:T(8,128)(2,1)S(1)} collective-permute-done((bf16[24,768]{1,0:T(8,128)(2,1)S(1)}, bf16[24,768]{1,0:T(8,128)(2,1)S(1)}, u32[]{:S(2)}, u32[]{:S(2)}) %collective-permute-start.12) | collective-permute-done | bytes 36896 | tf_op jit(solution)/shard_map/ppermute | solution.py:652
  115.8 3.3 %shard_map.186 = (f32[24,768]{1,0:T(8,128)S(1)}, bf16[24,768]{1,0:T(8,128)(2,1)S(1)}) custom-call(f32[24,768]{1,0:T(8,128)S(1)} %get-tuple-element.112.act_ref, bf16[24,768]{1,0:T(8,128)(2,1)S(1)} %get-tuple-element.113.xn2, bf16[24,768]{1,0:T(8,128)(2,1)S(1)} %collective-permute-done.12.refs_0_, bf16[576,768]{1,0:T(8,128)(2,1)} %get-tuple-element.114.refs_1_, ...), custom_call_target="tpu_custom_call" | custom-call | flops 169869312 | bytes 3538944 | tf_op jit(solution)/shard_map/pallas_call | solution.py:26
  119.5 2.4 %collective-permute-done.15.refs_0_ = bf16[24,768]{1,0:T(8,128)(2,1)S(1)} collective-permute-done((bf16[24,768]{1,0:T(8,128)(2,1)S(1)}, bf16[24,768]{1,0:T(8,128)(2,1)S(1)}, u32[]{:S(2)}, u32[]{:S(2)}) %collective-permute-start.15) | collective-permute-done | bytes 36896 | tf_op jit(solution)/shard_map/ppermute | solution.py:659
  122.0 0.8 shard_map.187
  122.8 19.8 %all_to_all.26 = bf16[32,24,128]{2,1,0:T(8,128)(2,1)S(1)} all-to-all(bf16[32,24,128]{2,1,0:T(8,128)(2,1)S(1)} %get-tuple-element.118), channel_id=1, replica_groups=mesh['row'=4,'col'=8] {'row','col'}, dimensions={0} | all-to-all | bytes 393216 | tf_op jit(solution)/shard_map/all_to_all | solution.py:662
  142.6 2.1 %shard_map.188 = f32[3,128]{1,0:T(4,128)} custom-call(bf16[256,128]{1,0:T(8,128)(2,1)S(1)} %copy-done.20, bf16[144,128]{1,0:T(8,128)(2,1)S(1)} %copy-done.15, bf16[144,128]{1,0:T(8,128)(2,1)S(1)} %copy-done.22, bf16[144,128]{1,0:T(8,128)(2,1)S(1)} %copy-done.24, bf16[768,128]{1,0:T(8,128)(2,1)S(1)} %bitcast.13, bf16[4,128,128]{2,1,0:T(8,128)(2,1)S(1)} %copy-done.16, ...), custom_call_target="tpu_custom_call" | custom-call | flops 100000000 | bytes 1000000 | tf_op jit(solution)/shard_map/pallas_call | solution.py:26
  (82 shorter events, 3.6 us)
Async XLA Ops:
  2.1 12.9 %copy-start.34 = (bf16[128,128]{1,0:T(8,128)(2,1)S(1)}, bf16[128,128]{1,0:T(8,128)(2,1)}, u32[]{:S(2)}) copy-start(bf16[128,128]{1,0:T(8,128)(2,1)} %w_out.4) | copy-start | bytes 98308
  2.6 12.3 %copy-start.14 = (bf16[144,128]{1,0:T(8,128)(2,1)}, bf16[144,128]{1,0:T(8,128)(2,1)S(1)}, u32[]{:S(2)}) copy-start(bf16[144,128]{1,0:T(8,128)(2,1)S(1)} %shard_map.172.own_ref) | copy-start | bytes 110596
  2.6 11.0 %collective-permute-start = (bf16[144,128]{1,0:T(8,128)(2,1)S(1)}, bf16[144,128]{1,0:T(8,128)(2,1)S(1)}, u32[]{:S(2)}, u32[]{:S(2)}) collective-permute-start(bf16[144,128]{1,0:T(8,128)(2,1)S(1)} %shard_map.172.own_ref), channel_id=1, source_target_pairs={{0,1},{1,2},{2,3},{3,4},{4,5},{5,6},{6,7},{7,8},{8,9},{9,10},{10,1... | collective-permute-start | bytes 110600 | tf_op jit(solution)/shard_map/ppermute | solution.py:513
  7.2 6.5 %collective-permute-start.1 = (bf16[144,128]{1,0:T(8,128)(2,1)S(1)}, bf16[144,128]{1,0:T(8,128)(2,1)S(1)}, u32[]{:S(2)}, u32[]{:S(2)}) collective-permute-start(bf16[144,128]{1,0:T(8,128)(2,1)S(1)} %shard_map.172.own_ref), channel_id=1, source_target_pairs={{1,0},{2,1},{3,2},{4,3},{5,4},{6,5},{7,6},{8,7},{9,8},{10,9},{11,1... | collective-permute-start | bytes 110600 | tf_op jit(solution)/shard_map/ppermute | solution.py:514
  9.1 1.3 copy-start.1
  10.4 1.1 copy-start.8
  11.4 3.6 %copy-start.33 = (bf16[4,128,128]{2,1,0:T(8,128)(2,1)S(1)}, bf16[4,128,128]{2,1,0:T(8,128)(2,1)}, u32[]{:S(2)}) copy-start(bf16[4,128,128]{2,1,0:T(8,128)(2,1)} %w_in.4) | copy-start | bytes 393220
  12.7 0.9 copy-start.2
  13.7 3.3 %copy-start.21 = (bf16[144,128]{1,0:T(8,128)(2,1)}, bf16[144,128]{1,0:T(8,128)(2,1)S(1)}, u32[]{:S(2)}) copy-start(bf16[144,128]{1,0:T(8,128)(2,1)S(1)} %collective-permute-done.prev_ref) | copy-start | bytes 110596
  13.7 4.0 %copy-start.23 = (bf16[144,128]{1,0:T(8,128)(2,1)}, bf16[144,128]{1,0:T(8,128)(2,1)S(1)}, u32[]{:S(2)}) copy-start(bf16[144,128]{1,0:T(8,128)(2,1)S(1)} %collective-permute-done.1.next_ref) | copy-start | bytes 110596
  13.7 14.3 %collective-permute-start.2 = (bf16[192,768]{1,0:T(8,128)(2,1)S(1)}, bf16[192,768]{1,0:T(8,128)(2,1)S(1)}, u32[]{:S(2)}, u32[]{:S(2)}) collective-permute-start(bf16[192,768]{1,0:T(8,128)(2,1)S(1)} %get-tuple-element.73), channel_id=1, source_target_pairs={{0,2},{1,3},{2,0},{3,1},{4,6},{5,7},{6,4},{7,5},{8,10},{9,11},{10,... | collective-permute-start | bytes 884744 | tf_op jit(solution)/shard_map/ppermute | solution.py:531
  17.6 10.4 %all-to-all-start = ((bf16[8,144,128]{2,1,0:T(8,128)(2,1)}), bf16[8,144,128]{2,1,0:T(8,128)(2,1)S(1)}, u32[]{:S(2)}, u32[]{:S(2)}) async-start(bf16[8,144,128]{2,1,0:T(8,128)(2,1)} %get-tuple-element.69), calls=%async_computation | async-start | bytes 589824 | tf_op jit(solution)/shard_map/all_to_all | solution.py:572
  22.2 5.8 %copy-start.31 = (bf16[192,768]{1,0:T(8,128)(2,1)S(1)}, bf16[192,768]{1,0:T(8,128)(2,1)}, u32[]{:S(2)}) copy-start(bf16[192,768]{1,0:T(8,128)(2,1)} %cond.1) | copy-start | bytes 884740
  22.2 5.8 %copy-start.32 = (bf16[128,768]{1,0:T(8,128)(2,1)S(1)}, bf16[128,768]{1,0:T(8,128)(2,1)}, u32[]{:S(2)}) copy-start(bf16[128,768]{1,0:T(8,128)(2,1)} %weight.1) | copy-start | bytes 589828
  28.0 1.3 copy-start.35
  32.8 9.0 %copy-start.5 = (f32[96,16,128]{2,1,0:T(8,128)}, f32[96,16,128]{2,1,0:T(8,128)S(1)}, u32[]{:S(2)}) copy-start(f32[96,16,128]{2,1,0:T(8,128)S(1)} %get-tuple-element.108.high) | copy-start | bytes 2359300
  32.8 27.6 %collective-permute-start.4 = (bf16[384,768]{1,0:T(8,128)(2,1)}, bf16[384,768]{1,0:T(8,128)(2,1)}, u32[]{:S(2)}, u32[]{:S(2)}) collective-permute-start(bf16[384,768]{1,0:T(8,128)(2,1)} %get-tuple-element.94), channel_id=1, source_target_pairs={{0,2},{1,3},{2,0},{3,1},{4,6},{5,7},{6,4},{7,5},{8,10},{9,11},{10,... | collective-permute-start | bytes 1769480 | tf_op jit(solution)/shard_map/ppermute | solution.py:627
  34.1 8.6 %collective-permute-start.3 = (bf16[96,768]{1,0:T(8,128)(2,1)S(1)}, bf16[96,768]{1,0:T(8,128)(2,1)S(1)}, u32[]{:S(2)}, u32[]{:S(2)}) collective-permute-start(bf16[96,768]{1,0:T(8,128)(2,1)S(1)} %get-tuple-element.79.here_ref), channel_id=1, source_target_pairs={{4,8},{7,9},{0,16},{3,17},{2,24},{1,25},{12,2},{15,3},{8,18},{9,19... | collective-permute-start | bytes 442376 | tf_op jit(solution)/shard_map/ppermute | solution.py:604
  39.3 3.4 %copy-start.7 = (f32[96,16,128]{2,1,0:T(8,128)S(1)}, f32[96,16,128]{2,1,0:T(8,128)}, u32[]{:S(2)}) copy-start(f32[96,16,128]{2,1,0:T(8,128)} %get-tuple-element.80.low) | copy-start | bytes 2359300
  39.3 3.4 %copy-start.27 = (s32[768]{0:T(1024)S(1)}, s32[768]{0:T(1024)}, u32[]{:S(2)}) copy-start(s32[768]{0:T(1024)} %mask_ref.3) | copy-start | bytes 9220
  41.8 5.0 %copy-start.17 = (f32[24,768]{1,0:T(8,128)}, f32[24,768]{1,0:T(8,128)S(1)}, u32[]{:S(2)}) copy-start(f32[24,768]{1,0:T(8,128)S(1)} %get-tuple-element.91.gate) | copy-start | bytes 221188
  42.7 15.6 %copy-start = (bf16[2,768,768]{2,1,0:T(8,128)(2,1)S(1)}, bf16[2,768,768]{2,1,0:T(8,128)(2,1)}, u32[]{:S(2)}) copy-start(bf16[2,768,768]{2,1,0:T(8,128)(2,1)} %w_out.6) | copy-start | bytes 7077892
  46.9 11.4 %all-to-all-start.1 = ((bf16[8,24,896]{2,1,0:T(8,128)(2,1)}), bf16[8,24,896]{2,1,0:T(8,128)(2,1)S(1)}, u32[]{:S(2)}, u32[]{:S(2)}) async-start(bf16[8,24,896]{2,1,0:T(8,128)(2,1)} %bitcast.4), calls=%async_computation.1 | async-start | bytes 688128 | tf_op jit(solution)/shard_map/all_to_all | solution.py:647
  52.3 13.8 %collective-permute-start.6 = (bf16[576,768]{1,0:T(8,128)(2,1)}, bf16[576,768]{1,0:T(8,128)(2,1)}, u32[]{:S(2)}, u32[]{:S(2)}) collective-permute-start(bf16[576,768]{1,0:T(8,128)(2,1)} %copy-done.2), channel_id=1, source_target_pairs={{0,1},{1,0},{2,3},{3,2},{4,5},{5,4},{6,7},{7,6},{8,9},{9,8},{10,11... | collective-permute-start | bytes 2654216 | tf_op jit(solution)/shard_map/ppermute | solution.py:629
  58.3 0.9 copy-start.18
  59.2 6.8 %copy-start.3 = (bf16[576,768]{1,0:T(8,128)(2,1)S(1)}, bf16[576,768]{1,0:T(8,128)(2,1)}, u32[]{:S(2)}) copy-start(bf16[576,768]{1,0:T(8,128)(2,1)} %copy-done.2) | copy-start | bytes 2654212
  60.4 5.6 %collective-permute-start.8 = (bf16[384,768]{1,0:T(8,128)(2,1)}, bf16[384,768]{1,0:T(8,128)(2,1)S(1)}, u32[]{:S(2)}, u32[]{:S(2)}) collective-permute-start(bf16[384,768]{1,0:T(8,128)(2,1)} %collective-permute-done.4.refs_4_), channel_id=1, source_target_pairs={{0,1},{1,0},{2,3},{3,2},{4,5},{5,4},{6,7},{7,6},{8,9},{9,8},{10,11... | collective-permute-start | bytes 1769480 | tf_op jit(solution)/shard_map/ppermute | solution.py:655
  62.3 23.9 %collective-permute-start.10 = (bf16[576,768]{1,0:T(8,128)(2,1)}, bf16[576,768]{1,0:T(8,128)(2,1)S(1)}, u32[]{:S(2)}, u32[]{:S(2)}) collective-permute-start(bf16[576,768]{1,0:T(8,128)(2,1)} %get-tuple-element.114.refs_1_), channel_id=1, source_target_pairs={{0,2},{1,3},{2,0},{3,1},{4,6},{5,7},{6,4},{7,5},{8,10},{9,11},{10,... | collective-permute-start | bytes 2654216 | tf_op jit(solution)/shard_map/ppermute | solution.py:650
  62.6 1.8 %collective-permute-start.7 = (bf16[192,768]{1,0:T(8,128)(2,1)S(1)}, bf16[192,768]{1,0:T(8,128)(2,1)S(1)}, u32[]{:S(2)}, u32[]{:S(2)}) collective-permute-start(bf16[192,768]{1,0:T(8,128)(2,1)S(1)} %collective-permute-done.2.refs_3_), channel_id=1, source_target_pairs={{0,1},{1,0},{2,3},{3,2},{4,5},{5,4},{6,7},{7,6},{8,9},{9,8},{10,11... | collective-permute-start | bytes 884744 | tf_op jit(solution)/shard_map/ppermute | solution.py:628
  62.9 3.1 %collective-permute-start.5 = (bf16[24,768]{1,0:T(8,128)(2,1)S(1)}, bf16[24,768]{1,0:T(8,128)(2,1)S(1)}, u32[]{:S(2)}, u32[]{:S(2)}) collective-permute-start(bf16[24,768]{1,0:T(8,128)(2,1)S(1)} %get-tuple-element.95.xn2), channel_id=1, source_target_pairs={{0,4},{1,5},{2,6},{3,7},{4,0},{5,1},{6,2},{7,3},{8,12},{9,13},{10,... | collective-permute-start | bytes 110600 | tf_op jit(solution)/shard_map/ppermute | solution.py:652
  69.0 3.2 %collective-permute-start.9 = (bf16[24,768]{1,0:T(8,128)(2,1)S(1)}, bf16[24,768]{1,0:T(8,128)(2,1)S(1)}, u32[]{:S(2)}, u32[]{:S(2)}) collective-permute-start(bf16[24,768]{1,0:T(8,128)(2,1)S(1)} %get-tuple-element.100), channel_id=1, source_target_pairs={{4,0},{5,1},{6,2},{7,3},{0,4},{1,5},{2,6},{3,7},{12,8},{13,9},{14,... | collective-permute-start | bytes 110600 | tf_op jit(solution)/shard_map/ppermute | solution.py:659
  73.7 12.5 %all-to-all-start.2 = ((bf16[8,24,768]{2,1,0:T(8,128)(2,1)}), bf16[8,24,768]{2,1,0:T(8,128)(2,1)S(1)}, u32[]{:S(2)}, u32[]{:S(2)}) async-start(bf16[8,24,768]{2,1,0:T(8,128)(2,1)} %copy-done.9), calls=%async_computation.2 | async-start | bytes 589824 | tf_op jit(solution)/shard_map/all_to_all | solution.py:662
  78.9 34.4 %collective-permute-start.13 = (bf16[576,768]{1,0:T(8,128)(2,1)}, bf16[576,768]{1,0:T(8,128)(2,1)}, u32[]{:S(2)}, u32[]{:S(2)}) collective-permute-start(bf16[576,768]{1,0:T(8,128)(2,1)} %get-tuple-element.114.refs_1_), channel_id=1, source_target_pairs={{0,1},{1,0},{2,3},{3,2},{4,5},{5,4},{6,7},{7,6},{8,9},{9,8},{10,11... | collective-permute-start | bytes 2654216 | tf_op jit(solution)/shard_map/ppermute | solution.py:629
  86.2 29.5 %collective-permute-start.14 = (bf16[576,768]{1,0:T(8,128)(2,1)S(1)}, bf16[576,768]{1,0:T(8,128)(2,1)S(1)}, u32[]{:S(2)}, u32[]{:S(2)}) collective-permute-start(bf16[576,768]{1,0:T(8,128)(2,1)S(1)} %collective-permute-done.10.refs_3_), channel_id=1, source_target_pairs={{0,1},{1,0},{2,3},{3,2},{4,5},{5,4},{6,7},{7,6},{8,9},{9,8},{10,11... | collective-permute-start | bytes 2654216 | tf_op jit(solution)/shard_map/ppermute | solution.py:631
  87.8 10.2 %collective-permute-start.11 = (bf16[96,768]{1,0:T(8,128)(2,1)S(1)}, bf16[96,768]{1,0:T(8,128)(2,1)S(1)}, u32[]{:S(2)}, u32[]{:S(2)}) collective-permute-start(bf16[96,768]{1,0:T(8,128)(2,1)S(1)} %constant_dynamic-slice_fusion.here_ref), channel_id=1, source_target_pairs={{4,8},{7,9},{0,16},{3,17},{2,24},{1,25},{12,2},{15,3},{8,18},{9,19... | collective-permute-start | bytes 442376 | tf_op jit(solution)/shard_map/ppermute | solution.py:604
  95.5 2.6 %copy-start.4 = (f32[96,16,128]{2,1,0:T(8,128)S(1)}, f32[96,16,128]{2,1,0:T(8,128)}, u32[]{:S(2)}) copy-start(f32[96,16,128]{2,1,0:T(8,128)} %get-tuple-element.107.low) | copy-start | bytes 2359300
  95.5 2.8 %copy-start.6 = (f32[96,16,128]{2,1,0:T(8,128)S(1)}, f32[96,16,128]{2,1,0:T(8,128)}, u32[]{:S(2)}) copy-start(f32[96,16,128]{2,1,0:T(8,128)} %copy-done.5) | copy-start | bytes 2359300
  98.3 13.3 %copy-start.12 = (f32[24,768]{1,0:T(8,128)S(1)}, f32[24,768]{1,0:T(8,128)}, u32[]{:S(2)}) copy-start(f32[24,768]{1,0:T(8,128)} %copy-done.10) | copy-start | bytes 221188
  112.9 2.9 %collective-permute-start.12 = (bf16[24,768]{1,0:T(8,128)(2,1)S(1)}, bf16[24,768]{1,0:T(8,128)(2,1)S(1)}, u32[]{:S(2)}, u32[]{:S(2)}) collective-permute-start(bf16[24,768]{1,0:T(8,128)(2,1)S(1)} %get-tuple-element.113.xn2), channel_id=1, source_target_pairs={{0,4},{1,5},{2,6},{3,7},{4,0},{5,1},{6,2},{7,3},{8,12},{9,13},{10,... | collective-permute-start | bytes 110600 | tf_op jit(solution)/shard_map/ppermute | solution.py:652
  115.7 6.2 %copy-start.13 = (bf16[768,128]{1,0:T(8,128)(2,1)S(1)}, bf16[768,128]{1,0:T(8,128)(2,1)}, u32[]{:S(2)}) copy-start(bf16[768,128]{1,0:T(8,128)(2,1)} %refs_1_.1) | copy-start | bytes 589828
  115.7 26.8 %copy-start.15 = (bf16[144,128]{1,0:T(8,128)(2,1)S(1)}, bf16[144,128]{1,0:T(8,128)(2,1)}, u32[]{:S(2)}) copy-start(bf16[144,128]{1,0:T(8,128)(2,1)} %copy-done.14) | copy-start | bytes 110596
  115.7 26.8 %copy-start.16 = (bf16[4,128,128]{2,1,0:T(8,128)(2,1)S(1)}, bf16[4,128,128]{2,1,0:T(8,128)(2,1)}, u32[]{:S(2)}) copy-start(bf16[4,128,128]{2,1,0:T(8,128)(2,1)} %w_in.7) | copy-start | bytes 393220
  115.7 26.8 %copy-start.20 = (bf16[256,128]{1,0:T(8,128)(2,1)S(1)}, bf16[256,128]{1,0:T(8,128)(2,1)}, u32[]{:S(2)}) copy-start(bf16[256,128]{1,0:T(8,128)(2,1)} %copy-done.19) | copy-start | bytes 196612
  115.8 26.8 %copy-start.22 = (bf16[144,128]{1,0:T(8,128)(2,1)S(1)}, bf16[144,128]{1,0:T(8,128)(2,1)}, u32[]{:S(2)}) copy-start(bf16[144,128]{1,0:T(8,128)(2,1)} %copy-done.21) | copy-start | bytes 110596
  115.8 26.8 %copy-start.24 = (bf16[144,128]{1,0:T(8,128)(2,1)S(1)}, bf16[144,128]{1,0:T(8,128)(2,1)}, u32[]{:S(2)}) copy-start(bf16[144,128]{1,0:T(8,128)(2,1)} %copy-done.23) | copy-start | bytes 110596
  115.8 26.8 %copy-start.25 = (bf16[128,128]{1,0:T(8,128)(2,1)S(1)}, bf16[128,128]{1,0:T(8,128)(2,1)}, u32[]{:S(2)}) copy-start(bf16[128,128]{1,0:T(8,128)(2,1)} %w_out.7) | copy-start | bytes 98308
  115.8 26.8 %copy-start.28 = (bf16[3,128]{1,0:T(4,128)(2,1)S(1)}, bf16[3,128]{1,0:T(4,128)(2,1)}, u32[]{:S(2)}) copy-start(bf16[3,128]{1,0:T(4,128)(2,1)} %pos.1) | copy-start | bytes 2308
  119.1 2.9 %collective-permute-start.15 = (bf16[24,768]{1,0:T(8,128)(2,1)S(1)}, bf16[24,768]{1,0:T(8,128)(2,1)S(1)}, u32[]{:S(2)}, u32[]{:S(2)}) collective-permute-start(bf16[24,768]{1,0:T(8,128)(2,1)S(1)} %get-tuple-element.117), channel_id=1, source_target_pairs={{4,0},{5,1},{6,2},{7,3},{0,4},{1,5},{2,6},{3,7},{12,8},{13,9},{14,... | collective-permute-start | bytes 110600 | tf_op jit(solution)/shard_map/ppermute | solution.py:659
  (7 other events, 4.9 us)

commit v5 on v4

--- a/solution.py
+++ b/solution.py
@@ -160,17 +160,26 @@
 
 
 def decoder_kernel(
-    natom, row_tokens, x1_ref, own_ref, prev_ref, next_ref, proj, w_in, w_out, pos, out
+    natom, x1_ref, own_ref, prev_ref, next_ref, proj_ref, edge_ref, w_in, w_out, pos, out
 ):
     rows = own_ref.shape[0] - EXTRA
+    proj = proj_ref[...].astype(F32)
+    edge = edge_ref[...].astype(F32)
     tokens = proj.shape[0]
-    me = device()[2]
+    _, col, me = device()
+    rest = tokens - HALO
+    below = jnp.where(col == 0, edge, proj[rest:])
+    above = jnp.where(col == lax.axis_size("col") - 1, edge, proj[:HALO])
+    tables = (
+        jnp.concatenate([proj[:rest], below], 0),
+        proj,
+        jnp.concatenate([above, proj[HALO:]], 0),
+    )
     spread = []
-    for k, ref in enumerate((prev_ref, own_ref, next_ref)):
+    for table, ref in zip(tables, (prev_ref, own_ref, next_ref)):
         spot = ref[rows:].astype(F32)[0:1].astype(jnp.int32)
-        spot = spot + (me + k - 1) // lax.axis_size("col") * row_tokens
         onehot = (iota((tokens, rows), 0) == spot).astype(F32).astype(BF16)
-        spread.append(dot_tn(onehot, proj[...]))
+        spread.append(dot_tn(onehot, table.astype(BF16)))
     spread = jnp.concatenate([spread[0][rows - HALO :], spread[1], spread[2][:HALO]], 0)
     x = (x1_ref[...].astype(F32) + spread).astype(BF16)
     xn = normed(x).astype(BF16)
@@ -518,7 +527,7 @@
     matrix = jax.ShapeDtypeStruct((3 * hid, width), BF16)
     upper, lower, *packed = call(
         pack_kernel,
-        [jax.ShapeDtypeStruct((rows_of * hid, width), BF16) for rows_of in (1, 2)]
+        [jax.ShapeDtypeStruct((3 * hid // 2, width), BF16)] * 2
         + [matrix] * BLOCKS,
         first_part,
         second_part,
@@ -657,20 +666,25 @@
             act, xn2, came_rows, ([packed[layer]], [beside[layer]], across[layer], beyond[layer])
         )
         parts = [lax.ppermute(part, everyone, back[d]) for d, part in enumerate(parts, 1)]
-        act, copies = close(act, parts, count if last else ncol, tok_atom if last else None)
-        axes = everyone if last else "col"
-        gathered = lax.all_to_all(copies, axes, 0, 0).reshape(copies.shape[0] * own, -1)
+        act, copies = close(act, parts, ncol, tok_atom if last else None)
+        gathered = lax.all_to_all(copies, "col", 0, 0).reshape(rows, -1)
         if not last:
             xn = gathered
 
+    bounds = [(r * ncol - 1, r * ncol) for r in range(1, nrow)]
+    bounds += [(b, a) for a, b in bounds]
+    edge = jnp.where(me_col == 0, gathered[:HALO], gathered[rows - HALO :])
+    edge = lax.ppermute(edge, everyone, bounds)
+
     return call(
-        functools.partial(decoder_kernel, natom, rows),
+        functools.partial(decoder_kernel, natom),
         jax.ShapeDtypeStruct((pos_out.shape[0], atoms), F32),
         ext,
         feat,
         prev,
         after,
         gathered,
+        edge,
         dec_in,
         dec_out,
         pos_out,

time: 146 us -> 138 us (0.945)
  the two profiles are of different devices: /device:TPU:1 before, /device:TPU:24 now
where the time goes in v5:
time: 138 us; the launch traced here: 136 us
  waiting for transfers between devices  36.9 us (27%)
  Pallas kernels  36.8 us (27%)
  starting transfers between devices  31.9 us (23%)
  blocking collectives  22 us (16%)
  local copies, waits for them, and re-layouts  8.35 us (6%)
    pallas_call x15, Pallas kernels, call(): pl.pallas_call(kernel, out_shape=outs, in_specs=[smem] * len(scalars) + [...  28.7 us
    all_to_all x2, blocking collectives, body(): message = lax.all_to_all(message.reshape(ncol, own, -1), 'col', 0, 0)  22 us
    all_to_all x2, waiting for transfers between devices, body(): gathered = lax.all_to_all(copies, 'col', 0, 0).reshape(rows, -1)  11.7 us
    unnamed x68, local copies, waits for them, and re-layouts  8.34 us
    pallas_call x2, Pallas kernels, bias_of(): pl.pallas_call(bias_kernel, grid=(half // step,), out_shape=[jax.ShapeDty...  8.04 us
    ppermute x2, starting transfers between devices, body(): came = lax.ppermute(send, everyone, pairs)  7.4 us
    ppermute x2, waiting for transfers between devices, body(): lax.ppermute(part, everyone, back[d])  6.79 us
    ppermute x2, waiting for transfers between devices, body(): lax.ppermute(xn2, everyone, shifts[d])  6.78 us
  transfers between devices with their start and end apart: 20, of which 9 were waited for; matrix products, arithmetic and copies ran while one was open for 0% of the time, Pallas kernels for 21%

profile of v5, /device:TPU:24, one launch (start us, length us, event | category | flops | bytes accessed | tf_op | source)
XLA Modules:
  0.0 136.4 jit_solution(15552371577035036964)
XLA Ops:
  0.0 0.8 copy-done.24
  0.8 0.7 copy-done.27
  1.4 0.7 copy-done.28
  2.6 1.9 %collective-permute-start = (bf16[144,128]{1,0:T(8,128)(2,1)S(1)}, bf16[144,128]{1,0:T(8,128)(2,1)S(1)}, u32[]{:S(2)}, u32[]{:S(2)}) collective-permute-start(bf16[144,128]{1,0:T(8,128)(2,1)S(1)} %shard_map.172.own_ref), channel_id=1, source_target_pairs={{0,1},{1,2},{2,3},{3,4},{4,5},{5,6},{6,7},{7,8},{8,9},{9,10},{10,1... | collective-permute-start | bytes 110600 | tf_op jit(solution)/shard_map/ppermute | solution.py:522
  4.6 5.4 %collective-permute-start.1 = (bf16[144,128]{1,0:T(8,128)(2,1)S(1)}, bf16[144,128]{1,0:T(8,128)(2,1)S(1)}, u32[]{:S(2)}, u32[]{:S(2)}) collective-permute-start(bf16[144,128]{1,0:T(8,128)(2,1)S(1)} %shard_map.172.own_ref), channel_id=1, source_target_pairs={{1,0},{2,1},{3,2},{4,3},{5,4},{6,5},{7,6},{8,7},{9,8},{10,9},{11,1... | collective-permute-start | bytes 110600 | tf_op jit(solution)/shard_map/ppermute | solution.py:523
  10.0 1.3 copy-done.1
  11.3 1.1 copy-done.6
  12.4 1.3 shard_map.173
  13.8 2.0 %shard_map.174 = (bf16[256,128]{1,0:T(8,128)(2,1)S(1)}, bf16[8,144,128]{2,1,0:T(8,128)(2,1)}) custom-call(bf16[144,128]{1,0:T(8,128)(2,1)S(1)} %shard_map.172.own_ref, bf16[144,128]{1,0:T(8,128)(2,1)S(1)} %collective-permute-done.prev_ref, bf16[144,128]{1,0:T(8,128)(2,1)S(1)} %collective-permute-done.1.next_ref, bf16[4,128,128]{2,1,0:T(8,128)(2,1)S(1)} %copy-done.31, ...), custom_call_target="tpu_custom_call" | custom-call | flops 100000000 | bytes 1000000 | tf_op jit(solution)/shard_map/pallas_call | solution.py:26
  15.8 0.6 copy-done.17
  16.4 3.4 %all-to-all-start = ((bf16[8,144,128]{2,1,0:T(8,128)(2,1)}), bf16[8,144,128]{2,1,0:T(8,128)(2,1)S(1)}, u32[]{:S(2)}, u32[]{:S(2)}) async-start(bf16[8,144,128]{2,1,0:T(8,128)(2,1)} %get-tuple-element.69), calls=%async_computation | async-start | bytes 589824 | tf_op jit(solution)/shard_map/all_to_all | solution.py:581
  19.9 4.6 %shard_map.175 = (f32[96,16,128]{2,1,0:T(8,128)}, f32[96,16,128]{2,1,0:T(8,128)}) custom-call(bf16[192,96,128]{2,1,0:T(8,128)(2,1)} %pair_ref.3, bf16[32,128]{1,0:T(8,128)(2,1)} %bitcast.17), custom_call_target="tpu_custom_call" | custom-call | flops 2000000000 | bytes 4000000 | tf_op jit(solution)/shard_map/pallas_call | solution.py:561
  24.5 3.5 %all-to-all-done.both_ref = bf16[8,144,128]{2,1,0:T(8,128)(2,1)S(1)} async-done(((bf16[8,144,128]{2,1,0:T(8,128)(2,1)}), bf16[8,144,128]{2,1,0:T(8,128)(2,1)S(1)}, u32[]{:S(2)}, u32[]{:S(2)}) %all-to-all-start) | async-done | bytes 294944 | tf_op jit(solution)/shard_map/all_to_all | solution.py:581
  28.0 1.3 shard_map.176
  29.3 4.3 %collective-permute-start.3 = (bf16[96,768]{1,0:T(8,128)(2,1)S(1)}, bf16[96,768]{1,0:T(8,128)(2,1)S(1)}, u32[]{:S(2)}, u32[]{:S(2)}) collective-permute-start(bf16[96,768]{1,0:T(8,128)(2,1)S(1)} %get-tuple-element.79.here_ref), channel_id=1, source_target_pairs={{4,8},{7,9},{0,16},{3,17},{2,24},{1,25},{12,2},{15,3},{8,18},{9,19... | collective-permute-start | bytes 442376 | tf_op jit(solution)/shard_map/ppermute | solution.py:613
  33.6 3.4 %shard_map.178 = (f32[96,16,128]{2,1,0:T(8,128)S(1)}, f32[96,16,128]{2,1,0:T(8,128)S(1)}) custom-call(bf16[192,96,128]{2,1,0:T(8,128)(2,1)} %pair_ref.3, bf16[32,128]{1,0:T(8,128)(2,1)S(1)} %bitcast.18), custom_call_target="tpu_custom_call" | custom-call | flops 2000000000 | bytes 4000000 | tf_op jit(solution)/shard_map/pallas_call | solution.py:561
  37.1 0.9 copy-done.3
  38.0 0.7 collective-permute-start.4
  38.6 2.4 %shard_map.177 = (bf16[192,768]{1,0:T(8,128)(2,1)S(1)}, bf16[768,768]{1,0:T(8,128)(2,1)S(1)}, bf16[768,768]{1,0:T(8,128)(2,1)S(1)}, f32[24,768]{1,0:T(8,128)S(1)}) custom-call(bf16[192,768]{1,0:T(8,128)(2,1)S(1)} %get-tuple-element.76.xn_ref, f32[24,768]{1,0:T(8,128)S(1)} %get-tuple-element.77.act_ref, bf16[2,4,768,768]{3,2,1,0:T(8,128)(2,1)} %w_in.6), custom_call_target="tpu_custom_call" | custom-call | flops 226492416 | bytes 4718592 | tf_op jit(solution)/shard_map/pallas_call | solution.py:26
  41.2 3.4 %shard_map.179 = bf16[192,896]{1,0:T(8,128)(2,1)S(1)} custom-call(s32[768]{0:T(1024)S(1)} %copy-done.25, bf16[192,768]{1,0:T(8,128)(2,1)S(1)} %get-tuple-element.78.query, bf16[96,768]{1,0:T(8,128)(2,1)S(1)} %get-tuple-element.79.here_ref, bf16[96,768]{1,0:T(8,128)(2,1)S(1)} %collective-permute-done.3.came_ref, f32[96,16,128]{2,1,0:T(8,128)S(1)} %copy-done.5, ...), custom_call_target="tpu_custom_call" | custom-call | flops 1000000000 | bytes 8000000 | tf_op jit(solution)/shard_map/pallas_call | solution.py:26
  44.6 10.3 %all_to_all.25.message = bf16[8,24,896]{2,1,0:T(8,128)(2,1)S(1)} all-to-all(bf16[8,24,896]{2,1,0:T(8,128)(2,1)S(1)} %bitcast.11), channel_id=1, replica_groups=mesh['row'=4,'col'=8] {'col'}, dimensions={0} | all-to-all | bytes 688128 | tf_op jit(solution)/shard_map/all_to_all | solution.py:656
  55.5 1.2 shard_map.180
  57.9 3.4 %collective-permute-done.5.refs_0_ = bf16[24,768]{1,0:T(8,128)(2,1)S(1)} collective-permute-done((bf16[24,768]{1,0:T(8,128)(2,1)S(1)}, bf16[24,768]{1,0:T(8,128)(2,1)S(1)}, u32[]{:S(2)}, u32[]{:S(2)}) %collective-permute-start.5) | collective-permute-done | bytes 36896 | tf_op jit(solution)/shard_map/ppermute | solution.py:661
  61.3 3.3 %shard_map.181 = (f32[24,768]{1,0:T(8,128)S(1)}, bf16[24,768]{1,0:T(8,128)(2,1)S(1)}) custom-call(f32[24,768]{1,0:T(8,128)S(1)} %get-tuple-element.92.act_ref, bf16[24,768]{1,0:T(8,128)(2,1)S(1)} %get-tuple-element.95.xn2, bf16[24,768]{1,0:T(8,128)(2,1)S(1)} %collective-permute-done.5.refs_0_, bf16[576,768]{1,0:T(8,128)(2,1)} %get-tuple-element.96.refs_1_, ...), custom_call_target="tpu_custom_call" | custom-call | flops 169869312 | bytes 3538944 | tf_op jit(solution)/shard_map/pallas_call | solution.py:26
  64.6 0.6 collective-permute-start.9
  65.2 3.4 %collective-permute-done.9.refs_0_ = bf16[24,768]{1,0:T(8,128)(2,1)S(1)} collective-permute-done((bf16[24,768]{1,0:T(8,128)(2,1)S(1)}, bf16[24,768]{1,0:T(8,128)(2,1)S(1)}, u32[]{:S(2)}, u32[]{:S(2)}) %collective-permute-start.9) | collective-permute-done | bytes 36896 | tf_op jit(solution)/shard_map/ppermute | solution.py:668
  68.8 0.7 copy-done.9
  69.6 0.6 copy-done.10
  70.2 3.4 %all-to-all-start.2 = ((bf16[8,24,768]{2,1,0:T(8,128)(2,1)}), bf16[8,24,768]{2,1,0:T(8,128)(2,1)S(1)}, u32[]{:S(2)}, u32[]{:S(2)}) async-start(bf16[8,24,768]{2,1,0:T(8,128)(2,1)} %copy-done.9), calls=%async_computation.2 | async-start | bytes 589824 | tf_op jit(solution)/shard_map/all_to_all | solution.py:670
  74.0 6.8 %all-to-all-done.2 = bf16[8,24,768]{2,1,0:T(8,128)(2,1)S(1)} async-done(((bf16[8,24,768]{2,1,0:T(8,128)(2,1)}), bf16[8,24,768]{2,1,0:T(8,128)(2,1)S(1)}, u32[]{:S(2)}, u32[]{:S(2)}) %all-to-all-start.2) | async-done | bytes 294944 | tf_op jit(solution)/shard_map/all_to_all | solution.py:670
  80.9 3.1 %collective-permute-start.11 = (bf16[96,768]{1,0:T(8,128)(2,1)S(1)}, bf16[96,768]{1,0:T(8,128)(2,1)S(1)}, u32[]{:S(2)}, u32[]{:S(2)}) collective-permute-start(bf16[96,768]{1,0:T(8,128)(2,1)S(1)} %constant_dynamic-slice_fusion.here_ref), channel_id=1, source_target_pairs={{4,8},{7,9},{0,16},{3,17},{2,24},{1,25},{12,2},{15,3},{8,18},{9,19... | collective-permute-start | bytes 442376 | tf_op jit(solution)/shard_map/ppermute | solution.py:613
  84.1 0.9 copy-done.11
  85.0 2.5 %shard_map.183 = (bf16[192,768]{1,0:T(8,128)(2,1)S(1)}, bf16[768,768]{1,0:T(8,128)(2,1)S(1)}, bf16[768,768]{1,0:T(8,128)(2,1)S(1)}, f32[24,768]{1,0:T(8,128)S(1)}) custom-call(bf16[192,768]{1,0:T(8,128)(2,1)S(1)} %bitcast.10, f32[24,768]{1,0:T(8,128)S(1)} %copy-done.11, bf16[2,4,768,768]{3,2,1,0:T(8,128)(2,1)} %w_in.6), custom_call_target="tpu_custom_call" | custom-call | flops 226492416 | bytes 4718592 | tf_op jit(solution)/shard_map/pallas_call | solution.py:26
  87.5 3.5 %collective-permute-done.11.came_ref = bf16[96,768]{1,0:T(8,128)(2,1)S(1)} collective-permute-done((bf16[96,768]{1,0:T(8,128)(2,1)S(1)}, bf16[96,768]{1,0:T(8,128)(2,1)S(1)}, u32[]{:S(2)}, u32[]{:S(2)}) %collective-permute-start.11) | collective-permute-done | bytes 147488 | tf_op jit(solution)/shard_map/ppermute | solution.py:613
  90.9 3.4 %shard_map.184 = bf16[192,896]{1,0:T(8,128)(2,1)S(1)} custom-call(s32[768]{0:T(1024)S(1)} %copy-done.25, bf16[192,768]{1,0:T(8,128)(2,1)S(1)} %get-tuple-element.105.query, bf16[96,768]{1,0:T(8,128)(2,1)S(1)} %constant_dynamic-slice_fusion.here_ref, bf16[96,768]{1,0:T(8,128)(2,1)S(1)} %collective-permute-done.11.came_ref, f32[96,16,128]{2,1,0:T(8,128)S(1)} %copy-done.2, ...), custom_call_target="tpu_custom_call" | custom-call | flops 1000000000 | bytes 8000000 | tf_op jit(solution)/shard_map/pallas_call | solution.py:26
  94.3 11.6 %all_to_all.26.message = bf16[8,24,896]{2,1,0:T(8,128)(2,1)S(1)} all-to-all(bf16[8,24,896]{2,1,0:T(8,128)(2,1)S(1)} %bitcast.12), channel_id=1, replica_groups=mesh['row'=4,'col'=8] {'col'}, dimensions={0} | all-to-all | bytes 688128 | tf_op jit(solution)/shard_map/all_to_all | solution.py:656
  106.0 1.2 shard_map.185
  107.2 0.6 collective-permute-start.12
  107.8 3.4 %collective-permute-done.12.refs_0_ = bf16[24,768]{1,0:T(8,128)(2,1)S(1)} collective-permute-done((bf16[24,768]{1,0:T(8,128)(2,1)S(1)}, bf16[24,768]{1,0:T(8,128)(2,1)S(1)}, u32[]{:S(2)}, u32[]{:S(2)}) %collective-permute-start.12) | collective-permute-done | bytes 36896 | tf_op jit(solution)/shard_map/ppermute | solution.py:661
  111.3 3.0 %shard_map.186 = (f32[24,768]{1,0:T(8,128)S(1)}, bf16[24,768]{1,0:T(8,128)(2,1)S(1)}) custom-call(f32[24,768]{1,0:T(8,128)S(1)} %get-tuple-element.112.act_ref, bf16[24,768]{1,0:T(8,128)(2,1)S(1)} %get-tuple-element.113.xn2, bf16[24,768]{1,0:T(8,128)(2,1)S(1)} %collective-permute-done.12.refs_0_, bf16[576,768]{1,0:T(8,128)(2,1)S(1)} %get-tuple-element.114.refs_1_, ...), custom_call_target="tpu_custom_call" | custom-call | flops 169869312 | bytes 3538944 | tf_op jit(solution)/shard_map/pallas_call | solution.py:26
  114.3 0.6 collective-permute-start.15
  114.9 3.4 %collective-permute-done.15.refs_0_ = bf16[24,768]{1,0:T(8,128)(2,1)S(1)} collective-permute-done((bf16[24,768]{1,0:T(8,128)(2,1)S(1)}, bf16[24,768]{1,0:T(8,128)(2,1)S(1)}, u32[]{:S(2)}, u32[]{:S(2)}) %collective-permute-start.15) | collective-permute-done | bytes 36896 | tf_op jit(solution)/shard_map/ppermute | solution.py:668
  118.3 0.9 shard_map.187
  119.2 3.3 %all-to-all-start.4 = ((bf16[8,24,128]{2,1,0:T(8,128)(2,1)}), bf16[8,24,128]{2,1,0:T(8,128)(2,1)S(1)}, u32[]{:S(2)}, u32[]{:S(2)}) async-start(bf16[8,24,128]{2,1,0:T(8,128)(2,1)} %get-tuple-element.118), calls=%async_computation.4 | async-start | bytes 98304 | tf_op jit(solution)/shard_map/all_to_all | solution.py:670
  122.6 4.9 %all-to-all-done.4 = bf16[8,24,128]{2,1,0:T(8,128)(2,1)S(1)} async-done(((bf16[8,24,128]{2,1,0:T(8,128)(2,1)}), bf16[8,24,128]{2,1,0:T(8,128)(2,1)S(1)}, u32[]{:S(2)}, u32[]{:S(2)}) %all-to-all-start.4) | async-done | bytes 49184 | tf_op jit(solution)/shard_map/all_to_all | solution.py:670
  127.5 2.2 %collective-permute-start.16 = (bf16[64,128]{1,0:T(8,128)(2,1)S(1)}, bf16[64,128]{1,0:T(8,128)(2,1)S(1)}, u32[]{:S(2)}, u32[]{:S(2)}) collective-permute-start(bf16[64,128]{1,0:T(8,128)(2,1)S(1)} %slice_select_fusion), channel_id=1, source_target_pairs={{7,8},{15,16},{23,24},{8,7},{16,15},{24,23}} | collective-permute-start | bytes 49160 | tf_op jit(solution)/shard_map/ppermute | solution.py:677
  129.7 4.7 %collective-permute-done.16.edge_ref = bf16[64,128]{1,0:T(8,128)(2,1)S(1)} collective-permute-done((bf16[64,128]{1,0:T(8,128)(2,1)S(1)}, bf16[64,128]{1,0:T(8,128)(2,1)S(1)}, u32[]{:S(2)}, u32[]{:S(2)}) %collective-permute-start.16) | collective-permute-done | bytes 16416 | tf_op jit(solution)/shard_map/ppermute | solution.py:677
  134.4 2.0 %shard_map.188 = f32[3,128]{1,0:T(4,128)} custom-call(bf16[256,128]{1,0:T(8,128)(2,1)S(1)} %copy-done.18, bf16[144,128]{1,0:T(8,128)(2,1)S(1)} %copy-done.15, bf16[144,128]{1,0:T(8,128)(2,1)S(1)} %copy-done.20, bf16[144,128]{1,0:T(8,128)(2,1)S(1)} %copy-done.22, bf16[192,128]{1,0:T(8,128)(2,1)S(1)} %bitcast.15, ...), custom_call_target="tpu_custom_call" | custom-call | flops 100000000 | bytes 1000000 | tf_op jit(solution)/shard_map/pallas_call | solution.py:26
  (81 shorter events, 3.2 us)
Async XLA Ops:
  2.1 11.7 %copy-start.32 = (bf16[128,128]{1,0:T(8,128)(2,1)S(1)}, bf16[128,128]{1,0:T(8,128)(2,1)}, u32[]{:S(2)}) copy-start(bf16[128,128]{1,0:T(8,128)(2,1)} %w_out.4) | copy-start | bytes 98308
  2.6 11.1 %copy-start.14 = (bf16[144,128]{1,0:T(8,128)(2,1)}, bf16[144,128]{1,0:T(8,128)(2,1)S(1)}, u32[]{:S(2)}) copy-start(bf16[144,128]{1,0:T(8,128)(2,1)S(1)} %shard_map.172.own_ref) | copy-start | bytes 110596
  2.6 11.0 %collective-permute-start = (bf16[144,128]{1,0:T(8,128)(2,1)S(1)}, bf16[144,128]{1,0:T(8,128)(2,1)S(1)}, u32[]{:S(2)}, u32[]{:S(2)}) collective-permute-start(bf16[144,128]{1,0:T(8,128)(2,1)S(1)} %shard_map.172.own_ref), channel_id=1, source_target_pairs={{0,1},{1,2},{2,3},{3,4},{4,5},{5,6},{6,7},{7,8},{8,9},{9,10},{10,1... | collective-permute-start | bytes 110600 | tf_op jit(solution)/shard_map/ppermute | solution.py:522
  4.6 9.1 %collective-permute-start.1 = (bf16[144,128]{1,0:T(8,128)(2,1)S(1)}, bf16[144,128]{1,0:T(8,128)(2,1)S(1)}, u32[]{:S(2)}, u32[]{:S(2)}) collective-permute-start(bf16[144,128]{1,0:T(8,128)(2,1)S(1)} %shard_map.172.own_ref), channel_id=1, source_target_pairs={{1,0},{2,1},{3,2},{4,3},{5,4},{6,5},{7,6},{8,7},{9,8},{10,9},{11,1... | collective-permute-start | bytes 110600 | tf_op jit(solution)/shard_map/ppermute | solution.py:523
  10.0 1.3 copy-start.1
  11.3 1.1 copy-start.6
  12.4 1.4 %copy-start.31 = (bf16[4,128,128]{2,1,0:T(8,128)(2,1)S(1)}, bf16[4,128,128]{2,1,0:T(8,128)(2,1)}, u32[]{:S(2)}) copy-start(bf16[4,128,128]{2,1,0:T(8,128)(2,1)} %w_in.4) | copy-start | bytes 393220
  13.6 2.1 %copy-start.19 = (bf16[144,128]{1,0:T(8,128)(2,1)}, bf16[144,128]{1,0:T(8,128)(2,1)S(1)}, u32[]{:S(2)}) copy-start(bf16[144,128]{1,0:T(8,128)(2,1)S(1)} %collective-permute-done.prev_ref) | copy-start | bytes 110596
  13.6 2.8 %copy-start.21 = (bf16[144,128]{1,0:T(8,128)(2,1)}, bf16[144,128]{1,0:T(8,128)(2,1)S(1)}, u32[]{:S(2)}) copy-start(bf16[144,128]{1,0:T(8,128)(2,1)S(1)} %collective-permute-done.1.next_ref) | copy-start | bytes 110596
  13.7 14.3 %collective-permute-start.2 = (bf16[288,768]{1,0:T(8,128)(2,1)S(1)}, bf16[288,768]{1,0:T(8,128)(2,1)S(1)}, u32[]{:S(2)}, u32[]{:S(2)}) collective-permute-start(bf16[288,768]{1,0:T(8,128)(2,1)S(1)} %get-tuple-element.73), channel_id=1, source_target_pairs={{0,2},{1,3},{2,0},{3,1},{4,6},{5,7},{6,4},{7,5},{8,10},{9,11},{10,... | collective-permute-start | bytes 1327112 | tf_op jit(solution)/shard_map/ppermute | solution.py:540
  16.4 11.6 %all-to-all-start = ((bf16[8,144,128]{2,1,0:T(8,128)(2,1)}), bf16[8,144,128]{2,1,0:T(8,128)(2,1)S(1)}, u32[]{:S(2)}, u32[]{:S(2)}) async-start(bf16[8,144,128]{2,1,0:T(8,128)(2,1)} %get-tuple-element.69), calls=%async_computation | async-start | bytes 589824 | tf_op jit(solution)/shard_map/all_to_all | solution.py:581
  19.8 8.2 %copy-start.29 = (bf16[192,768]{1,0:T(8,128)(2,1)S(1)}, bf16[192,768]{1,0:T(8,128)(2,1)}, u32[]{:S(2)}) copy-start(bf16[192,768]{1,0:T(8,128)(2,1)} %cond.1) | copy-start | bytes 884740
  19.8 8.2 %copy-start.30 = (bf16[128,768]{1,0:T(8,128)(2,1)S(1)}, bf16[128,768]{1,0:T(8,128)(2,1)}, u32[]{:S(2)}) copy-start(bf16[128,768]{1,0:T(8,128)(2,1)} %weight.1) | copy-start | bytes 589828
  28.0 1.3 copy-start.7
  28.0 5.6 %copy-start.33 = (bf16[2,128,16]{1,2,0:T(8,128)(2,1)S(1)}, bf16[2,128,16]{1,2,0:T(8,128)(2,1)}, u32[]{:S(2)}) copy-start(bf16[2,128,16]{1,2,0:T(8,128)(2,1)} %param.29) | copy-start | bytes 24580
  29.3 11.8 %collective-permute-start.3 = (bf16[96,768]{1,0:T(8,128)(2,1)S(1)}, bf16[96,768]{1,0:T(8,128)(2,1)S(1)}, u32[]{:S(2)}, u32[]{:S(2)}) collective-permute-start(bf16[96,768]{1,0:T(8,128)(2,1)S(1)} %get-tuple-element.79.here_ref), channel_id=1, source_target_pairs={{4,8},{7,9},{0,16},{3,17},{2,24},{1,25},{12,2},{15,3},{8,18},{9,19... | collective-permute-start | bytes 442376 | tf_op jit(solution)/shard_map/ppermute | solution.py:613
  37.0 0.9 copy-start.3
  38.0 18.8 %collective-permute-start.4 = (bf16[288,768]{1,0:T(8,128)(2,1)}, bf16[288,768]{1,0:T(8,128)(2,1)S(1)}, u32[]{:S(2)}, u32[]{:S(2)}) collective-permute-start(bf16[288,768]{1,0:T(8,128)(2,1)} %get-tuple-element.94), channel_id=1, source_target_pairs={{0,2},{1,3},{2,0},{3,1},{4,6},{5,7},{6,4},{7,5},{8,10},{9,11},{10,... | collective-permute-start | bytes 1327112 | tf_op jit(solution)/shard_map/ppermute | solution.py:636
  38.6 22.6 %collective-permute-start.6 = (bf16[576,768]{1,0:T(8,128)(2,1)}, bf16[576,768]{1,0:T(8,128)(2,1)S(1)}, u32[]{:S(2)}, u32[]{:S(2)}) collective-permute-start(bf16[576,768]{1,0:T(8,128)(2,1)} %get-tuple-element.96.refs_1_), channel_id=1, source_target_pairs={{0,1},{1,0},{2,3},{3,2},{4,5},{5,4},{6,7},{7,6},{8,9},{9,8},{10,11... | collective-permute-start | bytes 2654216 | tf_op jit(solution)/shard_map/ppermute | solution.py:638
  38.6 2.6 %copy-start.5 = (f32[96,16,128]{2,1,0:T(8,128)S(1)}, f32[96,16,128]{2,1,0:T(8,128)}, u32[]{:S(2)}) copy-start(f32[96,16,128]{2,1,0:T(8,128)} %get-tuple-element.80.low) | copy-start | bytes 2359300
  38.6 2.6 %copy-start.25 = (s32[768]{0:T(1024)S(1)}, s32[768]{0:T(1024)}, u32[]{:S(2)}) copy-start(s32[768]{0:T(1024)} %mask_ref.3) | copy-start | bytes 9220
  41.2 14.3 %copy-start.8 = (bf16[288,768]{1,0:T(8,128)(2,1)S(1)}, bf16[288,768]{1,0:T(8,128)(2,1)}, u32[]{:S(2)}) copy-start(bf16[288,768]{1,0:T(8,128)(2,1)} %copy-done.7) | copy-start | bytes 1327108
  41.2 14.3 %copy-start = (bf16[2,768,768]{2,1,0:T(8,128)(2,1)S(1)}, bf16[2,768,768]{2,1,0:T(8,128)(2,1)}, u32[]{:S(2)}) copy-start(bf16[2,768,768]{2,1,0:T(8,128)(2,1)} %w_out.6) | copy-start | bytes 7077892
  54.9 25.9 %collective-permute-start.10 = (bf16[576,768]{1,0:T(8,128)(2,1)S(1)}, bf16[576,768]{1,0:T(8,128)(2,1)}, u32[]{:S(2)}, u32[]{:S(2)}) collective-permute-start(bf16[576,768]{1,0:T(8,128)(2,1)S(1)} %get-tuple-element.114.refs_1_), channel_id=1, source_target_pairs={{0,2},{1,3},{2,0},{3,1},{4,6},{5,7},{6,4},{7,5},{8,10},{9,11},{10,... | collective-permute-start | bytes 2654216 | tf_op jit(solution)/shard_map/ppermute | solution.py:659
  55.5 2.4 %collective-permute-start.7 = (bf16[288,768]{1,0:T(8,128)(2,1)S(1)}, bf16[288,768]{1,0:T(8,128)(2,1)S(1)}, u32[]{:S(2)}, u32[]{:S(2)}) collective-permute-start(bf16[288,768]{1,0:T(8,128)(2,1)S(1)} %copy-done.8), channel_id=1, source_target_pairs={{0,1},{1,0},{2,3},{3,2},{4,5},{5,4},{6,7},{7,6},{8,9},{9,8},{10,11... | collective-permute-start | bytes 1327112 | tf_op jit(solution)/shard_map/ppermute | solution.py:637
  56.7 4.5 %collective-permute-start.8 = (bf16[288,768]{1,0:T(8,128)(2,1)S(1)}, bf16[288,768]{1,0:T(8,128)(2,1)S(1)}, u32[]{:S(2)}, u32[]{:S(2)}) collective-permute-start(bf16[288,768]{1,0:T(8,128)(2,1)S(1)} %collective-permute-done.4.refs_4_), channel_id=1, source_target_pairs={{0,1},{1,0},{2,3},{3,2},{4,5},{5,4},{6,7},{7,6},{8,9},{9,8},{10,11... | collective-permute-start | bytes 1327112 | tf_op jit(solution)/shard_map/ppermute | solution.py:664
  57.3 4.0 %collective-permute-start.5 = (bf16[24,768]{1,0:T(8,128)(2,1)S(1)}, bf16[24,768]{1,0:T(8,128)(2,1)S(1)}, u32[]{:S(2)}, u32[]{:S(2)}) collective-permute-start(bf16[24,768]{1,0:T(8,128)(2,1)S(1)} %get-tuple-element.95.xn2), channel_id=1, source_target_pairs={{0,4},{1,5},{2,6},{3,7},{4,0},{5,1},{6,2},{7,3},{8,12},{9,13},{10,... | collective-permute-start | bytes 110600 | tf_op jit(solution)/shard_map/ppermute | solution.py:661
  64.6 4.0 %collective-permute-start.9 = (bf16[24,768]{1,0:T(8,128)(2,1)S(1)}, bf16[24,768]{1,0:T(8,128)(2,1)S(1)}, u32[]{:S(2)}, u32[]{:S(2)}) collective-permute-start(bf16[24,768]{1,0:T(8,128)(2,1)S(1)} %get-tuple-element.100), channel_id=1, source_target_pairs={{4,0},{5,1},{6,2},{7,3},{0,4},{1,5},{2,6},{3,7},{12,8},{13,9},{14,... | collective-permute-start | bytes 110600 | tf_op jit(solution)/shard_map/ppermute | solution.py:668
  70.2 10.6 %all-to-all-start.2 = ((bf16[8,24,768]{2,1,0:T(8,128)(2,1)}), bf16[8,24,768]{2,1,0:T(8,128)(2,1)S(1)}, u32[]{:S(2)}, u32[]{:S(2)}) async-start(bf16[8,24,768]{2,1,0:T(8,128)(2,1)} %copy-done.9), calls=%async_computation.2 | async-start | bytes 589824 | tf_op jit(solution)/shard_map/all_to_all | solution.py:670
  73.6 34.2 %collective-permute-start.13 = (bf16[576,768]{1,0:T(8,128)(2,1)S(1)}, bf16[576,768]{1,0:T(8,128)(2,1)}, u32[]{:S(2)}, u32[]{:S(2)}) collective-permute-start(bf16[576,768]{1,0:T(8,128)(2,1)S(1)} %get-tuple-element.114.refs_1_), channel_id=1, source_target_pairs={{0,1},{1,0},{2,3},{3,2},{4,5},{5,4},{6,7},{7,6},{8,9},{9,8},{10,11... | collective-permute-start | bytes 2654216 | tf_op jit(solution)/shard_map/ppermute | solution.py:638
  80.9 30.3 %collective-permute-start.14 = (bf16[576,768]{1,0:T(8,128)(2,1)}, bf16[576,768]{1,0:T(8,128)(2,1)S(1)}, u32[]{:S(2)}, u32[]{:S(2)}) collective-permute-start(bf16[576,768]{1,0:T(8,128)(2,1)} %collective-permute-done.10.refs_3_), channel_id=1, source_target_pairs={{0,1},{1,0},{2,3},{3,2},{4,5},{5,4},{6,7},{7,6},{8,9},{9,8},{10,11... | collective-permute-start | bytes 2654216 | tf_op jit(solution)/shard_map/ppermute | solution.py:640
  80.9 10.0 %collective-permute-start.11 = (bf16[96,768]{1,0:T(8,128)(2,1)S(1)}, bf16[96,768]{1,0:T(8,128)(2,1)S(1)}, u32[]{:S(2)}, u32[]{:S(2)}) collective-permute-start(bf16[96,768]{1,0:T(8,128)(2,1)S(1)} %constant_dynamic-slice_fusion.here_ref), channel_id=1, source_target_pairs={{4,8},{7,9},{0,16},{3,17},{2,24},{1,25},{12,2},{15,3},{8,18},{9,19... | collective-permute-start | bytes 442376 | tf_op jit(solution)/shard_map/ppermute | solution.py:613
  84.1 0.9 copy-start.11
  85.0 6.0 %copy-start.2 = (f32[96,16,128]{2,1,0:T(8,128)S(1)}, f32[96,16,128]{2,1,0:T(8,128)}, u32[]{:S(2)}) copy-start(f32[96,16,128]{2,1,0:T(8,128)} %get-tuple-element.107.low) | copy-start | bytes 2359300
  85.0 6.0 %copy-start.4 = (f32[96,16,128]{2,1,0:T(8,128)S(1)}, f32[96,16,128]{2,1,0:T(8,128)}, u32[]{:S(2)}) copy-start(f32[96,16,128]{2,1,0:T(8,128)} %copy-done.3) | copy-start | bytes 2359300
  90.9 15.0 %copy-start.12 = (f32[24,768]{1,0:T(8,128)S(1)}, f32[24,768]{1,0:T(8,128)}, u32[]{:S(2)}) copy-start(f32[24,768]{1,0:T(8,128)} %copy-done.10) | copy-start | bytes 221188
  107.2 4.0 %collective-permute-start.12 = (bf16[24,768]{1,0:T(8,128)(2,1)S(1)}, bf16[24,768]{1,0:T(8,128)(2,1)S(1)}, u32[]{:S(2)}, u32[]{:S(2)}) collective-permute-start(bf16[24,768]{1,0:T(8,128)(2,1)S(1)} %get-tuple-element.113.xn2), channel_id=1, source_target_pairs={{0,4},{1,5},{2,6},{3,7},{4,0},{5,1},{6,2},{7,3},{8,12},{9,13},{10,... | collective-permute-start | bytes 110600 | tf_op jit(solution)/shard_map/ppermute | solution.py:661
  111.2 7.1 %copy-start.13 = (bf16[768,128]{1,0:T(8,128)(2,1)S(1)}, bf16[768,128]{1,0:T(8,128)(2,1)}, u32[]{:S(2)}) copy-start(bf16[768,128]{1,0:T(8,128)(2,1)} %refs_1_.1) | copy-start | bytes 589828
  111.2 23.1 %copy-start.15 = (bf16[144,128]{1,0:T(8,128)(2,1)S(1)}, bf16[144,128]{1,0:T(8,128)(2,1)}, u32[]{:S(2)}) copy-start(bf16[144,128]{1,0:T(8,128)(2,1)} %copy-done.14) | copy-start | bytes 110596
  111.2 23.1 %copy-start.16 = (bf16[4,128,128]{2,1,0:T(8,128)(2,1)S(1)}, bf16[4,128,128]{2,1,0:T(8,128)(2,1)}, u32[]{:S(2)}) copy-start(bf16[4,128,128]{2,1,0:T(8,128)(2,1)} %w_in.7) | copy-start | bytes 393220
  111.2 23.1 %copy-start.18 = (bf16[256,128]{1,0:T(8,128)(2,1)S(1)}, bf16[256,128]{1,0:T(8,128)(2,1)}, u32[]{:S(2)}) copy-start(bf16[256,128]{1,0:T(8,128)(2,1)} %copy-done.17) | copy-start | bytes 196612
  111.2 23.1 %copy-start.20 = (bf16[144,128]{1,0:T(8,128)(2,1)S(1)}, bf16[144,128]{1,0:T(8,128)(2,1)}, u32[]{:S(2)}) copy-start(bf16[144,128]{1,0:T(8,128)(2,1)} %copy-done.19) | copy-start | bytes 110596
  111.2 23.1 %copy-start.22 = (bf16[144,128]{1,0:T(8,128)(2,1)S(1)}, bf16[144,128]{1,0:T(8,128)(2,1)}, u32[]{:S(2)}) copy-start(bf16[144,128]{1,0:T(8,128)(2,1)} %copy-done.21) | copy-start | bytes 110596
  111.2 23.1 %copy-start.23 = (bf16[128,128]{1,0:T(8,128)(2,1)S(1)}, bf16[128,128]{1,0:T(8,128)(2,1)}, u32[]{:S(2)}) copy-start(bf16[128,128]{1,0:T(8,128)(2,1)} %w_out.7) | copy-start | bytes 98308
  111.2 23.1 %copy-start.26 = (bf16[3,128]{1,0:T(4,128)(2,1)S(1)}, bf16[3,128]{1,0:T(4,128)(2,1)}, u32[]{:S(2)}) copy-start(bf16[3,128]{1,0:T(4,128)(2,1)} %pos.1) | copy-start | bytes 2308
  114.3 4.0 %collective-permute-start.15 = (bf16[24,768]{1,0:T(8,128)(2,1)S(1)}, bf16[24,768]{1,0:T(8,128)(2,1)S(1)}, u32[]{:S(2)}, u32[]{:S(2)}) collective-permute-start(bf16[24,768]{1,0:T(8,128)(2,1)S(1)} %get-tuple-element.117), channel_id=1, source_target_pairs={{4,0},{5,1},{6,2},{7,3},{0,4},{1,5},{2,6},{3,7},{12,8},{13,9},{14,... | collective-permute-start | bytes 110600 | tf_op jit(solution)/shard_map/ppermute | solution.py:668
  119.2 8.2 %all-to-all-start.4 = ((bf16[8,24,128]{2,1,0:T(8,128)(2,1)}), bf16[8,24,128]{2,1,0:T(8,128)(2,1)S(1)}, u32[]{:S(2)}, u32[]{:S(2)}) async-start(bf16[8,24,128]{2,1,0:T(8,128)(2,1)} %get-tuple-element.118), calls=%async_computation.4 | async-start | bytes 98304 | tf_op jit(solution)/shard_map/all_to_all | solution.py:670
  127.5 6.8 %collective-permute-start.16 = (bf16[64,128]{1,0:T(8,128)(2,1)S(1)}, bf16[64,128]{1,0:T(8,128)(2,1)S(1)}, u32[]{:S(2)}, u32[]{:S(2)}) collective-permute-start(bf16[64,128]{1,0:T(8,128)(2,1)S(1)} %slice_select_fusion), channel_id=1, source_target_pairs={{7,8},{15,16},{23,24},{8,7},{16,15},{24,23}} | collective-permute-start | bytes 49160 | tf_op jit(solution)/shard_map/ppermute | solution.py:677
  (6 other events, 4.0 us)

commit v6 on v5

--- a/solution.py
+++ b/solution.py
@@ -208,15 +208,16 @@
     own[rows:] = tail.astype(F32).astype(BF16)
 
 
-def pack_kernel(first, second, upper, lower, *outs):
+def pack_kernel(first, second, *outs):
     hid = second.shape[1]
-    part = upper.shape[0]
-    for layer, out in enumerate(outs):
-        out[:hid] = first[layer, 0]
-        out[hid : 2 * hid] = first[layer, 1]
-        out[2 * hid :] = second[layer]
-    upper[...] = outs[0][:part]
-    lower[...] = outs[0][part:]
+    part = 3 * hid // 2
+    for layer in range(BLOCKS):
+        whole, upper, lower = outs[3 * layer : 3 * layer + 3]
+        whole[:hid] = first[layer, 0]
+        whole[hid : 2 * hid] = first[layer, 1]
+        whole[2 * hid :] = second[layer]
+        upper[...] = whole[:part]
+        lower[...] = whole[part:]
 
 
 def bias_kernel(pair_ref, weight, *outs):
@@ -307,7 +308,7 @@
     out_ref[:, width:] = jnp.where(spot < 3 * heads, packed, 0.0).astype(BF16)
 
 
-def mix_kernel(layer, heads, message, act_ref, gate, w_out, act_out, xn2_out, w_mix, sems):
+def mix_kernel(layer, heads, message, act_ref, gate, w_out, act_out, w_mix, sems):
     (copy,) = prepare([w_out.at[layer]], [w_mix], sems)
     copy.start()
     width = act_ref.shape[1]
@@ -337,16 +338,14 @@
         attn = attn + spread[j * own : (j + 1) * own] * message[j, :, :width].astype(F32)
     gated = (gate[...] * attn).astype(BF16)
     copy.wait()
-    act = act_ref[...] + dot(gated, w_mix[...])
-    act_out[...] = act
-    xn2_out[...] = normed(act).astype(BF16)
+    act_out[...] = act_ref[...] + dot(gated, w_mix[...])
 
 
 def mix(layer, message, act, gate, w_out, heads):
     own, width = act.shape
     return call(
         functools.partial(mix_kernel, layer, heads),
-        [jax.ShapeDtypeStruct((own, width), F32), jax.ShapeDtypeStruct((own, width), BF16)],
+        jax.ShapeDtypeStruct((own, width), F32),
         message,
         act,
         gate,
@@ -358,13 +357,13 @@
     )
 
 
-def transition_kernel(groups, pieces, act_ref, xn2, *refs):
+def transition_kernel(groups, pieces, act_ref, *refs):
     others, refs = refs[: groups - 1], refs[groups - 1 :]
     sources = []
     for number in pieces:
         sources.append(refs[:number])
         refs = refs[number:]
-    outs, (w_first, w_second, sems) = refs[:groups], refs[groups:]
+    base, send, w_first, w_second, sems = refs
     count, hid = w_second.shape[:2]
     plan = []
     for wanted, target in (((0, 2 * hid), w_first), ((2 * hid, 3 * hid), w_second)):
@@ -386,9 +385,17 @@
             if item[:2] == (first, j):
                 copy.wait()
 
-    own = act_ref.shape[0]
-    rows = jnp.concatenate([ref[...].astype(F32) for ref in (xn2, *others)], 0).astype(BF16)
-    total = jnp.zeros((rows.shape[0], rows.shape[1]), F32)
+    group = device()[1] // 4
+    came = [ref[...] for ref in (act_ref, *others)]
+    ordered = []
+    for place in range(groups):
+        rows = came[0]
+        for d in range(1, groups):
+            rows = jnp.where((group - place + groups) % groups == d, came[d], rows)
+        ordered.append(rows)
+    act = jnp.concatenate(ordered, 0)
+    rows = normed(act).astype(BF16)
+    total = jnp.zeros(act.shape, F32)
     hidden = []
     for j in range(count):
         arrived(True, j)
@@ -398,22 +405,19 @@
     for j in range(count):
         arrived(False, j)
         total = total + dot(hidden[j], w_second[j])
-    outs[0][...] = act_ref[...] + total[:own]
-    for k, out in enumerate(outs[1:], 1):
-        out[...] = total[k * own : (k + 1) * own].astype(BF16)
-
-
-def transition(act, xn2, others, weights):
+    base[...] = act + total
+    send[...] = total.astype(BF16)
+
+
+def transition(act, others, weights):
     own, width = act.shape
     blocks = len(weights)
     hid = sum(part.shape[0] for part in weights[0]) // 3
     parts = [part for source in weights for part in source]
     return call(
         functools.partial(transition_kernel, len(others) + 1, [len(source) for source in weights]),
-        [jax.ShapeDtypeStruct((own, width), F32)]
-        + [jax.ShapeDtypeStruct((own, width), BF16)] * len(others),
+        [jax.ShapeDtypeStruct(((len(others) + 1) * own, width), kind) for kind in (F32, BF16)],
         act,
-        xn2,
         *others,
         far=parts,
         scratch=[
@@ -428,36 +432,53 @@
 
 
 def close_kernel(project, act_ref, *refs):
-    *refs, act_out, all_ref = refs
+    *refs, act_out, out = refs
     if project:
         *refs, tok_atom = refs
     act = act_ref[...]
     for ref in refs:
         act = act + ref[...].astype(F32)
-    act_out[...] = act
+    own = act_out.shape[0]
+    mine = act[:own]
+    for k in range(1, act.shape[0] // own):
+        mine = jnp.where(device()[1] // 4 == k, act[k * own : (k + 1) * own], mine)
+    act_out[...] = mine
     normal = normed(act).astype(BF16)
     if project:
         normal = dot(normal, tok_atom[...]).astype(BF16)
-    for j in range(all_ref.shape[0]):
-        all_ref[j] = normal
-
-
-def close(act, parts, copies, tok_atom):
-    own, width = act.shape
+    out[...] = normal
+
+
+def close(own, act, parts, tok_atom):
+    rows, width = act.shape
     project = tok_atom is not None
     last = tok_atom.shape[1] if project else width
     return call(
         functools.partial(close_kernel, project),
-        [
-            jax.ShapeDtypeStruct((own, width), F32),
-            jax.ShapeDtypeStruct((copies, own, last), BF16),
-        ],
+        [jax.ShapeDtypeStruct((own, width), F32), jax.ShapeDtypeStruct((rows, last), BF16)],
         act,
         *parts,
         *([tok_atom] if project else []),
         flops=10**7,
         moved=10**6,
     )
+
+
+def row_of(mine, own):
+    nrow, ncol = lax.axis_size("row"), lax.axis_size("col")
+    parts = [mine]
+    for flip in range(1, 4):
+        parts.append(
+            lax.ppermute(mine, ("row", "col"), [(i, i ^ flip) for i in range(nrow * ncol)])
+        )
+    low = lax.axis_index("col") % 4
+    ordered = []
+    for place in range(4):
+        rows = parts[place]
+        for flip in range(1, 4):
+            rows = jnp.where(low == flip, parts[place ^ flip], rows)
+        ordered.append(rows.reshape(-1, 1, own, mine.shape[1]))
+    return jnp.concatenate(ordered, 1).reshape(-1, mine.shape[1])
 
 
 def key_source(rows, cols):
@@ -525,19 +546,20 @@
         (feat, jnp.swapaxes(trans_in, 2, 3), trans_out)
     )
     matrix = jax.ShapeDtypeStruct((3 * hid, width), BF16)
-    upper, lower, *packed = call(
+    half = jax.ShapeDtypeStruct((3 * hid // 2, width), BF16)
+    pieces = call(
         pack_kernel,
-        [jax.ShapeDtypeStruct((3 * hid // 2, width), BF16)] * 2
-        + [matrix] * BLOCKS,
+        [matrix, half, half] * BLOCKS,
         first_part,
         second_part,
         grant=48,
         moved=12 * trans_out.size,
     )
-    prev, after, upper = lax.optimization_barrier((prev, after, upper))
+    packed, upper, lower = pieces[::3], pieces[1::3], pieces[2::3]
+    prev, after, early = lax.optimization_barrier((prev, after, upper[0]))
     neighbour = [(i, i ^ 2) for i in range(count)]
     sibling = [(i, i ^ 1) for i in range(count)]
-    across = [[lax.ppermute(upper, everyone, neighbour)], []]
+    across = [[lax.ppermute(early, everyone, neighbour)], []]
 
     ext, copies = call(
         functools.partial(encoder_kernel, natom),
@@ -602,14 +624,13 @@
         [(r * ncol + c, r * ncol + (c + 4 * d) % ncol) for r in range(nrow) for c in range(ncol)]
         for d in range(peers)
     ]
-    back = [[(b, a) for a, b in pairs_of] for pairs_of in shifts]
     xn, weights = lax.optimization_barrier((xn, weights))
     beside, beyond = [], [[], []]
     for layer in range(BLOCKS):
         last = layer == BLOCKS - 1
         if layer:
             send = lax.dynamic_slice_in_dim(xn, share * cols, cols, 0)
-            send, xn, ready = lax.optimization_barrier((send, xn, across[1][0]))
+            send, xn = lax.optimization_barrier((send, xn))
         came = lax.ppermute(send, everyone, pairs)
         matrix = jax.ShapeDtypeStruct((width, width), BF16)
         query, w_key, w_val, gate = call(
@@ -630,14 +651,16 @@
         )
         if not layer:
             high = list(bias_of(1, weights))
-            high[0], lower, *ready = lax.optimization_barrier(
-                (high[0], lower, across[0][0], *packed)
+            high[0], late, *ready = lax.optimization_barrier(
+                (high[0], lower[0], across[0][0], *packed)
             )
-            across[0].append(lax.ppermute(lower, everyone, neighbour))
+            across[0].append(lax.ppermute(late, everyone, neighbour))
             beyond[0].append(lax.ppermute(ready[0], everyone, sibling))
             beside = [lax.ppermute(part, everyone, sibling) for part in ready[1:]]
         else:
             beyond[1].append(lax.ppermute(ready, everyone, sibling))
+            query, late = lax.optimization_barrier((query, lower[1]))
+            across[1].append(lax.ppermute(late, everyone, neighbour))
         message = call(
             attention_kernel,
             jax.ShapeDtypeStruct((rows, width + span), BF16),
@@ -655,19 +678,20 @@
         )
         message = lax.all_to_all(message.reshape(ncol, own, -1), "col", 0, 0)
         if not layer:
-            message, ready = lax.optimization_barrier((message, packed[1]))
+            message, ready = lax.optimization_barrier((message, upper[1]))
             across[1].append(lax.ppermute(ready, everyone, neighbour))
-        act, xn2 = mix(layer, message, act, gate, tok_out, heads)
-        came_rows = [lax.ppermute(xn2, everyone, shifts[d]) for d in range(1, peers)]
-        if not layer:
-            xn2, ready = lax.optimization_barrier((xn2, across[0][1]))
-            beyond[0].append(lax.ppermute(ready, everyone, sibling))
-        act, *parts = transition(
-            act, xn2, came_rows, ([packed[layer]], [beside[layer]], across[layer], beyond[layer])
+        act = mix(layer, message, act, gate, tok_out, heads)
+        came_rows = [lax.ppermute(act, everyone, shifts[d]) for d in range(1, peers)]
+        act, ready = lax.optimization_barrier((act, across[layer][1]))
+        beyond[layer].append(lax.ppermute(ready, everyone, sibling))
+        act, part = transition(
+            act, came_rows, ([packed[layer]], [beside[layer]], across[layer], beyond[layer])
         )
-        parts = [lax.ppermute(part, everyone, back[d]) for d, part in enumerate(parts, 1)]
-        act, copies = close(act, parts, ncol, tok_atom if last else None)
-        gathered = lax.all_to_all(copies, "col", 0, 0).reshape(rows, -1)
+        parts = [lax.ppermute(part, everyone, shifts[d]) for d in range(1, peers)]
+        act, mine = close(own, act, parts, tok_atom if last else None)
+        if not last:
+            mine, ready = lax.optimization_barrier((mine, across[1][0]))
+        gathered = row_of(mine, own)
         if not last:
             xn = gathered
 

time: 138 us -> 134 us (0.971)
  blocking collectives: 22 us -> 0 us
  waiting for transfers between devices: 36.9 us -> 48.4 us
  starting transfers between devices: 31.9 us -> 37 us
  Pallas kernels: 36.8 us -> 38.3 us
    all_to_all x2 -> x0, blocking collectives: 22 us -> none  [body(): message = lax.all_to_all(message.reshape(ncol, own, -1), 'col', 0, 0)]
    ppermute x7 -> x15, waiting for transfers between devices: 13.6 us -> 21.6 us  [the longest x2 7.84 us: body(): lax.ppermute(act, everyone, shifts[d])]
    ppermute x7 -> x15, starting transfers between devices: 3.76 us -> 7.77 us  [the longest x6 3.78 us: row_of(): lax.ppermute(mine, ('row', 'col'), [(i, i ^ flip) for i in range(nrow * n...]
    all_to_all x2, waiting for transfers between devices: 11.7 us -> 14.6 us  [body(): message = lax.all_to_all(message.reshape(ncol, own, -1), 'col', 0, 0)]
    pallas_call x15, Pallas kernels: 28.7 us -> 30.3 us  [call(): pl.pallas_call(kernel, out_shape=outs, in_specs=[smem] * len(scalars) + [...]
    unnamed x68 -> x64, local copies, waits for them, and re-layouts: 8.34 us -> 7.69 us
  transfers between devices with their start and end apart: 20 -> 28, of which waited for: 9 -> 13; matrix products, arithmetic and copies ran while one was open for 0% -> 0% of each run, Pallas kernels for 21% -> 23%
where the time goes in v6:
time: 134 us; the launch traced here: 132 us
  waiting for transfers between devices  48.4 us (36%)
  Pallas kernels  38.3 us (29%)
  starting transfers between devices  37 us (28%)
  local copies, waits for them, and re-layouts  7.71 us (6%)
    pallas_call x15, Pallas kernels, call(): pl.pallas_call(kernel, out_shape=outs, in_specs=[smem] * len(scalars) + [...  30.3 us
    all_to_all x2, waiting for transfers between devices, body(): message = lax.all_to_all(message.reshape(ncol, own, -1), 'col', 0, 0)  14.6 us
    pallas_call x2, Pallas kernels, bias_of(): pl.pallas_call(bias_kernel, grid=(half // step,), out_shape=[jax.ShapeDty...  7.99 us
    ppermute x2, waiting for transfers between devices, body(): lax.ppermute(act, everyone, shifts[d])  7.84 us
    all_to_all x2, starting transfers between devices, body(): message = lax.all_to_all(message.reshape(ncol, own, -1), 'col', 0, 0)  7.75 us
    unnamed x64, local copies, waits for them, and re-layouts  7.69 us
    ppermute x2, waiting for transfers between devices, body(): parts = [lax.ppermute(part, everyone, shifts[d]) for d in range(1, peers)]  7.58 us
    ppermute x6, waiting for transfers between devices, row_of(): lax.ppermute(mine, ('row', 'col'), [(i, i ^ flip) for i in range(nrow * n...  6.16 us
  transfers between devices with their start and end apart: 28, of which 13 were waited for; matrix products, arithmetic and copies ran while one was open for 0% of the time, Pallas kernels for 23%

profile of v6, /device:TPU:24, one launch (start us, length us, event | category | flops | bytes accessed | tf_op | source)
XLA Modules:
  0.0 132.0 jit_solution(3684544747389074026)
XLA Ops:
  0.0 0.8 copy-done.20
  0.8 0.7 copy-done.23
  1.4 0.7 copy-done.24
  2.6 1.9 %collective-permute-start = (bf16[144,128]{1,0:T(8,128)(2,1)S(1)}, bf16[144,128]{1,0:T(8,128)(2,1)S(1)}, u32[]{:S(2)}, u32[]{:S(2)}) collective-permute-start(bf16[144,128]{1,0:T(8,128)(2,1)S(1)} %shard_map.172.own_ref), channel_id=1, source_target_pairs={{0,1},{1,2},{2,3},{3,4},{4,5},{5,6},{6,7},{7,8},{8,9},{9,10},{10,1... | collective-permute-start | bytes 110600 | tf_op jit(solution)/shard_map/ppermute | solution.py:543
  4.6 5.4 %collective-permute-start.1 = (bf16[144,128]{1,0:T(8,128)(2,1)S(1)}, bf16[144,128]{1,0:T(8,128)(2,1)S(1)}, u32[]{:S(2)}, u32[]{:S(2)}) collective-permute-start(bf16[144,128]{1,0:T(8,128)(2,1)S(1)} %shard_map.172.own_ref), channel_id=1, source_target_pairs={{1,0},{2,1},{3,2},{4,3},{5,4},{6,5},{7,6},{8,7},{9,8},{10,9},{11,1... | collective-permute-start | bytes 110600 | tf_op jit(solution)/shard_map/ppermute | solution.py:544
  10.0 1.3 copy-done.1
  11.3 1.1 copy-done.4
  12.4 1.6 %shard_map.173 = (bf16[576,768]{1,0:T(8,128)(2,1)}, bf16[288,768]{1,0:T(8,128)(2,1)S(1)}, bf16[288,768]{1,0:T(8,128)(2,1)}, bf16[576,768]{1,0:T(8,128)(2,1)}, bf...) custom-call(bf16[2,2,192,768]{3,2,1,0:T(8,128)(2,1)S(1)} %bitcast.35, bf16[2,192,768]{2,1,0:T(8,128)(2,1)S(1)} %copy-done.4), custom_call_target="tpu_custom_call" | custom-call | bytes 3538944 | tf_op jit(solution)/shard_map/pallas_call | solution.py:26
  14.0 0.8 copy-done.25
  14.9 2.0 %shard_map.174 = (bf16[256,128]{1,0:T(8,128)(2,1)S(1)}, bf16[8,144,128]{2,1,0:T(8,128)(2,1)}) custom-call(bf16[144,128]{1,0:T(8,128)(2,1)S(1)} %shard_map.172.own_ref, bf16[144,128]{1,0:T(8,128)(2,1)S(1)} %collective-permute-done.prev_ref, bf16[144,128]{1,0:T(8,128)(2,1)S(1)} %collective-permute-done.1.next_ref, bf16[4,128,128]{2,1,0:T(8,128)(2,1)S(1)} %copy-done.29, ...), custom_call_target="tpu_custom_call" | custom-call | flops 100000000 | bytes 1000000 | tf_op jit(solution)/shard_map/pallas_call | solution.py:26
  16.9 3.4 %all-to-all-start = ((bf16[8,144,128]{2,1,0:T(8,128)(2,1)}), bf16[8,144,128]{2,1,0:T(8,128)(2,1)S(1)}, u32[]{:S(2)}, u32[]{:S(2)}) async-start(bf16[8,144,128]{2,1,0:T(8,128)(2,1)} %get-tuple-element.72), calls=%async_computation | async-start | bytes 589824 | tf_op jit(solution)/shard_map/all_to_all | solution.py:603
  20.3 4.6 %shard_map.175 = (f32[96,16,128]{2,1,0:T(8,128)}, f32[96,16,128]{2,1,0:T(8,128)}) custom-call(bf16[192,96,128]{2,1,0:T(8,128)(2,1)} %pair_ref.3, bf16[32,128]{1,0:T(8,128)(2,1)} %bitcast.39), custom_call_target="tpu_custom_call" | custom-call | flops 2000000000 | bytes 4000000 | tf_op jit(solution)/shard_map/pallas_call | solution.py:583
  24.9 4.2 %all-to-all-done.both_ref = bf16[8,144,128]{2,1,0:T(8,128)(2,1)S(1)} async-done(((bf16[8,144,128]{2,1,0:T(8,128)(2,1)}), bf16[8,144,128]{2,1,0:T(8,128)(2,1)S(1)}, u32[]{:S(2)}, u32[]{:S(2)}) %all-to-all-start) | async-done | bytes 294944 | tf_op jit(solution)/shard_map/all_to_all | solution.py:603
  29.1 1.3 shard_map.176
  30.5 3.5 %collective-permute-start.3 = (bf16[96,768]{1,0:T(8,128)(2,1)S(1)}, bf16[96,768]{1,0:T(8,128)(2,1)S(1)}, u32[]{:S(2)}, u32[]{:S(2)}) collective-permute-start(bf16[96,768]{1,0:T(8,128)(2,1)S(1)} %get-tuple-element.82.here_ref), channel_id=1, source_target_pairs={{4,8},{7,9},{0,16},{3,17},{2,24},{1,25},{12,2},{15,3},{8,18},{9,19... | collective-permute-start | bytes 442376 | tf_op jit(solution)/shard_map/ppermute | solution.py:634
  34.0 3.4 %shard_map.178 = (f32[96,16,128]{2,1,0:T(8,128)S(1)}, f32[96,16,128]{2,1,0:T(8,128)S(1)}) custom-call(bf16[192,96,128]{2,1,0:T(8,128)(2,1)} %pair_ref.3, bf16[32,128]{1,0:T(8,128)(2,1)S(1)} %bitcast.40), custom_call_target="tpu_custom_call" | custom-call | flops 2000000000 | bytes 4000000 | tf_op jit(solution)/shard_map/pallas_call | solution.py:583
  37.4 0.7 collective-permute-start.4
  38.2 2.4 %shard_map.177 = (bf16[192,768]{1,0:T(8,128)(2,1)S(1)}, bf16[768,768]{1,0:T(8,128)(2,1)S(1)}, bf16[768,768]{1,0:T(8,128)(2,1)S(1)}, f32[24,768]{1,0:T(8,128)S(1)}) custom-call(bf16[192,768]{1,0:T(8,128)(2,1)S(1)} %get-tuple-element.79.xn_ref, f32[24,768]{1,0:T(8,128)S(1)} %get-tuple-element.80.act_ref, bf16[2,4,768,768]{3,2,1,0:T(8,128)(2,1)} %w_in.6), custom_call_target="tpu_custom_call" | custom-call | flops 226492416 | bytes 4718592 | tf_op jit(solution)/shard_map/pallas_call | solution.py:26
  41.3 4.2 %shard_map.179 = bf16[192,896]{1,0:T(8,128)(2,1)} custom-call(s32[768]{0:T(1024)S(1)} %copy-done.21, bf16[192,768]{1,0:T(8,128)(2,1)S(1)} %get-tuple-element.81.query, bf16[96,768]{1,0:T(8,128)(2,1)S(1)} %get-tuple-element.82.here_ref, bf16[96,768]{1,0:T(8,128)(2,1)S(1)} %collective-permute-done.3.came_ref, f32[96,16,128]{2,1,0:T(8,128)S(1)} %copy-done.3, ...), custom_call_target="tpu_custom_call" | custom-call | flops 1000000000 | bytes 8000000 | tf_op jit(solution)/shard_map/pallas_call | solution.py:26
  45.5 4.0 %all-to-all-start.1 = ((bf16[8,24,896]{2,1,0:T(8,128)(2,1)}), bf16[8,24,896]{2,1,0:T(8,128)(2,1)S(1)}, u32[]{:S(2)}, u32[]{:S(2)}) async-start(bf16[8,24,896]{2,1,0:T(8,128)(2,1)} %bitcast.4), calls=%async_computation.1 | async-start | bytes 688128 | tf_op jit(solution)/shard_map/all_to_all | solution.py:679
  49.9 7.3 %all-to-all-done.1.message = bf16[8,24,896]{2,1,0:T(8,128)(2,1)S(1)} async-done(((bf16[8,24,896]{2,1,0:T(8,128)(2,1)}), bf16[8,24,896]{2,1,0:T(8,128)(2,1)S(1)}, u32[]{:S(2)}, u32[]{:S(2)}) %all-to-all-start.1) | async-done | bytes 344096 | tf_op jit(solution)/shard_map/all_to_all | solution.py:679
  57.2 0.9 copy-done.8
  58.1 0.9 copy-done.12
  59.0 1.0 shard_map.180.act_ref
  60.2 0.6 collective-permute-start.10
  61.4 3.8 %collective-permute-done.5.refs_0_ = f32[24,768]{1,0:T(8,128)S(1)} collective-permute-done((f32[24,768]{1,0:T(8,128)S(1)}, f32[24,768]{1,0:T(8,128)S(1)}, u32[]{:S(2)}, u32[]{:S(2)}) %collective-permute-start.5) | collective-permute-done | bytes 73760 | tf_op jit(solution)/shard_map/ppermute | solution.py:684
  65.2 3.2 %shard_map.181 = (f32[48,768]{1,0:T(8,128)S(1)}, bf16[48,768]{1,0:T(8,128)(2,1)S(1)}) custom-call(f32[24,768]{1,0:T(8,128)S(1)} %shard_map.180.act_ref, f32[24,768]{1,0:T(8,128)S(1)} %collective-permute-done.5.refs_0_, bf16[576,768]{1,0:T(8,128)(2,1)} %get-tuple-element.98.refs_1_, bf16[576,768]{1,0:T(8,128)(2,1)} %collective-permute-done.6.refs_2_, ...), custom_call_target="tpu_custom_call" | custom-call | flops 169869312 | bytes 3538944 | tf_op jit(solution)/shard_map/pallas_call | solution.py:26
  68.4 0.6 collective-permute-start.9
  69.0 3.8 %collective-permute-done.9.refs_0_ = bf16[48,768]{1,0:T(8,128)(2,1)S(1)} collective-permute-done((bf16[48,768]{1,0:T(8,128)(2,1)S(1)}, bf16[48,768]{1,0:T(8,128)(2,1)S(1)}, u32[]{:S(2)}, u32[]{:S(2)}) %collective-permute-start.9) | collective-permute-done | bytes 73760 | tf_op jit(solution)/shard_map/ppermute | solution.py:690
  73.1 1.5 %collective-permute-start.12 = (bf16[48,768]{1,0:T(8,128)(2,1)S(1)}, bf16[48,768]{1,0:T(8,128)(2,1)S(1)}, u32[]{:S(2)}, u32[]{:S(2)}) collective-permute-start(bf16[48,768]{1,0:T(8,128)(2,1)S(1)} %get-tuple-element.105), channel_id=1, source_target_pairs={{0,2},{1,3},{2,0},{3,1},{4,6},{5,7},{6,4},{7,5},{8,10},{9,11},{10,... | collective-permute-start | bytes 221192 | tf_op jit(solution)/shard_map/ppermute | solution.py:472
  74.9 2.7 %collective-permute-done.11 = bf16[48,768]{1,0:T(8,128)(2,1)S(1)} collective-permute-done((bf16[48,768]{1,0:T(8,128)(2,1)S(1)}, bf16[48,768]{1,0:T(8,128)(2,1)S(1)}, u32[]{:S(2)}, u32[]{:S(2)}) %collective-permute-start.11) | collective-permute-done | bytes 73760 | tf_op jit(solution)/shard_map/ppermute | solution.py:472
  77.6 1.6 %collective-permute-done.12 = bf16[48,768]{1,0:T(8,128)(2,1)S(1)} collective-permute-done((bf16[48,768]{1,0:T(8,128)(2,1)S(1)}, bf16[48,768]{1,0:T(8,128)(2,1)S(1)}, u32[]{:S(2)}, u32[]{:S(2)}) %collective-permute-start.12) | collective-permute-done | bytes 73760 | tf_op jit(solution)/shard_map/ppermute | solution.py:472
  79.3 2.6 %collective-permute-start.14 = (bf16[96,768]{1,0:T(8,128)(2,1)S(1)}, bf16[96,768]{1,0:T(8,128)(2,1)S(1)}, u32[]{:S(2)}, u32[]{:S(2)}) collective-permute-start(bf16[96,768]{1,0:T(8,128)(2,1)S(1)} %constant_dynamic-slice_fusion.here_ref), channel_id=1, source_target_pairs={{4,8},{7,9},{0,16},{3,17},{2,24},{1,25},{12,2},{15,3},{8,18},{9,19... | collective-permute-start | bytes 442376 | tf_op jit(solution)/shard_map/ppermute | solution.py:634
  82.0 2.4 %shard_map.183 = (bf16[192,768]{1,0:T(8,128)(2,1)S(1)}, bf16[768,768]{1,0:T(8,128)(2,1)S(1)}, bf16[768,768]{1,0:T(8,128)(2,1)S(1)}, f32[24,768]{1,0:T(8,128)S(1)}) custom-call(bf16[192,768]{1,0:T(8,128)(2,1)S(1)} %bitcast.34, f32[24,768]{1,0:T(8,128)S(1)} %get-tuple-element.107.act_ref, bf16[2,4,768,768]{3,2,1,0:T(8,128)(2,1)} %w_in.6), custom_call_target="tpu_custom_call" | custom-call | flops 226492416 | bytes 4718592 | tf_op jit(solution)/shard_map/pallas_call | solution.py:26
  85.0 4.1 %collective-permute-done.14.came_ref = bf16[96,768]{1,0:T(8,128)(2,1)S(1)} collective-permute-done((bf16[96,768]{1,0:T(8,128)(2,1)S(1)}, bf16[96,768]{1,0:T(8,128)(2,1)S(1)}, u32[]{:S(2)}, u32[]{:S(2)}) %collective-permute-start.14) | collective-permute-done | bytes 147488 | tf_op jit(solution)/shard_map/ppermute | solution.py:634
  89.1 4.2 %shard_map.184 = bf16[192,896]{1,0:T(8,128)(2,1)} custom-call(s32[768]{0:T(1024)S(1)} %copy-done.21, bf16[192,768]{1,0:T(8,128)(2,1)S(1)} %get-tuple-element.110.query, bf16[96,768]{1,0:T(8,128)(2,1)S(1)} %constant_dynamic-slice_fusion.here_ref, bf16[96,768]{1,0:T(8,128)(2,1)S(1)} %collective-permute-done.14.came_ref, f32[96,16,128]{2,1,0:T(8,128)S(1)} %copy-done.2, ...), custom_call_target="tpu_custom_call" | custom-call | flops 1000000000 | bytes 8000000 | tf_op jit(solution)/shard_map/pallas_call | solution.py:26
  93.3 3.8 %all-to-all-start.2 = ((bf16[8,24,896]{2,1,0:T(8,128)(2,1)}), bf16[8,24,896]{2,1,0:T(8,128)(2,1)S(1)}, u32[]{:S(2)}, u32[]{:S(2)}) async-start(bf16[8,24,896]{2,1,0:T(8,128)(2,1)} %bitcast.14), calls=%async_computation.2 | async-start | bytes 688128 | tf_op jit(solution)/shard_map/all_to_all | solution.py:679
  97.6 7.3 %all-to-all-done.2.message = bf16[8,24,896]{2,1,0:T(8,128)(2,1)S(1)} async-done(((bf16[8,24,896]{2,1,0:T(8,128)(2,1)}), bf16[8,24,896]{2,1,0:T(8,128)(2,1)S(1)}, u32[]{:S(2)}, u32[]{:S(2)}) %all-to-all-start.2) | async-done | bytes 344096 | tf_op jit(solution)/shard_map/all_to_all | solution.py:679
  104.9 1.0 shard_map.185.act_ref
  106.8 4.0 %collective-permute-done.16.refs_0_ = f32[24,768]{1,0:T(8,128)S(1)} collective-permute-done((f32[24,768]{1,0:T(8,128)S(1)}, f32[24,768]{1,0:T(8,128)S(1)}, u32[]{:S(2)}, u32[]{:S(2)}) %collective-permute-start.16) | collective-permute-done | bytes 73760 | tf_op jit(solution)/shard_map/ppermute | solution.py:684
  110.8 3.2 %shard_map.186 = (f32[48,768]{1,0:T(8,128)S(1)}, bf16[48,768]{1,0:T(8,128)(2,1)S(1)}) custom-call(f32[24,768]{1,0:T(8,128)S(1)} %shard_map.185.act_ref, f32[24,768]{1,0:T(8,128)S(1)} %collective-permute-done.16.refs_0_, bf16[576,768]{1,0:T(8,128)(2,1)} %get-tuple-element.119.refs_1_, bf16[576,768]{1,0:T(8,128)(2,1)} %collective-permute-done.17.refs_2_, ...), custom_call_target="tpu_custom_call" | custom-call | flops 169869312 | bytes 3538944 | tf_op jit(solution)/shard_map/pallas_call | solution.py:26
  114.7 3.8 %collective-permute-done.20.refs_0_ = bf16[48,768]{1,0:T(8,128)(2,1)S(1)} collective-permute-done((bf16[48,768]{1,0:T(8,128)(2,1)S(1)}, bf16[48,768]{1,0:T(8,128)(2,1)S(1)}, u32[]{:S(2)}, u32[]{:S(2)}) %collective-permute-start.20) | collective-permute-done | bytes 73760 | tf_op jit(solution)/shard_map/ppermute | solution.py:690
  118.5 0.8 shard_map.187
  119.9 1.3 collective-permute-start.23
  121.2 1.3 collective-permute-done.21
  123.1 3.0 %collective-permute-start.24 = (bf16[64,128]{1,0:T(8,128)(2,1)S(1)}, bf16[64,128]{1,0:T(8,128)(2,1)S(1)}, u32[]{:S(2)}, u32[]{:S(2)}) collective-permute-start(bf16[64,128]{1,0:T(8,128)(2,1)S(1)} %slice_select_fusion), channel_id=1, source_target_pairs={{7,8},{15,16},{23,24},{8,7},{16,15},{24,23}} | collective-permute-start | bytes 49160 | tf_op jit(solution)/shard_map/ppermute | solution.py:701
  126.1 3.9 %collective-permute-done.24.edge_ref = bf16[64,128]{1,0:T(8,128)(2,1)S(1)} collective-permute-done((bf16[64,128]{1,0:T(8,128)(2,1)S(1)}, bf16[64,128]{1,0:T(8,128)(2,1)S(1)}, u32[]{:S(2)}, u32[]{:S(2)}) %collective-permute-start.24) | collective-permute-done | bytes 16416 | tf_op jit(solution)/shard_map/ppermute | solution.py:701
  130.0 2.0 %shard_map.188 = f32[3,128]{1,0:T(4,128)} custom-call(bf16[256,128]{1,0:T(8,128)(2,1)S(1)} %copy-done.14, bf16[144,128]{1,0:T(8,128)(2,1)S(1)} %shard_map.172.own_ref, bf16[144,128]{1,0:T(8,128)(2,1)S(1)} %copy-done.16, bf16[144,128]{1,0:T(8,128)(2,1)S(1)} %copy-done.18, bf16[192,128]{1,0:T(8,128)(2,1)S(1)} %bitcast.37, ...), custom_call_target="tpu_custom_call" | custom-call | flops 100000000 | bytes 1000000 | tf_op jit(solution)/shard_map/pallas_call | solution.py:26
  (95 shorter events, 6.9 us)
Async XLA Ops:
  2.1 12.8 %copy-start.30 = (bf16[128,128]{1,0:T(8,128)(2,1)S(1)}, bf16[128,128]{1,0:T(8,128)(2,1)}, u32[]{:S(2)}) copy-start(bf16[128,128]{1,0:T(8,128)(2,1)} %w_out.4) | copy-start | bytes 98308
  2.6 12.1 %collective-permute-start = (bf16[144,128]{1,0:T(8,128)(2,1)S(1)}, bf16[144,128]{1,0:T(8,128)(2,1)S(1)}, u32[]{:S(2)}, u32[]{:S(2)}) collective-permute-start(bf16[144,128]{1,0:T(8,128)(2,1)S(1)} %shard_map.172.own_ref), channel_id=1, source_target_pairs={{0,1},{1,2},{2,3},{3,4},{4,5},{5,6},{6,7},{7,8},{8,9},{9,10},{10,1... | collective-permute-start | bytes 110600 | tf_op jit(solution)/shard_map/ppermute | solution.py:543
  4.6 10.2 %collective-permute-start.1 = (bf16[144,128]{1,0:T(8,128)(2,1)S(1)}, bf16[144,128]{1,0:T(8,128)(2,1)S(1)}, u32[]{:S(2)}, u32[]{:S(2)}) collective-permute-start(bf16[144,128]{1,0:T(8,128)(2,1)S(1)} %shard_map.172.own_ref), channel_id=1, source_target_pairs={{1,0},{2,1},{3,2},{4,3},{5,4},{6,5},{7,6},{8,7},{9,8},{10,9},{11,1... | collective-permute-start | bytes 110600 | tf_op jit(solution)/shard_map/ppermute | solution.py:544
  14.8 10.2 %copy-start.15 = (bf16[144,128]{1,0:T(8,128)(2,1)}, bf16[144,128]{1,0:T(8,128)(2,1)S(1)}, u32[]{:S(2)}) copy-start(bf16[144,128]{1,0:T(8,128)(2,1)S(1)} %collective-permute-done.prev_ref) | copy-start | bytes 110596
  14.8 10.2 %copy-start.17 = (bf16[144,128]{1,0:T(8,128)(2,1)}, bf16[144,128]{1,0:T(8,128)(2,1)S(1)}, u32[]{:S(2)}) copy-start(bf16[144,128]{1,0:T(8,128)(2,1)S(1)} %collective-permute-done.1.next_ref) | copy-start | bytes 110596
  14.8 14.3 %collective-permute-start.2 = (bf16[288,768]{1,0:T(8,128)(2,1)S(1)}, bf16[288,768]{1,0:T(8,128)(2,1)S(1)}, u32[]{:S(2)}, u32[]{:S(2)}) collective-permute-start(bf16[288,768]{1,0:T(8,128)(2,1)S(1)} %get-tuple-element.76), channel_id=1, source_target_pairs={{0,2},{1,3},{2,0},{3,1},{4,6},{5,7},{6,4},{7,5},{8,10},{9,11},{10,... | collective-permute-start | bytes 1327112 | tf_op jit(solution)/shard_map/ppermute | solution.py:562
  16.9 8.0 %copy-start.13 = (bf16[256,128]{1,0:T(8,128)(2,1)}, bf16[256,128]{1,0:T(8,128)(2,1)S(1)}, u32[]{:S(2)}) copy-start(bf16[256,128]{1,0:T(8,128)(2,1)S(1)} %get-tuple-element.70.x1_ref) | copy-start | bytes 196612
  16.9 12.2 %all-to-all-start = ((bf16[8,144,128]{2,1,0:T(8,128)(2,1)}), bf16[8,144,128]{2,1,0:T(8,128)(2,1)S(1)}, u32[]{:S(2)}, u32[]{:S(2)}) async-start(bf16[8,144,128]{2,1,0:T(8,128)(2,1)} %get-tuple-element.72), calls=%async_computation | async-start | bytes 589824 | tf_op jit(solution)/shard_map/all_to_all | solution.py:603
  20.3 8.8 %copy-start.27 = (bf16[192,768]{1,0:T(8,128)(2,1)S(1)}, bf16[192,768]{1,0:T(8,128)(2,1)}, u32[]{:S(2)}) copy-start(bf16[192,768]{1,0:T(8,128)(2,1)} %cond.1) | copy-start | bytes 884740
  20.3 8.8 %copy-start.28 = (bf16[128,768]{1,0:T(8,128)(2,1)S(1)}, bf16[128,768]{1,0:T(8,128)(2,1)}, u32[]{:S(2)}) copy-start(bf16[128,768]{1,0:T(8,128)(2,1)} %weight.1) | copy-start | bytes 589828
  29.1 4.8 %copy-start.31 = (bf16[2,128,16]{1,2,0:T(8,128)(2,1)S(1)}, bf16[2,128,16]{1,2,0:T(8,128)(2,1)}, u32[]{:S(2)}) copy-start(bf16[2,128,16]{1,2,0:T(8,128)(2,1)} %param.29) | copy-start | bytes 24580
  30.4 7.7 %copy-start.7 = (f32[24,768]{1,0:T(8,128)}, f32[24,768]{1,0:T(8,128)S(1)}, u32[]{:S(2)}) copy-start(f32[24,768]{1,0:T(8,128)S(1)} %get-tuple-element.80.act_ref) | copy-start | bytes 221188
  30.5 10.8 %collective-permute-start.3 = (bf16[96,768]{1,0:T(8,128)(2,1)S(1)}, bf16[96,768]{1,0:T(8,128)(2,1)S(1)}, u32[]{:S(2)}, u32[]{:S(2)}) collective-permute-start(bf16[96,768]{1,0:T(8,128)(2,1)S(1)} %get-tuple-element.82.here_ref), channel_id=1, source_target_pairs={{4,8},{7,9},{0,16},{3,17},{2,24},{1,25},{12,2},{15,3},{8,18},{9,19... | collective-permute-start | bytes 442376 | tf_op jit(solution)/shard_map/ppermute | solution.py:634
  37.4 22.7 %collective-permute-start.4 = (bf16[288,768]{1,0:T(8,128)(2,1)}, bf16[288,768]{1,0:T(8,128)(2,1)}, u32[]{:S(2)}, u32[]{:S(2)}) collective-permute-start(bf16[288,768]{1,0:T(8,128)(2,1)} %get-tuple-element.96), channel_id=1, source_target_pairs={{0,2},{1,3},{2,0},{3,1},{4,6},{5,7},{6,4},{7,5},{8,10},{9,11},{10,... | collective-permute-start | bytes 1327112 | tf_op jit(solution)/shard_map/ppermute | solution.py:657
  38.1 27.0 %collective-permute-start.6 = (bf16[576,768]{1,0:T(8,128)(2,1)}, bf16[576,768]{1,0:T(8,128)(2,1)}, u32[]{:S(2)}, u32[]{:S(2)}) collective-permute-start(bf16[576,768]{1,0:T(8,128)(2,1)} %get-tuple-element.98.refs_1_), channel_id=1, source_target_pairs={{0,1},{1,0},{2,3},{3,2},{4,5},{5,4},{6,7},{7,6},{8,9},{9,8},{10,11... | collective-permute-start | bytes 2654216 | tf_op jit(solution)/shard_map/ppermute | solution.py:659
  38.2 3.1 %copy-start.3 = (f32[96,16,128]{2,1,0:T(8,128)S(1)}, f32[96,16,128]{2,1,0:T(8,128)}, u32[]{:S(2)}) copy-start(f32[96,16,128]{2,1,0:T(8,128)} %get-tuple-element.83.low) | copy-start | bytes 2359300
  38.2 3.1 %copy-start.21 = (s32[768]{0:T(1024)S(1)}, s32[768]{0:T(1024)}, u32[]{:S(2)}) copy-start(s32[768]{0:T(1024)} %mask_ref.3) | copy-start | bytes 9220
  41.3 16.0 %copy-start = (bf16[2,768,768]{2,1,0:T(8,128)(2,1)S(1)}, bf16[2,768,768]{2,1,0:T(8,128)(2,1)}, u32[]{:S(2)}) copy-start(bf16[2,768,768]{2,1,0:T(8,128)(2,1)} %w_out.6) | copy-start | bytes 7077892
  45.5 11.8 %all-to-all-start.1 = ((bf16[8,24,896]{2,1,0:T(8,128)(2,1)}), bf16[8,24,896]{2,1,0:T(8,128)(2,1)S(1)}, u32[]{:S(2)}, u32[]{:S(2)}) async-start(bf16[8,24,896]{2,1,0:T(8,128)(2,1)} %bitcast.4), calls=%async_computation.1 | async-start | bytes 688128 | tf_op jit(solution)/shard_map/all_to_all | solution.py:679
  49.4 11.9 %collective-permute-start.7 = (bf16[288,768]{1,0:T(8,128)(2,1)}, bf16[288,768]{1,0:T(8,128)(2,1)}, u32[]{:S(2)}, u32[]{:S(2)}) collective-permute-start(bf16[288,768]{1,0:T(8,128)(2,1)} %copy-done.5), channel_id=1, source_target_pairs={{0,1},{1,0},{2,3},{3,2},{4,5},{5,4},{6,7},{7,6},{8,9},{9,8},{10,11... | collective-permute-start | bytes 1327112 | tf_op jit(solution)/shard_map/ppermute | solution.py:658
  59.0 6.1 %copy-start.6 = (bf16[288,768]{1,0:T(8,128)(2,1)S(1)}, bf16[288,768]{1,0:T(8,128)(2,1)}, u32[]{:S(2)}) copy-start(bf16[288,768]{1,0:T(8,128)(2,1)} %copy-done.5) | copy-start | bytes 1327108
  60.1 5.1 %collective-permute-start.8 = (bf16[288,768]{1,0:T(8,128)(2,1)}, bf16[288,768]{1,0:T(8,128)(2,1)S(1)}, u32[]{:S(2)}, u32[]{:S(2)}) collective-permute-start(bf16[288,768]{1,0:T(8,128)(2,1)} %collective-permute-done.4.refs_4_), channel_id=1, source_target_pairs={{0,1},{1,0},{2,3},{3,2},{4,5},{5,4},{6,7},{7,6},{8,9},{9,8},{10,11... | collective-permute-start | bytes 1327112 | tf_op jit(solution)/shard_map/ppermute | solution.py:686
  60.2 12.8 %collective-permute-start.10 = (bf16[288,768]{1,0:T(8,128)(2,1)S(1)}, bf16[288,768]{1,0:T(8,128)(2,1)}, u32[]{:S(2)}, u32[]{:S(2)}) collective-permute-start(bf16[288,768]{1,0:T(8,128)(2,1)S(1)} %copy-done.26), channel_id=1, source_target_pairs={{0,2},{1,3},{2,0},{3,1},{4,6},{5,7},{6,4},{7,5},{8,10},{9,11},{10,... | collective-permute-start | bytes 1327112 | tf_op jit(solution)/shard_map/ppermute | solution.py:682
  60.8 4.4 %collective-permute-start.5 = (f32[24,768]{1,0:T(8,128)S(1)}, f32[24,768]{1,0:T(8,128)S(1)}, u32[]{:S(2)}, u32[]{:S(2)}) collective-permute-start(f32[24,768]{1,0:T(8,128)S(1)} %shard_map.180.act_ref), channel_id=1, source_target_pairs={{0,4},{1,5},{2,6},{3,7},{4,0},{5,1},{6,2},{7,3},{8,12},{9,13},{10,... | collective-permute-start | bytes 221192 | tf_op jit(solution)/shard_map/ppermute | solution.py:684
  68.4 4.4 %collective-permute-start.9 = (bf16[48,768]{1,0:T(8,128)(2,1)S(1)}, bf16[48,768]{1,0:T(8,128)(2,1)S(1)}, u32[]{:S(2)}, u32[]{:S(2)}) collective-permute-start(bf16[48,768]{1,0:T(8,128)(2,1)S(1)} %get-tuple-element.102), channel_id=1, source_target_pairs={{0,4},{1,5},{2,6},{3,7},{4,0},{5,1},{6,2},{7,3},{8,12},{9,13},{10,... | collective-permute-start | bytes 221192 | tf_op jit(solution)/shard_map/ppermute | solution.py:690
  73.0 4.6 %collective-permute-start.11 = (bf16[48,768]{1,0:T(8,128)(2,1)S(1)}, bf16[48,768]{1,0:T(8,128)(2,1)S(1)}, u32[]{:S(2)}, u32[]{:S(2)}) collective-permute-start(bf16[48,768]{1,0:T(8,128)(2,1)S(1)} %get-tuple-element.105), channel_id=1, source_target_pairs={{0,3},{1,2},{2,1},{3,0},{4,7},{5,6},{6,5},{7,4},{8,11},{9,10},{10,... | collective-permute-start | bytes 221192 | tf_op jit(solution)/shard_map/ppermute | solution.py:472
  73.1 6.1 %collective-permute-start.12 = (bf16[48,768]{1,0:T(8,128)(2,1)S(1)}, bf16[48,768]{1,0:T(8,128)(2,1)S(1)}, u32[]{:S(2)}, u32[]{:S(2)}) collective-permute-start(bf16[48,768]{1,0:T(8,128)(2,1)S(1)} %get-tuple-element.105), channel_id=1, source_target_pairs={{0,2},{1,3},{2,0},{3,1},{4,6},{5,7},{6,4},{7,5},{8,10},{9,11},{10,... | collective-permute-start | bytes 221192 | tf_op jit(solution)/shard_map/ppermute | solution.py:472
  74.6 4.6 %collective-permute-start.13 = (bf16[48,768]{1,0:T(8,128)(2,1)S(1)}, bf16[48,768]{1,0:T(8,128)(2,1)S(1)}, u32[]{:S(2)}, u32[]{:S(2)}) collective-permute-start(bf16[48,768]{1,0:T(8,128)(2,1)S(1)} %get-tuple-element.105), channel_id=1, source_target_pairs={{0,1},{1,0},{2,3},{3,2},{4,5},{5,4},{6,7},{7,6},{8,9},{9,8},{10,11... | collective-permute-start | bytes 221192 | tf_op jit(solution)/shard_map/ppermute | solution.py:472
  79.3 9.8 %collective-permute-start.14 = (bf16[96,768]{1,0:T(8,128)(2,1)S(1)}, bf16[96,768]{1,0:T(8,128)(2,1)S(1)}, u32[]{:S(2)}, u32[]{:S(2)}) collective-permute-start(bf16[96,768]{1,0:T(8,128)(2,1)S(1)} %constant_dynamic-slice_fusion.here_ref), channel_id=1, source_target_pairs={{4,8},{7,9},{0,16},{3,17},{2,24},{1,25},{12,2},{15,3},{8,18},{9,19... | collective-permute-start | bytes 442376 | tf_op jit(solution)/shard_map/ppermute | solution.py:634
  81.9 7.2 %copy-start.2 = (f32[96,16,128]{2,1,0:T(8,128)S(1)}, f32[96,16,128]{2,1,0:T(8,128)}, u32[]{:S(2)}) copy-start(f32[96,16,128]{2,1,0:T(8,128)} %get-tuple-element.112.low) | copy-start | bytes 2359300
  84.4 21.6 %collective-permute-start.15 = (bf16[288,768]{1,0:T(8,128)(2,1)}, bf16[288,768]{1,0:T(8,128)(2,1)}, u32[]{:S(2)}, u32[]{:S(2)}) collective-permute-start(bf16[288,768]{1,0:T(8,128)(2,1)} %get-tuple-element.117), channel_id=1, source_target_pairs={{0,2},{1,3},{2,0},{3,1},{4,6},{5,7},{6,4},{7,5},{8,10},{9,11},{10,... | collective-permute-start | bytes 1327112 | tf_op jit(solution)/shard_map/ppermute | solution.py:663
  85.0 21.8 %collective-permute-start.17 = (bf16[576,768]{1,0:T(8,128)(2,1)}, bf16[576,768]{1,0:T(8,128)(2,1)}, u32[]{:S(2)}, u32[]{:S(2)}) collective-permute-start(bf16[576,768]{1,0:T(8,128)(2,1)} %get-tuple-element.119.refs_1_), channel_id=1, source_target_pairs={{0,1},{1,0},{2,3},{3,2},{4,5},{5,4},{6,7},{7,6},{8,9},{9,8},{10,11... | collective-permute-start | bytes 2654216 | tf_op jit(solution)/shard_map/ppermute | solution.py:659
  93.3 11.6 %all-to-all-start.2 = ((bf16[8,24,896]{2,1,0:T(8,128)(2,1)}), bf16[8,24,896]{2,1,0:T(8,128)(2,1)S(1)}, u32[]{:S(2)}, u32[]{:S(2)}) async-start(bf16[8,24,896]{2,1,0:T(8,128)(2,1)} %bitcast.14), calls=%async_computation.2 | async-start | bytes 688128 | tf_op jit(solution)/shard_map/all_to_all | solution.py:679
  97.1 9.7 %collective-permute-start.18 = (bf16[288,768]{1,0:T(8,128)(2,1)}, bf16[288,768]{1,0:T(8,128)(2,1)}, u32[]{:S(2)}, u32[]{:S(2)}) collective-permute-start(bf16[288,768]{1,0:T(8,128)(2,1)} %collective-permute-done.10.refs_3_), channel_id=1, source_target_pairs={{0,1},{1,0},{2,3},{3,2},{4,5},{5,4},{6,7},{7,6},{8,9},{9,8},{10,11... | collective-permute-start | bytes 1327112 | tf_op jit(solution)/shard_map/ppermute | solution.py:661
  106.0 12.5 %copy-start.9 = (bf16[768,128]{1,0:T(8,128)(2,1)S(1)}, bf16[768,128]{1,0:T(8,128)(2,1)}, u32[]{:S(2)}) copy-start(bf16[768,128]{1,0:T(8,128)(2,1)} %refs_1_.1) | copy-start | bytes 589828
  106.0 24.0 %copy-start.10 = (bf16[4,128,128]{2,1,0:T(8,128)(2,1)S(1)}, bf16[4,128,128]{2,1,0:T(8,128)(2,1)}, u32[]{:S(2)}) copy-start(bf16[4,128,128]{2,1,0:T(8,128)(2,1)} %w_in.7) | copy-start | bytes 393220
  106.0 23.9 %copy-start.14 = (bf16[256,128]{1,0:T(8,128)(2,1)S(1)}, bf16[256,128]{1,0:T(8,128)(2,1)}, u32[]{:S(2)}) copy-start(bf16[256,128]{1,0:T(8,128)(2,1)} %copy-done.13) | copy-start | bytes 196612
  106.0 23.9 %copy-start.16 = (bf16[144,128]{1,0:T(8,128)(2,1)S(1)}, bf16[144,128]{1,0:T(8,128)(2,1)}, u32[]{:S(2)}) copy-start(bf16[144,128]{1,0:T(8,128)(2,1)} %copy-done.15) | copy-start | bytes 110596
  106.0 23.9 %copy-start.18 = (bf16[144,128]{1,0:T(8,128)(2,1)S(1)}, bf16[144,128]{1,0:T(8,128)(2,1)}, u32[]{:S(2)}) copy-start(bf16[144,128]{1,0:T(8,128)(2,1)} %copy-done.17) | copy-start | bytes 110596
  106.0 23.9 %copy-start.19 = (bf16[128,128]{1,0:T(8,128)(2,1)S(1)}, bf16[128,128]{1,0:T(8,128)(2,1)}, u32[]{:S(2)}) copy-start(bf16[128,128]{1,0:T(8,128)(2,1)} %w_out.7) | copy-start | bytes 98308
  106.0 23.9 %copy-start.22 = (bf16[3,128]{1,0:T(4,128)(2,1)S(1)}, bf16[3,128]{1,0:T(4,128)(2,1)}, u32[]{:S(2)}) copy-start(bf16[3,128]{1,0:T(4,128)(2,1)} %pos.1) | copy-start | bytes 2308
  106.1 4.8 %collective-permute-start.19 = (bf16[288,768]{1,0:T(8,128)(2,1)}, bf16[288,768]{1,0:T(8,128)(2,1)S(1)}, u32[]{:S(2)}, u32[]{:S(2)}) collective-permute-start(bf16[288,768]{1,0:T(8,128)(2,1)} %collective-permute-done.15.refs_4_), channel_id=1, source_target_pairs={{0,1},{1,0},{2,3},{3,2},{4,5},{5,4},{6,7},{7,6},{8,9},{9,8},{10,11... | collective-permute-start | bytes 1327112 | tf_op jit(solution)/shard_map/ppermute | solution.py:686
  106.1 4.7 %collective-permute-start.16 = (f32[24,768]{1,0:T(8,128)S(1)}, f32[24,768]{1,0:T(8,128)S(1)}, u32[]{:S(2)}, u32[]{:S(2)}) collective-permute-start(f32[24,768]{1,0:T(8,128)S(1)} %shard_map.185.act_ref), channel_id=1, source_target_pairs={{0,4},{1,5},{2,6},{3,7},{4,0},{5,1},{6,2},{7,3},{8,12},{9,13},{10,... | collective-permute-start | bytes 221192 | tf_op jit(solution)/shard_map/ppermute | solution.py:684
  114.1 4.4 %collective-permute-start.20 = (bf16[48,768]{1,0:T(8,128)(2,1)S(1)}, bf16[48,768]{1,0:T(8,128)(2,1)S(1)}, u32[]{:S(2)}, u32[]{:S(2)}) collective-permute-start(bf16[48,768]{1,0:T(8,128)(2,1)S(1)} %get-tuple-element.123), channel_id=1, source_target_pairs={{0,4},{1,5},{2,6},{3,7},{4,0},{5,1},{6,2},{7,3},{8,12},{9,13},{10,... | collective-permute-start | bytes 221192 | tf_op jit(solution)/shard_map/ppermute | solution.py:690
  119.3 3.1 %collective-permute-start.21 = (bf16[48,128]{1,0:T(8,128)(2,1)S(1)}, bf16[48,128]{1,0:T(8,128)(2,1)S(1)}, u32[]{:S(2)}, u32[]{:S(2)}) collective-permute-start(bf16[48,128]{1,0:T(8,128)(2,1)S(1)} %get-tuple-element.124), channel_id=1, source_target_pairs={{0,3},{1,2},{2,1},{3,0},{4,7},{5,6},{6,5},{7,4},{8,11},{9,10},{10,... | collective-permute-start | bytes 36872 | tf_op jit(solution)/shard_map/ppermute | solution.py:472
  119.3 3.7 %collective-permute-start.22 = (bf16[48,128]{1,0:T(8,128)(2,1)S(1)}, bf16[48,128]{1,0:T(8,128)(2,1)S(1)}, u32[]{:S(2)}, u32[]{:S(2)}) collective-permute-start(bf16[48,128]{1,0:T(8,128)(2,1)S(1)} %get-tuple-element.124), channel_id=1, source_target_pairs={{0,2},{1,3},{2,0},{3,1},{4,6},{5,7},{6,4},{7,5},{8,10},{9,11},{10,... | collective-permute-start | bytes 36872 | tf_op jit(solution)/shard_map/ppermute | solution.py:472
  119.9 3.1 %collective-permute-start.23 = (bf16[48,128]{1,0:T(8,128)(2,1)S(1)}, bf16[48,128]{1,0:T(8,128)(2,1)S(1)}, u32[]{:S(2)}, u32[]{:S(2)}) collective-permute-start(bf16[48,128]{1,0:T(8,128)(2,1)S(1)} %get-tuple-element.124), channel_id=1, source_target_pairs={{0,1},{1,0},{2,3},{3,2},{4,5},{5,4},{6,7},{7,6},{8,9},{9,8},{10,11... | collective-permute-start | bytes 36872 | tf_op jit(solution)/shard_map/ppermute | solution.py:472
  123.1 6.9 %collective-permute-start.24 = (bf16[64,128]{1,0:T(8,128)(2,1)S(1)}, bf16[64,128]{1,0:T(8,128)(2,1)S(1)}, u32[]{:S(2)}, u32[]{:S(2)}) collective-permute-start(bf16[64,128]{1,0:T(8,128)(2,1)S(1)} %slice_select_fusion), channel_id=1, source_target_pairs={{7,8},{15,16},{23,24},{8,7},{16,15},{24,23}} | collective-permute-start | bytes 49160 | tf_op jit(solution)/shard_map/ppermute | solution.py:701
  (12 other events, 12.6 us)

commit v7 on v6

--- a/solution.py
+++ b/solution.py
@@ -652,13 +652,11 @@
         if not layer:
             high = list(bias_of(1, weights))
             high[0], late, *ready = lax.optimization_barrier(
-                (high[0], lower[0], across[0][0], *packed)
+                (high[0], lower[0], *packed)
             )
             across[0].append(lax.ppermute(late, everyone, neighbour))
-            beyond[0].append(lax.ppermute(ready[0], everyone, sibling))
-            beside = [lax.ppermute(part, everyone, sibling) for part in ready[1:]]
+            beside = [lax.ppermute(part, everyone, sibling) for part in ready]
         else:
-            beyond[1].append(lax.ppermute(ready, everyone, sibling))
             query, late = lax.optimization_barrier((query, lower[1]))
             across[1].append(lax.ppermute(late, everyone, neighbour))
         message = call(
@@ -682,15 +680,15 @@
             across[1].append(lax.ppermute(ready, everyone, neighbour))
         act = mix(layer, message, act, gate, tok_out, heads)
         came_rows = [lax.ppermute(act, everyone, shifts[d]) for d in range(1, peers)]
-        act, ready = lax.optimization_barrier((act, across[layer][1]))
-        beyond[layer].append(lax.ppermute(ready, everyone, sibling))
+        act, *ready = lax.optimization_barrier((act, *across[layer]))
+        beyond[layer] = [lax.ppermute(part, everyone, sibling) for part in ready]
         act, part = transition(
             act, came_rows, ([packed[layer]], [beside[layer]], across[layer], beyond[layer])
         )
         parts = [lax.ppermute(part, everyone, shifts[d]) for d in range(1, peers)]
         act, mine = close(own, act, parts, tok_atom if last else None)
         if not last:
-            mine, ready = lax.optimization_barrier((mine, across[1][0]))
+            mine, across[1][0] = lax.optimization_barrier((mine, across[1][0]))
         gathered = row_of(mine, own)
         if not last:
             xn = gathered

time: 134 us -> 133 us (level); the launches traced: 132 us -> 133 us
  blocking collectives: 0 us -> 24.3 us
  waiting for transfers between devices: 48.4 us -> 35.3 us
  starting transfers between devices: 37 us -> 27.1 us
    all_to_all x0 -> x2, blocking collectives: none -> 24.3 us  [body(): message = lax.all_to_all(message.reshape(ncol, own, -1), 'col', 0, 0)]
    all_to_all x2 -> x0, waiting for transfers between devices: 14.6 us -> none  [body(): message = lax.all_to_all(message.reshape(ncol, own, -1), 'col', 0, 0)]
    all_to_all x2 -> x0, starting transfers between devices: 7.75 us -> none  [body(): message = lax.all_to_all(message.reshape(ncol, own, -1), 'col', 0, 0)]
    unnamed x64 -> x56, local copies, waits for them, and re-layouts: 7.69 us -> 7.05 us
  transfers between devices with their start and end apart: 28 -> 26, of which waited for: 13 -> 11; matrix products, arithmetic and copies ran while one was open for 0% -> 0% of each run, Pallas kernels for 23% -> 22%
where the time goes in v7:
time: 133 us
  Pallas kernels  37.2 us (28%)
  waiting for transfers between devices  35.3 us (27%)
  starting transfers between devices  27.1 us (20%)
  blocking collectives  24.3 us (18%)
  local copies, waits for them, and re-layouts  7.07 us (5%)
    pallas_call x15, Pallas kernels, call(): pl.pallas_call(kernel, out_shape=outs, in_specs=[smem] * len(scalars) + [...  29.2 us
    all_to_all x2, blocking collectives, body(): message = lax.all_to_all(message.reshape(ncol, own, -1), 'col', 0, 0)  24.3 us
    pallas_call x2, Pallas kernels, bias_of(): pl.pallas_call(bias_kernel, grid=(half // step,), out_shape=[jax.ShapeDty...  8.03 us
    ppermute x2, waiting for transfers between devices, body(): parts = [lax.ppermute(part, everyone, shifts[d]) for d in range(1, peers)]  7.59 us
    ppermute x2, waiting for transfers between devices, body(): lax.ppermute(act, everyone, shifts[d])  7.58 us
    unnamed x56, local copies, waits for them, and re-layouts  7.05 us
    ppermute x6, waiting for transfers between devices, row_of(): lax.ppermute(mine, ('row', 'col'), [(i, i ^ flip) for i in range(nrow * n...  6.26 us
    ppermute x1, starting transfers between devices, body(): after = lax.ppermute(feat, everyone, [(b, a) for a, b in up])  5.44 us
  transfers between devices with their start and end apart: 26, of which 11 were waited for; matrix products, arithmetic and copies ran while one was open for 0% of the time, Pallas kernels for 22%

profile of v7, /device:TPU:24, one launch (start us, length us, event | category | flops | bytes accessed | tf_op | source)
XLA Modules:
  0.0 132.6 jit_solution(18151602516024377936)
XLA Ops:
  0.0 0.8 copy-done.14
  0.8 0.7 copy-done.17
  1.4 0.7 copy-done.18
  2.6 1.9 %collective-permute-start = (bf16[144,128]{1,0:T(8,128)(2,1)S(1)}, bf16[144,128]{1,0:T(8,128)(2,1)S(1)}, u32[]{:S(2)}, u32[]{:S(2)}) collective-permute-start(bf16[144,128]{1,0:T(8,128)(2,1)S(1)} %shard_map.172.own_ref), channel_id=1, source_target_pairs={{0,1},{1,2},{2,3},{3,4},{4,5},{5,6},{6,7},{7,8},{8,9},{9,10},{10,1... | collective-permute-start | bytes 110600 | tf_op jit(solution)/shard_map/ppermute | solution.py:543
  4.6 5.4 %collective-permute-start.1 = (bf16[144,128]{1,0:T(8,128)(2,1)S(1)}, bf16[144,128]{1,0:T(8,128)(2,1)S(1)}, u32[]{:S(2)}, u32[]{:S(2)}) collective-permute-start(bf16[144,128]{1,0:T(8,128)(2,1)S(1)} %shard_map.172.own_ref), channel_id=1, source_target_pairs={{1,0},{2,1},{3,2},{4,3},{5,4},{6,5},{7,6},{8,7},{9,8},{10,9},{11,1... | collective-permute-start | bytes 110600 | tf_op jit(solution)/shard_map/ppermute | solution.py:544
  10.0 1.3 copy-done.1
  11.3 1.1 copy-done.6
  12.4 1.4 %shard_map.173 = (bf16[576,768]{1,0:T(8,128)(2,1)}, bf16[288,768]{1,0:T(8,128)(2,1)S(1)}, bf16[288,768]{1,0:T(8,128)(2,1)}, bf16[576,768]{1,0:T(8,128)(2,1)S(1)}...) custom-call(bf16[2,2,192,768]{3,2,1,0:T(8,128)(2,1)S(1)} %bitcast.37, bf16[2,192,768]{2,1,0:T(8,128)(2,1)S(1)} %copy-done.6), custom_call_target="tpu_custom_call" | custom-call | bytes 3538944 | tf_op jit(solution)/shard_map/pallas_call | solution.py:26
  13.7 0.8 copy-done.19
  14.5 0.8 copy-done.21
  15.4 2.0 %shard_map.174 = (bf16[256,128]{1,0:T(8,128)(2,1)S(1)}, bf16[8,144,128]{2,1,0:T(8,128)(2,1)}) custom-call(bf16[144,128]{1,0:T(8,128)(2,1)S(1)} %shard_map.172.own_ref, bf16[144,128]{1,0:T(8,128)(2,1)S(1)} %collective-permute-done.prev_ref, bf16[144,128]{1,0:T(8,128)(2,1)S(1)} %collective-permute-done.1.next_ref, bf16[4,128,128]{2,1,0:T(8,128)(2,1)S(1)} %copy-done.25, ...), custom_call_target="tpu_custom_call" | custom-call | flops 100000000 | bytes 1000000 | tf_op jit(solution)/shard_map/pallas_call | solution.py:26
  17.4 3.4 %all-to-all-start = ((bf16[8,144,128]{2,1,0:T(8,128)(2,1)}), bf16[8,144,128]{2,1,0:T(8,128)(2,1)S(1)}, u32[]{:S(2)}, u32[]{:S(2)}) async-start(bf16[8,144,128]{2,1,0:T(8,128)(2,1)} %get-tuple-element.73), calls=%async_computation | async-start | bytes 589824 | tf_op jit(solution)/shard_map/all_to_all | solution.py:603
  20.9 4.6 %shard_map.175 = (f32[96,16,128]{2,1,0:T(8,128)}, f32[96,16,128]{2,1,0:T(8,128)}) custom-call(bf16[192,96,128]{2,1,0:T(8,128)(2,1)} %pair_ref.3, bf16[32,128]{1,0:T(8,128)(2,1)} %bitcast.41), custom_call_target="tpu_custom_call" | custom-call | flops 2000000000 | bytes 4000000 | tf_op jit(solution)/shard_map/pallas_call | solution.py:583
  25.5 4.1 %all-to-all-done.both_ref = bf16[8,144,128]{2,1,0:T(8,128)(2,1)S(1)} async-done(((bf16[8,144,128]{2,1,0:T(8,128)(2,1)}), bf16[8,144,128]{2,1,0:T(8,128)(2,1)S(1)}, u32[]{:S(2)}, u32[]{:S(2)}) %all-to-all-start) | async-done | bytes 294944 | tf_op jit(solution)/shard_map/all_to_all | solution.py:603
  29.6 1.3 shard_map.176
  30.9 3.2 %collective-permute-start.3 = (bf16[96,768]{1,0:T(8,128)(2,1)S(1)}, bf16[96,768]{1,0:T(8,128)(2,1)S(1)}, u32[]{:S(2)}, u32[]{:S(2)}) collective-permute-start(bf16[96,768]{1,0:T(8,128)(2,1)S(1)} %get-tuple-element.83.here_ref), channel_id=1, source_target_pairs={{4,8},{7,9},{0,16},{3,17},{2,24},{1,25},{12,2},{15,3},{8,18},{9,19... | collective-permute-start | bytes 442376 | tf_op jit(solution)/shard_map/ppermute | solution.py:634
  34.1 3.4 %shard_map.178 = (f32[96,16,128]{2,1,0:T(8,128)S(1)}, f32[96,16,128]{2,1,0:T(8,128)S(1)}) custom-call(bf16[192,96,128]{2,1,0:T(8,128)(2,1)} %pair_ref.3, bf16[32,128]{1,0:T(8,128)(2,1)S(1)} %bitcast.42), custom_call_target="tpu_custom_call" | custom-call | flops 2000000000 | bytes 4000000 | tf_op jit(solution)/shard_map/pallas_call | solution.py:583
  37.6 0.9 copy-done.3
  38.5 0.7 collective-permute-start.4
  39.2 2.4 %shard_map.177 = (bf16[192,768]{1,0:T(8,128)(2,1)S(1)}, bf16[768,768]{1,0:T(8,128)(2,1)S(1)}, bf16[768,768]{1,0:T(8,128)(2,1)S(1)}, f32[24,768]{1,0:T(8,128)S(1)}) custom-call(bf16[192,768]{1,0:T(8,128)(2,1)S(1)} %get-tuple-element.80.xn_ref, f32[24,768]{1,0:T(8,128)S(1)} %get-tuple-element.81.act_ref, bf16[2,4,768,768]{3,2,1,0:T(8,128)(2,1)} %w_in.6), custom_call_target="tpu_custom_call" | custom-call | flops 226492416 | bytes 4718592 | tf_op jit(solution)/shard_map/pallas_call | solution.py:26
  41.7 3.5 %shard_map.179 = bf16[192,896]{1,0:T(8,128)(2,1)S(1)} custom-call(s32[768]{0:T(1024)S(1)} %copy-done.15, bf16[192,768]{1,0:T(8,128)(2,1)S(1)} %get-tuple-element.82.query, bf16[96,768]{1,0:T(8,128)(2,1)S(1)} %get-tuple-element.83.here_ref, bf16[96,768]{1,0:T(8,128)(2,1)S(1)} %collective-permute-done.3.came_ref, f32[96,16,128]{2,1,0:T(8,128)S(1)} %copy-done.5, ...), custom_call_target="tpu_custom_call" | custom-call | flops 1000000000 | bytes 8000000 | tf_op jit(solution)/shard_map/pallas_call | solution.py:26
  45.2 11.7 %all_to_all.15.message = bf16[8,24,896]{2,1,0:T(8,128)(2,1)S(1)} all-to-all(bf16[8,24,896]{2,1,0:T(8,128)(2,1)S(1)} %bitcast.35), channel_id=1, replica_groups=mesh['row'=4,'col'=8] {'col'}, dimensions={0} | all-to-all | bytes 688128 | tf_op jit(solution)/shard_map/all_to_all | solution.py:677
  56.9 1.0 shard_map.180.act_ref
  59.6 3.8 %collective-permute-done.5.refs_0_ = f32[24,768]{1,0:T(8,128)S(1)} collective-permute-done((f32[24,768]{1,0:T(8,128)S(1)}, f32[24,768]{1,0:T(8,128)S(1)}, u32[]{:S(2)}, u32[]{:S(2)}) %collective-permute-start.5) | collective-permute-done | bytes 73760 | tf_op jit(solution)/shard_map/ppermute | solution.py:682
  63.5 3.5 %shard_map.181 = (f32[48,768]{1,0:T(8,128)S(1)}, bf16[48,768]{1,0:T(8,128)(2,1)S(1)}) custom-call(f32[24,768]{1,0:T(8,128)S(1)} %shard_map.180.act_ref, f32[24,768]{1,0:T(8,128)S(1)} %collective-permute-done.5.refs_0_, bf16[576,768]{1,0:T(8,128)(2,1)} %get-tuple-element.99.refs_1_, bf16[576,768]{1,0:T(8,128)(2,1)S(1)} %collective-permute-done.6.refs_2_, ...), custom_call_target="tpu_custom_call" | custom-call | flops 169869312 | bytes 3538944 | tf_op jit(solution)/shard_map/pallas_call | solution.py:26
  67.0 0.6 collective-permute-start.9
  67.6 3.8 %collective-permute-done.9.refs_0_ = bf16[48,768]{1,0:T(8,128)(2,1)S(1)} collective-permute-done((bf16[48,768]{1,0:T(8,128)(2,1)S(1)}, bf16[48,768]{1,0:T(8,128)(2,1)S(1)}, u32[]{:S(2)}, u32[]{:S(2)}) %collective-permute-start.9) | collective-permute-done | bytes 73760 | tf_op jit(solution)/shard_map/ppermute | solution.py:688
  71.7 1.5 %collective-permute-start.12 = (bf16[48,768]{1,0:T(8,128)(2,1)S(1)}, bf16[48,768]{1,0:T(8,128)(2,1)}, u32[]{:S(2)}, u32[]{:S(2)}) collective-permute-start(bf16[48,768]{1,0:T(8,128)(2,1)S(1)} %get-tuple-element.106), channel_id=1, source_target_pairs={{0,2},{1,3},{2,0},{3,1},{4,6},{5,7},{6,4},{7,5},{8,10},{9,11},{10,... | collective-permute-start | bytes 221192 | tf_op jit(solution)/shard_map/ppermute | solution.py:472
  73.6 2.8 %collective-permute-done.11 = bf16[48,768]{1,0:T(8,128)(2,1)} collective-permute-done((bf16[48,768]{1,0:T(8,128)(2,1)S(1)}, bf16[48,768]{1,0:T(8,128)(2,1)}, u32[]{:S(2)}, u32[]{:S(2)}) %collective-permute-start.11) | collective-permute-done | bytes 73760 | tf_op jit(solution)/shard_map/ppermute | solution.py:472
  76.3 1.6 %collective-permute-done.12 = bf16[48,768]{1,0:T(8,128)(2,1)} collective-permute-done((bf16[48,768]{1,0:T(8,128)(2,1)S(1)}, bf16[48,768]{1,0:T(8,128)(2,1)}, u32[]{:S(2)}, u32[]{:S(2)}) %collective-permute-start.12) | collective-permute-done | bytes 73760 | tf_op jit(solution)/shard_map/ppermute | solution.py:472
  78.0 1.0 select_select_fusion.3
  79.0 2.1 %collective-permute-start.14 = (bf16[96,768]{1,0:T(8,128)(2,1)S(1)}, bf16[96,768]{1,0:T(8,128)(2,1)S(1)}, u32[]{:S(2)}, u32[]{:S(2)}) collective-permute-start(bf16[96,768]{1,0:T(8,128)(2,1)S(1)} %constant_dynamic-slice_fusion.here_ref), channel_id=1, source_target_pairs={{4,8},{7,9},{0,16},{3,17},{2,24},{1,25},{12,2},{15,3},{8,18},{9,19... | collective-permute-start | bytes 442376 | tf_op jit(solution)/shard_map/ppermute | solution.py:634
  81.2 2.5 %shard_map.183 = (bf16[192,768]{1,0:T(8,128)(2,1)S(1)}, bf16[768,768]{1,0:T(8,128)(2,1)S(1)}, bf16[768,768]{1,0:T(8,128)(2,1)S(1)}, f32[24,768]{1,0:T(8,128)S(1)}) custom-call(bf16[192,768]{1,0:T(8,128)(2,1)S(1)} %bitcast.34, f32[24,768]{1,0:T(8,128)S(1)} %get-tuple-element.108.act_ref, bf16[2,4,768,768]{3,2,1,0:T(8,128)(2,1)} %w_in.6), custom_call_target="tpu_custom_call" | custom-call | flops 226492416 | bytes 4718592 | tf_op jit(solution)/shard_map/pallas_call | solution.py:26
  84.3 4.8 %collective-permute-done.14.came_ref = bf16[96,768]{1,0:T(8,128)(2,1)S(1)} collective-permute-done((bf16[96,768]{1,0:T(8,128)(2,1)S(1)}, bf16[96,768]{1,0:T(8,128)(2,1)S(1)}, u32[]{:S(2)}, u32[]{:S(2)}) %collective-permute-start.14) | collective-permute-done | bytes 147488 | tf_op jit(solution)/shard_map/ppermute | solution.py:634
  89.0 3.5 %shard_map.184 = bf16[192,896]{1,0:T(8,128)(2,1)S(1)} custom-call(s32[768]{0:T(1024)S(1)} %copy-done.15, bf16[192,768]{1,0:T(8,128)(2,1)S(1)} %get-tuple-element.111.query, bf16[96,768]{1,0:T(8,128)(2,1)S(1)} %constant_dynamic-slice_fusion.here_ref, bf16[96,768]{1,0:T(8,128)(2,1)S(1)} %collective-permute-done.14.came_ref, f32[96,16,128]{2,1,0:T(8,128)S(1)} %copy-done.2, ...), custom_call_target="tpu_custom_call" | custom-call | flops 1000000000 | bytes 8000000 | tf_op jit(solution)/shard_map/pallas_call | solution.py:26
  92.5 12.6 %all_to_all.16.message = bf16[8,24,896]{2,1,0:T(8,128)(2,1)S(1)} all-to-all(bf16[8,24,896]{2,1,0:T(8,128)(2,1)S(1)} %bitcast.36), channel_id=1, replica_groups=mesh['row'=4,'col'=8] {'col'}, dimensions={0} | all-to-all | bytes 688128 | tf_op jit(solution)/shard_map/all_to_all | solution.py:677
  105.1 1.0 shard_map.185.act_ref
  107.4 3.8 %collective-permute-done.16.refs_0_ = f32[24,768]{1,0:T(8,128)S(1)} collective-permute-done((f32[24,768]{1,0:T(8,128)S(1)}, f32[24,768]{1,0:T(8,128)S(1)}, u32[]{:S(2)}, u32[]{:S(2)}) %collective-permute-start.16) | collective-permute-done | bytes 73760 | tf_op jit(solution)/shard_map/ppermute | solution.py:682
  111.2 3.5 %shard_map.186 = (f32[48,768]{1,0:T(8,128)S(1)}, bf16[48,768]{1,0:T(8,128)(2,1)S(1)}) custom-call(f32[24,768]{1,0:T(8,128)S(1)} %shard_map.185.act_ref, f32[24,768]{1,0:T(8,128)S(1)} %collective-permute-done.16.refs_0_, bf16[576,768]{1,0:T(8,128)(2,1)S(1)} %get-tuple-element.121.refs_1_, bf16[576,768]{1,0:T(8,128)(2,1)S(1)} %collective-permute-done.17.refs_2_, ...), custom_call_target="tpu_custom_call" | custom-call | flops 169869312 | bytes 3538944 | tf_op jit(solution)/shard_map/pallas_call | solution.py:26
  114.7 0.6 collective-permute-start.20
  115.3 3.8 %collective-permute-done.20.refs_0_ = bf16[48,768]{1,0:T(8,128)(2,1)S(1)} collective-permute-done((bf16[48,768]{1,0:T(8,128)(2,1)S(1)}, bf16[48,768]{1,0:T(8,128)(2,1)S(1)}, u32[]{:S(2)}, u32[]{:S(2)}) %collective-permute-start.20) | collective-permute-done | bytes 73760 | tf_op jit(solution)/shard_map/ppermute | solution.py:688
  119.1 0.8 shard_map.187
  120.5 1.3 collective-permute-start.23
  121.8 1.3 collective-permute-done.21
  123.0 0.6 collective-permute-done.22
  123.7 1.9 %collective-permute-start.24 = (bf16[64,128]{1,0:T(8,128)(2,1)S(1)}, bf16[64,128]{1,0:T(8,128)(2,1)S(1)}, u32[]{:S(2)}, u32[]{:S(2)}) collective-permute-start(bf16[64,128]{1,0:T(8,128)(2,1)S(1)} %slice_select_fusion), channel_id=1, source_target_pairs={{7,8},{15,16},{23,24},{8,7},{16,15},{24,23}} | collective-permute-start | bytes 49160 | tf_op jit(solution)/shard_map/ppermute | solution.py:699
  125.6 4.9 %collective-permute-done.24.edge_ref = bf16[64,128]{1,0:T(8,128)(2,1)S(1)} collective-permute-done((bf16[64,128]{1,0:T(8,128)(2,1)S(1)}, bf16[64,128]{1,0:T(8,128)(2,1)S(1)}, u32[]{:S(2)}, u32[]{:S(2)}) %collective-permute-start.24) | collective-permute-done | bytes 16416 | tf_op jit(solution)/shard_map/ppermute | solution.py:699
  130.6 2.0 %shard_map.188 = f32[3,128]{1,0:T(4,128)} custom-call(bf16[256,128]{1,0:T(8,128)(2,1)S(1)} %get-tuple-element.71.x1_ref, bf16[144,128]{1,0:T(8,128)(2,1)S(1)} %shard_map.172.own_ref, bf16[144,128]{1,0:T(8,128)(2,1)S(1)} %collective-permute-done.prev_ref, bf16[144,128]{1,0:T(8,128)(2,1)S(1)} %copy-done.12, bf16[192,128]{1,0:T(8,128)(2,1)S(1)} %bitcast.39, ...), custom_call_target="tpu_custom_call" | custom-call | flops 100000000 | bytes 1000000 | tf_op jit(solution)/shard_map/pallas_call | solution.py:26
  (85 shorter events, 5.5 us)
Async XLA Ops:
  2.1 13.3 %copy-start.26 = (bf16[128,128]{1,0:T(8,128)(2,1)S(1)}, bf16[128,128]{1,0:T(8,128)(2,1)}, u32[]{:S(2)}) copy-start(bf16[128,128]{1,0:T(8,128)(2,1)} %w_out.4) | copy-start | bytes 98308
  2.6 12.6 %collective-permute-start = (bf16[144,128]{1,0:T(8,128)(2,1)S(1)}, bf16[144,128]{1,0:T(8,128)(2,1)S(1)}, u32[]{:S(2)}, u32[]{:S(2)}) collective-permute-start(bf16[144,128]{1,0:T(8,128)(2,1)S(1)} %shard_map.172.own_ref), channel_id=1, source_target_pairs={{0,1},{1,2},{2,3},{3,4},{4,5},{5,6},{6,7},{7,8},{8,9},{9,10},{10,1... | collective-permute-start | bytes 110600 | tf_op jit(solution)/shard_map/ppermute | solution.py:543
  4.6 10.7 %collective-permute-start.1 = (bf16[144,128]{1,0:T(8,128)(2,1)S(1)}, bf16[144,128]{1,0:T(8,128)(2,1)S(1)}, u32[]{:S(2)}, u32[]{:S(2)}) collective-permute-start(bf16[144,128]{1,0:T(8,128)(2,1)S(1)} %shard_map.172.own_ref), channel_id=1, source_target_pairs={{1,0},{2,1},{3,2},{4,3},{5,4},{6,5},{7,6},{8,7},{9,8},{10,9},{11,1... | collective-permute-start | bytes 110600 | tf_op jit(solution)/shard_map/ppermute | solution.py:544
  10.0 1.3 copy-start.1
  11.3 1.1 copy-start.6
  12.4 3.0 %copy-start.25 = (bf16[4,128,128]{2,1,0:T(8,128)(2,1)S(1)}, bf16[4,128,128]{2,1,0:T(8,128)(2,1)}, u32[]{:S(2)}) copy-start(bf16[4,128,128]{2,1,0:T(8,128)(2,1)} %w_in.4) | copy-start | bytes 393220
  15.3 10.2 %copy-start.11 = (bf16[144,128]{1,0:T(8,128)(2,1)}, bf16[144,128]{1,0:T(8,128)(2,1)S(1)}, u32[]{:S(2)}) copy-start(bf16[144,128]{1,0:T(8,128)(2,1)S(1)} %collective-permute-done.1.next_ref) | copy-start | bytes 110596
  15.3 14.3 %collective-permute-start.2 = (bf16[288,768]{1,0:T(8,128)(2,1)S(1)}, bf16[288,768]{1,0:T(8,128)(2,1)S(1)}, u32[]{:S(2)}, u32[]{:S(2)}) collective-permute-start(bf16[288,768]{1,0:T(8,128)(2,1)S(1)} %get-tuple-element.77), channel_id=1, source_target_pairs={{0,2},{1,3},{2,0},{3,1},{4,6},{5,7},{6,4},{7,5},{8,10},{9,11},{10,... | collective-permute-start | bytes 1327112 | tf_op jit(solution)/shard_map/ppermute | solution.py:562
  17.4 12.2 %all-to-all-start = ((bf16[8,144,128]{2,1,0:T(8,128)(2,1)}), bf16[8,144,128]{2,1,0:T(8,128)(2,1)S(1)}, u32[]{:S(2)}, u32[]{:S(2)}) async-start(bf16[8,144,128]{2,1,0:T(8,128)(2,1)} %get-tuple-element.73), calls=%async_computation | async-start | bytes 589824 | tf_op jit(solution)/shard_map/all_to_all | solution.py:603
  20.8 8.8 %copy-start.23 = (bf16[192,768]{1,0:T(8,128)(2,1)S(1)}, bf16[192,768]{1,0:T(8,128)(2,1)}, u32[]{:S(2)}) copy-start(bf16[192,768]{1,0:T(8,128)(2,1)} %cond.1) | copy-start | bytes 884740
  20.9 8.8 %copy-start.24 = (bf16[128,768]{1,0:T(8,128)(2,1)S(1)}, bf16[128,768]{1,0:T(8,128)(2,1)}, u32[]{:S(2)}) copy-start(bf16[128,768]{1,0:T(8,128)(2,1)} %weight.1) | copy-start | bytes 589828
  29.6 1.3 copy-start.7
  29.6 4.5 %copy-start.27 = (bf16[2,128,16]{1,2,0:T(8,128)(2,1)S(1)}, bf16[2,128,16]{1,2,0:T(8,128)(2,1)}, u32[]{:S(2)}) copy-start(bf16[2,128,16]{1,2,0:T(8,128)(2,1)} %param.29) | copy-start | bytes 24580
  30.9 10.7 %collective-permute-start.3 = (bf16[96,768]{1,0:T(8,128)(2,1)S(1)}, bf16[96,768]{1,0:T(8,128)(2,1)S(1)}, u32[]{:S(2)}, u32[]{:S(2)}) collective-permute-start(bf16[96,768]{1,0:T(8,128)(2,1)S(1)} %get-tuple-element.83.here_ref), channel_id=1, source_target_pairs={{4,8},{7,9},{0,16},{3,17},{2,24},{1,25},{12,2},{15,3},{8,18},{9,19... | collective-permute-start | bytes 442376 | tf_op jit(solution)/shard_map/ppermute | solution.py:634
  38.5 19.4 %collective-permute-start.4 = (bf16[288,768]{1,0:T(8,128)(2,1)}, bf16[288,768]{1,0:T(8,128)(2,1)S(1)}, u32[]{:S(2)}, u32[]{:S(2)}) collective-permute-start(bf16[288,768]{1,0:T(8,128)(2,1)} %get-tuple-element.97), channel_id=1, source_target_pairs={{0,2},{1,3},{2,0},{3,1},{4,6},{5,7},{6,4},{7,5},{8,10},{9,11},{10,... | collective-permute-start | bytes 1327112 | tf_op jit(solution)/shard_map/ppermute | solution.py:657
  39.2 24.3 %collective-permute-start.6 = (bf16[576,768]{1,0:T(8,128)(2,1)}, bf16[576,768]{1,0:T(8,128)(2,1)S(1)}, u32[]{:S(2)}, u32[]{:S(2)}) collective-permute-start(bf16[576,768]{1,0:T(8,128)(2,1)} %get-tuple-element.99.refs_1_), channel_id=1, source_target_pairs={{0,1},{1,0},{2,3},{3,2},{4,5},{5,4},{6,7},{7,6},{8,9},{9,8},{10,11... | collective-permute-start | bytes 2654216 | tf_op jit(solution)/shard_map/ppermute | solution.py:658
  39.2 2.6 %copy-start.5 = (f32[96,16,128]{2,1,0:T(8,128)S(1)}, f32[96,16,128]{2,1,0:T(8,128)}, u32[]{:S(2)}) copy-start(f32[96,16,128]{2,1,0:T(8,128)} %get-tuple-element.84.low) | copy-start | bytes 2359300
  39.2 2.6 %copy-start.15 = (s32[768]{0:T(1024)S(1)}, s32[768]{0:T(1024)}, u32[]{:S(2)}) copy-start(s32[768]{0:T(1024)} %mask_ref.3) | copy-start | bytes 9220
  41.7 15.2 %copy-start = (bf16[2,768,768]{2,1,0:T(8,128)(2,1)S(1)}, bf16[2,768,768]{2,1,0:T(8,128)(2,1)}, u32[]{:S(2)}) copy-start(bf16[2,768,768]{2,1,0:T(8,128)(2,1)} %w_out.6) | copy-start | bytes 7077892
  56.9 1.1 copy-start.8
  56.9 1.6 %copy-start.22 = (bf16[288,768]{1,0:T(8,128)(2,1)S(1)}, bf16[288,768]{1,0:T(8,128)(2,1)}, u32[]{:S(2)}) copy-start(bf16[288,768]{1,0:T(8,128)(2,1)} %copy-done.21) | copy-start | bytes 1327108
  57.9 5.5 %collective-permute-start.7 = (bf16[288,768]{1,0:T(8,128)(2,1)S(1)}, bf16[288,768]{1,0:T(8,128)(2,1)S(1)}, u32[]{:S(2)}, u32[]{:S(2)}) collective-permute-start(bf16[288,768]{1,0:T(8,128)(2,1)S(1)} %copy-done.8), channel_id=1, source_target_pairs={{0,1},{1,0},{2,3},{3,2},{4,5},{5,4},{6,7},{7,6},{8,9},{9,8},{10,11... | collective-permute-start | bytes 1327112 | tf_op jit(solution)/shard_map/ppermute | solution.py:684
  58.0 5.4 %collective-permute-start.8 = (bf16[288,768]{1,0:T(8,128)(2,1)S(1)}, bf16[288,768]{1,0:T(8,128)(2,1)S(1)}, u32[]{:S(2)}, u32[]{:S(2)}) collective-permute-start(bf16[288,768]{1,0:T(8,128)(2,1)S(1)} %collective-permute-done.4.refs_4_), channel_id=1, source_target_pairs={{0,1},{1,0},{2,3},{3,2},{4,5},{5,4},{6,7},{7,6},{8,9},{9,8},{10,11... | collective-permute-start | bytes 1327112 | tf_op jit(solution)/shard_map/ppermute | solution.py:684
  58.5 13.1 %collective-permute-start.10 = (bf16[288,768]{1,0:T(8,128)(2,1)S(1)}, bf16[288,768]{1,0:T(8,128)(2,1)}, u32[]{:S(2)}, u32[]{:S(2)}) collective-permute-start(bf16[288,768]{1,0:T(8,128)(2,1)S(1)} %copy-done.22), channel_id=1, source_target_pairs={{0,2},{1,3},{2,0},{3,1},{4,6},{5,7},{6,4},{7,5},{8,10},{9,11},{10,... | collective-permute-start | bytes 1327112 | tf_op jit(solution)/shard_map/ppermute | solution.py:680
  59.1 4.4 %collective-permute-start.5 = (f32[24,768]{1,0:T(8,128)S(1)}, f32[24,768]{1,0:T(8,128)S(1)}, u32[]{:S(2)}, u32[]{:S(2)}) collective-permute-start(f32[24,768]{1,0:T(8,128)S(1)} %shard_map.180.act_ref), channel_id=1, source_target_pairs={{0,4},{1,5},{2,6},{3,7},{4,0},{5,1},{6,2},{7,3},{8,12},{9,13},{10,... | collective-permute-start | bytes 221192 | tf_op jit(solution)/shard_map/ppermute | solution.py:682
  67.0 4.4 %collective-permute-start.9 = (bf16[48,768]{1,0:T(8,128)(2,1)S(1)}, bf16[48,768]{1,0:T(8,128)(2,1)S(1)}, u32[]{:S(2)}, u32[]{:S(2)}) collective-permute-start(bf16[48,768]{1,0:T(8,128)(2,1)S(1)} %get-tuple-element.103), channel_id=1, source_target_pairs={{0,4},{1,5},{2,6},{3,7},{4,0},{5,1},{6,2},{7,3},{8,12},{9,13},{10,... | collective-permute-start | bytes 221192 | tf_op jit(solution)/shard_map/ppermute | solution.py:688
  71.6 4.7 %collective-permute-start.11 = (bf16[48,768]{1,0:T(8,128)(2,1)S(1)}, bf16[48,768]{1,0:T(8,128)(2,1)}, u32[]{:S(2)}, u32[]{:S(2)}) collective-permute-start(bf16[48,768]{1,0:T(8,128)(2,1)S(1)} %get-tuple-element.106), channel_id=1, source_target_pairs={{0,3},{1,2},{2,1},{3,0},{4,7},{5,6},{6,5},{7,4},{8,11},{9,10},{10,... | collective-permute-start | bytes 221192 | tf_op jit(solution)/shard_map/ppermute | solution.py:472
  71.7 6.2 %collective-permute-start.12 = (bf16[48,768]{1,0:T(8,128)(2,1)S(1)}, bf16[48,768]{1,0:T(8,128)(2,1)}, u32[]{:S(2)}, u32[]{:S(2)}) collective-permute-start(bf16[48,768]{1,0:T(8,128)(2,1)S(1)} %get-tuple-element.106), channel_id=1, source_target_pairs={{0,2},{1,3},{2,0},{3,1},{4,6},{5,7},{6,4},{7,5},{8,10},{9,11},{10,... | collective-permute-start | bytes 221192 | tf_op jit(solution)/shard_map/ppermute | solution.py:472
  73.2 4.7 %collective-permute-start.13 = (bf16[48,768]{1,0:T(8,128)(2,1)S(1)}, bf16[48,768]{1,0:T(8,128)(2,1)}, u32[]{:S(2)}, u32[]{:S(2)}) collective-permute-start(bf16[48,768]{1,0:T(8,128)(2,1)S(1)} %get-tuple-element.106), channel_id=1, source_target_pairs={{0,1},{1,0},{2,3},{3,2},{4,5},{5,4},{6,7},{7,6},{8,9},{9,8},{10,11... | collective-permute-start | bytes 221192 | tf_op jit(solution)/shard_map/ppermute | solution.py:472
  79.0 10.0 %collective-permute-start.14 = (bf16[96,768]{1,0:T(8,128)(2,1)S(1)}, bf16[96,768]{1,0:T(8,128)(2,1)S(1)}, u32[]{:S(2)}, u32[]{:S(2)}) collective-permute-start(bf16[96,768]{1,0:T(8,128)(2,1)S(1)} %constant_dynamic-slice_fusion.here_ref), channel_id=1, source_target_pairs={{4,8},{7,9},{0,16},{3,17},{2,24},{1,25},{12,2},{15,3},{8,18},{9,19... | collective-permute-start | bytes 442376 | tf_op jit(solution)/shard_map/ppermute | solution.py:634
  81.1 2.6 %copy-start.20 = (bf16[288,768]{1,0:T(8,128)(2,1)S(1)}, bf16[288,768]{1,0:T(8,128)(2,1)}, u32[]{:S(2)}) copy-start(bf16[288,768]{1,0:T(8,128)(2,1)} %copy-done.19) | copy-start | bytes 1327108
  81.1 7.9 %copy-start.2 = (f32[96,16,128]{2,1,0:T(8,128)S(1)}, f32[96,16,128]{2,1,0:T(8,128)}, u32[]{:S(2)}) copy-start(f32[96,16,128]{2,1,0:T(8,128)} %get-tuple-element.113.low) | copy-start | bytes 2359300
  81.2 7.9 %copy-start.4 = (f32[96,16,128]{2,1,0:T(8,128)S(1)}, f32[96,16,128]{2,1,0:T(8,128)}, u32[]{:S(2)}) copy-start(f32[96,16,128]{2,1,0:T(8,128)} %copy-done.3) | copy-start | bytes 2359300
  83.7 22.5 %collective-permute-start.15 = (bf16[288,768]{1,0:T(8,128)(2,1)S(1)}, bf16[288,768]{1,0:T(8,128)(2,1)S(1)}, u32[]{:S(2)}, u32[]{:S(2)}) collective-permute-start(bf16[288,768]{1,0:T(8,128)(2,1)S(1)} %copy-done.20), channel_id=1, source_target_pairs={{0,2},{1,3},{2,0},{3,1},{4,6},{5,7},{6,4},{7,5},{8,10},{9,11},{10,... | collective-permute-start | bytes 1327112 | tf_op jit(solution)/shard_map/ppermute | solution.py:661
  84.3 23.1 %collective-permute-start.17 = (bf16[576,768]{1,0:T(8,128)(2,1)S(1)}, bf16[576,768]{1,0:T(8,128)(2,1)S(1)}, u32[]{:S(2)}, u32[]{:S(2)}) collective-permute-start(bf16[576,768]{1,0:T(8,128)(2,1)S(1)} %get-tuple-element.121.refs_1_), channel_id=1, source_target_pairs={{0,1},{1,0},{2,3},{3,2},{4,5},{5,4},{6,7},{7,6},{8,9},{9,8},{10,11... | collective-permute-start | bytes 2654216 | tf_op jit(solution)/shard_map/ppermute | solution.py:658
  106.2 12.9 %copy-start.9 = (bf16[768,128]{1,0:T(8,128)(2,1)S(1)}, bf16[768,128]{1,0:T(8,128)(2,1)}, u32[]{:S(2)}) copy-start(bf16[768,128]{1,0:T(8,128)(2,1)} %refs_1_.1) | copy-start | bytes 589828
  106.2 24.3 %copy-start.10 = (bf16[4,128,128]{2,1,0:T(8,128)(2,1)S(1)}, bf16[4,128,128]{2,1,0:T(8,128)(2,1)}, u32[]{:S(2)}) copy-start(bf16[4,128,128]{2,1,0:T(8,128)(2,1)} %w_in.7) | copy-start | bytes 393220
  106.2 24.3 %copy-start.12 = (bf16[144,128]{1,0:T(8,128)(2,1)S(1)}, bf16[144,128]{1,0:T(8,128)(2,1)}, u32[]{:S(2)}) copy-start(bf16[144,128]{1,0:T(8,128)(2,1)} %copy-done.11) | copy-start | bytes 110596
  106.2 24.3 %copy-start.13 = (bf16[128,128]{1,0:T(8,128)(2,1)S(1)}, bf16[128,128]{1,0:T(8,128)(2,1)}, u32[]{:S(2)}) copy-start(bf16[128,128]{1,0:T(8,128)(2,1)} %w_out.7) | copy-start | bytes 98308
  106.2 24.3 %copy-start.16 = (bf16[3,128]{1,0:T(4,128)(2,1)S(1)}, bf16[3,128]{1,0:T(4,128)(2,1)}, u32[]{:S(2)}) copy-start(bf16[3,128]{1,0:T(4,128)(2,1)} %pos.1) | copy-start | bytes 2308
  106.2 4.9 %collective-permute-start.18 = (bf16[288,768]{1,0:T(8,128)(2,1)}, bf16[288,768]{1,0:T(8,128)(2,1)S(1)}, u32[]{:S(2)}, u32[]{:S(2)}) collective-permute-start(bf16[288,768]{1,0:T(8,128)(2,1)} %collective-permute-done.10.refs_3_), channel_id=1, source_target_pairs={{0,1},{1,0},{2,3},{3,2},{4,5},{5,4},{6,7},{7,6},{8,9},{9,8},{10,11... | collective-permute-start | bytes 1327112 | tf_op jit(solution)/shard_map/ppermute | solution.py:684
  106.3 4.9 %collective-permute-start.19 = (bf16[288,768]{1,0:T(8,128)(2,1)S(1)}, bf16[288,768]{1,0:T(8,128)(2,1)S(1)}, u32[]{:S(2)}, u32[]{:S(2)}) collective-permute-start(bf16[288,768]{1,0:T(8,128)(2,1)S(1)} %collective-permute-done.15.refs_4_), channel_id=1, source_target_pairs={{0,1},{1,0},{2,3},{3,2},{4,5},{5,4},{6,7},{7,6},{8,9},{9,8},{10,11... | collective-permute-start | bytes 1327112 | tf_op jit(solution)/shard_map/ppermute | solution.py:684
  106.8 4.4 %collective-permute-start.16 = (f32[24,768]{1,0:T(8,128)S(1)}, f32[24,768]{1,0:T(8,128)S(1)}, u32[]{:S(2)}, u32[]{:S(2)}) collective-permute-start(f32[24,768]{1,0:T(8,128)S(1)} %shard_map.185.act_ref), channel_id=1, source_target_pairs={{0,4},{1,5},{2,6},{3,7},{4,0},{5,1},{6,2},{7,3},{8,12},{9,13},{10,... | collective-permute-start | bytes 221192 | tf_op jit(solution)/shard_map/ppermute | solution.py:682
  114.7 4.4 %collective-permute-start.20 = (bf16[48,768]{1,0:T(8,128)(2,1)S(1)}, bf16[48,768]{1,0:T(8,128)(2,1)S(1)}, u32[]{:S(2)}, u32[]{:S(2)}) collective-permute-start(bf16[48,768]{1,0:T(8,128)(2,1)S(1)} %get-tuple-element.125), channel_id=1, source_target_pairs={{0,4},{1,5},{2,6},{3,7},{4,0},{5,1},{6,2},{7,3},{8,12},{9,13},{10,... | collective-permute-start | bytes 221192 | tf_op jit(solution)/shard_map/ppermute | solution.py:688
  119.9 3.1 %collective-permute-start.21 = (bf16[48,128]{1,0:T(8,128)(2,1)S(1)}, bf16[48,128]{1,0:T(8,128)(2,1)S(1)}, u32[]{:S(2)}, u32[]{:S(2)}) collective-permute-start(bf16[48,128]{1,0:T(8,128)(2,1)S(1)} %get-tuple-element.126), channel_id=1, source_target_pairs={{0,3},{1,2},{2,1},{3,0},{4,7},{5,6},{6,5},{7,4},{8,11},{9,10},{10,... | collective-permute-start | bytes 36872 | tf_op jit(solution)/shard_map/ppermute | solution.py:472
  119.9 3.7 %collective-permute-start.22 = (bf16[48,128]{1,0:T(8,128)(2,1)S(1)}, bf16[48,128]{1,0:T(8,128)(2,1)S(1)}, u32[]{:S(2)}, u32[]{:S(2)}) collective-permute-start(bf16[48,128]{1,0:T(8,128)(2,1)S(1)} %get-tuple-element.126), channel_id=1, source_target_pairs={{0,2},{1,3},{2,0},{3,1},{4,6},{5,7},{6,4},{7,5},{8,10},{9,11},{10,... | collective-permute-start | bytes 36872 | tf_op jit(solution)/shard_map/ppermute | solution.py:472
  120.5 3.1 %collective-permute-start.23 = (bf16[48,128]{1,0:T(8,128)(2,1)S(1)}, bf16[48,128]{1,0:T(8,128)(2,1)S(1)}, u32[]{:S(2)}, u32[]{:S(2)}) collective-permute-start(bf16[48,128]{1,0:T(8,128)(2,1)S(1)} %get-tuple-element.126), channel_id=1, source_target_pairs={{0,1},{1,0},{2,3},{3,2},{4,5},{5,4},{6,7},{7,6},{8,9},{9,8},{10,11... | collective-permute-start | bytes 36872 | tf_op jit(solution)/shard_map/ppermute | solution.py:472
  123.7 6.9 %collective-permute-start.24 = (bf16[64,128]{1,0:T(8,128)(2,1)S(1)}, bf16[64,128]{1,0:T(8,128)(2,1)S(1)}, u32[]{:S(2)}, u32[]{:S(2)}) collective-permute-start(bf16[64,128]{1,0:T(8,128)(2,1)S(1)} %slice_select_fusion), channel_id=1, source_target_pairs={{7,8},{15,16},{23,24},{8,7},{16,15},{24,23}} | collective-permute-start | bytes 49160 | tf_op jit(solution)/shard_map/ppermute | solution.py:699
  (6 other events, 4.5 us)

commit v8 on v7

--- a/solution.py
+++ b/solution.py
@@ -484,16 +484,14 @@
 def key_source(rows, cols):
     nrow, ncol = lax.axis_size("row"), lax.axis_size("col")
     shares = rows // cols
+    chips = ncol // shares
     pairs = []
     for owner in range(nrow):
-        free = [list(range(share, ncol, shares)) for share in range(shares)]
-        for r in range(nrow):
+        near = sorted(range(chips), key=lambda chip: bin((chip ^ owner) % chips).count("1"))
+        others = sorted((r for r in range(nrow) if r != owner), key=lambda r: -abs(r - owner))
+        for chip, r in zip(near, others):
             for share in range(shares):
-                if r != owner:
-                    spot = (2 * ((r + owner) % 2) + share) % (ncol // shares) * shares + share
-                    source = spot if spot in free[share] else free[share][0]
-                    free[share].remove(source)
-                    pairs.append((owner * ncol + source, r * ncol + owner * shares + share))
+                pairs.append((owner * ncol + chip * shares + share, r * ncol + owner * shares + share))
     return pairs
 
 
@@ -552,7 +550,7 @@
         [matrix, half, half] * BLOCKS,
         first_part,
         second_part,
-        grant=48,
+        grant=60,
         moved=12 * trans_out.size,
     )
     packed, upper, lower = pieces[::3], pieces[1::3], pieces[2::3]
@@ -693,9 +691,9 @@
         if not last:
             xn = gathered
 
-    bounds = [(r * ncol - 1, r * ncol) for r in range(1, nrow)]
-    bounds += [(b, a) for a, b in bounds]
-    edge = jnp.where(me_col == 0, gathered[:HALO], gathered[rows - HALO :])
+    bounds = [(r * ncol, (r + 1) * ncol) for r in range(nrow - 1)]
+    bounds += [((r + 2) * ncol - 1, (r + 1) * ncol - 1) for r in range(nrow - 1)]
+    edge = jnp.where(me_col == 0, gathered[rows - HALO :], gathered[:HALO])
     edge = lax.ppermute(edge, everyone, bounds)
 
     return call(

time: 133 us -> 128 us (0.962)
  local copies, waits for them, and re-layouts: 7.07 us -> 2.26 us
  blocking collectives: 24.3 us -> 22.2 us
  Pallas kernels: 37.2 us -> 39.3 us
  waiting for transfers between devices: 35.3 us -> 33.4 us
  starting transfers between devices: 27.1 us -> 28.8 us
    unnamed x56 -> x46, local copies, waits for them, and re-layouts: 7.05 us -> 2.24 us
    ppermute x1, starting transfers between devices: 0.68 us -> 3.6 us  [body(): across[0].append(lax.ppermute(late, everyone, neighbour))]
    ppermute x2, starting transfers between devices: 5.27 us -> 2.9 us  [body(): came = lax.ppermute(send, everyone, pairs)]
    all_to_all x2, blocking collectives: 24.3 us -> 22.2 us  [body(): message = lax.all_to_all(message.reshape(ncol, own, -1), 'col', 0, 0)]
    pallas_call x15, Pallas kernels: 29.2 us -> 31.3 us  [call(): pl.pallas_call(kernel, out_shape=outs, in_specs=[smem] * len(scalars) + [...]
    ppermute x1, starting transfers between devices: 0.55 us -> 2.24 us  [body(): across[1].append(lax.ppermute(late, everyone, neighbour))]
    ppermute x2, waiting for transfers between devices: 4.77 us -> 3.25 us  [body(): came = lax.ppermute(send, everyone, pairs)]
  transfers between devices with their start and end apart: 26 -> 26, of which waited for: 11 -> 11; matrix products, arithmetic and copies ran while one was open for 0% -> 0% of each run, Pallas kernels for 22% -> 24%
where the time goes in v8:
time: 128 us; the launch traced here: 127 us
  Pallas kernels  39.3 us (31%)
  waiting for transfers between devices  33.4 us (26%)
  starting transfers between devices  28.8 us (22%)
  blocking collectives  22.2 us (17%)
  local copies, waits for them, and re-layouts  2.26 us (2%)
    pallas_call x15, Pallas kernels, call(): pl.pallas_call(kernel, out_shape=outs, in_specs=[smem] * len(scalars) + [...  31.3 us
    all_to_all x2, blocking collectives, body(): message = lax.all_to_all(message.reshape(ncol, own, -1), 'col', 0, 0)  22.2 us
    pallas_call x2, Pallas kernels, bias_of(): pl.pallas_call(bias_kernel, grid=(half // step,), out_shape=[jax.ShapeDty...  8.01 us
    ppermute x2, waiting for transfers between devices, body(): lax.ppermute(act, everyone, shifts[d])  7.58 us
    ppermute x2, waiting for transfers between devices, body(): parts = [lax.ppermute(part, everyone, shifts[d]) for d in range(1, peers)]  7.57 us
    ppermute x6, waiting for transfers between devices, row_of(): lax.ppermute(mine, ('row', 'col'), [(i, i ^ flip) for i in range(nrow * n...  6.26 us
    ppermute x1, starting transfers between devices, body(): after = lax.ppermute(feat, everyone, [(b, a) for a, b in up])  5.44 us
    all_to_all x1, waiting for transfers between devices, body(): both = lax.all_to_all(copies, 'col', 0, 0)  4.39 us
  transfers between devices with their start and end apart: 26, of which 11 were waited for; matrix products, arithmetic and copies ran while one was open for 0% of the time, Pallas kernels for 24%

profile of v8, /device:TPU:24, one launch (start us, length us, event | category | flops | bytes accessed | tf_op | source)
XLA Modules:
  0.0 127.4 jit_solution(15746054061638795002)
XLA Ops:
  0.0 0.8 copy-done.10
  0.8 0.7 copy-done.13
  1.4 0.7 copy-done.14
  2.6 1.9 %collective-permute-start = (bf16[144,128]{1,0:T(8,128)(2,1)S(1)}, bf16[144,128]{1,0:T(8,128)(2,1)S(1)}, u32[]{:S(2)}, u32[]{:S(2)}) collective-permute-start(bf16[144,128]{1,0:T(8,128)(2,1)S(1)} %shard_map.172.own_ref), channel_id=1, source_target_pairs={{0,1},{1,2},{2,3},{3,4},{4,5},{5,6},{6,7},{7,8},{8,9},{9,10},{10,1... | collective-permute-start | bytes 110600 | tf_op jit(solution)/shard_map/ppermute | solution.py:541
  4.6 5.4 %collective-permute-start.1 = (bf16[144,128]{1,0:T(8,128)(2,1)S(1)}, bf16[144,128]{1,0:T(8,128)(2,1)S(1)}, u32[]{:S(2)}, u32[]{:S(2)}) collective-permute-start(bf16[144,128]{1,0:T(8,128)(2,1)S(1)} %shard_map.172.own_ref), channel_id=1, source_target_pairs={{1,0},{2,1},{3,2},{4,3},{5,4},{6,5},{7,6},{8,7},{9,8},{10,9},{11,1... | collective-permute-start | bytes 110600 | tf_op jit(solution)/shard_map/ppermute | solution.py:542
  10.0 3.3 %shard_map.173 = (bf16[576,768]{1,0:T(8,128)(2,1)}, bf16[288,768]{1,0:T(8,128)(2,1)}, bf16[288,768]{1,0:T(8,128)(2,1)}, bf16[576,768]{1,0:T(8,128)(2,1)}, bf16[2...) custom-call(bf16[2,2,192,768]{3,2,1,0:T(8,128)(2,1)} %bitcast.42, bf16[2,192,768]{2,1,0:T(8,128)(2,1)} %second), custom_call_target="tpu_custom_call" | custom-call | bytes 3538944 | tf_op jit(solution)/shard_map/pallas_call | solution.py:26
  13.4 2.0 %shard_map.174 = (bf16[256,128]{1,0:T(8,128)(2,1)S(1)}, bf16[8,144,128]{2,1,0:T(8,128)(2,1)}) custom-call(bf16[144,128]{1,0:T(8,128)(2,1)S(1)} %shard_map.172.own_ref, bf16[144,128]{1,0:T(8,128)(2,1)S(1)} %collective-permute-done.prev_ref, bf16[144,128]{1,0:T(8,128)(2,1)S(1)} %collective-permute-done.1.next_ref, bf16[4,128,128]{2,1,0:T(8,128)(2,1)S(1)} %copy-done.17, ...), custom_call_target="tpu_custom_call" | custom-call | flops 100000000 | bytes 1000000 | tf_op jit(solution)/shard_map/pallas_call | solution.py:26
  15.4 3.4 %all-to-all-start = ((bf16[8,144,128]{2,1,0:T(8,128)(2,1)}), bf16[8,144,128]{2,1,0:T(8,128)(2,1)S(1)}, u32[]{:S(2)}, u32[]{:S(2)}) async-start(bf16[8,144,128]{2,1,0:T(8,128)(2,1)} %get-tuple-element.73), calls=%async_computation | async-start | bytes 589824 | tf_op jit(solution)/shard_map/all_to_all | solution.py:601
  18.9 4.6 %shard_map.175 = (f32[96,16,128]{2,1,0:T(8,128)}, f32[96,16,128]{2,1,0:T(8,128)}) custom-call(bf16[192,96,128]{2,1,0:T(8,128)(2,1)} %pair_ref.3, bf16[32,128]{1,0:T(8,128)(2,1)} %bitcast.40), custom_call_target="tpu_custom_call" | custom-call | flops 2000000000 | bytes 4000000 | tf_op jit(solution)/shard_map/pallas_call | solution.py:581
  23.4 4.4 %all-to-all-done.both_ref = bf16[8,144,128]{2,1,0:T(8,128)(2,1)S(1)} async-done(((bf16[8,144,128]{2,1,0:T(8,128)(2,1)}), bf16[8,144,128]{2,1,0:T(8,128)(2,1)S(1)}, u32[]{:S(2)}, u32[]{:S(2)}) %all-to-all-start) | async-done | bytes 294944 | tf_op jit(solution)/shard_map/all_to_all | solution.py:601
  27.9 1.3 %shard_map.176 = (f32[24,768]{1,0:T(8,128)S(1)}, bf16[192,768]{1,0:T(8,128)(2,1)S(1)}, bf16[96,768]{1,0:T(8,128)(2,1)S(1)}) custom-call(bf16[8,144,128]{2,1,0:T(8,128)(2,1)S(1)} %all-to-all-done.both_ref, bf16[128,768]{1,0:T(8,128)(2,1)S(1)} %copy-done.16, bf16[192,768]{1,0:T(8,128)(2,1)S(1)} %copy-done.15), custom_call_target="tpu_custom_call" | custom-call | flops 1000000000 | bytes 1000000 | tf_op jit(solution)/shard_map/pallas_call | solution.py:26
  29.2 1.4 %collective-permute-start.3 = (bf16[96,768]{1,0:T(8,128)(2,1)S(1)}, bf16[96,768]{1,0:T(8,128)(2,1)S(1)}, u32[]{:S(2)}, u32[]{:S(2)}) collective-permute-start(bf16[96,768]{1,0:T(8,128)(2,1)S(1)} %get-tuple-element.83.here_ref), channel_id=1, source_target_pairs={{0,24},{1,25},{2,16},{3,17},{4,8},{5,9},{10,26},{11,27},{8,2},{9,3... | collective-permute-start | bytes 442376 | tf_op jit(solution)/shard_map/ppermute | solution.py:632
  30.6 3.4 %shard_map.178 = (f32[96,16,128]{2,1,0:T(8,128)S(1)}, f32[96,16,128]{2,1,0:T(8,128)S(1)}) custom-call(bf16[192,96,128]{2,1,0:T(8,128)(2,1)} %pair_ref.3, bf16[32,128]{1,0:T(8,128)(2,1)S(1)} %bitcast.41), custom_call_target="tpu_custom_call" | custom-call | flops 2000000000 | bytes 4000000 | tf_op jit(solution)/shard_map/pallas_call | solution.py:581
  34.1 3.6 %collective-permute-start.4 = (bf16[288,768]{1,0:T(8,128)(2,1)S(1)}, bf16[288,768]{1,0:T(8,128)(2,1)S(1)}, u32[]{:S(2)}, u32[]{:S(2)}) collective-permute-start(bf16[288,768]{1,0:T(8,128)(2,1)S(1)} %copy-done.22), channel_id=1, source_target_pairs={{0,2},{1,3},{2,0},{3,1},{4,6},{5,7},{6,4},{7,5},{8,10},{9,11},{10,... | collective-permute-start | bytes 1327112 | tf_op jit(solution)/shard_map/ppermute | solution.py:655
  37.7 2.4 %shard_map.177 = (bf16[192,768]{1,0:T(8,128)(2,1)S(1)}, bf16[768,768]{1,0:T(8,128)(2,1)S(1)}, bf16[768,768]{1,0:T(8,128)(2,1)S(1)}, f32[24,768]{1,0:T(8,128)S(1)}) custom-call(bf16[192,768]{1,0:T(8,128)(2,1)S(1)} %get-tuple-element.80.xn_ref, f32[24,768]{1,0:T(8,128)S(1)} %get-tuple-element.81.act_ref, bf16[2,4,768,768]{3,2,1,0:T(8,128)(2,1)} %w_in.6), custom_call_target="tpu_custom_call" | custom-call | flops 226492416 | bytes 4718592 | tf_op jit(solution)/shard_map/pallas_call | solution.py:26
  40.2 3.5 %shard_map.179 = bf16[192,896]{1,0:T(8,128)(2,1)S(1)} custom-call(s32[768]{0:T(1024)S(1)} %copy-done.11, bf16[192,768]{1,0:T(8,128)(2,1)S(1)} %get-tuple-element.82.query, bf16[96,768]{1,0:T(8,128)(2,1)S(1)} %get-tuple-element.83.here_ref, bf16[96,768]{1,0:T(8,128)(2,1)S(1)} %collective-permute-done.3.came_ref, f32[96,16,128]{2,1,0:T(8,128)S(1)} %copy-done.4, ...), custom_call_target="tpu_custom_call" | custom-call | flops 1000000000 | bytes 8000000 | tf_op jit(solution)/shard_map/pallas_call | solution.py:26
  43.7 10.6 %all_to_all.15.message = bf16[8,24,896]{2,1,0:T(8,128)(2,1)S(1)} all-to-all(bf16[8,24,896]{2,1,0:T(8,128)(2,1)S(1)} %bitcast.35), channel_id=1, replica_groups=mesh['row'=4,'col'=8] {'col'}, dimensions={0} | all-to-all | bytes 688128 | tf_op jit(solution)/shard_map/all_to_all | solution.py:675
  54.3 1.0 shard_map.180.act_ref
  55.9 0.6 collective-permute-start.10
  56.5 0.6 collective-permute-start.5
  57.1 3.8 %collective-permute-done.5.refs_0_ = f32[24,768]{1,0:T(8,128)S(1)} collective-permute-done((f32[24,768]{1,0:T(8,128)S(1)}, f32[24,768]{1,0:T(8,128)S(1)}, u32[]{:S(2)}, u32[]{:S(2)}) %collective-permute-start.5) | collective-permute-done | bytes 73760 | tf_op jit(solution)/shard_map/ppermute | solution.py:680
  60.9 3.7 %shard_map.181 = (f32[48,768]{1,0:T(8,128)S(1)}, bf16[48,768]{1,0:T(8,128)(2,1)S(1)}) custom-call(f32[24,768]{1,0:T(8,128)S(1)} %shard_map.180.act_ref, f32[24,768]{1,0:T(8,128)S(1)} %collective-permute-done.5.refs_0_, bf16[576,768]{1,0:T(8,128)(2,1)S(1)} %copy-done.2, bf16[576,768]{1,0:T(8,128)(2,1)S(1)} %collective-permute-done.6.refs_2_, ...), custom_call_target="tpu_custom_call" | custom-call | flops 169869312 | bytes 3538944 | tf_op jit(solution)/shard_map/pallas_call | solution.py:26
  64.6 0.6 collective-permute-start.9
  65.2 3.8 %collective-permute-done.9.refs_0_ = bf16[48,768]{1,0:T(8,128)(2,1)S(1)} collective-permute-done((bf16[48,768]{1,0:T(8,128)(2,1)S(1)}, bf16[48,768]{1,0:T(8,128)(2,1)S(1)}, u32[]{:S(2)}, u32[]{:S(2)}) %collective-permute-start.9) | collective-permute-done | bytes 73760 | tf_op jit(solution)/shard_map/ppermute | solution.py:686
  69.3 1.5 %collective-permute-start.12 = (bf16[48,768]{1,0:T(8,128)(2,1)S(1)}, bf16[48,768]{1,0:T(8,128)(2,1)}, u32[]{:S(2)}, u32[]{:S(2)}) collective-permute-start(bf16[48,768]{1,0:T(8,128)(2,1)S(1)} %get-tuple-element.106), channel_id=1, source_target_pairs={{0,2},{1,3},{2,0},{3,1},{4,6},{5,7},{6,4},{7,5},{8,10},{9,11},{10,... | collective-permute-start | bytes 221192 | tf_op jit(solution)/shard_map/ppermute | solution.py:472
  71.1 2.7 %collective-permute-done.11 = bf16[48,768]{1,0:T(8,128)(2,1)S(1)} collective-permute-done((bf16[48,768]{1,0:T(8,128)(2,1)S(1)}, bf16[48,768]{1,0:T(8,128)(2,1)S(1)}, u32[]{:S(2)}, u32[]{:S(2)}) %collective-permute-start.11) | collective-permute-done | bytes 73760 | tf_op jit(solution)/shard_map/ppermute | solution.py:472
  73.8 1.7 %collective-permute-done.12 = bf16[48,768]{1,0:T(8,128)(2,1)} collective-permute-done((bf16[48,768]{1,0:T(8,128)(2,1)S(1)}, bf16[48,768]{1,0:T(8,128)(2,1)}, u32[]{:S(2)}, u32[]{:S(2)}) %collective-permute-start.12) | collective-permute-done | bytes 73760 | tf_op jit(solution)/shard_map/ppermute | solution.py:472
  75.5 1.0 select_select_fusion.3
  76.6 1.5 %collective-permute-start.14 = (bf16[96,768]{1,0:T(8,128)(2,1)S(1)}, bf16[96,768]{1,0:T(8,128)(2,1)S(1)}, u32[]{:S(2)}, u32[]{:S(2)}) collective-permute-start(bf16[96,768]{1,0:T(8,128)(2,1)S(1)} %constant_dynamic-slice_fusion.here_ref), channel_id=1, source_target_pairs={{0,24},{1,25},{2,16},{3,17},{4,8},{5,9},{10,26},{11,27},{8,2},{9,3... | collective-permute-start | bytes 442376 | tf_op jit(solution)/shard_map/ppermute | solution.py:632
  78.1 2.5 %shard_map.183 = (bf16[192,768]{1,0:T(8,128)(2,1)S(1)}, bf16[768,768]{1,0:T(8,128)(2,1)S(1)}, bf16[768,768]{1,0:T(8,128)(2,1)S(1)}, f32[24,768]{1,0:T(8,128)S(1)}) custom-call(bf16[192,768]{1,0:T(8,128)(2,1)S(1)} %bitcast.34, f32[24,768]{1,0:T(8,128)S(1)} %get-tuple-element.108.act_ref, bf16[2,4,768,768]{3,2,1,0:T(8,128)(2,1)} %w_in.6), custom_call_target="tpu_custom_call" | custom-call | flops 226492416 | bytes 4718592 | tf_op jit(solution)/shard_map/pallas_call | solution.py:26
  80.6 2.2 %collective-permute-start.15 = (bf16[288,768]{1,0:T(8,128)(2,1)S(1)}, bf16[288,768]{1,0:T(8,128)(2,1)S(1)}, u32[]{:S(2)}, u32[]{:S(2)}) collective-permute-start(bf16[288,768]{1,0:T(8,128)(2,1)S(1)} %copy-done.20), channel_id=1, source_target_pairs={{0,2},{1,3},{2,0},{3,1},{4,6},{5,7},{6,4},{7,5},{8,10},{9,11},{10,... | collective-permute-start | bytes 1327112 | tf_op jit(solution)/shard_map/ppermute | solution.py:659
  82.9 3.2 %collective-permute-done.14.came_ref = bf16[96,768]{1,0:T(8,128)(2,1)S(1)} collective-permute-done((bf16[96,768]{1,0:T(8,128)(2,1)S(1)}, bf16[96,768]{1,0:T(8,128)(2,1)S(1)}, u32[]{:S(2)}, u32[]{:S(2)}) %collective-permute-start.14) | collective-permute-done | bytes 147488 | tf_op jit(solution)/shard_map/ppermute | solution.py:632
  86.1 3.5 %shard_map.184 = bf16[192,896]{1,0:T(8,128)(2,1)S(1)} custom-call(s32[768]{0:T(1024)S(1)} %copy-done.11, bf16[192,768]{1,0:T(8,128)(2,1)S(1)} %get-tuple-element.111.query, bf16[96,768]{1,0:T(8,128)(2,1)S(1)} %constant_dynamic-slice_fusion.here_ref, bf16[96,768]{1,0:T(8,128)(2,1)S(1)} %collective-permute-done.14.came_ref, f32[96,16,128]{2,1,0:T(8,128)S(1)} %copy-done.3, ...), custom_call_target="tpu_custom_call" | custom-call | flops 1000000000 | bytes 8000000 | tf_op jit(solution)/shard_map/pallas_call | solution.py:26
  89.6 11.6 %all_to_all.16.message = bf16[8,24,896]{2,1,0:T(8,128)(2,1)S(1)} all-to-all(bf16[8,24,896]{2,1,0:T(8,128)(2,1)S(1)} %bitcast.36), channel_id=1, replica_groups=mesh['row'=4,'col'=8] {'col'}, dimensions={0} | all-to-all | bytes 688128 | tf_op jit(solution)/shard_map/all_to_all | solution.py:675
  101.2 1.0 shard_map.185.act_ref
  102.9 0.6 collective-permute-start.16
  103.5 3.8 %collective-permute-done.16.refs_0_ = f32[24,768]{1,0:T(8,128)S(1)} collective-permute-done((f32[24,768]{1,0:T(8,128)S(1)}, f32[24,768]{1,0:T(8,128)S(1)}, u32[]{:S(2)}, u32[]{:S(2)}) %collective-permute-start.16) | collective-permute-done | bytes 73760 | tf_op jit(solution)/shard_map/ppermute | solution.py:680
  107.3 3.5 %shard_map.186 = (f32[48,768]{1,0:T(8,128)S(1)}, bf16[48,768]{1,0:T(8,128)(2,1)S(1)}) custom-call(f32[24,768]{1,0:T(8,128)S(1)} %shard_map.185.act_ref, f32[24,768]{1,0:T(8,128)S(1)} %collective-permute-done.16.refs_0_, bf16[576,768]{1,0:T(8,128)(2,1)S(1)} %copy-done.1, bf16[576,768]{1,0:T(8,128)(2,1)S(1)} %collective-permute-done.17.refs_2_, ...), custom_call_target="tpu_custom_call" | custom-call | flops 169869312 | bytes 3538944 | tf_op jit(solution)/shard_map/pallas_call | solution.py:26
  110.7 0.6 collective-permute-start.20
  111.4 3.8 %collective-permute-done.20.refs_0_ = bf16[48,768]{1,0:T(8,128)(2,1)S(1)} collective-permute-done((bf16[48,768]{1,0:T(8,128)(2,1)S(1)}, bf16[48,768]{1,0:T(8,128)(2,1)S(1)}, u32[]{:S(2)}, u32[]{:S(2)}) %collective-permute-start.20) | collective-permute-done | bytes 73760 | tf_op jit(solution)/shard_map/ppermute | solution.py:686
  115.2 0.8 shard_map.187
  116.0 0.6 collective-permute-start.22
  116.6 1.3 collective-permute-start.23
  117.8 1.3 collective-permute-done.21
  119.1 0.6 collective-permute-done.22
  119.8 1.3 %collective-permute-start.24 = (bf16[64,128]{1,0:T(8,128)(2,1)S(1)}, bf16[64,128]{1,0:T(8,128)(2,1)S(1)}, u32[]{:S(2)}, u32[]{:S(2)}) collective-permute-start(bf16[64,128]{1,0:T(8,128)(2,1)S(1)} %slice_select_fusion), channel_id=1, source_target_pairs={{0,8},{8,16},{16,24},{15,7},{23,15},{31,23}} | collective-permute-start | bytes 49160 | tf_op jit(solution)/shard_map/ppermute | solution.py:697
  121.1 4.3 %collective-permute-done.24.edge_ref = bf16[64,128]{1,0:T(8,128)(2,1)S(1)} collective-permute-done((bf16[64,128]{1,0:T(8,128)(2,1)S(1)}, bf16[64,128]{1,0:T(8,128)(2,1)S(1)}, u32[]{:S(2)}, u32[]{:S(2)}) %collective-permute-start.24) | collective-permute-done | bytes 16416 | tf_op jit(solution)/shard_map/ppermute | solution.py:697
  125.4 2.0 %shard_map.188 = f32[3,128]{1,0:T(4,128)} custom-call(bf16[256,128]{1,0:T(8,128)(2,1)S(1)} %get-tuple-element.71.x1_ref, bf16[144,128]{1,0:T(8,128)(2,1)S(1)} %shard_map.172.own_ref, bf16[144,128]{1,0:T(8,128)(2,1)S(1)} %collective-permute-done.prev_ref, bf16[144,128]{1,0:T(8,128)(2,1)S(1)} %collective-permute-done.1.next_ref, ...), custom_call_target="tpu_custom_call" | custom-call | flops 100000000 | bytes 1000000 | tf_op jit(solution)/shard_map/pallas_call | solution.py:26
  (75 shorter events, 2.7 us)
Async XLA Ops:
  0.0 0.8 copy-start.10
  0.8 0.7 copy-start.13
  2.1 11.3 %copy-start.17 = (bf16[4,128,128]{2,1,0:T(8,128)(2,1)S(1)}, bf16[4,128,128]{2,1,0:T(8,128)(2,1)}, u32[]{:S(2)}) copy-start(bf16[4,128,128]{2,1,0:T(8,128)(2,1)} %w_in.4) | copy-start | bytes 393220
  2.1 11.3 %copy-start.18 = (bf16[128,128]{1,0:T(8,128)(2,1)S(1)}, bf16[128,128]{1,0:T(8,128)(2,1)}, u32[]{:S(2)}) copy-start(bf16[128,128]{1,0:T(8,128)(2,1)} %w_out.4) | copy-start | bytes 98308
  2.6 10.6 %collective-permute-start = (bf16[144,128]{1,0:T(8,128)(2,1)S(1)}, bf16[144,128]{1,0:T(8,128)(2,1)S(1)}, u32[]{:S(2)}, u32[]{:S(2)}) collective-permute-start(bf16[144,128]{1,0:T(8,128)(2,1)S(1)} %shard_map.172.own_ref), channel_id=1, source_target_pairs={{0,1},{1,2},{2,3},{3,4},{4,5},{5,6},{6,7},{7,8},{8,9},{9,10},{10,1... | collective-permute-start | bytes 110600 | tf_op jit(solution)/shard_map/ppermute | solution.py:541
  4.6 8.7 %collective-permute-start.1 = (bf16[144,128]{1,0:T(8,128)(2,1)S(1)}, bf16[144,128]{1,0:T(8,128)(2,1)S(1)}, u32[]{:S(2)}, u32[]{:S(2)}) collective-permute-start(bf16[144,128]{1,0:T(8,128)(2,1)S(1)} %shard_map.172.own_ref), channel_id=1, source_target_pairs={{1,0},{2,1},{3,2},{4,3},{5,4},{6,5},{7,6},{8,7},{9,8},{10,9},{11,1... | collective-permute-start | bytes 110600 | tf_op jit(solution)/shard_map/ppermute | solution.py:542
  13.3 14.6 %collective-permute-start.2 = (bf16[288,768]{1,0:T(8,128)(2,1)}, bf16[288,768]{1,0:T(8,128)(2,1)S(1)}, u32[]{:S(2)}, u32[]{:S(2)}) collective-permute-start(bf16[288,768]{1,0:T(8,128)(2,1)} %get-tuple-element.77), channel_id=1, source_target_pairs={{0,2},{1,3},{2,0},{3,1},{4,6},{5,7},{6,4},{7,5},{8,10},{9,11},{10,... | collective-permute-start | bytes 1327112 | tf_op jit(solution)/shard_map/ppermute | solution.py:560
  15.4 12.4 %all-to-all-start = ((bf16[8,144,128]{2,1,0:T(8,128)(2,1)}), bf16[8,144,128]{2,1,0:T(8,128)(2,1)S(1)}, u32[]{:S(2)}, u32[]{:S(2)}) async-start(bf16[8,144,128]{2,1,0:T(8,128)(2,1)} %get-tuple-element.73), calls=%async_computation | async-start | bytes 589824 | tf_op jit(solution)/shard_map/all_to_all | solution.py:601
  18.8 9.0 %copy-start.15 = (bf16[192,768]{1,0:T(8,128)(2,1)S(1)}, bf16[192,768]{1,0:T(8,128)(2,1)}, u32[]{:S(2)}) copy-start(bf16[192,768]{1,0:T(8,128)(2,1)} %cond.1) | copy-start | bytes 884740
  18.9 9.0 %copy-start.16 = (bf16[128,768]{1,0:T(8,128)(2,1)S(1)}, bf16[128,768]{1,0:T(8,128)(2,1)}, u32[]{:S(2)}) copy-start(bf16[128,768]{1,0:T(8,128)(2,1)} %weight.1) | copy-start | bytes 589828
  27.8 1.3 %copy-start.5 = (bf16[288,768]{1,0:T(8,128)(2,1)}, bf16[288,768]{1,0:T(8,128)(2,1)S(1)}, u32[]{:S(2)}) copy-start(bf16[288,768]{1,0:T(8,128)(2,1)S(1)} %collective-permute-done.2.refs_3_) | copy-start | bytes 1327108
  27.9 2.8 %copy-start.19 = (bf16[2,128,16]{1,2,0:T(8,128)(2,1)S(1)}, bf16[2,128,16]{1,2,0:T(8,128)(2,1)}, u32[]{:S(2)}) copy-start(bf16[2,128,16]{1,2,0:T(8,128)(2,1)} %param.29) | copy-start | bytes 24580
  29.2 4.9 %copy-start.22 = (bf16[288,768]{1,0:T(8,128)(2,1)S(1)}, bf16[288,768]{1,0:T(8,128)(2,1)}, u32[]{:S(2)}) copy-start(bf16[288,768]{1,0:T(8,128)(2,1)} %get-tuple-element.97) | copy-start | bytes 1327108
  29.2 8.5 %copy-start.2 = (bf16[576,768]{1,0:T(8,128)(2,1)S(1)}, bf16[576,768]{1,0:T(8,128)(2,1)}, u32[]{:S(2)}) copy-start(bf16[576,768]{1,0:T(8,128)(2,1)} %get-tuple-element.99.refs_1_) | copy-start | bytes 2654212
  29.2 11.0 %collective-permute-start.3 = (bf16[96,768]{1,0:T(8,128)(2,1)S(1)}, bf16[96,768]{1,0:T(8,128)(2,1)S(1)}, u32[]{:S(2)}, u32[]{:S(2)}) collective-permute-start(bf16[96,768]{1,0:T(8,128)(2,1)S(1)} %get-tuple-element.83.here_ref), channel_id=1, source_target_pairs={{0,24},{1,25},{2,16},{3,17},{4,8},{5,9},{10,26},{11,27},{8,2},{9,3... | collective-permute-start | bytes 442376 | tf_op jit(solution)/shard_map/ppermute | solution.py:632
  34.1 21.3 %collective-permute-start.4 = (bf16[288,768]{1,0:T(8,128)(2,1)S(1)}, bf16[288,768]{1,0:T(8,128)(2,1)S(1)}, u32[]{:S(2)}, u32[]{:S(2)}) collective-permute-start(bf16[288,768]{1,0:T(8,128)(2,1)S(1)} %copy-done.22), channel_id=1, source_target_pairs={{0,2},{1,3},{2,0},{3,1},{4,6},{5,7},{6,4},{7,5},{8,10},{9,11},{10,... | collective-permute-start | bytes 1327112 | tf_op jit(solution)/shard_map/ppermute | solution.py:655
  37.7 23.2 %collective-permute-start.6 = (bf16[576,768]{1,0:T(8,128)(2,1)S(1)}, bf16[576,768]{1,0:T(8,128)(2,1)S(1)}, u32[]{:S(2)}, u32[]{:S(2)}) collective-permute-start(bf16[576,768]{1,0:T(8,128)(2,1)S(1)} %copy-done.2), channel_id=1, source_target_pairs={{0,1},{1,0},{2,3},{3,2},{4,5},{5,4},{6,7},{7,6},{8,9},{9,8},{10,11... | collective-permute-start | bytes 2654216 | tf_op jit(solution)/shard_map/ppermute | solution.py:656
  37.7 2.6 %copy-start.4 = (f32[96,16,128]{2,1,0:T(8,128)S(1)}, f32[96,16,128]{2,1,0:T(8,128)}, u32[]{:S(2)}) copy-start(f32[96,16,128]{2,1,0:T(8,128)} %get-tuple-element.84.low) | copy-start | bytes 2359300
  37.7 2.6 %copy-start.11 = (s32[768]{0:T(1024)S(1)}, s32[768]{0:T(1024)}, u32[]{:S(2)}) copy-start(s32[768]{0:T(1024)} %mask_ref.3) | copy-start | bytes 9220
  40.2 14.1 %copy-start = (bf16[2,768,768]{2,1,0:T(8,128)(2,1)S(1)}, bf16[2,768,768]{2,1,0:T(8,128)(2,1)}, u32[]{:S(2)}) copy-start(bf16[2,768,768]{2,1,0:T(8,128)(2,1)} %w_out.6) | copy-start | bytes 7077892
  54.3 1.1 copy-start.6
  54.3 1.6 %copy-start.21 = (bf16[288,768]{1,0:T(8,128)(2,1)S(1)}, bf16[288,768]{1,0:T(8,128)(2,1)}, u32[]{:S(2)}) copy-start(bf16[288,768]{1,0:T(8,128)(2,1)} %get-tuple-element.105) | copy-start | bytes 1327108
  55.4 5.5 %collective-permute-start.7 = (bf16[288,768]{1,0:T(8,128)(2,1)S(1)}, bf16[288,768]{1,0:T(8,128)(2,1)S(1)}, u32[]{:S(2)}, u32[]{:S(2)}) collective-permute-start(bf16[288,768]{1,0:T(8,128)(2,1)S(1)} %copy-done.6), channel_id=1, source_target_pairs={{0,1},{1,0},{2,3},{3,2},{4,5},{5,4},{6,7},{7,6},{8,9},{9,8},{10,11... | collective-permute-start | bytes 1327112 | tf_op jit(solution)/shard_map/ppermute | solution.py:682
  55.4 5.4 %collective-permute-start.8 = (bf16[288,768]{1,0:T(8,128)(2,1)S(1)}, bf16[288,768]{1,0:T(8,128)(2,1)S(1)}, u32[]{:S(2)}, u32[]{:S(2)}) collective-permute-start(bf16[288,768]{1,0:T(8,128)(2,1)S(1)} %collective-permute-done.4.refs_4_), channel_id=1, source_target_pairs={{0,1},{1,0},{2,3},{3,2},{4,5},{5,4},{6,7},{7,6},{8,9},{9,8},{10,11... | collective-permute-start | bytes 1327112 | tf_op jit(solution)/shard_map/ppermute | solution.py:682
  55.9 13.3 %collective-permute-start.10 = (bf16[288,768]{1,0:T(8,128)(2,1)S(1)}, bf16[288,768]{1,0:T(8,128)(2,1)}, u32[]{:S(2)}, u32[]{:S(2)}) collective-permute-start(bf16[288,768]{1,0:T(8,128)(2,1)S(1)} %copy-done.21), channel_id=1, source_target_pairs={{0,2},{1,3},{2,0},{3,1},{4,6},{5,7},{6,4},{7,5},{8,10},{9,11},{10,... | collective-permute-start | bytes 1327112 | tf_op jit(solution)/shard_map/ppermute | solution.py:678
  56.5 4.4 %collective-permute-start.5 = (f32[24,768]{1,0:T(8,128)S(1)}, f32[24,768]{1,0:T(8,128)S(1)}, u32[]{:S(2)}, u32[]{:S(2)}) collective-permute-start(f32[24,768]{1,0:T(8,128)S(1)} %shard_map.180.act_ref), channel_id=1, source_target_pairs={{0,4},{1,5},{2,6},{3,7},{4,0},{5,1},{6,2},{7,3},{8,12},{9,13},{10,... | collective-permute-start | bytes 221192 | tf_op jit(solution)/shard_map/ppermute | solution.py:680
  64.6 4.4 %collective-permute-start.9 = (bf16[48,768]{1,0:T(8,128)(2,1)S(1)}, bf16[48,768]{1,0:T(8,128)(2,1)S(1)}, u32[]{:S(2)}, u32[]{:S(2)}) collective-permute-start(bf16[48,768]{1,0:T(8,128)(2,1)S(1)} %get-tuple-element.103), channel_id=1, source_target_pairs={{0,4},{1,5},{2,6},{3,7},{4,0},{5,1},{6,2},{7,3},{8,12},{9,13},{10,... | collective-permute-start | bytes 221192 | tf_op jit(solution)/shard_map/ppermute | solution.py:686
  69.2 4.6 %collective-permute-start.11 = (bf16[48,768]{1,0:T(8,128)(2,1)S(1)}, bf16[48,768]{1,0:T(8,128)(2,1)S(1)}, u32[]{:S(2)}, u32[]{:S(2)}) collective-permute-start(bf16[48,768]{1,0:T(8,128)(2,1)S(1)} %get-tuple-element.106), channel_id=1, source_target_pairs={{0,3},{1,2},{2,1},{3,0},{4,7},{5,6},{6,5},{7,4},{8,11},{9,10},{10,... | collective-permute-start | bytes 221192 | tf_op jit(solution)/shard_map/ppermute | solution.py:472
  69.3 6.2 %collective-permute-start.12 = (bf16[48,768]{1,0:T(8,128)(2,1)S(1)}, bf16[48,768]{1,0:T(8,128)(2,1)}, u32[]{:S(2)}, u32[]{:S(2)}) collective-permute-start(bf16[48,768]{1,0:T(8,128)(2,1)S(1)} %get-tuple-element.106), channel_id=1, source_target_pairs={{0,2},{1,3},{2,0},{3,1},{4,6},{5,7},{6,4},{7,5},{8,10},{9,11},{10,... | collective-permute-start | bytes 221192 | tf_op jit(solution)/shard_map/ppermute | solution.py:472
  70.8 4.7 %collective-permute-start.13 = (bf16[48,768]{1,0:T(8,128)(2,1)S(1)}, bf16[48,768]{1,0:T(8,128)(2,1)}, u32[]{:S(2)}, u32[]{:S(2)}) collective-permute-start(bf16[48,768]{1,0:T(8,128)(2,1)S(1)} %get-tuple-element.106), channel_id=1, source_target_pairs={{0,1},{1,0},{2,3},{3,2},{4,5},{5,4},{6,7},{7,6},{8,9},{9,8},{10,11... | collective-permute-start | bytes 221192 | tf_op jit(solution)/shard_map/ppermute | solution.py:472
  76.6 9.5 %collective-permute-start.14 = (bf16[96,768]{1,0:T(8,128)(2,1)S(1)}, bf16[96,768]{1,0:T(8,128)(2,1)S(1)}, u32[]{:S(2)}, u32[]{:S(2)}) collective-permute-start(bf16[96,768]{1,0:T(8,128)(2,1)S(1)} %constant_dynamic-slice_fusion.here_ref), channel_id=1, source_target_pairs={{0,24},{1,25},{2,16},{3,17},{4,8},{5,9},{10,26},{11,27},{8,2},{9,3... | collective-permute-start | bytes 442376 | tf_op jit(solution)/shard_map/ppermute | solution.py:632
  78.1 2.6 %copy-start.20 = (bf16[288,768]{1,0:T(8,128)(2,1)S(1)}, bf16[288,768]{1,0:T(8,128)(2,1)}, u32[]{:S(2)}) copy-start(bf16[288,768]{1,0:T(8,128)(2,1)} %get-tuple-element.119) | copy-start | bytes 1327108
  78.1 4.8 %copy-start.1 = (bf16[576,768]{1,0:T(8,128)(2,1)S(1)}, bf16[576,768]{1,0:T(8,128)(2,1)}, u32[]{:S(2)}) copy-start(bf16[576,768]{1,0:T(8,128)(2,1)} %get-tuple-element.121.refs_1_) | copy-start | bytes 2654212
  78.1 8.0 %copy-start.3 = (f32[96,16,128]{2,1,0:T(8,128)S(1)}, f32[96,16,128]{2,1,0:T(8,128)}, u32[]{:S(2)}) copy-start(f32[96,16,128]{2,1,0:T(8,128)} %get-tuple-element.113.low) | copy-start | bytes 2359300
  80.6 21.7 %collective-permute-start.15 = (bf16[288,768]{1,0:T(8,128)(2,1)S(1)}, bf16[288,768]{1,0:T(8,128)(2,1)S(1)}, u32[]{:S(2)}, u32[]{:S(2)}) collective-permute-start(bf16[288,768]{1,0:T(8,128)(2,1)S(1)} %copy-done.20), channel_id=1, source_target_pairs={{0,2},{1,3},{2,0},{3,1},{4,6},{5,7},{6,4},{7,5},{8,10},{9,11},{10,... | collective-permute-start | bytes 1327112 | tf_op jit(solution)/shard_map/ppermute | solution.py:659
  82.9 20.6 %collective-permute-start.17 = (bf16[576,768]{1,0:T(8,128)(2,1)S(1)}, bf16[576,768]{1,0:T(8,128)(2,1)S(1)}, u32[]{:S(2)}, u32[]{:S(2)}) collective-permute-start(bf16[576,768]{1,0:T(8,128)(2,1)S(1)} %copy-done.1), channel_id=1, source_target_pairs={{0,1},{1,0},{2,3},{3,2},{4,5},{5,4},{6,7},{7,6},{8,9},{9,8},{10,11... | collective-permute-start | bytes 2654216 | tf_op jit(solution)/shard_map/ppermute | solution.py:656
  102.3 12.9 %copy-start.7 = (bf16[768,128]{1,0:T(8,128)(2,1)S(1)}, bf16[768,128]{1,0:T(8,128)(2,1)}, u32[]{:S(2)}) copy-start(bf16[768,128]{1,0:T(8,128)(2,1)} %refs_1_.1) | copy-start | bytes 589828
  102.3 23.1 %copy-start.8 = (bf16[4,128,128]{2,1,0:T(8,128)(2,1)S(1)}, bf16[4,128,128]{2,1,0:T(8,128)(2,1)}, u32[]{:S(2)}) copy-start(bf16[4,128,128]{2,1,0:T(8,128)(2,1)} %w_in.7) | copy-start | bytes 393220
  102.3 23.1 %copy-start.9 = (bf16[128,128]{1,0:T(8,128)(2,1)S(1)}, bf16[128,128]{1,0:T(8,128)(2,1)}, u32[]{:S(2)}) copy-start(bf16[128,128]{1,0:T(8,128)(2,1)} %w_out.7) | copy-start | bytes 98308
  102.3 23.1 %copy-start.12 = (bf16[3,128]{1,0:T(4,128)(2,1)S(1)}, bf16[3,128]{1,0:T(4,128)(2,1)}, u32[]{:S(2)}) copy-start(bf16[3,128]{1,0:T(4,128)(2,1)} %pos.1) | copy-start | bytes 2308
  102.3 4.9 %collective-permute-start.18 = (bf16[288,768]{1,0:T(8,128)(2,1)}, bf16[288,768]{1,0:T(8,128)(2,1)S(1)}, u32[]{:S(2)}, u32[]{:S(2)}) collective-permute-start(bf16[288,768]{1,0:T(8,128)(2,1)} %collective-permute-done.10.refs_3_), channel_id=1, source_target_pairs={{0,1},{1,0},{2,3},{3,2},{4,5},{5,4},{6,7},{7,6},{8,9},{9,8},{10,11... | collective-permute-start | bytes 1327112 | tf_op jit(solution)/shard_map/ppermute | solution.py:682
  102.4 4.9 %collective-permute-start.19 = (bf16[288,768]{1,0:T(8,128)(2,1)S(1)}, bf16[288,768]{1,0:T(8,128)(2,1)S(1)}, u32[]{:S(2)}, u32[]{:S(2)}) collective-permute-start(bf16[288,768]{1,0:T(8,128)(2,1)S(1)} %collective-permute-done.15.refs_4_), channel_id=1, source_target_pairs={{0,1},{1,0},{2,3},{3,2},{4,5},{5,4},{6,7},{7,6},{8,9},{9,8},{10,11... | collective-permute-start | bytes 1327112 | tf_op jit(solution)/shard_map/ppermute | solution.py:682
  102.9 4.4 %collective-permute-start.16 = (f32[24,768]{1,0:T(8,128)S(1)}, f32[24,768]{1,0:T(8,128)S(1)}, u32[]{:S(2)}, u32[]{:S(2)}) collective-permute-start(f32[24,768]{1,0:T(8,128)S(1)} %shard_map.185.act_ref), channel_id=1, source_target_pairs={{0,4},{1,5},{2,6},{3,7},{4,0},{5,1},{6,2},{7,3},{8,12},{9,13},{10,... | collective-permute-start | bytes 221192 | tf_op jit(solution)/shard_map/ppermute | solution.py:680
  110.7 4.4 %collective-permute-start.20 = (bf16[48,768]{1,0:T(8,128)(2,1)S(1)}, bf16[48,768]{1,0:T(8,128)(2,1)S(1)}, u32[]{:S(2)}, u32[]{:S(2)}) collective-permute-start(bf16[48,768]{1,0:T(8,128)(2,1)S(1)} %get-tuple-element.125), channel_id=1, source_target_pairs={{0,4},{1,5},{2,6},{3,7},{4,0},{5,1},{6,2},{7,3},{8,12},{9,13},{10,... | collective-permute-start | bytes 221192 | tf_op jit(solution)/shard_map/ppermute | solution.py:686
  116.0 3.1 %collective-permute-start.21 = (bf16[48,128]{1,0:T(8,128)(2,1)S(1)}, bf16[48,128]{1,0:T(8,128)(2,1)S(1)}, u32[]{:S(2)}, u32[]{:S(2)}) collective-permute-start(bf16[48,128]{1,0:T(8,128)(2,1)S(1)} %get-tuple-element.126), channel_id=1, source_target_pairs={{0,3},{1,2},{2,1},{3,0},{4,7},{5,6},{6,5},{7,4},{8,11},{9,10},{10,... | collective-permute-start | bytes 36872 | tf_op jit(solution)/shard_map/ppermute | solution.py:472
  116.0 3.7 %collective-permute-start.22 = (bf16[48,128]{1,0:T(8,128)(2,1)S(1)}, bf16[48,128]{1,0:T(8,128)(2,1)S(1)}, u32[]{:S(2)}, u32[]{:S(2)}) collective-permute-start(bf16[48,128]{1,0:T(8,128)(2,1)S(1)} %get-tuple-element.126), channel_id=1, source_target_pairs={{0,2},{1,3},{2,0},{3,1},{4,6},{5,7},{6,4},{7,5},{8,10},{9,11},{10,... | collective-permute-start | bytes 36872 | tf_op jit(solution)/shard_map/ppermute | solution.py:472
  116.6 3.1 %collective-permute-start.23 = (bf16[48,128]{1,0:T(8,128)(2,1)S(1)}, bf16[48,128]{1,0:T(8,128)(2,1)S(1)}, u32[]{:S(2)}, u32[]{:S(2)}) collective-permute-start(bf16[48,128]{1,0:T(8,128)(2,1)S(1)} %get-tuple-element.126), channel_id=1, source_target_pairs={{0,1},{1,0},{2,3},{3,2},{4,5},{5,4},{6,7},{7,6},{8,9},{9,8},{10,11... | collective-permute-start | bytes 36872 | tf_op jit(solution)/shard_map/ppermute | solution.py:472
  119.8 5.6 %collective-permute-start.24 = (bf16[64,128]{1,0:T(8,128)(2,1)S(1)}, bf16[64,128]{1,0:T(8,128)(2,1)S(1)}, u32[]{:S(2)}, u32[]{:S(2)}) collective-permute-start(bf16[64,128]{1,0:T(8,128)(2,1)S(1)} %slice_select_fusion), channel_id=1, source_target_pairs={{0,8},{8,16},{16,24},{15,7},{23,15},{31,23}} | collective-permute-start | bytes 49160 | tf_op jit(solution)/shard_map/ppermute | solution.py:697
  (1 other events, 0.7 us)

commit v9 on v8

--- a/solution.py
+++ b/solution.py
@@ -208,16 +208,17 @@
     own[rows:] = tail.astype(F32).astype(BF16)
 
 
-def pack_kernel(first, second, *outs):
+def pack_kernel(cuts, first, second, *outs):
     hid = second.shape[1]
-    part = 3 * hid // 2
-    for layer in range(BLOCKS):
-        whole, upper, lower = outs[3 * layer : 3 * layer + 3]
+    outs = list(outs)
+    for layer, cut in enumerate(cuts):
+        whole = outs.pop(0)
         whole[:hid] = first[layer, 0]
         whole[hid : 2 * hid] = first[layer, 1]
         whole[2 * hid :] = second[layer]
-        upper[...] = whole[:part]
-        lower[...] = whole[part:]
+        size = 3 * hid // cut
+        for k in range(cut):
+            outs.pop(0)[...] = whole[k * size : (k + 1) * size]
 
 
 def bias_kernel(pair_ref, weight, *outs):
@@ -544,17 +545,25 @@
         (feat, jnp.swapaxes(trans_in, 2, 3), trans_out)
     )
     matrix = jax.ShapeDtypeStruct((3 * hid, width), BF16)
-    half = jax.ShapeDtypeStruct((3 * hid // 2, width), BF16)
+    cuts = (3, 2)
     pieces = call(
-        pack_kernel,
-        [matrix, half, half] * BLOCKS,
+        functools.partial(pack_kernel, cuts),
+        [
+            jax.ShapeDtypeStruct((3 * hid // parts, width), BF16)
+            for cut in cuts
+            for parts in [1] + [cut] * cut
+        ],
         first_part,
         second_part,
         grant=60,
         moved=12 * trans_out.size,
     )
-    packed, upper, lower = pieces[::3], pieces[1::3], pieces[2::3]
-    prev, after, early = lax.optimization_barrier((prev, after, upper[0]))
+    packed, cut_up = [], []
+    for cut in cuts:
+        packed.append(pieces[0])
+        cut_up.append(pieces[1 : 1 + cut])
+        pieces = pieces[1 + cut :]
+    prev, after, early = lax.optimization_barrier((prev, after, cut_up[0][0]))
     neighbour = [(i, i ^ 2) for i in range(count)]
     sibling = [(i, i ^ 1) for i in range(count)]
     across = [[lax.ppermute(early, everyone, neighbour)], []]
@@ -574,18 +583,17 @@
         moved=10**6,
     )
     span = -(-cols // 128) * 128
-    half = rows // 2
     step = 24
+    early_steps = rows // step * 5 // 8
 
     def bias_of(part, weights):
+        begin, end = ((0, early_steps), (early_steps, rows // step))[part]
         return pl.pallas_call(
             bias_kernel,
-            grid=(half // step,),
-            out_shape=[jax.ShapeDtypeStruct((half, heads, span), F32)] * BLOCKS,
+            grid=(end - begin,),
+            out_shape=[jax.ShapeDtypeStruct(((end - begin) * step, heads, span), F32)] * BLOCKS,
             in_specs=[
-                pl.BlockSpec(
-                    (step, cols, pair.shape[2]), lambda i: (i + part * (half // step), 0, 0)
-                ),
+                pl.BlockSpec((step, cols, pair.shape[2]), lambda i: (i + begin, 0, 0)),
                 pl.BlockSpec(weights.shape, lambda i: (0, 0)),
             ],
             out_specs=[pl.BlockSpec((step, heads, span), lambda i: (i, 0, 0))] * BLOCKS,
@@ -649,13 +657,12 @@
         )
         if not layer:
             high = list(bias_of(1, weights))
-            high[0], late, *ready = lax.optimization_barrier(
-                (high[0], lower[0], *packed)
-            )
-            across[0].append(lax.ppermute(late, everyone, neighbour))
+            high[0], *late = lax.optimization_barrier((high[0], *cut_up[0][1:]))
+            across[0] += [lax.ppermute(part, everyone, neighbour) for part in late]
+            high[0], *ready = lax.optimization_barrier((high[0], *packed))
             beside = [lax.ppermute(part, everyone, sibling) for part in ready]
         else:
-            query, late = lax.optimization_barrier((query, lower[1]))
+            query, late = lax.optimization_barrier((query, cut_up[1][1]))
             across[1].append(lax.ppermute(late, everyone, neighbour))
         message = call(
             attention_kernel,
@@ -674,7 +681,7 @@
         )
         message = lax.all_to_all(message.reshape(ncol, own, -1), "col", 0, 0)
         if not layer:
-            message, ready = lax.optimization_barrier((message, upper[1]))
+            message, ready = lax.optimization_barrier((message, cut_up[1][0]))
             across[1].append(lax.ppermute(ready, everyone, neighbour))
         act = mix(layer, message, act, gate, tok_out, heads)
         came_rows = [lax.ppermute(act, everyone, shifts[d]) for d in range(1, peers)]

time: 128 us -> 132 us (1.031)
  blocking collectives: 22.2 us -> 11.3 us
  waiting for transfers between devices: 33.4 us -> 44.3 us
  starting transfers between devices: 28.8 us -> 33.1 us
    all_to_all x2 -> x1, blocking collectives: 22.2 us -> 11.3 us  [body(): message = lax.all_to_all(message.reshape(ncol, own, -1), 'col', 0, 0)]
    ppermute x1 -> x2, waiting for transfers between devices: 0.01 us -> 9.65 us  [body(): across[0] += [lax.ppermute(part, everyone, neighbour) for part in late]]
    all_to_all x0 -> x1, waiting for transfers between devices: none -> 6.02 us  [body(): message = lax.all_to_all(message.reshape(ncol, own, -1), 'col', 0, 0)]
    all_to_all x0 -> x1, starting transfers between devices: none -> 4.57 us  [body(): message = lax.all_to_all(message.reshape(ncol, own, -1), 'col', 0, 0)]
    ppermute x2, waiting for transfers between devices: 7.58 us -> 3.79 us  [body(): lax.ppermute(act, everyone, shifts[d])]
    all_to_all x1, waiting for transfers between devices: 4.39 us -> 1.58 us  [body(): both = lax.all_to_all(copies, 'col', 0, 0)]
    ppermute x4 -> x5, waiting for transfers between devices: 0.01 us -> 2.12 us  [body(): beyond[layer] = [lax.ppermute(part, everyone, sibling) for part in ready]]
    ppermute x2, waiting for transfers between devices: 3.25 us -> 4.9 us  [body(): came = lax.ppermute(send, everyone, pairs)]
  transfers between devices with their start and end apart: 26 -> 29, of which waited for: 11 -> 17; matrix products, arithmetic and copies ran while one was open for 0% -> 0% of each run, Pallas kernels for 24% -> 24%
where the time goes in v9:
time: 132 us
  waiting for transfers between devices  44.3 us (34%)
  Pallas kernels  40.1 us (30%)
  starting transfers between devices  33.1 us (25%)
  blocking collectives  11.3 us (9%)
  local copies, waits for them, and re-layouts  2.19 us (2%)
    pallas_call x15, Pallas kernels, call(): pl.pallas_call(kernel, out_shape=outs, in_specs=[smem] * len(scalars) + [...  31.6 us
    all_to_all x1, blocking collectives, body(): message = lax.all_to_all(message.reshape(ncol, own, -1), 'col', 0, 0)  11.3 us
    ppermute x2, waiting for transfers between devices, body(): across[0] += [lax.ppermute(part, everyone, neighbour) for part in late]  9.65 us
    pallas_call x2, Pallas kernels, bias_of(): pl.pallas_call(bias_kernel, grid=(end - begin,), out_shape=[jax.ShapeDtyp...  8.57 us
    ppermute x2, waiting for transfers between devices, body(): parts = [lax.ppermute(part, everyone, shifts[d]) for d in range(1, peers)]  6.73 us
    all_to_all x1, waiting for transfers between devices, body(): message = lax.all_to_all(message.reshape(ncol, own, -1), 'col', 0, 0)  6.02 us
    ppermute x1, starting transfers between devices, body(): after = lax.ppermute(feat, everyone, [(b, a) for a, b in up])  5.44 us
    ppermute x6, waiting for transfers between devices, row_of(): lax.ppermute(mine, ('row', 'col'), [(i, i ^ flip) for i in range(nrow * n...  5.18 us
  transfers between devices with their start and end apart: 29, of which 17 were waited for; matrix products, arithmetic and copies ran while one was open for 0% of the time, Pallas kernels for 24%

profile of v9, /device:TPU:24, one launch (start us, length us, event | category | flops | bytes accessed | tf_op | source)
XLA Modules:
  0.0 131.7 jit_solution(6680592339141248002)
XLA Ops:
  0.0 0.8 copy-done.13
  0.8 0.7 copy-done.16
  1.4 0.7 copy-done.17
  2.6 1.9 %collective-permute-start = (bf16[144,128]{1,0:T(8,128)(2,1)S(1)}, bf16[144,128]{1,0:T(8,128)(2,1)S(1)}, u32[]{:S(2)}, u32[]{:S(2)}) collective-permute-start(bf16[144,128]{1,0:T(8,128)(2,1)S(1)} %shard_map.172.own_ref), channel_id=1, source_target_pairs={{0,1},{1,2},{2,3},{3,4},{4,5},{5,6},{6,7},{7,8},{8,9},{9,10},{10,1... | collective-permute-start | bytes 110600 | tf_op jit(solution)/shard_map/ppermute | solution.py:542
  4.6 5.4 %collective-permute-start.1 = (bf16[144,128]{1,0:T(8,128)(2,1)S(1)}, bf16[144,128]{1,0:T(8,128)(2,1)S(1)}, u32[]{:S(2)}, u32[]{:S(2)}) collective-permute-start(bf16[144,128]{1,0:T(8,128)(2,1)S(1)} %shard_map.172.own_ref), channel_id=1, source_target_pairs={{1,0},{2,1},{3,2},{4,3},{5,4},{6,5},{7,6},{8,7},{9,8},{10,9},{11,1... | collective-permute-start | bytes 110600 | tf_op jit(solution)/shard_map/ppermute | solution.py:543
  10.0 3.3 %shard_map.173 = (bf16[576,768]{1,0:T(8,128)(2,1)}, bf16[192,768]{1,0:T(8,128)(2,1)}, bf16[192,768]{1,0:T(8,128)(2,1)}, bf16[192,768]{1,0:T(8,128)(2,1)}, bf16[5...) custom-call(bf16[2,2,192,768]{3,2,1,0:T(8,128)(2,1)} %bitcast.41, bf16[2,192,768]{2,1,0:T(8,128)(2,1)} %second), custom_call_target="tpu_custom_call" | custom-call | bytes 3538944 | tf_op jit(solution)/shard_map/pallas_call | solution.py:26
  13.4 2.0 %shard_map.174 = (bf16[256,128]{1,0:T(8,128)(2,1)S(1)}, bf16[8,144,128]{2,1,0:T(8,128)(2,1)}) custom-call(bf16[144,128]{1,0:T(8,128)(2,1)S(1)} %shard_map.172.own_ref, bf16[144,128]{1,0:T(8,128)(2,1)S(1)} %collective-permute-done.prev_ref, bf16[144,128]{1,0:T(8,128)(2,1)S(1)} %collective-permute-done.1.next_ref, bf16[4,128,128]{2,1,0:T(8,128)(2,1)S(1)} %copy-done.20, ...), custom_call_target="tpu_custom_call" | custom-call | flops 100000000 | bytes 1000000 | tf_op jit(solution)/shard_map/pallas_call | solution.py:26
  15.5 3.4 %all-to-all-start = ((bf16[8,144,128]{2,1,0:T(8,128)(2,1)}), bf16[8,144,128]{2,1,0:T(8,128)(2,1)S(1)}, u32[]{:S(2)}, u32[]{:S(2)}) async-start(bf16[8,144,128]{2,1,0:T(8,128)(2,1)} %get-tuple-element.77), calls=%async_computation | async-start | bytes 589824 | tf_op jit(solution)/shard_map/all_to_all | solution.py:609
  18.9 5.6 %shard_map.175 = (f32[120,16,128]{2,1,0:T(8,128)}, f32[120,16,128]{2,1,0:T(8,128)}) custom-call(bf16[192,96,128]{2,1,0:T(8,128)(2,1)} %pair_ref.3, bf16[32,128]{1,0:T(8,128)(2,1)} %bitcast.39), custom_call_target="tpu_custom_call" | custom-call | flops 2000000000 | bytes 4000000 | tf_op jit(solution)/shard_map/pallas_call | solution.py:591
  24.5 1.6 %all-to-all-done.both_ref = bf16[8,144,128]{2,1,0:T(8,128)(2,1)S(1)} async-done(((bf16[8,144,128]{2,1,0:T(8,128)(2,1)}), bf16[8,144,128]{2,1,0:T(8,128)(2,1)S(1)}, u32[]{:S(2)}, u32[]{:S(2)}) %all-to-all-start) | async-done | bytes 294944 | tf_op jit(solution)/shard_map/all_to_all | solution.py:609
  26.1 1.3 shard_map.176
  27.5 1.3 collective-permute-start.3
  28.8 3.0 %shard_map.178 = (f32[72,16,128]{2,1,0:T(8,128)S(1)}, f32[72,16,128]{2,1,0:T(8,128)S(1)}) custom-call(bf16[192,96,128]{2,1,0:T(8,128)(2,1)} %pair_ref.3, bf16[32,128]{1,0:T(8,128)(2,1)S(1)} %bitcast.40), custom_call_target="tpu_custom_call" | custom-call | flops 2000000000 | bytes 4000000 | tf_op jit(solution)/shard_map/pallas_call | solution.py:591
  31.8 2.5 %shard_map.177 = (bf16[192,768]{1,0:T(8,128)(2,1)S(1)}, bf16[768,768]{1,0:T(8,128)(2,1)S(1)}, bf16[768,768]{1,0:T(8,128)(2,1)S(1)}, f32[24,768]{1,0:T(8,128)S(1)}) custom-call(bf16[192,768]{1,0:T(8,128)(2,1)S(1)} %get-tuple-element.84.xn_ref, f32[24,768]{1,0:T(8,128)S(1)} %get-tuple-element.85.act_ref, bf16[2,4,768,768]{3,2,1,0:T(8,128)(2,1)} %w_in.6), custom_call_target="tpu_custom_call" | custom-call | flops 226492416 | bytes 4718592 | tf_op jit(solution)/shard_map/pallas_call | solution.py:26
  34.3 2.0 %collective-permute-done.3.came_ref = bf16[96,768]{1,0:T(8,128)(2,1)S(1)} collective-permute-done((bf16[96,768]{1,0:T(8,128)(2,1)S(1)}, bf16[96,768]{1,0:T(8,128)(2,1)S(1)}, u32[]{:S(2)}, u32[]{:S(2)}) %collective-permute-start.3) | collective-permute-done | bytes 147488 | tf_op jit(solution)/shard_map/ppermute | solution.py:640
  36.3 4.1 %shard_map.179 = bf16[192,896]{1,0:T(8,128)(2,1)} custom-call(s32[768]{0:T(1024)S(1)} %copy-done.14, bf16[192,768]{1,0:T(8,128)(2,1)S(1)} %get-tuple-element.86.query, bf16[96,768]{1,0:T(8,128)(2,1)S(1)} %get-tuple-element.87.here_ref, bf16[96,768]{1,0:T(8,128)(2,1)S(1)} %collective-permute-done.3.came_ref, f32[120,16,128]{2,1,0:T(8,128)S(1)} %copy-done.2, ...), custom_call_target="tpu_custom_call" | custom-call | flops 1000000000 | bytes 8000000 | tf_op jit(solution)/shard_map/pallas_call | solution.py:26
  40.4 4.6 %all-to-all-start.1 = ((bf16[8,24,896]{2,1,0:T(8,128)(2,1)}), bf16[8,24,896]{2,1,0:T(8,128)(2,1)S(1)}, u32[]{:S(2)}, u32[]{:S(2)}) async-start(bf16[8,24,896]{2,1,0:T(8,128)(2,1)} %bitcast.4), calls=%async_computation.1 | async-start | bytes 688128 | tf_op jit(solution)/shard_map/all_to_all | solution.py:682
  45.0 2.2 %collective-permute-start.4 = (bf16[192,768]{1,0:T(8,128)(2,1)}, bf16[192,768]{1,0:T(8,128)(2,1)}, u32[]{:S(2)}, u32[]{:S(2)}) collective-permute-start(bf16[192,768]{1,0:T(8,128)(2,1)} %get-tuple-element.103), channel_id=1, source_target_pairs={{0,2},{1,3},{2,0},{3,1},{4,6},{5,7},{6,4},{7,5},{8,10},{9,11},{10,... | collective-permute-start | bytes 884744 | tf_op jit(solution)/shard_map/ppermute | solution.py:661
  47.2 6.0 %all-to-all-done.1.message = bf16[8,24,896]{2,1,0:T(8,128)(2,1)S(1)} async-done(((bf16[8,24,896]{2,1,0:T(8,128)(2,1)}), bf16[8,24,896]{2,1,0:T(8,128)(2,1)S(1)}, u32[]{:S(2)}, u32[]{:S(2)}) %all-to-all-start.1) | async-done | bytes 344096 | tf_op jit(solution)/shard_map/all_to_all | solution.py:682
  53.3 1.0 shard_map.180.act_ref
  54.3 0.7 collective-permute-start.6
  55.5 3.3 %collective-permute-done.4.refs_4_ = bf16[192,768]{1,0:T(8,128)(2,1)} collective-permute-done((bf16[192,768]{1,0:T(8,128)(2,1)}, bf16[192,768]{1,0:T(8,128)(2,1)}, u32[]{:S(2)}, u32[]{:S(2)}) %collective-permute-start.4) | collective-permute-done | bytes 294944 | tf_op jit(solution)/shard_map/ppermute | solution.py:661
  58.8 6.3 %collective-permute-done.5.refs_5_ = bf16[192,768]{1,0:T(8,128)(2,1)} collective-permute-done((bf16[192,768]{1,0:T(8,128)(2,1)}, bf16[192,768]{1,0:T(8,128)(2,1)}, u32[]{:S(2)}, u32[]{:S(2)}) %collective-permute-start.5) | collective-permute-done | bytes 294944 | tf_op jit(solution)/shard_map/ppermute | solution.py:661
  65.7 1.4 %collective-permute-done.8.refs_6_ = bf16[192,768]{1,0:T(8,128)(2,1)S(1)} collective-permute-done((bf16[192,768]{1,0:T(8,128)(2,1)S(1)}, bf16[192,768]{1,0:T(8,128)(2,1)S(1)}, u32[]{:S(2)}, u32[]{:S(2)}) %collective-permute-start.8) | collective-permute-done | bytes 294944 | tf_op jit(solution)/shard_map/ppermute | solution.py:689
  67.8 3.3 %shard_map.181 = (f32[48,768]{1,0:T(8,128)S(1)}, bf16[48,768]{1,0:T(8,128)(2,1)S(1)}) custom-call(f32[24,768]{1,0:T(8,128)S(1)} %shard_map.180.act_ref, f32[24,768]{1,0:T(8,128)S(1)} %collective-permute-done.6.refs_0_, bf16[576,768]{1,0:T(8,128)(2,1)} %get-tuple-element.106.refs_1_, bf16[576,768]{1,0:T(8,128)(2,1)} %collective-permute-done.7.refs_2_, ...), custom_call_target="tpu_custom_call" | custom-call | flops 169869312 | bytes 3538944 | tf_op jit(solution)/shard_map/pallas_call | solution.py:26
  71.1 1.5 %collective-permute-start.11 = (bf16[48,768]{1,0:T(8,128)(2,1)S(1)}, bf16[48,768]{1,0:T(8,128)(2,1)S(1)}, u32[]{:S(2)}, u32[]{:S(2)}) collective-permute-start(bf16[48,768]{1,0:T(8,128)(2,1)S(1)} %get-tuple-element.111), channel_id=1, source_target_pairs={{0,4},{1,5},{2,6},{3,7},{4,0},{5,1},{6,2},{7,3},{8,12},{9,13},{10,... | collective-permute-start | bytes 221192 | tf_op jit(solution)/shard_map/ppermute | solution.py:693
  72.5 2.9 %collective-permute-done.11.refs_0_ = bf16[48,768]{1,0:T(8,128)(2,1)S(1)} collective-permute-done((bf16[48,768]{1,0:T(8,128)(2,1)S(1)}, bf16[48,768]{1,0:T(8,128)(2,1)S(1)}, u32[]{:S(2)}, u32[]{:S(2)}) %collective-permute-start.11) | collective-permute-done | bytes 73760 | tf_op jit(solution)/shard_map/ppermute | solution.py:693
  76.4 1.2 collective-permute-start.15
  77.6 2.1 %collective-permute-done.13 = bf16[48,768]{1,0:T(8,128)(2,1)S(1)} collective-permute-done((bf16[48,768]{1,0:T(8,128)(2,1)S(1)}, bf16[48,768]{1,0:T(8,128)(2,1)S(1)}, u32[]{:S(2)}, u32[]{:S(2)}) %collective-permute-start.13) | collective-permute-done | bytes 73760 | tf_op jit(solution)/shard_map/ppermute | solution.py:473
  79.7 1.2 collective-permute-done.14
  81.0 1.5 %collective-permute-start.16 = (bf16[96,768]{1,0:T(8,128)(2,1)S(1)}, bf16[96,768]{1,0:T(8,128)(2,1)S(1)}, u32[]{:S(2)}, u32[]{:S(2)}) collective-permute-start(bf16[96,768]{1,0:T(8,128)(2,1)S(1)} %constant_dynamic-slice_fusion.here_ref), channel_id=1, source_target_pairs={{0,24},{1,25},{2,16},{3,17},{4,8},{5,9},{10,26},{11,27},{8,2},{9,3... | collective-permute-start | bytes 442376 | tf_op jit(solution)/shard_map/ppermute | solution.py:640
  82.6 2.5 %shard_map.183 = (bf16[192,768]{1,0:T(8,128)(2,1)S(1)}, bf16[768,768]{1,0:T(8,128)(2,1)S(1)}, bf16[768,768]{1,0:T(8,128)(2,1)S(1)}, f32[24,768]{1,0:T(8,128)S(1)}) custom-call(bf16[192,768]{1,0:T(8,128)(2,1)S(1)} %bitcast.34, f32[24,768]{1,0:T(8,128)S(1)} %get-tuple-element.116.act_ref, bf16[2,4,768,768]{3,2,1,0:T(8,128)(2,1)} %w_in.6), custom_call_target="tpu_custom_call" | custom-call | flops 226492416 | bytes 4718592 | tf_op jit(solution)/shard_map/pallas_call | solution.py:26
  85.1 2.6 %collective-permute-start.17 = (bf16[288,768]{1,0:T(8,128)(2,1)S(1)}, bf16[288,768]{1,0:T(8,128)(2,1)S(1)}, u32[]{:S(2)}, u32[]{:S(2)}) collective-permute-start(bf16[288,768]{1,0:T(8,128)(2,1)S(1)} %copy-done.23), channel_id=1, source_target_pairs={{0,2},{1,3},{2,0},{3,1},{4,6},{5,7},{6,4},{7,5},{8,10},{9,11},{10,... | collective-permute-start | bytes 1327112 | tf_op jit(solution)/shard_map/ppermute | solution.py:666
  87.7 2.9 %collective-permute-done.16.came_ref = bf16[96,768]{1,0:T(8,128)(2,1)S(1)} collective-permute-done((bf16[96,768]{1,0:T(8,128)(2,1)S(1)}, bf16[96,768]{1,0:T(8,128)(2,1)S(1)}, u32[]{:S(2)}, u32[]{:S(2)}) %collective-permute-start.16) | collective-permute-done | bytes 147488 | tf_op jit(solution)/shard_map/ppermute | solution.py:640
  90.6 3.5 %shard_map.184 = bf16[192,896]{1,0:T(8,128)(2,1)S(1)} custom-call(s32[768]{0:T(1024)S(1)} %copy-done.14, bf16[192,768]{1,0:T(8,128)(2,1)S(1)} %get-tuple-element.119.query, bf16[96,768]{1,0:T(8,128)(2,1)S(1)} %constant_dynamic-slice_fusion.here_ref, bf16[96,768]{1,0:T(8,128)(2,1)S(1)} %collective-permute-done.16.came_ref, f32[120,16,128]{2,1,0:T(8,128)S(1)} %copy-done.1, ...), custom_call_target="tpu_custom_call" | custom-call | flops 1000000000 | bytes 8000000 | tf_op jit(solution)/shard_map/pallas_call | solution.py:26
  94.1 11.3 %all_to_all.15.message = bf16[8,24,896]{2,1,0:T(8,128)(2,1)S(1)} all-to-all(bf16[8,24,896]{2,1,0:T(8,128)(2,1)S(1)} %bitcast.35), channel_id=1, replica_groups=mesh['row'=4,'col'=8] {'col'}, dimensions={0} | all-to-all | bytes 688128 | tf_op jit(solution)/shard_map/all_to_all | solution.py:682
  105.4 1.0 shard_map.185.act_ref
  107.7 3.8 %collective-permute-done.18.refs_0_ = f32[24,768]{1,0:T(8,128)S(1)} collective-permute-done((f32[24,768]{1,0:T(8,128)S(1)}, f32[24,768]{1,0:T(8,128)S(1)}, u32[]{:S(2)}, u32[]{:S(2)}) %collective-permute-start.18) | collective-permute-done | bytes 73760 | tf_op jit(solution)/shard_map/ppermute | solution.py:687
  111.5 3.5 %shard_map.186 = (f32[48,768]{1,0:T(8,128)S(1)}, bf16[48,768]{1,0:T(8,128)(2,1)S(1)}) custom-call(f32[24,768]{1,0:T(8,128)S(1)} %shard_map.185.act_ref, f32[24,768]{1,0:T(8,128)S(1)} %collective-permute-done.18.refs_0_, bf16[576,768]{1,0:T(8,128)(2,1)S(1)} %copy-done.3, bf16[576,768]{1,0:T(8,128)(2,1)S(1)} %collective-permute-done.19.refs_2_, ...), custom_call_target="tpu_custom_call" | custom-call | flops 169869312 | bytes 3538944 | tf_op jit(solution)/shard_map/pallas_call | solution.py:26
  115.0 0.6 collective-permute-start.22
  115.6 3.8 %collective-permute-done.22.refs_0_ = bf16[48,768]{1,0:T(8,128)(2,1)S(1)} collective-permute-done((bf16[48,768]{1,0:T(8,128)(2,1)S(1)}, bf16[48,768]{1,0:T(8,128)(2,1)S(1)}, u32[]{:S(2)}, u32[]{:S(2)}) %collective-permute-start.22) | collective-permute-done | bytes 73760 | tf_op jit(solution)/shard_map/ppermute | solution.py:693
  119.4 0.8 shard_map.187
  120.8 1.3 collective-permute-start.25
  122.1 1.3 collective-permute-done.23
  123.3 0.6 collective-permute-done.24
  124.0 1.3 collective-permute-start.26
  125.3 4.3 %collective-permute-done.26.edge_ref = bf16[64,128]{1,0:T(8,128)(2,1)S(1)} collective-permute-done((bf16[64,128]{1,0:T(8,128)(2,1)S(1)}, bf16[64,128]{1,0:T(8,128)(2,1)S(1)}, u32[]{:S(2)}, u32[]{:S(2)}) %collective-permute-start.26) | collective-permute-done | bytes 16416 | tf_op jit(solution)/shard_map/ppermute | solution.py:704
  129.6 2.0 %shard_map.188 = f32[3,128]{1,0:T(4,128)} custom-call(bf16[256,128]{1,0:T(8,128)(2,1)S(1)} %get-tuple-element.75.x1_ref, bf16[144,128]{1,0:T(8,128)(2,1)S(1)} %shard_map.172.own_ref, bf16[144,128]{1,0:T(8,128)(2,1)S(1)} %copy-done.9, bf16[144,128]{1,0:T(8,128)(2,1)S(1)} %copy-done.11, bf16[192,128]{1,0:T(8,128)(2,1)S(1)} %bitcast.37, ...), custom_call_target="tpu_custom_call" | custom-call | flops 100000000 | bytes 1000000 | tf_op jit(solution)/shard_map/pallas_call | solution.py:26
  (84 shorter events, 5.3 us)
Async XLA Ops:
  2.1 11.3 %copy-start.20 = (bf16[4,128,128]{2,1,0:T(8,128)(2,1)S(1)}, bf16[4,128,128]{2,1,0:T(8,128)(2,1)}, u32[]{:S(2)}) copy-start(bf16[4,128,128]{2,1,0:T(8,128)(2,1)} %w_in.4) | copy-start | bytes 393220
  2.1 11.3 %copy-start.21 = (bf16[128,128]{1,0:T(8,128)(2,1)S(1)}, bf16[128,128]{1,0:T(8,128)(2,1)}, u32[]{:S(2)}) copy-start(bf16[128,128]{1,0:T(8,128)(2,1)} %w_out.4) | copy-start | bytes 98308
  2.6 10.7 %collective-permute-start = (bf16[144,128]{1,0:T(8,128)(2,1)S(1)}, bf16[144,128]{1,0:T(8,128)(2,1)S(1)}, u32[]{:S(2)}, u32[]{:S(2)}) collective-permute-start(bf16[144,128]{1,0:T(8,128)(2,1)S(1)} %shard_map.172.own_ref), channel_id=1, source_target_pairs={{0,1},{1,2},{2,3},{3,4},{4,5},{5,6},{6,7},{7,8},{8,9},{9,10},{10,1... | collective-permute-start | bytes 110600 | tf_op jit(solution)/shard_map/ppermute | solution.py:542
  4.6 8.7 %collective-permute-start.1 = (bf16[144,128]{1,0:T(8,128)(2,1)S(1)}, bf16[144,128]{1,0:T(8,128)(2,1)S(1)}, u32[]{:S(2)}, u32[]{:S(2)}) collective-permute-start(bf16[144,128]{1,0:T(8,128)(2,1)S(1)} %shard_map.172.own_ref), channel_id=1, source_target_pairs={{1,0},{2,1},{3,2},{4,3},{5,4},{6,5},{7,6},{8,7},{9,8},{10,9},{11,1... | collective-permute-start | bytes 110600 | tf_op jit(solution)/shard_map/ppermute | solution.py:543
  13.3 11.2 %copy-start.8 = (bf16[144,128]{1,0:T(8,128)(2,1)}, bf16[144,128]{1,0:T(8,128)(2,1)S(1)}, u32[]{:S(2)}) copy-start(bf16[144,128]{1,0:T(8,128)(2,1)S(1)} %collective-permute-done.prev_ref) | copy-start | bytes 110596
  13.3 11.2 %copy-start.10 = (bf16[144,128]{1,0:T(8,128)(2,1)}, bf16[144,128]{1,0:T(8,128)(2,1)S(1)}, u32[]{:S(2)}) copy-start(bf16[144,128]{1,0:T(8,128)(2,1)S(1)} %collective-permute-done.1.next_ref) | copy-start | bytes 110596
  13.3 12.8 %collective-permute-start.2 = (bf16[192,768]{1,0:T(8,128)(2,1)}, bf16[192,768]{1,0:T(8,128)(2,1)S(1)}, u32[]{:S(2)}, u32[]{:S(2)}) collective-permute-start(bf16[192,768]{1,0:T(8,128)(2,1)} %get-tuple-element.81), channel_id=1, source_target_pairs={{0,2},{1,3},{2,0},{3,1},{4,6},{5,7},{6,4},{7,5},{8,10},{9,11},{10,... | collective-permute-start | bytes 884744 | tf_op jit(solution)/shard_map/ppermute | solution.py:569
  15.5 10.6 %all-to-all-start = ((bf16[8,144,128]{2,1,0:T(8,128)(2,1)}), bf16[8,144,128]{2,1,0:T(8,128)(2,1)S(1)}, u32[]{:S(2)}, u32[]{:S(2)}) async-start(bf16[8,144,128]{2,1,0:T(8,128)(2,1)} %get-tuple-element.77), calls=%async_computation | async-start | bytes 589824 | tf_op jit(solution)/shard_map/all_to_all | solution.py:609
  18.9 7.2 %copy-start.18 = (bf16[192,768]{1,0:T(8,128)(2,1)S(1)}, bf16[192,768]{1,0:T(8,128)(2,1)}, u32[]{:S(2)}) copy-start(bf16[192,768]{1,0:T(8,128)(2,1)} %cond.1) | copy-start | bytes 884740
  18.9 7.2 %copy-start.19 = (bf16[128,768]{1,0:T(8,128)(2,1)S(1)}, bf16[128,768]{1,0:T(8,128)(2,1)}, u32[]{:S(2)}) copy-start(bf16[128,768]{1,0:T(8,128)(2,1)} %weight.1) | copy-start | bytes 589828
  26.1 2.6 %copy-start.22 = (bf16[2,128,16]{1,2,0:T(8,128)(2,1)S(1)}, bf16[2,128,16]{1,2,0:T(8,128)(2,1)}, u32[]{:S(2)}) copy-start(bf16[2,128,16]{1,2,0:T(8,128)(2,1)} %param.29) | copy-start | bytes 24580
  27.5 8.8 %collective-permute-start.3 = (bf16[96,768]{1,0:T(8,128)(2,1)S(1)}, bf16[96,768]{1,0:T(8,128)(2,1)S(1)}, u32[]{:S(2)}, u32[]{:S(2)}) collective-permute-start(bf16[96,768]{1,0:T(8,128)(2,1)S(1)} %get-tuple-element.87.here_ref), channel_id=1, source_target_pairs={{0,24},{1,25},{2,16},{3,17},{4,8},{5,9},{10,26},{11,27},{8,2},{9,3... | collective-permute-start | bytes 442376 | tf_op jit(solution)/shard_map/ppermute | solution.py:640
  31.7 36.1 %collective-permute-start.7 = (bf16[576,768]{1,0:T(8,128)(2,1)}, bf16[576,768]{1,0:T(8,128)(2,1)}, u32[]{:S(2)}, u32[]{:S(2)}) collective-permute-start(bf16[576,768]{1,0:T(8,128)(2,1)} %get-tuple-element.106.refs_1_), channel_id=1, source_target_pairs={{0,1},{1,0},{2,3},{3,2},{4,5},{5,4},{6,7},{7,6},{8,9},{9,8},{10,11... | collective-permute-start | bytes 2654216 | tf_op jit(solution)/shard_map/ppermute | solution.py:663
  31.8 4.5 %copy-start.2 = (f32[120,16,128]{2,1,0:T(8,128)S(1)}, f32[120,16,128]{2,1,0:T(8,128)}, u32[]{:S(2)}) copy-start(f32[120,16,128]{2,1,0:T(8,128)} %get-tuple-element.88.low) | copy-start | bytes 2949124
  31.8 4.5 %copy-start.14 = (s32[768]{0:T(1024)S(1)}, s32[768]{0:T(1024)}, u32[]{:S(2)}) copy-start(s32[768]{0:T(1024)} %mask_ref.3) | copy-start | bytes 9220
  36.3 17.0 %copy-start = (bf16[2,768,768]{2,1,0:T(8,128)(2,1)S(1)}, bf16[2,768,768]{2,1,0:T(8,128)(2,1)}, u32[]{:S(2)}) copy-start(bf16[2,768,768]{2,1,0:T(8,128)(2,1)} %w_out.6) | copy-start | bytes 7077892
  40.4 12.9 %all-to-all-start.1 = ((bf16[8,24,896]{2,1,0:T(8,128)(2,1)}), bf16[8,24,896]{2,1,0:T(8,128)(2,1)S(1)}, u32[]{:S(2)}, u32[]{:S(2)}) async-start(bf16[8,24,896]{2,1,0:T(8,128)(2,1)} %bitcast.4), calls=%async_computation.1 | async-start | bytes 688128 | tf_op jit(solution)/shard_map/all_to_all | solution.py:682
  45.0 13.9 %collective-permute-start.4 = (bf16[192,768]{1,0:T(8,128)(2,1)}, bf16[192,768]{1,0:T(8,128)(2,1)}, u32[]{:S(2)}, u32[]{:S(2)}) collective-permute-start(bf16[192,768]{1,0:T(8,128)(2,1)} %get-tuple-element.103), channel_id=1, source_target_pairs={{0,2},{1,3},{2,0},{3,1},{4,6},{5,7},{6,4},{7,5},{8,10},{9,11},{10,... | collective-permute-start | bytes 884744 | tf_op jit(solution)/shard_map/ppermute | solution.py:661
  47.2 18.0 %collective-permute-start.5 = (bf16[192,768]{1,0:T(8,128)(2,1)}, bf16[192,768]{1,0:T(8,128)(2,1)}, u32[]{:S(2)}, u32[]{:S(2)}) collective-permute-start(bf16[192,768]{1,0:T(8,128)(2,1)} %get-tuple-element.104), channel_id=1, source_target_pairs={{0,2},{1,3},{2,0},{3,1},{4,6},{5,7},{6,4},{7,5},{8,10},{9,11},{10,... | collective-permute-start | bytes 884744 | tf_op jit(solution)/shard_map/ppermute | solution.py:661
  53.3 11.9 %copy-start.5 = (bf16[192,768]{1,0:T(8,128)(2,1)S(1)}, bf16[192,768]{1,0:T(8,128)(2,1)}, u32[]{:S(2)}) copy-start(bf16[192,768]{1,0:T(8,128)(2,1)} %copy-done.4) | copy-start | bytes 884740
  54.3 11.4 %collective-permute-start.6 = (f32[24,768]{1,0:T(8,128)S(1)}, f32[24,768]{1,0:T(8,128)S(1)}, u32[]{:S(2)}, u32[]{:S(2)}) collective-permute-start(f32[24,768]{1,0:T(8,128)S(1)} %shard_map.180.act_ref), channel_id=1, source_target_pairs={{0,4},{1,5},{2,6},{3,7},{4,0},{5,1},{6,2},{7,3},{8,12},{9,13},{10,... | collective-permute-start | bytes 221192 | tf_op jit(solution)/shard_map/ppermute | solution.py:687
  55.0 20.7 %collective-permute-start.12 = (bf16[288,768]{1,0:T(8,128)(2,1)S(1)}, bf16[288,768]{1,0:T(8,128)(2,1)}, u32[]{:S(2)}, u32[]{:S(2)}) collective-permute-start(bf16[288,768]{1,0:T(8,128)(2,1)S(1)} %copy-done.24), channel_id=1, source_target_pairs={{0,2},{1,3},{2,0},{3,1},{4,6},{5,7},{6,4},{7,5},{8,10},{9,11},{10,... | collective-permute-start | bytes 1327112 | tf_op jit(solution)/shard_map/ppermute | solution.py:685
  65.2 2.0 %collective-permute-start.8 = (bf16[192,768]{1,0:T(8,128)(2,1)S(1)}, bf16[192,768]{1,0:T(8,128)(2,1)S(1)}, u32[]{:S(2)}, u32[]{:S(2)}) collective-permute-start(bf16[192,768]{1,0:T(8,128)(2,1)S(1)} %copy-done.5), channel_id=1, source_target_pairs={{0,1},{1,0},{2,3},{3,2},{4,5},{5,4},{6,7},{7,6},{8,9},{9,8},{10,11... | collective-permute-start | bytes 884744 | tf_op jit(solution)/shard_map/ppermute | solution.py:689
  65.2 2.2 %collective-permute-start.9 = (bf16[192,768]{1,0:T(8,128)(2,1)}, bf16[192,768]{1,0:T(8,128)(2,1)S(1)}, u32[]{:S(2)}, u32[]{:S(2)}) collective-permute-start(bf16[192,768]{1,0:T(8,128)(2,1)} %collective-permute-done.4.refs_4_), channel_id=1, source_target_pairs={{0,1},{1,0},{2,3},{3,2},{4,5},{5,4},{6,7},{7,6},{8,9},{9,8},{10,11... | collective-permute-start | bytes 884744 | tf_op jit(solution)/shard_map/ppermute | solution.py:689
  65.7 2.1 %collective-permute-start.10 = (bf16[192,768]{1,0:T(8,128)(2,1)}, bf16[192,768]{1,0:T(8,128)(2,1)S(1)}, u32[]{:S(2)}, u32[]{:S(2)}) collective-permute-start(bf16[192,768]{1,0:T(8,128)(2,1)} %collective-permute-done.5.refs_5_), channel_id=1, source_target_pairs={{0,1},{1,0},{2,3},{3,2},{4,5},{5,4},{6,7},{7,6},{8,9},{9,8},{10,11... | collective-permute-start | bytes 884744 | tf_op jit(solution)/shard_map/ppermute | solution.py:689
  71.1 4.4 %collective-permute-start.11 = (bf16[48,768]{1,0:T(8,128)(2,1)S(1)}, bf16[48,768]{1,0:T(8,128)(2,1)S(1)}, u32[]{:S(2)}, u32[]{:S(2)}) collective-permute-start(bf16[48,768]{1,0:T(8,128)(2,1)S(1)} %get-tuple-element.111), channel_id=1, source_target_pairs={{0,4},{1,5},{2,6},{3,7},{4,0},{5,1},{6,2},{7,3},{8,12},{9,13},{10,... | collective-permute-start | bytes 221192 | tf_op jit(solution)/shard_map/ppermute | solution.py:693
  75.7 4.0 %collective-permute-start.13 = (bf16[48,768]{1,0:T(8,128)(2,1)S(1)}, bf16[48,768]{1,0:T(8,128)(2,1)S(1)}, u32[]{:S(2)}, u32[]{:S(2)}) collective-permute-start(bf16[48,768]{1,0:T(8,128)(2,1)S(1)} %get-tuple-element.114), channel_id=1, source_target_pairs={{0,3},{1,2},{2,1},{3,0},{4,7},{5,6},{6,5},{7,4},{8,11},{9,10},{10,... | collective-permute-start | bytes 221192 | tf_op jit(solution)/shard_map/ppermute | solution.py:473
  75.8 5.2 %collective-permute-start.14 = (bf16[48,768]{1,0:T(8,128)(2,1)S(1)}, bf16[48,768]{1,0:T(8,128)(2,1)S(1)}, u32[]{:S(2)}, u32[]{:S(2)}) collective-permute-start(bf16[48,768]{1,0:T(8,128)(2,1)S(1)} %get-tuple-element.114), channel_id=1, source_target_pairs={{0,2},{1,3},{2,0},{3,1},{4,6},{5,7},{6,4},{7,5},{8,10},{9,11},{10,... | collective-permute-start | bytes 221192 | tf_op jit(solution)/shard_map/ppermute | solution.py:473
  76.4 4.6 %collective-permute-start.15 = (bf16[48,768]{1,0:T(8,128)(2,1)S(1)}, bf16[48,768]{1,0:T(8,128)(2,1)S(1)}, u32[]{:S(2)}, u32[]{:S(2)}) collective-permute-start(bf16[48,768]{1,0:T(8,128)(2,1)S(1)} %get-tuple-element.114), channel_id=1, source_target_pairs={{0,1},{1,0},{2,3},{3,2},{4,5},{5,4},{6,7},{7,6},{8,9},{9,8},{10,11... | collective-permute-start | bytes 221192 | tf_op jit(solution)/shard_map/ppermute | solution.py:473
  81.0 9.6 %collective-permute-start.16 = (bf16[96,768]{1,0:T(8,128)(2,1)S(1)}, bf16[96,768]{1,0:T(8,128)(2,1)S(1)}, u32[]{:S(2)}, u32[]{:S(2)}) collective-permute-start(bf16[96,768]{1,0:T(8,128)(2,1)S(1)} %constant_dynamic-slice_fusion.here_ref), channel_id=1, source_target_pairs={{0,24},{1,25},{2,16},{3,17},{4,8},{5,9},{10,26},{11,27},{8,2},{9,3... | collective-permute-start | bytes 442376 | tf_op jit(solution)/shard_map/ppermute | solution.py:640
  82.5 5.2 %copy-start.3 = (bf16[576,768]{1,0:T(8,128)(2,1)S(1)}, bf16[576,768]{1,0:T(8,128)(2,1)}, u32[]{:S(2)}) copy-start(bf16[576,768]{1,0:T(8,128)(2,1)} %get-tuple-element.129.refs_1_) | copy-start | bytes 2654212
  82.5 8.1 %copy-start.1 = (f32[120,16,128]{2,1,0:T(8,128)S(1)}, f32[120,16,128]{2,1,0:T(8,128)}, u32[]{:S(2)}) copy-start(f32[120,16,128]{2,1,0:T(8,128)} %get-tuple-element.121.low) | copy-start | bytes 2949124
  85.1 21.4 %collective-permute-start.17 = (bf16[288,768]{1,0:T(8,128)(2,1)S(1)}, bf16[288,768]{1,0:T(8,128)(2,1)S(1)}, u32[]{:S(2)}, u32[]{:S(2)}) collective-permute-start(bf16[288,768]{1,0:T(8,128)(2,1)S(1)} %copy-done.23), channel_id=1, source_target_pairs={{0,2},{1,3},{2,0},{3,1},{4,6},{5,7},{6,4},{7,5},{8,10},{9,11},{10,... | collective-permute-start | bytes 1327112 | tf_op jit(solution)/shard_map/ppermute | solution.py:666
  87.7 20.0 %collective-permute-start.19 = (bf16[576,768]{1,0:T(8,128)(2,1)S(1)}, bf16[576,768]{1,0:T(8,128)(2,1)S(1)}, u32[]{:S(2)}, u32[]{:S(2)}) collective-permute-start(bf16[576,768]{1,0:T(8,128)(2,1)S(1)} %copy-done.3), channel_id=1, source_target_pairs={{0,1},{1,0},{2,3},{3,2},{4,5},{5,4},{6,7},{7,6},{8,9},{9,8},{10,11... | collective-permute-start | bytes 2654216 | tf_op jit(solution)/shard_map/ppermute | solution.py:663
  106.5 12.9 %copy-start.6 = (bf16[768,128]{1,0:T(8,128)(2,1)S(1)}, bf16[768,128]{1,0:T(8,128)(2,1)}, u32[]{:S(2)}) copy-start(bf16[768,128]{1,0:T(8,128)(2,1)} %refs_1_.1) | copy-start | bytes 589828
  106.5 23.1 %copy-start.7 = (bf16[4,128,128]{2,1,0:T(8,128)(2,1)S(1)}, bf16[4,128,128]{2,1,0:T(8,128)(2,1)}, u32[]{:S(2)}) copy-start(bf16[4,128,128]{2,1,0:T(8,128)(2,1)} %w_in.7) | copy-start | bytes 393220
  106.5 23.1 %copy-start.9 = (bf16[144,128]{1,0:T(8,128)(2,1)S(1)}, bf16[144,128]{1,0:T(8,128)(2,1)}, u32[]{:S(2)}) copy-start(bf16[144,128]{1,0:T(8,128)(2,1)} %copy-done.8) | copy-start | bytes 110596
  106.5 23.1 %copy-start.11 = (bf16[144,128]{1,0:T(8,128)(2,1)S(1)}, bf16[144,128]{1,0:T(8,128)(2,1)}, u32[]{:S(2)}) copy-start(bf16[144,128]{1,0:T(8,128)(2,1)} %copy-done.10) | copy-start | bytes 110596
  106.5 23.1 %copy-start.12 = (bf16[128,128]{1,0:T(8,128)(2,1)S(1)}, bf16[128,128]{1,0:T(8,128)(2,1)}, u32[]{:S(2)}) copy-start(bf16[128,128]{1,0:T(8,128)(2,1)} %w_out.7) | copy-start | bytes 98308
  106.5 23.1 %copy-start.15 = (bf16[3,128]{1,0:T(4,128)(2,1)S(1)}, bf16[3,128]{1,0:T(4,128)(2,1)}, u32[]{:S(2)}) copy-start(bf16[3,128]{1,0:T(4,128)(2,1)} %pos.1) | copy-start | bytes 2308
  106.5 4.9 %collective-permute-start.20 = (bf16[288,768]{1,0:T(8,128)(2,1)}, bf16[288,768]{1,0:T(8,128)(2,1)S(1)}, u32[]{:S(2)}, u32[]{:S(2)}) collective-permute-start(bf16[288,768]{1,0:T(8,128)(2,1)} %collective-permute-done.12.refs_3_), channel_id=1, source_target_pairs={{0,1},{1,0},{2,3},{3,2},{4,5},{5,4},{6,7},{7,6},{8,9},{9,8},{10,11... | collective-permute-start | bytes 1327112 | tf_op jit(solution)/shard_map/ppermute | solution.py:689
  106.6 4.9 %collective-permute-start.21 = (bf16[288,768]{1,0:T(8,128)(2,1)S(1)}, bf16[288,768]{1,0:T(8,128)(2,1)S(1)}, u32[]{:S(2)}, u32[]{:S(2)}) collective-permute-start(bf16[288,768]{1,0:T(8,128)(2,1)S(1)} %collective-permute-done.17.refs_4_), channel_id=1, source_target_pairs={{0,1},{1,0},{2,3},{3,2},{4,5},{5,4},{6,7},{7,6},{8,9},{9,8},{10,11... | collective-permute-start | bytes 1327112 | tf_op jit(solution)/shard_map/ppermute | solution.py:689
  107.1 4.4 %collective-permute-start.18 = (f32[24,768]{1,0:T(8,128)S(1)}, f32[24,768]{1,0:T(8,128)S(1)}, u32[]{:S(2)}, u32[]{:S(2)}) collective-permute-start(f32[24,768]{1,0:T(8,128)S(1)} %shard_map.185.act_ref), channel_id=1, source_target_pairs={{0,4},{1,5},{2,6},{3,7},{4,0},{5,1},{6,2},{7,3},{8,12},{9,13},{10,... | collective-permute-start | bytes 221192 | tf_op jit(solution)/shard_map/ppermute | solution.py:687
  115.0 4.4 %collective-permute-start.22 = (bf16[48,768]{1,0:T(8,128)(2,1)S(1)}, bf16[48,768]{1,0:T(8,128)(2,1)S(1)}, u32[]{:S(2)}, u32[]{:S(2)}) collective-permute-start(bf16[48,768]{1,0:T(8,128)(2,1)S(1)} %get-tuple-element.133), channel_id=1, source_target_pairs={{0,4},{1,5},{2,6},{3,7},{4,0},{5,1},{6,2},{7,3},{8,12},{9,13},{10,... | collective-permute-start | bytes 221192 | tf_op jit(solution)/shard_map/ppermute | solution.py:693
  120.2 3.1 %collective-permute-start.23 = (bf16[48,128]{1,0:T(8,128)(2,1)S(1)}, bf16[48,128]{1,0:T(8,128)(2,1)S(1)}, u32[]{:S(2)}, u32[]{:S(2)}) collective-permute-start(bf16[48,128]{1,0:T(8,128)(2,1)S(1)} %get-tuple-element.134), channel_id=1, source_target_pairs={{0,3},{1,2},{2,1},{3,0},{4,7},{5,6},{6,5},{7,4},{8,11},{9,10},{10,... | collective-permute-start | bytes 36872 | tf_op jit(solution)/shard_map/ppermute | solution.py:473
  120.2 3.7 %collective-permute-start.24 = (bf16[48,128]{1,0:T(8,128)(2,1)S(1)}, bf16[48,128]{1,0:T(8,128)(2,1)S(1)}, u32[]{:S(2)}, u32[]{:S(2)}) collective-permute-start(bf16[48,128]{1,0:T(8,128)(2,1)S(1)} %get-tuple-element.134), channel_id=1, source_target_pairs={{0,2},{1,3},{2,0},{3,1},{4,6},{5,7},{6,4},{7,5},{8,10},{9,11},{10,... | collective-permute-start | bytes 36872 | tf_op jit(solution)/shard_map/ppermute | solution.py:473
  120.8 3.1 %collective-permute-start.25 = (bf16[48,128]{1,0:T(8,128)(2,1)S(1)}, bf16[48,128]{1,0:T(8,128)(2,1)S(1)}, u32[]{:S(2)}, u32[]{:S(2)}) collective-permute-start(bf16[48,128]{1,0:T(8,128)(2,1)S(1)} %get-tuple-element.134), channel_id=1, source_target_pairs={{0,1},{1,0},{2,3},{3,2},{4,5},{5,4},{6,7},{7,6},{8,9},{9,8},{10,11... | collective-permute-start | bytes 36872 | tf_op jit(solution)/shard_map/ppermute | solution.py:473
  124.0 5.6 %collective-permute-start.26 = (bf16[64,128]{1,0:T(8,128)(2,1)S(1)}, bf16[64,128]{1,0:T(8,128)(2,1)S(1)}, u32[]{:S(2)}, u32[]{:S(2)}) collective-permute-start(bf16[64,128]{1,0:T(8,128)(2,1)S(1)} %slice_select_fusion), channel_id=1, source_target_pairs={{0,8},{8,16},{16,24},{15,7},{23,15},{31,23}} | collective-permute-start | bytes 49160 | tf_op jit(solution)/shard_map/ppermute | solution.py:704
  (6 other events, 7.7 us)

commit v10 on v9

--- a/solution.py
+++ b/solution.py
@@ -216,9 +216,11 @@
         whole[:hid] = first[layer, 0]
         whole[hid : 2 * hid] = first[layer, 1]
         whole[2 * hid :] = second[layer]
-        size = 3 * hid // cut
-        for k in range(cut):
-            outs.pop(0)[...] = whole[k * size : (k + 1) * size]
+        begin = 0
+        for sixths in cut:
+            end = begin + sixths * (3 * hid // 6)
+            outs.pop(0)[...] = whole[begin:end]
+            begin = end
 
 
 def bias_kernel(pair_ref, weight, *outs):
@@ -545,13 +547,13 @@
         (feat, jnp.swapaxes(trans_in, 2, 3), trans_out)
     )
     matrix = jax.ShapeDtypeStruct((3 * hid, width), BF16)
-    cuts = (3, 2)
+    cuts = ((2, 3, 1), (3, 3))
     pieces = call(
         functools.partial(pack_kernel, cuts),
         [
-            jax.ShapeDtypeStruct((3 * hid // parts, width), BF16)
+            jax.ShapeDtypeStruct((sixths * (3 * hid // 6), width), BF16)
             for cut in cuts
-            for parts in [1] + [cut] * cut
+            for sixths in (6,) + cut
         ],
         first_part,
         second_part,
@@ -561,8 +563,8 @@
     packed, cut_up = [], []
     for cut in cuts:
         packed.append(pieces[0])
-        cut_up.append(pieces[1 : 1 + cut])
-        pieces = pieces[1 + cut :]
+        cut_up.append(pieces[1 : 1 + len(cut)])
+        pieces = pieces[1 + len(cut) :]
     prev, after, early = lax.optimization_barrier((prev, after, cut_up[0][0]))
     neighbour = [(i, i ^ 2) for i in range(count)]
     sibling = [(i, i ^ 1) for i in range(count)]

time: 132 us -> 128 us (0.970)
  waiting for transfers between devices: 44.3 us -> 34.8 us
  starting transfers between devices: 33.1 us -> 36.3 us
  local copies, waits for them, and re-layouts: 2.19 us -> 3.85 us
    ppermute x2, waiting for transfers between devices: 9.65 us -> 0.01 us  [body(): across[0] += [lax.ppermute(part, everyone, neighbour) for part in late]]
    ppermute x2, waiting for transfers between devices: 3.79 us -> 6.69 us  [body(): lax.ppermute(act, everyone, shifts[d])]
    ppermute x2, waiting for transfers between devices: 4.9 us -> 2.23 us  [body(): came = lax.ppermute(send, everyone, pairs)]
    ppermute x2, starting transfers between devices: 2.26 us -> 4.57 us  [body(): across[0] += [lax.ppermute(part, everyone, neighbour) for part in late]]
    unnamed x50 -> x58, local copies, waits for them, and re-layouts: 2.17 us -> 3.83 us
  transfers between devices with their start and end apart: 29 -> 29, of which waited for: 17 -> 13; matrix products, arithmetic and copies ran while one was open for 0% -> 0% of each run, Pallas kernels for 24% -> 25%
where the time goes in v10:
time: 128 us; the launch traced here: 127 us
  Pallas kernels  40.2 us (31%)
  starting transfers between devices  36.3 us (28%)
  waiting for transfers between devices  34.8 us (27%)
  blocking collectives  11.7 us (9%)
  local copies, waits for them, and re-layouts  3.85 us (3%)
    pallas_call x15, Pallas kernels, call(): pl.pallas_call(kernel, out_shape=outs, in_specs=[smem] * len(scalars) + [...  31.6 us
    all_to_all x1, blocking collectives, body(): message = lax.all_to_all(message.reshape(ncol, own, -1), 'col', 0, 0)  11.7 us
    pallas_call x2, Pallas kernels, bias_of(): pl.pallas_call(bias_kernel, grid=(end - begin,), out_shape=[jax.ShapeDtyp...  8.61 us
    ppermute x2, waiting for transfers between devices, body(): lax.ppermute(act, everyone, shifts[d])  6.69 us
    ppermute x2, waiting for transfers between devices, body(): parts = [lax.ppermute(part, everyone, shifts[d]) for d in range(1, peers)]  6.52 us
    all_to_all x1, waiting for transfers between devices, body(): message = lax.all_to_all(message.reshape(ncol, own, -1), 'col', 0, 0)  6.1 us
    ppermute x6, waiting for transfers between devices, row_of(): lax.ppermute(mine, ('row', 'col'), [(i, i ^ flip) for i in range(nrow * n...  6.01 us
    ppermute x1, starting transfers between devices, body(): after = lax.ppermute(feat, everyone, [(b, a) for a, b in up])  5.44 us
  transfers between devices with their start and end apart: 29, of which 13 were waited for; matrix products, arithmetic and copies ran while one was open for 0% of the time, Pallas kernels for 25%

profile of v10, /device:TPU:24, one launch (start us, length us, event | category | flops | bytes accessed | tf_op | source)
XLA Modules:
  0.0 127.5 jit_solution(17199089627403911988)
XLA Ops:
  0.0 0.8 copy-done.17
  0.8 0.7 copy-done.20
  1.4 0.7 copy-done.21
  2.6 1.9 %collective-permute-start = (bf16[144,128]{1,0:T(8,128)(2,1)S(1)}, bf16[144,128]{1,0:T(8,128)(2,1)S(1)}, u32[]{:S(2)}, u32[]{:S(2)}) collective-permute-start(bf16[144,128]{1,0:T(8,128)(2,1)S(1)} %shard_map.172.own_ref), channel_id=1, source_target_pairs={{0,1},{1,2},{2,3},{3,4},{4,5},{5,6},{6,7},{7,8},{8,9},{9,10},{10,1... | collective-permute-start | bytes 110600 | tf_op jit(solution)/shard_map/ppermute | solution.py:544
  4.6 5.4 %collective-permute-start.1 = (bf16[144,128]{1,0:T(8,128)(2,1)S(1)}, bf16[144,128]{1,0:T(8,128)(2,1)S(1)}, u32[]{:S(2)}, u32[]{:S(2)}) collective-permute-start(bf16[144,128]{1,0:T(8,128)(2,1)S(1)} %shard_map.172.own_ref), channel_id=1, source_target_pairs={{1,0},{2,1},{3,2},{4,3},{5,4},{6,5},{7,6},{8,7},{9,8},{10,9},{11,1... | collective-permute-start | bytes 110600 | tf_op jit(solution)/shard_map/ppermute | solution.py:545
  10.0 3.3 %shard_map.173 = (bf16[576,768]{1,0:T(8,128)(2,1)}, bf16[192,768]{1,0:T(8,128)(2,1)}, bf16[288,768]{1,0:T(8,128)(2,1)}, bf16[96,768]{1,0:T(8,128)(2,1)}, bf16[57...) custom-call(bf16[2,2,192,768]{3,2,1,0:T(8,128)(2,1)} %bitcast.41, bf16[2,192,768]{2,1,0:T(8,128)(2,1)} %second), custom_call_target="tpu_custom_call" | custom-call | bytes 3538944 | tf_op jit(solution)/shard_map/pallas_call | solution.py:26
  13.4 2.0 %shard_map.174 = (bf16[256,128]{1,0:T(8,128)(2,1)S(1)}, bf16[8,144,128]{2,1,0:T(8,128)(2,1)}) custom-call(bf16[144,128]{1,0:T(8,128)(2,1)S(1)} %shard_map.172.own_ref, bf16[144,128]{1,0:T(8,128)(2,1)S(1)} %collective-permute-done.prev_ref, bf16[144,128]{1,0:T(8,128)(2,1)S(1)} %collective-permute-done.1.next_ref, bf16[4,128,128]{2,1,0:T(8,128)(2,1)S(1)} %copy-done.24, ...), custom_call_target="tpu_custom_call" | custom-call | flops 100000000 | bytes 1000000 | tf_op jit(solution)/shard_map/pallas_call | solution.py:26
  15.5 0.6 copy-done.10
  16.1 3.4 %all-to-all-start = ((bf16[8,144,128]{2,1,0:T(8,128)(2,1)}), bf16[8,144,128]{2,1,0:T(8,128)(2,1)S(1)}, u32[]{:S(2)}, u32[]{:S(2)}) async-start(bf16[8,144,128]{2,1,0:T(8,128)(2,1)} %get-tuple-element.77), calls=%async_computation | async-start | bytes 589824 | tf_op jit(solution)/shard_map/all_to_all | solution.py:611
  19.6 5.6 %shard_map.175 = (f32[120,16,128]{2,1,0:T(8,128)}, f32[120,16,128]{2,1,0:T(8,128)}) custom-call(bf16[192,96,128]{2,1,0:T(8,128)(2,1)} %pair_ref.3, bf16[32,128]{1,0:T(8,128)(2,1)} %bitcast.39), custom_call_target="tpu_custom_call" | custom-call | flops 2000000000 | bytes 4000000 | tf_op jit(solution)/shard_map/pallas_call | solution.py:593
  25.2 1.5 %all-to-all-done.both_ref = bf16[8,144,128]{2,1,0:T(8,128)(2,1)S(1)} async-done(((bf16[8,144,128]{2,1,0:T(8,128)(2,1)}), bf16[8,144,128]{2,1,0:T(8,128)(2,1)S(1)}, u32[]{:S(2)}, u32[]{:S(2)}) %all-to-all-start) | async-done | bytes 294944 | tf_op jit(solution)/shard_map/all_to_all | solution.py:611
  26.8 1.3 %shard_map.176 = (f32[24,768]{1,0:T(8,128)S(1)}, bf16[192,768]{1,0:T(8,128)(2,1)S(1)}, bf16[96,768]{1,0:T(8,128)(2,1)S(1)}) custom-call(bf16[8,144,128]{2,1,0:T(8,128)(2,1)S(1)} %all-to-all-done.both_ref, bf16[128,768]{1,0:T(8,128)(2,1)S(1)} %copy-done.23, bf16[192,768]{1,0:T(8,128)(2,1)S(1)} %copy-done.22), custom_call_target="tpu_custom_call" | custom-call | flops 1000000000 | bytes 1000000 | tf_op jit(solution)/shard_map/pallas_call | solution.py:26
  28.1 1.3 %collective-permute-start.3 = (bf16[96,768]{1,0:T(8,128)(2,1)S(1)}, bf16[96,768]{1,0:T(8,128)(2,1)S(1)}, u32[]{:S(2)}, u32[]{:S(2)}) collective-permute-start(bf16[96,768]{1,0:T(8,128)(2,1)S(1)} %get-tuple-element.87.here_ref), channel_id=1, source_target_pairs={{0,24},{1,25},{2,16},{3,17},{4,8},{5,9},{10,26},{11,27},{8,2},{9,3... | collective-permute-start | bytes 442376 | tf_op jit(solution)/shard_map/ppermute | solution.py:642
  29.4 3.0 %shard_map.178 = (f32[72,16,128]{2,1,0:T(8,128)S(1)}, f32[72,16,128]{2,1,0:T(8,128)S(1)}) custom-call(bf16[192,96,128]{2,1,0:T(8,128)(2,1)} %pair_ref.3, bf16[32,128]{1,0:T(8,128)(2,1)S(1)} %bitcast.40), custom_call_target="tpu_custom_call" | custom-call | flops 2000000000 | bytes 4000000 | tf_op jit(solution)/shard_map/pallas_call | solution.py:593
  32.4 2.4 %collective-permute-start.4 = (bf16[288,768]{1,0:T(8,128)(2,1)}, bf16[288,768]{1,0:T(8,128)(2,1)}, u32[]{:S(2)}, u32[]{:S(2)}) collective-permute-start(bf16[288,768]{1,0:T(8,128)(2,1)} %get-tuple-element.103), channel_id=1, source_target_pairs={{0,2},{1,3},{2,0},{3,1},{4,6},{5,7},{6,4},{7,5},{8,10},{9,11},{10,... | collective-permute-start | bytes 1327112 | tf_op jit(solution)/shard_map/ppermute | solution.py:663
  34.8 2.5 %shard_map.177 = (bf16[192,768]{1,0:T(8,128)(2,1)S(1)}, bf16[768,768]{1,0:T(8,128)(2,1)S(1)}, bf16[768,768]{1,0:T(8,128)(2,1)S(1)}, f32[24,768]{1,0:T(8,128)S(1)}) custom-call(bf16[192,768]{1,0:T(8,128)(2,1)S(1)} %get-tuple-element.84.xn_ref, f32[24,768]{1,0:T(8,128)S(1)} %get-tuple-element.85.act_ref, bf16[2,4,768,768]{3,2,1,0:T(8,128)(2,1)} %w_in.6), custom_call_target="tpu_custom_call" | custom-call | flops 226492416 | bytes 4718592 | tf_op jit(solution)/shard_map/pallas_call | solution.py:26
  37.4 4.2 %shard_map.179 = bf16[192,896]{1,0:T(8,128)(2,1)} custom-call(s32[768]{0:T(1024)S(1)} %copy-done.18, bf16[192,768]{1,0:T(8,128)(2,1)S(1)} %get-tuple-element.86.query, bf16[96,768]{1,0:T(8,128)(2,1)S(1)} %get-tuple-element.87.here_ref, bf16[96,768]{1,0:T(8,128)(2,1)S(1)} %collective-permute-done.3.came_ref, f32[120,16,128]{2,1,0:T(8,128)S(1)} %copy-done.2, ...), custom_call_target="tpu_custom_call" | custom-call | flops 1000000000 | bytes 8000000 | tf_op jit(solution)/shard_map/pallas_call | solution.py:26
  41.6 4.1 %all-to-all-start.1 = ((bf16[8,24,896]{2,1,0:T(8,128)(2,1)}), bf16[8,24,896]{2,1,0:T(8,128)(2,1)S(1)}, u32[]{:S(2)}, u32[]{:S(2)}) async-start(bf16[8,24,896]{2,1,0:T(8,128)(2,1)} %bitcast.4), calls=%async_computation.1 | async-start | bytes 688128 | tf_op jit(solution)/shard_map/all_to_all | solution.py:684
  45.7 2.2 %collective-permute-start.5 = (bf16[96,768]{1,0:T(8,128)(2,1)}, bf16[96,768]{1,0:T(8,128)(2,1)S(1)}, u32[]{:S(2)}, u32[]{:S(2)}) collective-permute-start(bf16[96,768]{1,0:T(8,128)(2,1)} %get-tuple-element.104), channel_id=1, source_target_pairs={{0,2},{1,3},{2,0},{3,1},{4,6},{5,7},{6,4},{7,5},{8,10},{9,11},{10,... | collective-permute-start | bytes 442376 | tf_op jit(solution)/shard_map/ppermute | solution.py:663
  47.9 6.1 %all-to-all-done.1.message = bf16[8,24,896]{2,1,0:T(8,128)(2,1)S(1)} async-done(((bf16[8,24,896]{2,1,0:T(8,128)(2,1)}), bf16[8,24,896]{2,1,0:T(8,128)(2,1)S(1)}, u32[]{:S(2)}, u32[]{:S(2)}) %all-to-all-start.1) | async-done | bytes 344096 | tf_op jit(solution)/shard_map/all_to_all | solution.py:684
  54.0 0.9 copy-done.9
  54.9 1.0 shard_map.180.act_ref
  56.6 1.4 %collective-permute-start.6 = (f32[24,768]{1,0:T(8,128)S(1)}, f32[24,768]{1,0:T(8,128)S(1)}, u32[]{:S(2)}, u32[]{:S(2)}) collective-permute-start(f32[24,768]{1,0:T(8,128)S(1)} %shard_map.180.act_ref), channel_id=1, source_target_pairs={{0,4},{1,5},{2,6},{3,7},{4,0},{5,1},{6,2},{7,3},{8,12},{9,13},{10,... | collective-permute-start | bytes 221192 | tf_op jit(solution)/shard_map/ppermute | solution.py:689
  58.0 2.9 %collective-permute-done.6.refs_0_ = f32[24,768]{1,0:T(8,128)S(1)} collective-permute-done((f32[24,768]{1,0:T(8,128)S(1)}, f32[24,768]{1,0:T(8,128)S(1)}, u32[]{:S(2)}, u32[]{:S(2)}) %collective-permute-start.6) | collective-permute-done | bytes 73760 | tf_op jit(solution)/shard_map/ppermute | solution.py:689
  61.0 1.4 %collective-permute-done.10.refs_8_ = bf16[96,768]{1,0:T(8,128)(2,1)S(1)} collective-permute-done((bf16[96,768]{1,0:T(8,128)(2,1)S(1)}, bf16[96,768]{1,0:T(8,128)(2,1)S(1)}, u32[]{:S(2)}, u32[]{:S(2)}) %collective-permute-start.10) | collective-permute-done | bytes 147488 | tf_op jit(solution)/shard_map/ppermute | solution.py:691
  62.3 3.3 %shard_map.181 = (f32[48,768]{1,0:T(8,128)S(1)}, bf16[48,768]{1,0:T(8,128)(2,1)S(1)}) custom-call(f32[24,768]{1,0:T(8,128)S(1)} %shard_map.180.act_ref, f32[24,768]{1,0:T(8,128)S(1)} %collective-permute-done.6.refs_0_, bf16[576,768]{1,0:T(8,128)(2,1)} %get-tuple-element.106.refs_1_, bf16[576,768]{1,0:T(8,128)(2,1)} %collective-permute-done.7.refs_2_, ...), custom_call_target="tpu_custom_call" | custom-call | flops 169869312 | bytes 3538944 | tf_op jit(solution)/shard_map/pallas_call | solution.py:26
  65.6 1.7 %collective-permute-start.11 = (bf16[48,768]{1,0:T(8,128)(2,1)S(1)}, bf16[48,768]{1,0:T(8,128)(2,1)S(1)}, u32[]{:S(2)}, u32[]{:S(2)}) collective-permute-start(bf16[48,768]{1,0:T(8,128)(2,1)S(1)} %get-tuple-element.111), channel_id=1, source_target_pairs={{0,4},{1,5},{2,6},{3,7},{4,0},{5,1},{6,2},{7,3},{8,12},{9,13},{10,... | collective-permute-start | bytes 221192 | tf_op jit(solution)/shard_map/ppermute | solution.py:695
  67.3 2.7 %collective-permute-done.11.refs_0_ = bf16[48,768]{1,0:T(8,128)(2,1)S(1)} collective-permute-done((bf16[48,768]{1,0:T(8,128)(2,1)S(1)}, bf16[48,768]{1,0:T(8,128)(2,1)S(1)}, u32[]{:S(2)}, u32[]{:S(2)}) %collective-permute-start.11) | collective-permute-done | bytes 73760 | tf_op jit(solution)/shard_map/ppermute | solution.py:695
  70.8 1.5 %collective-permute-start.14 = (bf16[48,768]{1,0:T(8,128)(2,1)S(1)}, bf16[48,768]{1,0:T(8,128)(2,1)S(1)}, u32[]{:S(2)}, u32[]{:S(2)}) collective-permute-start(bf16[48,768]{1,0:T(8,128)(2,1)S(1)} %get-tuple-element.114), channel_id=1, source_target_pairs={{0,2},{1,3},{2,0},{3,1},{4,6},{5,7},{6,4},{7,5},{8,10},{9,11},{10,... | collective-permute-start | bytes 221192 | tf_op jit(solution)/shard_map/ppermute | solution.py:475
  72.3 2.3 %collective-permute-done.13 = bf16[48,768]{1,0:T(8,128)(2,1)S(1)} collective-permute-done((bf16[48,768]{1,0:T(8,128)(2,1)S(1)}, bf16[48,768]{1,0:T(8,128)(2,1)S(1)}, u32[]{:S(2)}, u32[]{:S(2)}) %collective-permute-start.13) | collective-permute-done | bytes 73760 | tf_op jit(solution)/shard_map/ppermute | solution.py:475
  74.5 1.9 %collective-permute-done.14 = bf16[48,768]{1,0:T(8,128)(2,1)S(1)} collective-permute-done((bf16[48,768]{1,0:T(8,128)(2,1)S(1)}, bf16[48,768]{1,0:T(8,128)(2,1)S(1)}, u32[]{:S(2)}, u32[]{:S(2)}) %collective-permute-start.14) | collective-permute-done | bytes 73760 | tf_op jit(solution)/shard_map/ppermute | solution.py:475
  76.5 1.5 %collective-permute-start.16 = (bf16[96,768]{1,0:T(8,128)(2,1)S(1)}, bf16[96,768]{1,0:T(8,128)(2,1)S(1)}, u32[]{:S(2)}, u32[]{:S(2)}) collective-permute-start(bf16[96,768]{1,0:T(8,128)(2,1)S(1)} %constant_dynamic-slice_fusion.here_ref), channel_id=1, source_target_pairs={{0,24},{1,25},{2,16},{3,17},{4,8},{5,9},{10,26},{11,27},{8,2},{9,3... | collective-permute-start | bytes 442376 | tf_op jit(solution)/shard_map/ppermute | solution.py:642
  78.0 2.5 %shard_map.183 = (bf16[192,768]{1,0:T(8,128)(2,1)S(1)}, bf16[768,768]{1,0:T(8,128)(2,1)S(1)}, bf16[768,768]{1,0:T(8,128)(2,1)S(1)}, f32[24,768]{1,0:T(8,128)S(1)}) custom-call(bf16[192,768]{1,0:T(8,128)(2,1)S(1)} %bitcast.34, f32[24,768]{1,0:T(8,128)S(1)} %get-tuple-element.116.act_ref, bf16[2,4,768,768]{3,2,1,0:T(8,128)(2,1)} %w_in.6), custom_call_target="tpu_custom_call" | custom-call | flops 226492416 | bytes 4718592 | tf_op jit(solution)/shard_map/pallas_call | solution.py:26
  80.6 3.3 %collective-permute-start.17 = (bf16[288,768]{1,0:T(8,128)(2,1)S(1)}, bf16[288,768]{1,0:T(8,128)(2,1)S(1)}, u32[]{:S(2)}, u32[]{:S(2)}) collective-permute-start(bf16[288,768]{1,0:T(8,128)(2,1)S(1)} %copy-done.27), channel_id=1, source_target_pairs={{0,2},{1,3},{2,0},{3,1},{4,6},{5,7},{6,4},{7,5},{8,10},{9,11},{10,... | collective-permute-start | bytes 1327112 | tf_op jit(solution)/shard_map/ppermute | solution.py:668
  83.9 2.2 %collective-permute-done.16.came_ref = bf16[96,768]{1,0:T(8,128)(2,1)S(1)} collective-permute-done((bf16[96,768]{1,0:T(8,128)(2,1)S(1)}, bf16[96,768]{1,0:T(8,128)(2,1)S(1)}, u32[]{:S(2)}, u32[]{:S(2)}) %collective-permute-start.16) | collective-permute-done | bytes 147488 | tf_op jit(solution)/shard_map/ppermute | solution.py:642
  86.1 3.5 %shard_map.184 = bf16[192,896]{1,0:T(8,128)(2,1)S(1)} custom-call(s32[768]{0:T(1024)S(1)} %copy-done.18, bf16[192,768]{1,0:T(8,128)(2,1)S(1)} %get-tuple-element.119.query, bf16[96,768]{1,0:T(8,128)(2,1)S(1)} %constant_dynamic-slice_fusion.here_ref, bf16[96,768]{1,0:T(8,128)(2,1)S(1)} %collective-permute-done.16.came_ref, f32[120,16,128]{2,1,0:T(8,128)S(1)} %copy-done.1, ...), custom_call_target="tpu_custom_call" | custom-call | flops 1000000000 | bytes 8000000 | tf_op jit(solution)/shard_map/pallas_call | solution.py:26
  89.6 11.7 %all_to_all.15.message = bf16[8,24,896]{2,1,0:T(8,128)(2,1)S(1)} all-to-all(bf16[8,24,896]{2,1,0:T(8,128)(2,1)S(1)} %bitcast.35), channel_id=1, replica_groups=mesh['row'=4,'col'=8] {'col'}, dimensions={0} | all-to-all | bytes 688128 | tf_op jit(solution)/shard_map/all_to_all | solution.py:684
  101.3 1.0 shard_map.185.act_ref
  103.5 3.8 %collective-permute-done.18.refs_0_ = f32[24,768]{1,0:T(8,128)S(1)} collective-permute-done((f32[24,768]{1,0:T(8,128)S(1)}, f32[24,768]{1,0:T(8,128)S(1)}, u32[]{:S(2)}, u32[]{:S(2)}) %collective-permute-start.18) | collective-permute-done | bytes 73760 | tf_op jit(solution)/shard_map/ppermute | solution.py:689
  107.3 3.5 %shard_map.186 = (f32[48,768]{1,0:T(8,128)S(1)}, bf16[48,768]{1,0:T(8,128)(2,1)S(1)}) custom-call(f32[24,768]{1,0:T(8,128)S(1)} %shard_map.185.act_ref, f32[24,768]{1,0:T(8,128)S(1)} %collective-permute-done.18.refs_0_, bf16[576,768]{1,0:T(8,128)(2,1)S(1)} %copy-done.3, bf16[576,768]{1,0:T(8,128)(2,1)S(1)} %collective-permute-done.19.refs_2_, ...), custom_call_target="tpu_custom_call" | custom-call | flops 169869312 | bytes 3538944 | tf_op jit(solution)/shard_map/pallas_call | solution.py:26
  110.8 0.6 collective-permute-start.22
  111.4 3.8 %collective-permute-done.22.refs_0_ = bf16[48,768]{1,0:T(8,128)(2,1)S(1)} collective-permute-done((bf16[48,768]{1,0:T(8,128)(2,1)S(1)}, bf16[48,768]{1,0:T(8,128)(2,1)S(1)}, u32[]{:S(2)}, u32[]{:S(2)}) %collective-permute-start.22) | collective-permute-done | bytes 73760 | tf_op jit(solution)/shard_map/ppermute | solution.py:695
  115.2 0.8 shard_map.187
  116.6 1.3 collective-permute-start.25
  117.9 1.3 collective-permute-done.23
  119.8 1.3 %collective-permute-start.26 = (bf16[64,128]{1,0:T(8,128)(2,1)S(1)}, bf16[64,128]{1,0:T(8,128)(2,1)S(1)}, u32[]{:S(2)}, u32[]{:S(2)}) collective-permute-start(bf16[64,128]{1,0:T(8,128)(2,1)S(1)} %slice_select_fusion), channel_id=1, source_target_pairs={{0,8},{8,16},{16,24},{15,7},{23,15},{31,23}} | collective-permute-start | bytes 49160 | tf_op jit(solution)/shard_map/ppermute | solution.py:706
  121.1 4.3 %collective-permute-done.26.edge_ref = bf16[64,128]{1,0:T(8,128)(2,1)S(1)} collective-permute-done((bf16[64,128]{1,0:T(8,128)(2,1)S(1)}, bf16[64,128]{1,0:T(8,128)(2,1)S(1)}, u32[]{:S(2)}, u32[]{:S(2)}) %collective-permute-start.26) | collective-permute-done | bytes 16416 | tf_op jit(solution)/shard_map/ppermute | solution.py:706
  125.5 2.0 %shard_map.188 = f32[3,128]{1,0:T(4,128)} custom-call(bf16[256,128]{1,0:T(8,128)(2,1)S(1)} %copy-done.11, bf16[144,128]{1,0:T(8,128)(2,1)S(1)} %shard_map.172.own_ref, bf16[144,128]{1,0:T(8,128)(2,1)S(1)} %copy-done.13, bf16[144,128]{1,0:T(8,128)(2,1)S(1)} %copy-done.15, bf16[192,128]{1,0:T(8,128)(2,1)S(1)} %bitcast.37, ...), custom_call_target="tpu_custom_call" | custom-call | flops 100000000 | bytes 1000000 | tf_op jit(solution)/shard_map/pallas_call | solution.py:26
  (92 shorter events, 4.8 us)
Async XLA Ops:
  2.1 11.3 %copy-start.24 = (bf16[4,128,128]{2,1,0:T(8,128)(2,1)S(1)}, bf16[4,128,128]{2,1,0:T(8,128)(2,1)}, u32[]{:S(2)}) copy-start(bf16[4,128,128]{2,1,0:T(8,128)(2,1)} %w_in.4) | copy-start | bytes 393220
  2.1 11.3 %copy-start.25 = (bf16[128,128]{1,0:T(8,128)(2,1)S(1)}, bf16[128,128]{1,0:T(8,128)(2,1)}, u32[]{:S(2)}) copy-start(bf16[128,128]{1,0:T(8,128)(2,1)} %w_out.4) | copy-start | bytes 98308
  2.6 10.7 %collective-permute-start = (bf16[144,128]{1,0:T(8,128)(2,1)S(1)}, bf16[144,128]{1,0:T(8,128)(2,1)S(1)}, u32[]{:S(2)}, u32[]{:S(2)}) collective-permute-start(bf16[144,128]{1,0:T(8,128)(2,1)S(1)} %shard_map.172.own_ref), channel_id=1, source_target_pairs={{0,1},{1,2},{2,3},{3,4},{4,5},{5,6},{6,7},{7,8},{8,9},{9,10},{10,1... | collective-permute-start | bytes 110600 | tf_op jit(solution)/shard_map/ppermute | solution.py:544
  4.6 8.7 %collective-permute-start.1 = (bf16[144,128]{1,0:T(8,128)(2,1)S(1)}, bf16[144,128]{1,0:T(8,128)(2,1)S(1)}, u32[]{:S(2)}, u32[]{:S(2)}) collective-permute-start(bf16[144,128]{1,0:T(8,128)(2,1)S(1)} %shard_map.172.own_ref), channel_id=1, source_target_pairs={{1,0},{2,1},{3,2},{4,3},{5,4},{6,5},{7,6},{8,7},{9,8},{10,9},{11,1... | collective-permute-start | bytes 110600 | tf_op jit(solution)/shard_map/ppermute | solution.py:545
  13.3 2.8 %copy-start.14 = (bf16[144,128]{1,0:T(8,128)(2,1)}, bf16[144,128]{1,0:T(8,128)(2,1)S(1)}, u32[]{:S(2)}) copy-start(bf16[144,128]{1,0:T(8,128)(2,1)S(1)} %collective-permute-done.1.next_ref) | copy-start | bytes 110596
  13.3 13.4 %collective-permute-start.2 = (bf16[192,768]{1,0:T(8,128)(2,1)}, bf16[192,768]{1,0:T(8,128)(2,1)S(1)}, u32[]{:S(2)}, u32[]{:S(2)}) collective-permute-start(bf16[192,768]{1,0:T(8,128)(2,1)} %get-tuple-element.81), channel_id=1, source_target_pairs={{0,2},{1,3},{2,0},{3,1},{4,6},{5,7},{6,4},{7,5},{8,10},{9,11},{10,... | collective-permute-start | bytes 884744 | tf_op jit(solution)/shard_map/ppermute | solution.py:571
  16.1 10.6 %all-to-all-start = ((bf16[8,144,128]{2,1,0:T(8,128)(2,1)}), bf16[8,144,128]{2,1,0:T(8,128)(2,1)S(1)}, u32[]{:S(2)}, u32[]{:S(2)}) async-start(bf16[8,144,128]{2,1,0:T(8,128)(2,1)} %get-tuple-element.77), calls=%async_computation | async-start | bytes 589824 | tf_op jit(solution)/shard_map/all_to_all | solution.py:611
  19.5 7.2 %copy-start.22 = (bf16[192,768]{1,0:T(8,128)(2,1)S(1)}, bf16[192,768]{1,0:T(8,128)(2,1)}, u32[]{:S(2)}) copy-start(bf16[192,768]{1,0:T(8,128)(2,1)} %cond.1) | copy-start | bytes 884740
  19.6 7.2 %copy-start.23 = (bf16[128,768]{1,0:T(8,128)(2,1)S(1)}, bf16[128,768]{1,0:T(8,128)(2,1)}, u32[]{:S(2)}) copy-start(bf16[128,768]{1,0:T(8,128)(2,1)} %weight.1) | copy-start | bytes 589828
  26.8 2.6 %copy-start.26 = (bf16[2,128,16]{1,2,0:T(8,128)(2,1)S(1)}, bf16[2,128,16]{1,2,0:T(8,128)(2,1)}, u32[]{:S(2)}) copy-start(bf16[2,128,16]{1,2,0:T(8,128)(2,1)} %param.29) | copy-start | bytes 24580
  28.1 9.1 %collective-permute-start.3 = (bf16[96,768]{1,0:T(8,128)(2,1)S(1)}, bf16[96,768]{1,0:T(8,128)(2,1)S(1)}, u32[]{:S(2)}, u32[]{:S(2)}) collective-permute-start(bf16[96,768]{1,0:T(8,128)(2,1)S(1)} %get-tuple-element.87.here_ref), channel_id=1, source_target_pairs={{0,24},{1,25},{2,16},{3,17},{4,8},{5,9},{10,26},{11,27},{8,2},{9,3... | collective-permute-start | bytes 442376 | tf_op jit(solution)/shard_map/ppermute | solution.py:642
  32.4 23.6 %collective-permute-start.4 = (bf16[288,768]{1,0:T(8,128)(2,1)}, bf16[288,768]{1,0:T(8,128)(2,1)}, u32[]{:S(2)}, u32[]{:S(2)}) collective-permute-start(bf16[288,768]{1,0:T(8,128)(2,1)} %get-tuple-element.103), channel_id=1, source_target_pairs={{0,2},{1,3},{2,0},{3,1},{4,6},{5,7},{6,4},{7,5},{8,10},{9,11},{10,... | collective-permute-start | bytes 1327112 | tf_op jit(solution)/shard_map/ppermute | solution.py:663
  34.8 27.6 %collective-permute-start.7 = (bf16[576,768]{1,0:T(8,128)(2,1)}, bf16[576,768]{1,0:T(8,128)(2,1)}, u32[]{:S(2)}, u32[]{:S(2)}) collective-permute-start(bf16[576,768]{1,0:T(8,128)(2,1)} %get-tuple-element.106.refs_1_), channel_id=1, source_target_pairs={{0,1},{1,0},{2,3},{3,2},{4,5},{5,4},{6,7},{7,6},{8,9},{9,8},{10,11... | collective-permute-start | bytes 2654216 | tf_op jit(solution)/shard_map/ppermute | solution.py:665
  34.8 2.6 %copy-start.2 = (f32[120,16,128]{2,1,0:T(8,128)S(1)}, f32[120,16,128]{2,1,0:T(8,128)}, u32[]{:S(2)}) copy-start(f32[120,16,128]{2,1,0:T(8,128)} %get-tuple-element.88.low) | copy-start | bytes 2949124
  34.8 2.6 %copy-start.18 = (s32[768]{0:T(1024)S(1)}, s32[768]{0:T(1024)}, u32[]{:S(2)}) copy-start(s32[768]{0:T(1024)} %mask_ref.3) | copy-start | bytes 9220
  37.2 4.3 %copy-start.8 = (f32[24,768]{1,0:T(8,128)}, f32[24,768]{1,0:T(8,128)S(1)}, u32[]{:S(2)}) copy-start(f32[24,768]{1,0:T(8,128)S(1)} %get-tuple-element.101.gate) | copy-start | bytes 221188
  37.4 16.6 %copy-start = (bf16[2,768,768]{2,1,0:T(8,128)(2,1)S(1)}, bf16[2,768,768]{2,1,0:T(8,128)(2,1)}, u32[]{:S(2)}) copy-start(bf16[2,768,768]{2,1,0:T(8,128)(2,1)} %w_out.6) | copy-start | bytes 7077892
  41.6 12.4 %all-to-all-start.1 = ((bf16[8,24,896]{2,1,0:T(8,128)(2,1)}), bf16[8,24,896]{2,1,0:T(8,128)(2,1)S(1)}, u32[]{:S(2)}, u32[]{:S(2)}) async-start(bf16[8,24,896]{2,1,0:T(8,128)(2,1)} %bitcast.4), calls=%async_computation.1 | async-start | bytes 688128 | tf_op jit(solution)/shard_map/all_to_all | solution.py:684
  45.7 10.2 %collective-permute-start.5 = (bf16[96,768]{1,0:T(8,128)(2,1)}, bf16[96,768]{1,0:T(8,128)(2,1)S(1)}, u32[]{:S(2)}, u32[]{:S(2)}) collective-permute-start(bf16[96,768]{1,0:T(8,128)(2,1)} %get-tuple-element.104), channel_id=1, source_target_pairs={{0,2},{1,3},{2,0},{3,1},{4,6},{5,7},{6,4},{7,5},{8,10},{9,11},{10,... | collective-permute-start | bytes 442376 | tf_op jit(solution)/shard_map/ppermute | solution.py:663
  55.9 6.4 %collective-permute-start.9 = (bf16[288,768]{1,0:T(8,128)(2,1)}, bf16[288,768]{1,0:T(8,128)(2,1)S(1)}, u32[]{:S(2)}, u32[]{:S(2)}) collective-permute-start(bf16[288,768]{1,0:T(8,128)(2,1)} %collective-permute-done.4.refs_4_), channel_id=1, source_target_pairs={{0,1},{1,0},{2,3},{3,2},{4,5},{5,4},{6,7},{7,6},{8,9},{9,8},{10,11... | collective-permute-start | bytes 1327112 | tf_op jit(solution)/shard_map/ppermute | solution.py:691
  56.0 14.2 %collective-permute-start.12 = (bf16[288,768]{1,0:T(8,128)(2,1)S(1)}, bf16[288,768]{1,0:T(8,128)(2,1)}, u32[]{:S(2)}, u32[]{:S(2)}) collective-permute-start(bf16[288,768]{1,0:T(8,128)(2,1)S(1)} %copy-done.28), channel_id=1, source_target_pairs={{0,2},{1,3},{2,0},{3,1},{4,6},{5,7},{6,4},{7,5},{8,10},{9,11},{10,... | collective-permute-start | bytes 1327112 | tf_op jit(solution)/shard_map/ppermute | solution.py:687
  56.2 6.1 %collective-permute-start.8 = (bf16[192,768]{1,0:T(8,128)(2,1)S(1)}, bf16[192,768]{1,0:T(8,128)(2,1)S(1)}, u32[]{:S(2)}, u32[]{:S(2)}) collective-permute-start(bf16[192,768]{1,0:T(8,128)(2,1)S(1)} %copy-done.5), channel_id=1, source_target_pairs={{0,1},{1,0},{2,3},{3,2},{4,5},{5,4},{6,7},{7,6},{8,9},{9,8},{10,11... | collective-permute-start | bytes 884744 | tf_op jit(solution)/shard_map/ppermute | solution.py:691
  56.6 4.4 %collective-permute-start.6 = (f32[24,768]{1,0:T(8,128)S(1)}, f32[24,768]{1,0:T(8,128)S(1)}, u32[]{:S(2)}, u32[]{:S(2)}) collective-permute-start(f32[24,768]{1,0:T(8,128)S(1)} %shard_map.180.act_ref), channel_id=1, source_target_pairs={{0,4},{1,5},{2,6},{3,7},{4,0},{5,1},{6,2},{7,3},{8,12},{9,13},{10,... | collective-permute-start | bytes 221192 | tf_op jit(solution)/shard_map/ppermute | solution.py:689
  61.0 1.4 %collective-permute-start.10 = (bf16[96,768]{1,0:T(8,128)(2,1)S(1)}, bf16[96,768]{1,0:T(8,128)(2,1)S(1)}, u32[]{:S(2)}, u32[]{:S(2)}) collective-permute-start(bf16[96,768]{1,0:T(8,128)(2,1)S(1)} %collective-permute-done.5.refs_5_), channel_id=1, source_target_pairs={{0,1},{1,0},{2,3},{3,2},{4,5},{5,4},{6,7},{7,6},{8,9},{9,8},{10,11... | collective-permute-start | bytes 442376 | tf_op jit(solution)/shard_map/ppermute | solution.py:691
  65.6 4.4 %collective-permute-start.11 = (bf16[48,768]{1,0:T(8,128)(2,1)S(1)}, bf16[48,768]{1,0:T(8,128)(2,1)S(1)}, u32[]{:S(2)}, u32[]{:S(2)}) collective-permute-start(bf16[48,768]{1,0:T(8,128)(2,1)S(1)} %get-tuple-element.111), channel_id=1, source_target_pairs={{0,4},{1,5},{2,6},{3,7},{4,0},{5,1},{6,2},{7,3},{8,12},{9,13},{10,... | collective-permute-start | bytes 221192 | tf_op jit(solution)/shard_map/ppermute | solution.py:695
  70.2 4.3 %collective-permute-start.13 = (bf16[48,768]{1,0:T(8,128)(2,1)S(1)}, bf16[48,768]{1,0:T(8,128)(2,1)S(1)}, u32[]{:S(2)}, u32[]{:S(2)}) collective-permute-start(bf16[48,768]{1,0:T(8,128)(2,1)S(1)} %get-tuple-element.114), channel_id=1, source_target_pairs={{0,3},{1,2},{2,1},{3,0},{4,7},{5,6},{6,5},{7,4},{8,11},{9,10},{10,... | collective-permute-start | bytes 221192 | tf_op jit(solution)/shard_map/ppermute | solution.py:475
  70.8 5.7 %collective-permute-start.14 = (bf16[48,768]{1,0:T(8,128)(2,1)S(1)}, bf16[48,768]{1,0:T(8,128)(2,1)S(1)}, u32[]{:S(2)}, u32[]{:S(2)}) collective-permute-start(bf16[48,768]{1,0:T(8,128)(2,1)S(1)} %get-tuple-element.114), channel_id=1, source_target_pairs={{0,2},{1,3},{2,0},{3,1},{4,6},{5,7},{6,4},{7,5},{8,10},{9,11},{10,... | collective-permute-start | bytes 221192 | tf_op jit(solution)/shard_map/ppermute | solution.py:475
  72.2 4.2 %collective-permute-start.15 = (bf16[48,768]{1,0:T(8,128)(2,1)S(1)}, bf16[48,768]{1,0:T(8,128)(2,1)S(1)}, u32[]{:S(2)}, u32[]{:S(2)}) collective-permute-start(bf16[48,768]{1,0:T(8,128)(2,1)S(1)} %get-tuple-element.114), channel_id=1, source_target_pairs={{0,1},{1,0},{2,3},{3,2},{4,5},{5,4},{6,7},{7,6},{8,9},{9,8},{10,11... | collective-permute-start | bytes 221192 | tf_op jit(solution)/shard_map/ppermute | solution.py:475
  76.5 9.6 %collective-permute-start.16 = (bf16[96,768]{1,0:T(8,128)(2,1)S(1)}, bf16[96,768]{1,0:T(8,128)(2,1)S(1)}, u32[]{:S(2)}, u32[]{:S(2)}) collective-permute-start(bf16[96,768]{1,0:T(8,128)(2,1)S(1)} %constant_dynamic-slice_fusion.here_ref), channel_id=1, source_target_pairs={{0,24},{1,25},{2,16},{3,17},{4,8},{5,9},{10,26},{11,27},{8,2},{9,3... | collective-permute-start | bytes 442376 | tf_op jit(solution)/shard_map/ppermute | solution.py:642
  78.0 5.8 %copy-start.3 = (bf16[576,768]{1,0:T(8,128)(2,1)S(1)}, bf16[576,768]{1,0:T(8,128)(2,1)}, u32[]{:S(2)}) copy-start(bf16[576,768]{1,0:T(8,128)(2,1)} %get-tuple-element.129.refs_1_) | copy-start | bytes 2654212
  78.0 8.1 %copy-start.1 = (f32[120,16,128]{2,1,0:T(8,128)S(1)}, f32[120,16,128]{2,1,0:T(8,128)}, u32[]{:S(2)}) copy-start(f32[120,16,128]{2,1,0:T(8,128)} %get-tuple-element.121.low) | copy-start | bytes 2949124
  80.6 21.8 %collective-permute-start.17 = (bf16[288,768]{1,0:T(8,128)(2,1)S(1)}, bf16[288,768]{1,0:T(8,128)(2,1)S(1)}, u32[]{:S(2)}, u32[]{:S(2)}) collective-permute-start(bf16[288,768]{1,0:T(8,128)(2,1)S(1)} %copy-done.27), channel_id=1, source_target_pairs={{0,2},{1,3},{2,0},{3,1},{4,6},{5,7},{6,4},{7,5},{8,10},{9,11},{10,... | collective-permute-start | bytes 1327112 | tf_op jit(solution)/shard_map/ppermute | solution.py:668
  83.9 19.7 %collective-permute-start.19 = (bf16[576,768]{1,0:T(8,128)(2,1)S(1)}, bf16[576,768]{1,0:T(8,128)(2,1)S(1)}, u32[]{:S(2)}, u32[]{:S(2)}) collective-permute-start(bf16[576,768]{1,0:T(8,128)(2,1)S(1)} %copy-done.3), channel_id=1, source_target_pairs={{0,1},{1,0},{2,3},{3,2},{4,5},{5,4},{6,7},{7,6},{8,9},{9,8},{10,11... | collective-permute-start | bytes 2654216 | tf_op jit(solution)/shard_map/ppermute | solution.py:665
  102.3 12.9 %copy-start.6 = (bf16[768,128]{1,0:T(8,128)(2,1)S(1)}, bf16[768,128]{1,0:T(8,128)(2,1)}, u32[]{:S(2)}) copy-start(bf16[768,128]{1,0:T(8,128)(2,1)} %refs_1_.1) | copy-start | bytes 589828
  102.3 23.1 %copy-start.7 = (bf16[4,128,128]{2,1,0:T(8,128)(2,1)S(1)}, bf16[4,128,128]{2,1,0:T(8,128)(2,1)}, u32[]{:S(2)}) copy-start(bf16[4,128,128]{2,1,0:T(8,128)(2,1)} %w_in.7) | copy-start | bytes 393220
  102.3 23.1 %copy-start.11 = (bf16[256,128]{1,0:T(8,128)(2,1)S(1)}, bf16[256,128]{1,0:T(8,128)(2,1)}, u32[]{:S(2)}) copy-start(bf16[256,128]{1,0:T(8,128)(2,1)} %copy-done.10) | copy-start | bytes 196612
  102.3 23.1 %copy-start.13 = (bf16[144,128]{1,0:T(8,128)(2,1)S(1)}, bf16[144,128]{1,0:T(8,128)(2,1)}, u32[]{:S(2)}) copy-start(bf16[144,128]{1,0:T(8,128)(2,1)} %copy-done.12) | copy-start | bytes 110596
  102.3 23.1 %copy-start.15 = (bf16[144,128]{1,0:T(8,128)(2,1)S(1)}, bf16[144,128]{1,0:T(8,128)(2,1)}, u32[]{:S(2)}) copy-start(bf16[144,128]{1,0:T(8,128)(2,1)} %copy-done.14) | copy-start | bytes 110596
  102.4 23.1 %copy-start.16 = (bf16[128,128]{1,0:T(8,128)(2,1)S(1)}, bf16[128,128]{1,0:T(8,128)(2,1)}, u32[]{:S(2)}) copy-start(bf16[128,128]{1,0:T(8,128)(2,1)} %w_out.7) | copy-start | bytes 98308
  102.4 23.1 %copy-start.19 = (bf16[3,128]{1,0:T(4,128)(2,1)S(1)}, bf16[3,128]{1,0:T(4,128)(2,1)}, u32[]{:S(2)}) copy-start(bf16[3,128]{1,0:T(4,128)(2,1)} %pos.1) | copy-start | bytes 2308
  102.4 4.9 %collective-permute-start.20 = (bf16[288,768]{1,0:T(8,128)(2,1)}, bf16[288,768]{1,0:T(8,128)(2,1)S(1)}, u32[]{:S(2)}, u32[]{:S(2)}) collective-permute-start(bf16[288,768]{1,0:T(8,128)(2,1)} %collective-permute-done.12.refs_3_), channel_id=1, source_target_pairs={{0,1},{1,0},{2,3},{3,2},{4,5},{5,4},{6,7},{7,6},{8,9},{9,8},{10,11... | collective-permute-start | bytes 1327112 | tf_op jit(solution)/shard_map/ppermute | solution.py:691
  102.5 4.9 %collective-permute-start.21 = (bf16[288,768]{1,0:T(8,128)(2,1)S(1)}, bf16[288,768]{1,0:T(8,128)(2,1)S(1)}, u32[]{:S(2)}, u32[]{:S(2)}) collective-permute-start(bf16[288,768]{1,0:T(8,128)(2,1)S(1)} %collective-permute-done.17.refs_4_), channel_id=1, source_target_pairs={{0,1},{1,0},{2,3},{3,2},{4,5},{5,4},{6,7},{7,6},{8,9},{9,8},{10,11... | collective-permute-start | bytes 1327112 | tf_op jit(solution)/shard_map/ppermute | solution.py:691
  103.0 4.4 %collective-permute-start.18 = (f32[24,768]{1,0:T(8,128)S(1)}, f32[24,768]{1,0:T(8,128)S(1)}, u32[]{:S(2)}, u32[]{:S(2)}) collective-permute-start(f32[24,768]{1,0:T(8,128)S(1)} %shard_map.185.act_ref), channel_id=1, source_target_pairs={{0,4},{1,5},{2,6},{3,7},{4,0},{5,1},{6,2},{7,3},{8,12},{9,13},{10,... | collective-permute-start | bytes 221192 | tf_op jit(solution)/shard_map/ppermute | solution.py:689
  110.8 4.4 %collective-permute-start.22 = (bf16[48,768]{1,0:T(8,128)(2,1)S(1)}, bf16[48,768]{1,0:T(8,128)(2,1)S(1)}, u32[]{:S(2)}, u32[]{:S(2)}) collective-permute-start(bf16[48,768]{1,0:T(8,128)(2,1)S(1)} %get-tuple-element.133), channel_id=1, source_target_pairs={{0,4},{1,5},{2,6},{3,7},{4,0},{5,1},{6,2},{7,3},{8,12},{9,13},{10,... | collective-permute-start | bytes 221192 | tf_op jit(solution)/shard_map/ppermute | solution.py:695
  116.0 3.1 %collective-permute-start.23 = (bf16[48,128]{1,0:T(8,128)(2,1)S(1)}, bf16[48,128]{1,0:T(8,128)(2,1)S(1)}, u32[]{:S(2)}, u32[]{:S(2)}) collective-permute-start(bf16[48,128]{1,0:T(8,128)(2,1)S(1)} %get-tuple-element.134), channel_id=1, source_target_pairs={{0,3},{1,2},{2,1},{3,0},{4,7},{5,6},{6,5},{7,4},{8,11},{9,10},{10,... | collective-permute-start | bytes 36872 | tf_op jit(solution)/shard_map/ppermute | solution.py:475
  116.0 3.7 %collective-permute-start.24 = (bf16[48,128]{1,0:T(8,128)(2,1)S(1)}, bf16[48,128]{1,0:T(8,128)(2,1)S(1)}, u32[]{:S(2)}, u32[]{:S(2)}) collective-permute-start(bf16[48,128]{1,0:T(8,128)(2,1)S(1)} %get-tuple-element.134), channel_id=1, source_target_pairs={{0,2},{1,3},{2,0},{3,1},{4,6},{5,7},{6,4},{7,5},{8,10},{9,11},{10,... | collective-permute-start | bytes 36872 | tf_op jit(solution)/shard_map/ppermute | solution.py:475
  116.6 3.1 %collective-permute-start.25 = (bf16[48,128]{1,0:T(8,128)(2,1)S(1)}, bf16[48,128]{1,0:T(8,128)(2,1)S(1)}, u32[]{:S(2)}, u32[]{:S(2)}) collective-permute-start(bf16[48,128]{1,0:T(8,128)(2,1)S(1)} %get-tuple-element.134), channel_id=1, source_target_pairs={{0,1},{1,0},{2,3},{3,2},{4,5},{5,4},{6,7},{7,6},{8,9},{9,8},{10,11... | collective-permute-start | bytes 36872 | tf_op jit(solution)/shard_map/ppermute | solution.py:475
  119.8 5.6 %collective-permute-start.26 = (bf16[64,128]{1,0:T(8,128)(2,1)S(1)}, bf16[64,128]{1,0:T(8,128)(2,1)S(1)}, u32[]{:S(2)}, u32[]{:S(2)}) collective-permute-start(bf16[64,128]{1,0:T(8,128)(2,1)S(1)} %slice_select_fusion), channel_id=1, source_target_pairs={{0,8},{8,16},{16,24},{15,7},{23,15},{31,23}} | collective-permute-start | bytes 49160 | tf_op jit(solution)/shard_map/ppermute | solution.py:706
  (10 other events, 12.1 us)

commit v11 on v10

--- a/solution.py
+++ b/solution.py
@@ -659,8 +659,8 @@
         )
         if not layer:
             high = list(bias_of(1, weights))
-            high[0], *late = lax.optimization_barrier((high[0], *cut_up[0][1:]))
-            across[0] += [lax.ppermute(part, everyone, neighbour) for part in late]
+            high[0], late = lax.optimization_barrier((high[0], cut_up[0][1]))
+            across[0].append(lax.ppermute(late, everyone, neighbour))
             high[0], *ready = lax.optimization_barrier((high[0], *packed))
             beside = [lax.ppermute(part, everyone, sibling) for part in ready]
         else:
@@ -683,7 +683,8 @@
         )
         message = lax.all_to_all(message.reshape(ncol, own, -1), "col", 0, 0)
         if not layer:
-            message, ready = lax.optimization_barrier((message, cut_up[1][0]))
+            message, late, ready = lax.optimization_barrier((message, cut_up[0][2], cut_up[1][0]))
+            across[0].append(lax.ppermute(late, everyone, neighbour))
             across[1].append(lax.ppermute(ready, everyone, neighbour))
         act = mix(layer, message, act, gate, tok_out, heads)
         came_rows = [lax.ppermute(act, everyone, shifts[d]) for d in range(1, peers)]

time: 128 us -> 136 us (1.062)
  waiting for transfers between devices: 34.8 us -> 48.3 us
  starting transfers between devices: 36.3 us -> 33.2 us
  local copies, waits for them, and re-layouts: 3.85 us -> 2.19 us
    ppermute x2, waiting for transfers between devices: 0.01 us -> 10.1 us  [body(): across[0].append(lax.ppermute(late, everyone, neighbour))]
    ppermute x2, waiting for transfers between devices: 2.23 us -> 5.58 us  [body(): came = lax.ppermute(send, everyone, pairs)]
    ppermute x2, starting transfers between devices: 4.57 us -> 2.27 us  [body(): across[0].append(lax.ppermute(late, everyone, neighbour))]
    unnamed x58 -> x48, local copies, waits for them, and re-layouts: 3.83 us -> 2.17 us
    ppermute x1, starting transfers between devices: 3.28 us -> 1.82 us  [body(): across[1].append(lax.ppermute(late, everyone, neighbour))]
  transfers between devices with their start and end apart: 29 -> 29, of which waited for: 13 -> 16; matrix products, arithmetic and copies ran while one was open for 0% -> 0% of each run, Pallas kernels for 25% -> 21%
where the time goes in v11:
time: 136 us
  waiting for transfers between devices  48.3 us (36%)
  Pallas kernels  40.1 us (29%)
  starting transfers between devices  33.2 us (24%)
  blocking collectives  11.4 us (8%)
  local copies, waits for them, and re-layouts  2.19 us (2%)
    pallas_call x15, Pallas kernels, call(): pl.pallas_call(kernel, out_shape=outs, in_specs=[smem] * len(scalars) + [...  31.6 us
    all_to_all x1, blocking collectives, body(): message = lax.all_to_all(message.reshape(ncol, own, -1), 'col', 0, 0)  11.4 us
    ppermute x2, waiting for transfers between devices, body(): across[0].append(lax.ppermute(late, everyone, neighbour))  10.1 us
    pallas_call x2, Pallas kernels, bias_of(): pl.pallas_call(bias_kernel, grid=(end - begin,), out_shape=[jax.ShapeDtyp...  8.57 us
    ppermute x2, waiting for transfers between devices, body(): lax.ppermute(act, everyone, shifts[d])  6.58 us
    ppermute x2, waiting for transfers between devices, body(): parts = [lax.ppermute(part, everyone, shifts[d]) for d in range(1, peers)]  6.48 us
    ppermute x6, waiting for transfers between devices, row_of(): lax.ppermute(mine, ('row', 'col'), [(i, i ^ flip) for i in range(nrow * n...  6.12 us
    all_to_all x1, waiting for transfers between devices, body(): message = lax.all_to_all(message.reshape(ncol, own, -1), 'col', 0, 0)  6.1 us
  transfers between devices with their start and end apart: 29, of which 16 were waited for; matrix products, arithmetic and copies ran while one was open for 0% of the time, Pallas kernels for 21%

profile of v11, /device:TPU:24, one launch (start us, length us, event | category | flops | bytes accessed | tf_op | source)
XLA Modules:
  0.0 135.7 jit_solution(1387193294337493253)
XLA Ops:
  0.0 0.8 copy-done.12
  0.8 0.7 copy-done.15
  1.4 0.7 copy-done.16
  2.6 1.9 %collective-permute-start = (bf16[144,128]{1,0:T(8,128)(2,1)S(1)}, bf16[144,128]{1,0:T(8,128)(2,1)S(1)}, u32[]{:S(2)}, u32[]{:S(2)}) collective-permute-start(bf16[144,128]{1,0:T(8,128)(2,1)S(1)} %shard_map.172.own_ref), channel_id=1, source_target_pairs={{0,1},{1,2},{2,3},{3,4},{4,5},{5,6},{6,7},{7,8},{8,9},{9,10},{10,1... | collective-permute-start | bytes 110600 | tf_op jit(solution)/shard_map/ppermute | solution.py:544
  4.6 5.4 %collective-permute-start.1 = (bf16[144,128]{1,0:T(8,128)(2,1)S(1)}, bf16[144,128]{1,0:T(8,128)(2,1)S(1)}, u32[]{:S(2)}, u32[]{:S(2)}) collective-permute-start(bf16[144,128]{1,0:T(8,128)(2,1)S(1)} %shard_map.172.own_ref), channel_id=1, source_target_pairs={{1,0},{2,1},{3,2},{4,3},{5,4},{6,5},{7,6},{8,7},{9,8},{10,9},{11,1... | collective-permute-start | bytes 110600 | tf_op jit(solution)/shard_map/ppermute | solution.py:545
  10.0 3.2 %shard_map.173 = (bf16[576,768]{1,0:T(8,128)(2,1)}, bf16[192,768]{1,0:T(8,128)(2,1)}, bf16[288,768]{1,0:T(8,128)(2,1)}, bf16[96,768]{1,0:T(8,128)(2,1)}, bf16[57...) custom-call(bf16[2,2,192,768]{3,2,1,0:T(8,128)(2,1)} %bitcast.41, bf16[2,192,768]{2,1,0:T(8,128)(2,1)} %second), custom_call_target="tpu_custom_call" | custom-call | bytes 3538944 | tf_op jit(solution)/shard_map/pallas_call | solution.py:26
  13.4 2.0 %shard_map.174 = (bf16[256,128]{1,0:T(8,128)(2,1)S(1)}, bf16[8,144,128]{2,1,0:T(8,128)(2,1)}) custom-call(bf16[144,128]{1,0:T(8,128)(2,1)S(1)} %shard_map.172.own_ref, bf16[144,128]{1,0:T(8,128)(2,1)S(1)} %collective-permute-done.prev_ref, bf16[144,128]{1,0:T(8,128)(2,1)S(1)} %collective-permute-done.1.next_ref, bf16[4,128,128]{2,1,0:T(8,128)(2,1)S(1)} %copy-done.19, ...), custom_call_target="tpu_custom_call" | custom-call | flops 100000000 | bytes 1000000 | tf_op jit(solution)/shard_map/pallas_call | solution.py:26
  15.4 3.4 %all-to-all-start = ((bf16[8,144,128]{2,1,0:T(8,128)(2,1)}), bf16[8,144,128]{2,1,0:T(8,128)(2,1)S(1)}, u32[]{:S(2)}, u32[]{:S(2)}) async-start(bf16[8,144,128]{2,1,0:T(8,128)(2,1)} %get-tuple-element.77), calls=%async_computation | async-start | bytes 589824 | tf_op jit(solution)/shard_map/all_to_all | solution.py:611
  18.8 5.6 %shard_map.175 = (f32[120,16,128]{2,1,0:T(8,128)}, f32[120,16,128]{2,1,0:T(8,128)}) custom-call(bf16[192,96,128]{2,1,0:T(8,128)(2,1)} %pair_ref.3, bf16[32,128]{1,0:T(8,128)(2,1)} %bitcast.39), custom_call_target="tpu_custom_call" | custom-call | flops 2000000000 | bytes 4000000 | tf_op jit(solution)/shard_map/pallas_call | solution.py:593
  24.5 1.6 %all-to-all-done.both_ref = bf16[8,144,128]{2,1,0:T(8,128)(2,1)S(1)} async-done(((bf16[8,144,128]{2,1,0:T(8,128)(2,1)}), bf16[8,144,128]{2,1,0:T(8,128)(2,1)S(1)}, u32[]{:S(2)}, u32[]{:S(2)}) %all-to-all-start) | async-done | bytes 294944 | tf_op jit(solution)/shard_map/all_to_all | solution.py:611
  26.1 1.3 shard_map.176
  27.4 1.3 collective-permute-start.3
  28.7 3.0 %shard_map.178 = (f32[72,16,128]{2,1,0:T(8,128)S(1)}, f32[72,16,128]{2,1,0:T(8,128)S(1)}) custom-call(bf16[192,96,128]{2,1,0:T(8,128)(2,1)} %pair_ref.3, bf16[32,128]{1,0:T(8,128)(2,1)S(1)} %bitcast.40), custom_call_target="tpu_custom_call" | custom-call | flops 2000000000 | bytes 4000000 | tf_op jit(solution)/shard_map/pallas_call | solution.py:593
  31.6 2.5 %shard_map.177 = (bf16[192,768]{1,0:T(8,128)(2,1)S(1)}, bf16[768,768]{1,0:T(8,128)(2,1)S(1)}, bf16[768,768]{1,0:T(8,128)(2,1)S(1)}, f32[24,768]{1,0:T(8,128)S(1)}) custom-call(bf16[192,768]{1,0:T(8,128)(2,1)S(1)} %get-tuple-element.84.xn_ref, f32[24,768]{1,0:T(8,128)S(1)} %get-tuple-element.85.act_ref, bf16[2,4,768,768]{3,2,1,0:T(8,128)(2,1)} %w_in.6), custom_call_target="tpu_custom_call" | custom-call | flops 226492416 | bytes 4718592 | tf_op jit(solution)/shard_map/pallas_call | solution.py:26
  34.1 2.1 %collective-permute-done.3.came_ref = bf16[96,768]{1,0:T(8,128)(2,1)S(1)} collective-permute-done((bf16[96,768]{1,0:T(8,128)(2,1)S(1)}, bf16[96,768]{1,0:T(8,128)(2,1)S(1)}, u32[]{:S(2)}, u32[]{:S(2)}) %collective-permute-start.3) | collective-permute-done | bytes 147488 | tf_op jit(solution)/shard_map/ppermute | solution.py:642
  36.2 4.1 %shard_map.179 = bf16[192,896]{1,0:T(8,128)(2,1)} custom-call(s32[768]{0:T(1024)S(1)} %copy-done.13, bf16[192,768]{1,0:T(8,128)(2,1)S(1)} %get-tuple-element.86.query, bf16[96,768]{1,0:T(8,128)(2,1)S(1)} %get-tuple-element.87.here_ref, bf16[96,768]{1,0:T(8,128)(2,1)S(1)} %collective-permute-done.3.came_ref, f32[120,16,128]{2,1,0:T(8,128)S(1)} %copy-done.2, ...), custom_call_target="tpu_custom_call" | custom-call | flops 1000000000 | bytes 8000000 | tf_op jit(solution)/shard_map/pallas_call | solution.py:26
  40.3 4.6 %all-to-all-start.1 = ((bf16[8,24,896]{2,1,0:T(8,128)(2,1)}), bf16[8,24,896]{2,1,0:T(8,128)(2,1)S(1)}, u32[]{:S(2)}, u32[]{:S(2)}) async-start(bf16[8,24,896]{2,1,0:T(8,128)(2,1)} %bitcast.4), calls=%async_computation.1 | async-start | bytes 688128 | tf_op jit(solution)/shard_map/all_to_all | solution.py:684
  45.0 2.2 %collective-permute-start.4 = (bf16[288,768]{1,0:T(8,128)(2,1)}, bf16[288,768]{1,0:T(8,128)(2,1)}, u32[]{:S(2)}, u32[]{:S(2)}) collective-permute-start(bf16[288,768]{1,0:T(8,128)(2,1)} %get-tuple-element.103), channel_id=1, source_target_pairs={{0,2},{1,3},{2,0},{3,1},{4,6},{5,7},{6,4},{7,5},{8,10},{9,11},{10,... | collective-permute-start | bytes 1327112 | tf_op jit(solution)/shard_map/ppermute | solution.py:663
  47.1 6.1 %all-to-all-done.1.message = bf16[8,24,896]{2,1,0:T(8,128)(2,1)S(1)} async-done(((bf16[8,24,896]{2,1,0:T(8,128)(2,1)}), bf16[8,24,896]{2,1,0:T(8,128)(2,1)S(1)}, u32[]{:S(2)}, u32[]{:S(2)}) %all-to-all-start.1) | async-done | bytes 344096 | tf_op jit(solution)/shard_map/all_to_all | solution.py:684
  53.3 1.0 shard_map.180.act_ref
  54.4 7.6 %collective-permute-done.4.refs_4_ = bf16[288,768]{1,0:T(8,128)(2,1)} collective-permute-done((bf16[288,768]{1,0:T(8,128)(2,1)}, bf16[288,768]{1,0:T(8,128)(2,1)}, u32[]{:S(2)}, u32[]{:S(2)}) %collective-permute-start.4) | collective-permute-done | bytes 442400 | tf_op jit(solution)/shard_map/ppermute | solution.py:663
  62.0 2.5 %collective-permute-done.5.refs_5_ = bf16[96,768]{1,0:T(8,128)(2,1)S(1)} collective-permute-done((bf16[96,768]{1,0:T(8,128)(2,1)}, bf16[96,768]{1,0:T(8,128)(2,1)S(1)}, u32[]{:S(2)}, u32[]{:S(2)}) %collective-permute-start.5) | collective-permute-done | bytes 147488 | tf_op jit(solution)/shard_map/ppermute | solution.py:687
  65.1 1.7 %collective-permute-start.6 = (f32[24,768]{1,0:T(8,128)S(1)}, f32[24,768]{1,0:T(8,128)S(1)}, u32[]{:S(2)}, u32[]{:S(2)}) collective-permute-start(f32[24,768]{1,0:T(8,128)S(1)} %shard_map.180.act_ref), channel_id=1, source_target_pairs={{0,4},{1,5},{2,6},{3,7},{4,0},{5,1},{6,2},{7,3},{8,12},{9,13},{10,... | collective-permute-start | bytes 221192 | tf_op jit(solution)/shard_map/ppermute | solution.py:690
  66.8 2.8 %collective-permute-done.6.refs_0_ = f32[24,768]{1,0:T(8,128)S(1)} collective-permute-done((f32[24,768]{1,0:T(8,128)S(1)}, f32[24,768]{1,0:T(8,128)S(1)}, u32[]{:S(2)}, u32[]{:S(2)}) %collective-permute-start.6) | collective-permute-done | bytes 73760 | tf_op jit(solution)/shard_map/ppermute | solution.py:690
  69.6 1.4 %collective-permute-done.10.refs_8_ = bf16[96,768]{1,0:T(8,128)(2,1)S(1)} collective-permute-done((bf16[96,768]{1,0:T(8,128)(2,1)S(1)}, bf16[96,768]{1,0:T(8,128)(2,1)S(1)}, u32[]{:S(2)}, u32[]{:S(2)}) %collective-permute-start.10) | collective-permute-done | bytes 147488 | tf_op jit(solution)/shard_map/ppermute | solution.py:692
  71.0 3.3 %shard_map.181 = (f32[48,768]{1,0:T(8,128)S(1)}, bf16[48,768]{1,0:T(8,128)(2,1)S(1)}) custom-call(f32[24,768]{1,0:T(8,128)S(1)} %shard_map.180.act_ref, f32[24,768]{1,0:T(8,128)S(1)} %collective-permute-done.6.refs_0_, bf16[576,768]{1,0:T(8,128)(2,1)S(1)} %copy-done.4, bf16[576,768]{1,0:T(8,128)(2,1)} %collective-permute-done.7.refs_2_, ...), custom_call_target="tpu_custom_call" | custom-call | flops 169869312 | bytes 3538944 | tf_op jit(solution)/shard_map/pallas_call | solution.py:26
  74.2 1.7 %collective-permute-start.11 = (bf16[48,768]{1,0:T(8,128)(2,1)S(1)}, bf16[48,768]{1,0:T(8,128)(2,1)S(1)}, u32[]{:S(2)}, u32[]{:S(2)}) collective-permute-start(bf16[48,768]{1,0:T(8,128)(2,1)S(1)} %get-tuple-element.111), channel_id=1, source_target_pairs={{0,4},{1,5},{2,6},{3,7},{4,0},{5,1},{6,2},{7,3},{8,12},{9,13},{10,... | collective-permute-start | bytes 221192 | tf_op jit(solution)/shard_map/ppermute | solution.py:696
  76.0 2.7 %collective-permute-done.11.refs_0_ = bf16[48,768]{1,0:T(8,128)(2,1)S(1)} collective-permute-done((bf16[48,768]{1,0:T(8,128)(2,1)S(1)}, bf16[48,768]{1,0:T(8,128)(2,1)S(1)}, u32[]{:S(2)}, u32[]{:S(2)}) %collective-permute-start.11) | collective-permute-done | bytes 73760 | tf_op jit(solution)/shard_map/ppermute | solution.py:696
  79.2 1.5 %collective-permute-start.14 = (bf16[48,768]{1,0:T(8,128)(2,1)S(1)}, bf16[48,768]{1,0:T(8,128)(2,1)S(1)}, u32[]{:S(2)}, u32[]{:S(2)}) collective-permute-start(bf16[48,768]{1,0:T(8,128)(2,1)S(1)} %get-tuple-element.114), channel_id=1, source_target_pairs={{0,2},{1,3},{2,0},{3,1},{4,6},{5,7},{6,4},{7,5},{8,10},{9,11},{10,... | collective-permute-start | bytes 221192 | tf_op jit(solution)/shard_map/ppermute | solution.py:475
  80.8 2.4 %collective-permute-done.13 = bf16[48,768]{1,0:T(8,128)(2,1)S(1)} collective-permute-done((bf16[48,768]{1,0:T(8,128)(2,1)S(1)}, bf16[48,768]{1,0:T(8,128)(2,1)S(1)}, u32[]{:S(2)}, u32[]{:S(2)}) %collective-permute-start.13) | collective-permute-done | bytes 73760 | tf_op jit(solution)/shard_map/ppermute | solution.py:475
  83.3 1.8 %collective-permute-done.14 = bf16[48,768]{1,0:T(8,128)(2,1)S(1)} collective-permute-done((bf16[48,768]{1,0:T(8,128)(2,1)S(1)}, bf16[48,768]{1,0:T(8,128)(2,1)S(1)}, u32[]{:S(2)}, u32[]{:S(2)}) %collective-permute-start.14) | collective-permute-done | bytes 73760 | tf_op jit(solution)/shard_map/ppermute | solution.py:475
  85.2 1.5 %collective-permute-start.16 = (bf16[96,768]{1,0:T(8,128)(2,1)S(1)}, bf16[96,768]{1,0:T(8,128)(2,1)S(1)}, u32[]{:S(2)}, u32[]{:S(2)}) collective-permute-start(bf16[96,768]{1,0:T(8,128)(2,1)S(1)} %constant_dynamic-slice_fusion.here_ref), channel_id=1, source_target_pairs={{0,24},{1,25},{2,16},{3,17},{4,8},{5,9},{10,26},{11,27},{8,2},{9,3... | collective-permute-start | bytes 442376 | tf_op jit(solution)/shard_map/ppermute | solution.py:642
  86.7 2.5 %shard_map.183 = (bf16[192,768]{1,0:T(8,128)(2,1)S(1)}, bf16[768,768]{1,0:T(8,128)(2,1)S(1)}, bf16[768,768]{1,0:T(8,128)(2,1)S(1)}, f32[24,768]{1,0:T(8,128)S(1)}) custom-call(bf16[192,768]{1,0:T(8,128)(2,1)S(1)} %bitcast.34, f32[24,768]{1,0:T(8,128)S(1)} %get-tuple-element.116.act_ref, bf16[2,4,768,768]{3,2,1,0:T(8,128)(2,1)} %w_in.6), custom_call_target="tpu_custom_call" | custom-call | flops 226492416 | bytes 4718592 | tf_op jit(solution)/shard_map/pallas_call | solution.py:26
  89.3 1.8 %collective-permute-start.17 = (bf16[288,768]{1,0:T(8,128)(2,1)S(1)}, bf16[288,768]{1,0:T(8,128)(2,1)S(1)}, u32[]{:S(2)}, u32[]{:S(2)}) collective-permute-start(bf16[288,768]{1,0:T(8,128)(2,1)S(1)} %copy-done.22), channel_id=1, source_target_pairs={{0,2},{1,3},{2,0},{3,1},{4,6},{5,7},{6,4},{7,5},{8,10},{9,11},{10,... | collective-permute-start | bytes 1327112 | tf_op jit(solution)/shard_map/ppermute | solution.py:668
  91.1 3.5 %collective-permute-done.16.came_ref = bf16[96,768]{1,0:T(8,128)(2,1)S(1)} collective-permute-done((bf16[96,768]{1,0:T(8,128)(2,1)S(1)}, bf16[96,768]{1,0:T(8,128)(2,1)S(1)}, u32[]{:S(2)}, u32[]{:S(2)}) %collective-permute-start.16) | collective-permute-done | bytes 147488 | tf_op jit(solution)/shard_map/ppermute | solution.py:642
  94.6 3.5 %shard_map.184 = bf16[192,896]{1,0:T(8,128)(2,1)S(1)} custom-call(s32[768]{0:T(1024)S(1)} %copy-done.13, bf16[192,768]{1,0:T(8,128)(2,1)S(1)} %get-tuple-element.119.query, bf16[96,768]{1,0:T(8,128)(2,1)S(1)} %constant_dynamic-slice_fusion.here_ref, bf16[96,768]{1,0:T(8,128)(2,1)S(1)} %collective-permute-done.16.came_ref, f32[120,16,128]{2,1,0:T(8,128)S(1)} %copy-done.1, ...), custom_call_target="tpu_custom_call" | custom-call | flops 1000000000 | bytes 8000000 | tf_op jit(solution)/shard_map/pallas_call | solution.py:26
  98.1 11.4 %all_to_all.15.message = bf16[8,24,896]{2,1,0:T(8,128)(2,1)S(1)} all-to-all(bf16[8,24,896]{2,1,0:T(8,128)(2,1)S(1)} %bitcast.35), channel_id=1, replica_groups=mesh['row'=4,'col'=8] {'col'}, dimensions={0} | all-to-all | bytes 688128 | tf_op jit(solution)/shard_map/all_to_all | solution.py:684
  109.5 1.0 shard_map.185.act_ref
  111.8 3.8 %collective-permute-done.18.refs_0_ = f32[24,768]{1,0:T(8,128)S(1)} collective-permute-done((f32[24,768]{1,0:T(8,128)S(1)}, f32[24,768]{1,0:T(8,128)S(1)}, u32[]{:S(2)}, u32[]{:S(2)}) %collective-permute-start.18) | collective-permute-done | bytes 73760 | tf_op jit(solution)/shard_map/ppermute | solution.py:690
  115.6 3.5 %shard_map.186 = (f32[48,768]{1,0:T(8,128)S(1)}, bf16[48,768]{1,0:T(8,128)(2,1)S(1)}) custom-call(f32[24,768]{1,0:T(8,128)S(1)} %shard_map.185.act_ref, f32[24,768]{1,0:T(8,128)S(1)} %collective-permute-done.18.refs_0_, bf16[576,768]{1,0:T(8,128)(2,1)S(1)} %copy-done.3, bf16[576,768]{1,0:T(8,128)(2,1)S(1)} %collective-permute-done.19.refs_2_, ...), custom_call_target="tpu_custom_call" | custom-call | flops 169869312 | bytes 3538944 | tf_op jit(solution)/shard_map/pallas_call | solution.py:26
  119.0 0.6 collective-permute-start.22
  119.7 3.8 %collective-permute-done.22.refs_0_ = bf16[48,768]{1,0:T(8,128)(2,1)S(1)} collective-permute-done((bf16[48,768]{1,0:T(8,128)(2,1)S(1)}, bf16[48,768]{1,0:T(8,128)(2,1)S(1)}, u32[]{:S(2)}, u32[]{:S(2)}) %collective-permute-start.22) | collective-permute-done | bytes 73760 | tf_op jit(solution)/shard_map/ppermute | solution.py:696
  123.5 0.8 shard_map.187
  124.9 1.3 collective-permute-start.25
  126.2 1.3 collective-permute-done.23
  128.1 1.3 collective-permute-start.26
  129.4 4.3 %collective-permute-done.26.edge_ref = bf16[64,128]{1,0:T(8,128)(2,1)S(1)} collective-permute-done((bf16[64,128]{1,0:T(8,128)(2,1)S(1)}, bf16[64,128]{1,0:T(8,128)(2,1)S(1)}, u32[]{:S(2)}, u32[]{:S(2)}) %collective-permute-start.26) | collective-permute-done | bytes 16416 | tf_op jit(solution)/shard_map/ppermute | solution.py:707
  133.7 2.0 %shard_map.188 = f32[3,128]{1,0:T(4,128)} custom-call(bf16[256,128]{1,0:T(8,128)(2,1)S(1)} %get-tuple-element.75.x1_ref, bf16[144,128]{1,0:T(8,128)(2,1)S(1)} %shard_map.172.own_ref, bf16[144,128]{1,0:T(8,128)(2,1)S(1)} %copy-done.8, bf16[144,128]{1,0:T(8,128)(2,1)S(1)} %copy-done.10, bf16[192,128]{1,0:T(8,128)(2,1)S(1)} %bitcast.37, ...), custom_call_target="tpu_custom_call" | custom-call | flops 100000000 | bytes 1000000 | tf_op jit(solution)/shard_map/pallas_call | solution.py:26
  (82 shorter events, 4.6 us)
Async XLA Ops:
  2.1 11.3 %copy-start.19 = (bf16[4,128,128]{2,1,0:T(8,128)(2,1)S(1)}, bf16[4,128,128]{2,1,0:T(8,128)(2,1)}, u32[]{:S(2)}) copy-start(bf16[4,128,128]{2,1,0:T(8,128)(2,1)} %w_in.4) | copy-start | bytes 393220
  2.1 11.3 %copy-start.20 = (bf16[128,128]{1,0:T(8,128)(2,1)S(1)}, bf16[128,128]{1,0:T(8,128)(2,1)}, u32[]{:S(2)}) copy-start(bf16[128,128]{1,0:T(8,128)(2,1)} %w_out.4) | copy-start | bytes 98308
  2.6 10.6 %collective-permute-start = (bf16[144,128]{1,0:T(8,128)(2,1)S(1)}, bf16[144,128]{1,0:T(8,128)(2,1)S(1)}, u32[]{:S(2)}, u32[]{:S(2)}) collective-permute-start(bf16[144,128]{1,0:T(8,128)(2,1)S(1)} %shard_map.172.own_ref), channel_id=1, source_target_pairs={{0,1},{1,2},{2,3},{3,4},{4,5},{5,6},{6,7},{7,8},{8,9},{9,10},{10,1... | collective-permute-start | bytes 110600 | tf_op jit(solution)/shard_map/ppermute | solution.py:544
  4.6 8.7 %collective-permute-start.1 = (bf16[144,128]{1,0:T(8,128)(2,1)S(1)}, bf16[144,128]{1,0:T(8,128)(2,1)S(1)}, u32[]{:S(2)}, u32[]{:S(2)}) collective-permute-start(bf16[144,128]{1,0:T(8,128)(2,1)S(1)} %shard_map.172.own_ref), channel_id=1, source_target_pairs={{1,0},{2,1},{3,2},{4,3},{5,4},{6,5},{7,6},{8,7},{9,8},{10,9},{11,1... | collective-permute-start | bytes 110600 | tf_op jit(solution)/shard_map/ppermute | solution.py:545
  13.2 11.2 %copy-start.7 = (bf16[144,128]{1,0:T(8,128)(2,1)}, bf16[144,128]{1,0:T(8,128)(2,1)S(1)}, u32[]{:S(2)}) copy-start(bf16[144,128]{1,0:T(8,128)(2,1)S(1)} %collective-permute-done.prev_ref) | copy-start | bytes 110596
  13.2 11.2 %copy-start.9 = (bf16[144,128]{1,0:T(8,128)(2,1)}, bf16[144,128]{1,0:T(8,128)(2,1)S(1)}, u32[]{:S(2)}) copy-start(bf16[144,128]{1,0:T(8,128)(2,1)S(1)} %collective-permute-done.1.next_ref) | copy-start | bytes 110596
  13.3 12.8 %collective-permute-start.2 = (bf16[192,768]{1,0:T(8,128)(2,1)}, bf16[192,768]{1,0:T(8,128)(2,1)}, u32[]{:S(2)}, u32[]{:S(2)}) collective-permute-start(bf16[192,768]{1,0:T(8,128)(2,1)} %get-tuple-element.81), channel_id=1, source_target_pairs={{0,2},{1,3},{2,0},{3,1},{4,6},{5,7},{6,4},{7,5},{8,10},{9,11},{10,... | collective-permute-start | bytes 884744 | tf_op jit(solution)/shard_map/ppermute | solution.py:571
  15.4 10.6 %all-to-all-start = ((bf16[8,144,128]{2,1,0:T(8,128)(2,1)}), bf16[8,144,128]{2,1,0:T(8,128)(2,1)S(1)}, u32[]{:S(2)}, u32[]{:S(2)}) async-start(bf16[8,144,128]{2,1,0:T(8,128)(2,1)} %get-tuple-element.77), calls=%async_computation | async-start | bytes 589824 | tf_op jit(solution)/shard_map/all_to_all | solution.py:611
  18.8 7.2 %copy-start.17 = (bf16[192,768]{1,0:T(8,128)(2,1)S(1)}, bf16[192,768]{1,0:T(8,128)(2,1)}, u32[]{:S(2)}) copy-start(bf16[192,768]{1,0:T(8,128)(2,1)} %cond.1) | copy-start | bytes 884740
  18.8 7.2 %copy-start.18 = (bf16[128,768]{1,0:T(8,128)(2,1)S(1)}, bf16[128,768]{1,0:T(8,128)(2,1)}, u32[]{:S(2)}) copy-start(bf16[128,768]{1,0:T(8,128)(2,1)} %weight.1) | copy-start | bytes 589828
  27.4 8.8 %collective-permute-start.3 = (bf16[96,768]{1,0:T(8,128)(2,1)S(1)}, bf16[96,768]{1,0:T(8,128)(2,1)S(1)}, u32[]{:S(2)}, u32[]{:S(2)}) collective-permute-start(bf16[96,768]{1,0:T(8,128)(2,1)S(1)} %get-tuple-element.87.here_ref), channel_id=1, source_target_pairs={{0,24},{1,25},{2,16},{3,17},{4,8},{5,9},{10,26},{11,27},{8,2},{9,3... | collective-permute-start | bytes 442376 | tf_op jit(solution)/shard_map/ppermute | solution.py:642
  31.6 4.6 %copy-start.2 = (f32[120,16,128]{2,1,0:T(8,128)S(1)}, f32[120,16,128]{2,1,0:T(8,128)}, u32[]{:S(2)}) copy-start(f32[120,16,128]{2,1,0:T(8,128)} %get-tuple-element.88.low) | copy-start | bytes 2949124
  31.6 4.6 %copy-start.13 = (s32[768]{0:T(1024)S(1)}, s32[768]{0:T(1024)}, u32[]{:S(2)}) copy-start(s32[768]{0:T(1024)} %mask_ref.3) | copy-start | bytes 9220
  36.2 17.1 %copy-start = (bf16[2,768,768]{2,1,0:T(8,128)(2,1)S(1)}, bf16[2,768,768]{2,1,0:T(8,128)(2,1)}, u32[]{:S(2)}) copy-start(bf16[2,768,768]{2,1,0:T(8,128)(2,1)} %w_out.6) | copy-start | bytes 7077892
  40.3 12.9 %all-to-all-start.1 = ((bf16[8,24,896]{2,1,0:T(8,128)(2,1)}), bf16[8,24,896]{2,1,0:T(8,128)(2,1)S(1)}, u32[]{:S(2)}, u32[]{:S(2)}) async-start(bf16[8,24,896]{2,1,0:T(8,128)(2,1)} %bitcast.4), calls=%async_computation.1 | async-start | bytes 688128 | tf_op jit(solution)/shard_map/all_to_all | solution.py:684
  45.0 17.0 %collective-permute-start.4 = (bf16[288,768]{1,0:T(8,128)(2,1)}, bf16[288,768]{1,0:T(8,128)(2,1)}, u32[]{:S(2)}, u32[]{:S(2)}) collective-permute-start(bf16[288,768]{1,0:T(8,128)(2,1)} %get-tuple-element.103), channel_id=1, source_target_pairs={{0,2},{1,3},{2,0},{3,1},{4,6},{5,7},{6,4},{7,5},{8,10},{9,11},{10,... | collective-permute-start | bytes 1327112 | tf_op jit(solution)/shard_map/ppermute | solution.py:663
  47.1 23.8 %collective-permute-start.7 = (bf16[576,768]{1,0:T(8,128)(2,1)}, bf16[576,768]{1,0:T(8,128)(2,1)}, u32[]{:S(2)}, u32[]{:S(2)}) collective-permute-start(bf16[576,768]{1,0:T(8,128)(2,1)} %get-tuple-element.106.refs_1_), channel_id=1, source_target_pairs={{0,1},{1,0},{2,3},{3,2},{4,5},{5,4},{6,7},{7,6},{8,9},{9,8},{10,11... | collective-permute-start | bytes 2654216 | tf_op jit(solution)/shard_map/ppermute | solution.py:665
  53.2 11.3 %collective-permute-start.5 = (bf16[96,768]{1,0:T(8,128)(2,1)}, bf16[96,768]{1,0:T(8,128)(2,1)S(1)}, u32[]{:S(2)}, u32[]{:S(2)}) collective-permute-start(bf16[96,768]{1,0:T(8,128)(2,1)} %get-tuple-element.104), channel_id=1, source_target_pairs={{0,2},{1,3},{2,0},{3,1},{4,6},{5,7},{6,4},{7,5},{8,10},{9,11},{10,... | collective-permute-start | bytes 442376 | tf_op jit(solution)/shard_map/ppermute | solution.py:687
  53.3 11.2 %copy-start.23 = (bf16[288,768]{1,0:T(8,128)(2,1)S(1)}, bf16[288,768]{1,0:T(8,128)(2,1)}, u32[]{:S(2)}) copy-start(bf16[288,768]{1,0:T(8,128)(2,1)} %get-tuple-element.113) | copy-start | bytes 1327108
  53.3 17.6 %copy-start.4 = (bf16[576,768]{1,0:T(8,128)(2,1)S(1)}, bf16[576,768]{1,0:T(8,128)(2,1)}, u32[]{:S(2)}) copy-start(bf16[576,768]{1,0:T(8,128)(2,1)} %get-tuple-element.106.refs_1_) | copy-start | bytes 2654212
  64.5 6.4 %collective-permute-start.9 = (bf16[288,768]{1,0:T(8,128)(2,1)}, bf16[288,768]{1,0:T(8,128)(2,1)S(1)}, u32[]{:S(2)}, u32[]{:S(2)}) collective-permute-start(bf16[288,768]{1,0:T(8,128)(2,1)} %collective-permute-done.4.refs_4_), channel_id=1, source_target_pairs={{0,1},{1,0},{2,3},{3,2},{4,5},{5,4},{6,7},{7,6},{8,9},{9,8},{10,11... | collective-permute-start | bytes 1327112 | tf_op jit(solution)/shard_map/ppermute | solution.py:692
  64.5 14.4 %collective-permute-start.12 = (bf16[288,768]{1,0:T(8,128)(2,1)S(1)}, bf16[288,768]{1,0:T(8,128)(2,1)}, u32[]{:S(2)}, u32[]{:S(2)}) collective-permute-start(bf16[288,768]{1,0:T(8,128)(2,1)S(1)} %copy-done.23), channel_id=1, source_target_pairs={{0,2},{1,3},{2,0},{3,1},{4,6},{5,7},{6,4},{7,5},{8,10},{9,11},{10,... | collective-permute-start | bytes 1327112 | tf_op jit(solution)/shard_map/ppermute | solution.py:688
  64.9 6.1 %collective-permute-start.8 = (bf16[192,768]{1,0:T(8,128)(2,1)}, bf16[192,768]{1,0:T(8,128)(2,1)S(1)}, u32[]{:S(2)}, u32[]{:S(2)}) collective-permute-start(bf16[192,768]{1,0:T(8,128)(2,1)} %collective-permute-done.2.refs_3_), channel_id=1, source_target_pairs={{0,1},{1,0},{2,3},{3,2},{4,5},{5,4},{6,7},{7,6},{8,9},{9,8},{10,11... | collective-permute-start | bytes 884744 | tf_op jit(solution)/shard_map/ppermute | solution.py:692
  65.1 4.5 %collective-permute-start.6 = (f32[24,768]{1,0:T(8,128)S(1)}, f32[24,768]{1,0:T(8,128)S(1)}, u32[]{:S(2)}, u32[]{:S(2)}) collective-permute-start(f32[24,768]{1,0:T(8,128)S(1)} %shard_map.180.act_ref), channel_id=1, source_target_pairs={{0,4},{1,5},{2,6},{3,7},{4,0},{5,1},{6,2},{7,3},{8,12},{9,13},{10,... | collective-permute-start | bytes 221192 | tf_op jit(solution)/shard_map/ppermute | solution.py:690
  69.6 1.4 %collective-permute-start.10 = (bf16[96,768]{1,0:T(8,128)(2,1)S(1)}, bf16[96,768]{1,0:T(8,128)(2,1)S(1)}, u32[]{:S(2)}, u32[]{:S(2)}) collective-permute-start(bf16[96,768]{1,0:T(8,128)(2,1)S(1)} %collective-permute-done.5.refs_5_), channel_id=1, source_target_pairs={{0,1},{1,0},{2,3},{3,2},{4,5},{5,4},{6,7},{7,6},{8,9},{9,8},{10,11... | collective-permute-start | bytes 442376 | tf_op jit(solution)/shard_map/ppermute | solution.py:692
  74.2 4.4 %collective-permute-start.11 = (bf16[48,768]{1,0:T(8,128)(2,1)S(1)}, bf16[48,768]{1,0:T(8,128)(2,1)S(1)}, u32[]{:S(2)}, u32[]{:S(2)}) collective-permute-start(bf16[48,768]{1,0:T(8,128)(2,1)S(1)} %get-tuple-element.111), channel_id=1, source_target_pairs={{0,4},{1,5},{2,6},{3,7},{4,0},{5,1},{6,2},{7,3},{8,12},{9,13},{10,... | collective-permute-start | bytes 221192 | tf_op jit(solution)/shard_map/ppermute | solution.py:696
  78.9 4.4 %collective-permute-start.13 = (bf16[48,768]{1,0:T(8,128)(2,1)S(1)}, bf16[48,768]{1,0:T(8,128)(2,1)S(1)}, u32[]{:S(2)}, u32[]{:S(2)}) collective-permute-start(bf16[48,768]{1,0:T(8,128)(2,1)S(1)} %get-tuple-element.114), channel_id=1, source_target_pairs={{0,3},{1,2},{2,1},{3,0},{4,7},{5,6},{6,5},{7,4},{8,11},{9,10},{10,... | collective-permute-start | bytes 221192 | tf_op jit(solution)/shard_map/ppermute | solution.py:475
  79.2 5.9 %collective-permute-start.14 = (bf16[48,768]{1,0:T(8,128)(2,1)S(1)}, bf16[48,768]{1,0:T(8,128)(2,1)S(1)}, u32[]{:S(2)}, u32[]{:S(2)}) collective-permute-start(bf16[48,768]{1,0:T(8,128)(2,1)S(1)} %get-tuple-element.114), channel_id=1, source_target_pairs={{0,2},{1,3},{2,0},{3,1},{4,6},{5,7},{6,4},{7,5},{8,10},{9,11},{10,... | collective-permute-start | bytes 221192 | tf_op jit(solution)/shard_map/ppermute | solution.py:475
  80.7 4.4 %collective-permute-start.15 = (bf16[48,768]{1,0:T(8,128)(2,1)S(1)}, bf16[48,768]{1,0:T(8,128)(2,1)S(1)}, u32[]{:S(2)}, u32[]{:S(2)}) collective-permute-start(bf16[48,768]{1,0:T(8,128)(2,1)S(1)} %get-tuple-element.114), channel_id=1, source_target_pairs={{0,1},{1,0},{2,3},{3,2},{4,5},{5,4},{6,7},{7,6},{8,9},{9,8},{10,11... | collective-permute-start | bytes 221192 | tf_op jit(solution)/shard_map/ppermute | solution.py:475
  85.2 9.4 %collective-permute-start.16 = (bf16[96,768]{1,0:T(8,128)(2,1)S(1)}, bf16[96,768]{1,0:T(8,128)(2,1)S(1)}, u32[]{:S(2)}, u32[]{:S(2)}) collective-permute-start(bf16[96,768]{1,0:T(8,128)(2,1)S(1)} %constant_dynamic-slice_fusion.here_ref), channel_id=1, source_target_pairs={{0,24},{1,25},{2,16},{3,17},{4,8},{5,9},{10,26},{11,27},{8,2},{9,3... | collective-permute-start | bytes 442376 | tf_op jit(solution)/shard_map/ppermute | solution.py:642
  86.7 4.4 %copy-start.3 = (bf16[576,768]{1,0:T(8,128)(2,1)S(1)}, bf16[576,768]{1,0:T(8,128)(2,1)}, u32[]{:S(2)}) copy-start(bf16[576,768]{1,0:T(8,128)(2,1)} %get-tuple-element.129.refs_1_) | copy-start | bytes 2654212
  86.7 7.9 %copy-start.1 = (f32[120,16,128]{2,1,0:T(8,128)S(1)}, f32[120,16,128]{2,1,0:T(8,128)}, u32[]{:S(2)}) copy-start(f32[120,16,128]{2,1,0:T(8,128)} %get-tuple-element.121.low) | copy-start | bytes 2949124
  89.3 21.4 %collective-permute-start.17 = (bf16[288,768]{1,0:T(8,128)(2,1)S(1)}, bf16[288,768]{1,0:T(8,128)(2,1)S(1)}, u32[]{:S(2)}, u32[]{:S(2)}) collective-permute-start(bf16[288,768]{1,0:T(8,128)(2,1)S(1)} %copy-done.22), channel_id=1, source_target_pairs={{0,2},{1,3},{2,0},{3,1},{4,6},{5,7},{6,4},{7,5},{8,10},{9,11},{10,... | collective-permute-start | bytes 1327112 | tf_op jit(solution)/shard_map/ppermute | solution.py:668
  91.1 20.7 %collective-permute-start.19 = (bf16[576,768]{1,0:T(8,128)(2,1)S(1)}, bf16[576,768]{1,0:T(8,128)(2,1)S(1)}, u32[]{:S(2)}, u32[]{:S(2)}) collective-permute-start(bf16[576,768]{1,0:T(8,128)(2,1)S(1)} %copy-done.3), channel_id=1, source_target_pairs={{0,1},{1,0},{2,3},{3,2},{4,5},{5,4},{6,7},{7,6},{8,9},{9,8},{10,11... | collective-permute-start | bytes 2654216 | tf_op jit(solution)/shard_map/ppermute | solution.py:665
  110.6 12.9 %copy-start.5 = (bf16[768,128]{1,0:T(8,128)(2,1)S(1)}, bf16[768,128]{1,0:T(8,128)(2,1)}, u32[]{:S(2)}) copy-start(bf16[768,128]{1,0:T(8,128)(2,1)} %refs_1_.1) | copy-start | bytes 589828
  110.6 23.1 %copy-start.6 = (bf16[4,128,128]{2,1,0:T(8,128)(2,1)S(1)}, bf16[4,128,128]{2,1,0:T(8,128)(2,1)}, u32[]{:S(2)}) copy-start(bf16[4,128,128]{2,1,0:T(8,128)(2,1)} %w_in.7) | copy-start | bytes 393220
  110.6 23.1 %copy-start.8 = (bf16[144,128]{1,0:T(8,128)(2,1)S(1)}, bf16[144,128]{1,0:T(8,128)(2,1)}, u32[]{:S(2)}) copy-start(bf16[144,128]{1,0:T(8,128)(2,1)} %copy-done.7) | copy-start | bytes 110596
  110.6 23.1 %copy-start.10 = (bf16[144,128]{1,0:T(8,128)(2,1)S(1)}, bf16[144,128]{1,0:T(8,128)(2,1)}, u32[]{:S(2)}) copy-start(bf16[144,128]{1,0:T(8,128)(2,1)} %copy-done.9) | copy-start | bytes 110596
  110.6 23.1 %copy-start.11 = (bf16[128,128]{1,0:T(8,128)(2,1)S(1)}, bf16[128,128]{1,0:T(8,128)(2,1)}, u32[]{:S(2)}) copy-start(bf16[128,128]{1,0:T(8,128)(2,1)} %w_out.7) | copy-start | bytes 98308
  110.6 23.1 %copy-start.14 = (bf16[3,128]{1,0:T(4,128)(2,1)S(1)}, bf16[3,128]{1,0:T(4,128)(2,1)}, u32[]{:S(2)}) copy-start(bf16[3,128]{1,0:T(4,128)(2,1)} %pos.1) | copy-start | bytes 2308
  110.6 4.9 %collective-permute-start.20 = (bf16[288,768]{1,0:T(8,128)(2,1)}, bf16[288,768]{1,0:T(8,128)(2,1)S(1)}, u32[]{:S(2)}, u32[]{:S(2)}) collective-permute-start(bf16[288,768]{1,0:T(8,128)(2,1)} %collective-permute-done.12.refs_3_), channel_id=1, source_target_pairs={{0,1},{1,0},{2,3},{3,2},{4,5},{5,4},{6,7},{7,6},{8,9},{9,8},{10,11... | collective-permute-start | bytes 1327112 | tf_op jit(solution)/shard_map/ppermute | solution.py:692
  110.7 4.9 %collective-permute-start.21 = (bf16[288,768]{1,0:T(8,128)(2,1)S(1)}, bf16[288,768]{1,0:T(8,128)(2,1)S(1)}, u32[]{:S(2)}, u32[]{:S(2)}) collective-permute-start(bf16[288,768]{1,0:T(8,128)(2,1)S(1)} %collective-permute-done.17.refs_4_), channel_id=1, source_target_pairs={{0,1},{1,0},{2,3},{3,2},{4,5},{5,4},{6,7},{7,6},{8,9},{9,8},{10,11... | collective-permute-start | bytes 1327112 | tf_op jit(solution)/shard_map/ppermute | solution.py:692
  111.2 4.4 %collective-permute-start.18 = (f32[24,768]{1,0:T(8,128)S(1)}, f32[24,768]{1,0:T(8,128)S(1)}, u32[]{:S(2)}, u32[]{:S(2)}) collective-permute-start(f32[24,768]{1,0:T(8,128)S(1)} %shard_map.185.act_ref), channel_id=1, source_target_pairs={{0,4},{1,5},{2,6},{3,7},{4,0},{5,1},{6,2},{7,3},{8,12},{9,13},{10,... | collective-permute-start | bytes 221192 | tf_op jit(solution)/shard_map/ppermute | solution.py:690
  119.0 4.4 %collective-permute-start.22 = (bf16[48,768]{1,0:T(8,128)(2,1)S(1)}, bf16[48,768]{1,0:T(8,128)(2,1)S(1)}, u32[]{:S(2)}, u32[]{:S(2)}) collective-permute-start(bf16[48,768]{1,0:T(8,128)(2,1)S(1)} %get-tuple-element.133), channel_id=1, source_target_pairs={{0,4},{1,5},{2,6},{3,7},{4,0},{5,1},{6,2},{7,3},{8,12},{9,13},{10,... | collective-permute-start | bytes 221192 | tf_op jit(solution)/shard_map/ppermute | solution.py:696
  124.3 3.1 %collective-permute-start.23 = (bf16[48,128]{1,0:T(8,128)(2,1)S(1)}, bf16[48,128]{1,0:T(8,128)(2,1)S(1)}, u32[]{:S(2)}, u32[]{:S(2)}) collective-permute-start(bf16[48,128]{1,0:T(8,128)(2,1)S(1)} %get-tuple-element.134), channel_id=1, source_target_pairs={{0,3},{1,2},{2,1},{3,0},{4,7},{5,6},{6,5},{7,4},{8,11},{9,10},{10,... | collective-permute-start | bytes 36872 | tf_op jit(solution)/shard_map/ppermute | solution.py:475
  124.3 3.7 %collective-permute-start.24 = (bf16[48,128]{1,0:T(8,128)(2,1)S(1)}, bf16[48,128]{1,0:T(8,128)(2,1)S(1)}, u32[]{:S(2)}, u32[]{:S(2)}) collective-permute-start(bf16[48,128]{1,0:T(8,128)(2,1)S(1)} %get-tuple-element.134), channel_id=1, source_target_pairs={{0,2},{1,3},{2,0},{3,1},{4,6},{5,7},{6,4},{7,5},{8,10},{9,11},{10,... | collective-permute-start | bytes 36872 | tf_op jit(solution)/shard_map/ppermute | solution.py:475
  124.9 3.1 %collective-permute-start.25 = (bf16[48,128]{1,0:T(8,128)(2,1)S(1)}, bf16[48,128]{1,0:T(8,128)(2,1)S(1)}, u32[]{:S(2)}, u32[]{:S(2)}) collective-permute-start(bf16[48,128]{1,0:T(8,128)(2,1)S(1)} %get-tuple-element.134), channel_id=1, source_target_pairs={{0,1},{1,0},{2,3},{3,2},{4,5},{5,4},{6,7},{7,6},{8,9},{9,8},{10,11... | collective-permute-start | bytes 36872 | tf_op jit(solution)/shard_map/ppermute | solution.py:475
  128.1 5.6 %collective-permute-start.26 = (bf16[64,128]{1,0:T(8,128)(2,1)S(1)}, bf16[64,128]{1,0:T(8,128)(2,1)S(1)}, u32[]{:S(2)}, u32[]{:S(2)}) collective-permute-start(bf16[64,128]{1,0:T(8,128)(2,1)S(1)} %slice_select_fusion), channel_id=1, source_target_pairs={{0,8},{8,16},{16,24},{15,7},{23,15},{31,23}} | collective-permute-start | bytes 49160 | tf_op jit(solution)/shard_map/ppermute | solution.py:707
  (5 other events, 7.3 us)

commit v12 on v10

--- a/solution.py
+++ b/solution.py
@@ -547,7 +547,7 @@
         (feat, jnp.swapaxes(trans_in, 2, 3), trans_out)
     )
     matrix = jax.ShapeDtypeStruct((3 * hid, width), BF16)
-    cuts = ((2, 3, 1), (3, 3))
+    cuts = ((3, 3), (3, 3))
     pieces = call(
         functools.partial(pack_kernel, cuts),
         [

time: 128 us -> 129 us (level)
  blocking collectives: 11.7 us -> 22.2 us
  starting transfers between devices: 36.3 us -> 28.6 us
  waiting for transfers between devices: 34.8 us -> 32 us
    all_to_all x1 -> x2, blocking collectives: 11.7 us -> 22.2 us  [body(): message = lax.all_to_all(message.reshape(ncol, own, -1), 'col', 0, 0)]
    all_to_all x1 -> x0, waiting for transfers between devices: 6.1 us -> none  [body(): message = lax.all_to_all(message.reshape(ncol, own, -1), 'col', 0, 0)]
    all_to_all x1 -> x0, starting transfers between devices: 4.13 us -> none  [body(): message = lax.all_to_all(message.reshape(ncol, own, -1), 'col', 0, 0)]
    ppermute x5 -> x4, waiting for transfers between devices: 1.38 us -> 0.01 us  [body(): beyond[layer] = [lax.ppermute(part, everyone, sibling) for part in ready]]
    ppermute x2 -> x1, starting transfers between devices: 4.57 us -> 3.6 us  [body(): across[0] += [lax.ppermute(part, everyone, neighbour) for part in late]]
    unnamed x58 -> x50, local copies, waits for them, and re-layouts: 3.83 us -> 2.93 us
  transfers between devices with their start and end apart: 29 -> 26, of which waited for: 13 -> 11; matrix products, arithmetic and copies ran while one was open for 0% -> 0% of each run, Pallas kernels for 25% -> 25%
where the time goes in v12:
time: 129 us; the launch traced here: 128 us
  Pallas kernels  40.6 us (31%)
  waiting for transfers between devices  32 us (25%)
  starting transfers between devices  28.6 us (22%)
  blocking collectives  22.2 us (17%)
  local copies, waits for them, and re-layouts  2.95 us (2%)
    pallas_call x15, Pallas kernels, call(): pl.pallas_call(kernel, out_shape=outs, in_specs=[smem] * len(scalars) + [...  32.1 us
    all_to_all x2, blocking collectives, body(): message = lax.all_to_all(message.reshape(ncol, own, -1), 'col', 0, 0)  22.2 us
    pallas_call x2, Pallas kernels, bias_of(): pl.pallas_call(bias_kernel, grid=(end - begin,), out_shape=[jax.ShapeDtyp...  8.56 us
    ppermute x2, waiting for transfers between devices, body(): parts = [lax.ppermute(part, everyone, shifts[d]) for d in range(1, peers)]  7.59 us
    ppermute x2, waiting for transfers between devices, body(): lax.ppermute(act, everyone, shifts[d])  7.58 us
    ppermute x6, waiting for transfers between devices, row_of(): lax.ppermute(mine, ('row', 'col'), [(i, i ^ flip) for i in range(nrow * n...  6.47 us
    ppermute x1, starting transfers between devices, body(): after = lax.ppermute(feat, everyone, [(b, a) for a, b in up])  5.44 us
    ppermute x1, waiting for transfers between devices, body(): edge = lax.ppermute(edge, everyone, bounds)  4.33 us
  transfers between devices with their start and end apart: 26, of which 11 were waited for; matrix products, arithmetic and copies ran while one was open for 0% of the time, Pallas kernels for 25%

profile of v12, /device:TPU:24, one launch (start us, length us, event | category | flops | bytes accessed | tf_op | source)
XLA Modules:
  0.0 127.9 jit_solution(11000870696326511563)
XLA Ops:
  0.0 0.8 copy-done.12
  0.8 0.7 copy-done.15
  1.4 0.7 copy-done.16
  2.6 1.9 %collective-permute-start = (bf16[144,128]{1,0:T(8,128)(2,1)S(1)}, bf16[144,128]{1,0:T(8,128)(2,1)S(1)}, u32[]{:S(2)}, u32[]{:S(2)}) collective-permute-start(bf16[144,128]{1,0:T(8,128)(2,1)S(1)} %shard_map.172.own_ref), channel_id=1, source_target_pairs={{0,1},{1,2},{2,3},{3,4},{4,5},{5,6},{6,7},{7,8},{8,9},{9,10},{10,1... | collective-permute-start | bytes 110600 | tf_op jit(solution)/shard_map/ppermute | solution.py:544
  4.6 5.4 %collective-permute-start.1 = (bf16[144,128]{1,0:T(8,128)(2,1)S(1)}, bf16[144,128]{1,0:T(8,128)(2,1)S(1)}, u32[]{:S(2)}, u32[]{:S(2)}) collective-permute-start(bf16[144,128]{1,0:T(8,128)(2,1)S(1)} %shard_map.172.own_ref), channel_id=1, source_target_pairs={{1,0},{2,1},{3,2},{4,3},{5,4},{6,5},{7,6},{8,7},{9,8},{10,9},{11,1... | collective-permute-start | bytes 110600 | tf_op jit(solution)/shard_map/ppermute | solution.py:545
  10.0 3.3 %shard_map.173 = (bf16[576,768]{1,0:T(8,128)(2,1)}, bf16[288,768]{1,0:T(8,128)(2,1)}, bf16[288,768]{1,0:T(8,128)(2,1)}, bf16[576,768]{1,0:T(8,128)(2,1)}, bf16[2...) custom-call(bf16[2,2,192,768]{3,2,1,0:T(8,128)(2,1)} %bitcast.42, bf16[2,192,768]{2,1,0:T(8,128)(2,1)} %second), custom_call_target="tpu_custom_call" | custom-call | bytes 3538944 | tf_op jit(solution)/shard_map/pallas_call | solution.py:26
  13.5 2.0 %shard_map.174 = (bf16[256,128]{1,0:T(8,128)(2,1)S(1)}, bf16[8,144,128]{2,1,0:T(8,128)(2,1)}) custom-call(bf16[144,128]{1,0:T(8,128)(2,1)S(1)} %shard_map.172.own_ref, bf16[144,128]{1,0:T(8,128)(2,1)S(1)} %collective-permute-done.prev_ref, bf16[144,128]{1,0:T(8,128)(2,1)S(1)} %collective-permute-done.1.next_ref, bf16[4,128,128]{2,1,0:T(8,128)(2,1)S(1)} %copy-done.19, ...), custom_call_target="tpu_custom_call" | custom-call | flops 100000000 | bytes 1000000 | tf_op jit(solution)/shard_map/pallas_call | solution.py:26
  15.5 0.6 copy-done.7
  16.1 3.4 %all-to-all-start = ((bf16[8,144,128]{2,1,0:T(8,128)(2,1)}), bf16[8,144,128]{2,1,0:T(8,128)(2,1)S(1)}, u32[]{:S(2)}, u32[]{:S(2)}) async-start(bf16[8,144,128]{2,1,0:T(8,128)(2,1)} %get-tuple-element.74), calls=%async_computation | async-start | bytes 589824 | tf_op jit(solution)/shard_map/all_to_all | solution.py:611
  19.6 5.6 %shard_map.175 = (f32[120,16,128]{2,1,0:T(8,128)}, f32[120,16,128]{2,1,0:T(8,128)}) custom-call(bf16[192,96,128]{2,1,0:T(8,128)(2,1)} %pair_ref.3, bf16[32,128]{1,0:T(8,128)(2,1)} %bitcast.40), custom_call_target="tpu_custom_call" | custom-call | flops 2000000000 | bytes 4000000 | tf_op jit(solution)/shard_map/pallas_call | solution.py:593
  25.2 2.7 %all-to-all-done.both_ref = bf16[8,144,128]{2,1,0:T(8,128)(2,1)S(1)} async-done(((bf16[8,144,128]{2,1,0:T(8,128)(2,1)}), bf16[8,144,128]{2,1,0:T(8,128)(2,1)S(1)}, u32[]{:S(2)}, u32[]{:S(2)}) %all-to-all-start) | async-done | bytes 294944 | tf_op jit(solution)/shard_map/all_to_all | solution.py:611
  27.9 1.3 %shard_map.176 = (f32[24,768]{1,0:T(8,128)S(1)}, bf16[192,768]{1,0:T(8,128)(2,1)S(1)}, bf16[96,768]{1,0:T(8,128)(2,1)S(1)}) custom-call(bf16[8,144,128]{2,1,0:T(8,128)(2,1)S(1)} %all-to-all-done.both_ref, bf16[128,768]{1,0:T(8,128)(2,1)S(1)} %copy-done.18, bf16[192,768]{1,0:T(8,128)(2,1)S(1)} %copy-done.17), custom_call_target="tpu_custom_call" | custom-call | flops 1000000000 | bytes 1000000 | tf_op jit(solution)/shard_map/pallas_call | solution.py:26
  29.3 1.4 %collective-permute-start.3 = (bf16[96,768]{1,0:T(8,128)(2,1)S(1)}, bf16[96,768]{1,0:T(8,128)(2,1)S(1)}, u32[]{:S(2)}, u32[]{:S(2)}) collective-permute-start(bf16[96,768]{1,0:T(8,128)(2,1)S(1)} %get-tuple-element.84.here_ref), channel_id=1, source_target_pairs={{0,24},{1,25},{2,16},{3,17},{4,8},{5,9},{10,26},{11,27},{8,2},{9,3... | collective-permute-start | bytes 442376 | tf_op jit(solution)/shard_map/ppermute | solution.py:642
  30.7 3.0 %shard_map.178 = (f32[72,16,128]{2,1,0:T(8,128)S(1)}, f32[72,16,128]{2,1,0:T(8,128)S(1)}) custom-call(bf16[192,96,128]{2,1,0:T(8,128)(2,1)} %pair_ref.3, bf16[32,128]{1,0:T(8,128)(2,1)S(1)} %bitcast.41), custom_call_target="tpu_custom_call" | custom-call | flops 2000000000 | bytes 4000000 | tf_op jit(solution)/shard_map/pallas_call | solution.py:593
  33.7 3.6 %collective-permute-start.4 = (bf16[288,768]{1,0:T(8,128)(2,1)S(1)}, bf16[288,768]{1,0:T(8,128)(2,1)S(1)}, u32[]{:S(2)}, u32[]{:S(2)}) collective-permute-start(bf16[288,768]{1,0:T(8,128)(2,1)S(1)} %copy-done.24), channel_id=1, source_target_pairs={{0,2},{1,3},{2,0},{3,1},{4,6},{5,7},{6,4},{7,5},{8,10},{9,11},{10,... | collective-permute-start | bytes 1327112 | tf_op jit(solution)/shard_map/ppermute | solution.py:663
  37.3 2.5 %shard_map.177 = (bf16[192,768]{1,0:T(8,128)(2,1)S(1)}, bf16[768,768]{1,0:T(8,128)(2,1)S(1)}, bf16[768,768]{1,0:T(8,128)(2,1)S(1)}, f32[24,768]{1,0:T(8,128)S(1)}) custom-call(bf16[192,768]{1,0:T(8,128)(2,1)S(1)} %get-tuple-element.81.xn_ref, f32[24,768]{1,0:T(8,128)S(1)} %get-tuple-element.82.act_ref, bf16[2,4,768,768]{3,2,1,0:T(8,128)(2,1)} %w_in.6), custom_call_target="tpu_custom_call" | custom-call | flops 226492416 | bytes 4718592 | tf_op jit(solution)/shard_map/pallas_call | solution.py:26
  39.9 3.5 %shard_map.179 = bf16[192,896]{1,0:T(8,128)(2,1)S(1)} custom-call(s32[768]{0:T(1024)S(1)} %copy-done.13, bf16[192,768]{1,0:T(8,128)(2,1)S(1)} %get-tuple-element.83.query, bf16[96,768]{1,0:T(8,128)(2,1)S(1)} %get-tuple-element.84.here_ref, bf16[96,768]{1,0:T(8,128)(2,1)S(1)} %collective-permute-done.3.came_ref, f32[120,16,128]{2,1,0:T(8,128)S(1)} %copy-done.2, ...), custom_call_target="tpu_custom_call" | custom-call | flops 1000000000 | bytes 8000000 | tf_op jit(solution)/shard_map/pallas_call | solution.py:26
  43.4 10.6 %all_to_all.15.message = bf16[8,24,896]{2,1,0:T(8,128)(2,1)S(1)} all-to-all(bf16[8,24,896]{2,1,0:T(8,128)(2,1)S(1)} %bitcast.35), channel_id=1, replica_groups=mesh['row'=4,'col'=8] {'col'}, dimensions={0} | all-to-all | bytes 688128 | tf_op jit(solution)/shard_map/all_to_all | solution.py:684
  53.9 1.0 shard_map.180.act_ref
  56.1 0.6 collective-permute-start.5
  56.7 3.8 %collective-permute-done.5.refs_0_ = f32[24,768]{1,0:T(8,128)S(1)} collective-permute-done((f32[24,768]{1,0:T(8,128)S(1)}, f32[24,768]{1,0:T(8,128)S(1)}, u32[]{:S(2)}, u32[]{:S(2)}) %collective-permute-start.5) | collective-permute-done | bytes 73760 | tf_op jit(solution)/shard_map/ppermute | solution.py:689
  60.5 3.5 %shard_map.181 = (f32[48,768]{1,0:T(8,128)S(1)}, bf16[48,768]{1,0:T(8,128)(2,1)S(1)}) custom-call(f32[24,768]{1,0:T(8,128)S(1)} %shard_map.180.act_ref, f32[24,768]{1,0:T(8,128)S(1)} %collective-permute-done.5.refs_0_, bf16[576,768]{1,0:T(8,128)(2,1)S(1)} %copy-done.4, bf16[576,768]{1,0:T(8,128)(2,1)S(1)} %collective-permute-done.6.refs_2_, ...), custom_call_target="tpu_custom_call" | custom-call | flops 169869312 | bytes 3538944 | tf_op jit(solution)/shard_map/pallas_call | solution.py:26
  64.0 0.6 collective-permute-start.9
  64.6 3.8 %collective-permute-done.9.refs_0_ = bf16[48,768]{1,0:T(8,128)(2,1)S(1)} collective-permute-done((bf16[48,768]{1,0:T(8,128)(2,1)S(1)}, bf16[48,768]{1,0:T(8,128)(2,1)S(1)}, u32[]{:S(2)}, u32[]{:S(2)}) %collective-permute-start.9) | collective-permute-done | bytes 73760 | tf_op jit(solution)/shard_map/ppermute | solution.py:695
  68.4 0.8 shard_map.182
  69.2 1.5 %collective-permute-start.12 = (bf16[48,768]{1,0:T(8,128)(2,1)}, bf16[48,768]{1,0:T(8,128)(2,1)}, u32[]{:S(2)}, u32[]{:S(2)}) collective-permute-start(bf16[48,768]{1,0:T(8,128)(2,1)} %get-tuple-element.108), channel_id=1, source_target_pairs={{0,2},{1,3},{2,0},{3,1},{4,6},{5,7},{6,4},{7,5},{8,10},{9,11},{10,... | collective-permute-start | bytes 221192 | tf_op jit(solution)/shard_map/ppermute | solution.py:475
  71.1 3.0 %collective-permute-done.11 = bf16[48,768]{1,0:T(8,128)(2,1)} collective-permute-done((bf16[48,768]{1,0:T(8,128)(2,1)}, bf16[48,768]{1,0:T(8,128)(2,1)}, u32[]{:S(2)}, u32[]{:S(2)}) %collective-permute-start.11) | collective-permute-done | bytes 73760 | tf_op jit(solution)/shard_map/ppermute | solution.py:475
  74.1 1.6 %collective-permute-done.12 = bf16[48,768]{1,0:T(8,128)(2,1)} collective-permute-done((bf16[48,768]{1,0:T(8,128)(2,1)}, bf16[48,768]{1,0:T(8,128)(2,1)}, u32[]{:S(2)}, u32[]{:S(2)}) %collective-permute-start.12) | collective-permute-done | bytes 73760 | tf_op jit(solution)/shard_map/ppermute | solution.py:475
  75.7 1.0 select_select_fusion.3
  76.8 1.5 %collective-permute-start.14 = (bf16[96,768]{1,0:T(8,128)(2,1)S(1)}, bf16[96,768]{1,0:T(8,128)(2,1)S(1)}, u32[]{:S(2)}, u32[]{:S(2)}) collective-permute-start(bf16[96,768]{1,0:T(8,128)(2,1)S(1)} %constant_dynamic-slice_fusion.here_ref), channel_id=1, source_target_pairs={{0,24},{1,25},{2,16},{3,17},{4,8},{5,9},{10,26},{11,27},{8,2},{9,3... | collective-permute-start | bytes 442376 | tf_op jit(solution)/shard_map/ppermute | solution.py:642
  78.3 2.5 %shard_map.183 = (bf16[192,768]{1,0:T(8,128)(2,1)S(1)}, bf16[768,768]{1,0:T(8,128)(2,1)S(1)}, bf16[768,768]{1,0:T(8,128)(2,1)S(1)}, f32[24,768]{1,0:T(8,128)S(1)}) custom-call(bf16[192,768]{1,0:T(8,128)(2,1)S(1)} %bitcast.34, f32[24,768]{1,0:T(8,128)S(1)} %get-tuple-element.110.act_ref, bf16[2,4,768,768]{3,2,1,0:T(8,128)(2,1)} %w_in.6), custom_call_target="tpu_custom_call" | custom-call | flops 226492416 | bytes 4718592 | tf_op jit(solution)/shard_map/pallas_call | solution.py:26
  80.9 2.2 %collective-permute-start.15 = (bf16[288,768]{1,0:T(8,128)(2,1)S(1)}, bf16[288,768]{1,0:T(8,128)(2,1)S(1)}, u32[]{:S(2)}, u32[]{:S(2)}) collective-permute-start(bf16[288,768]{1,0:T(8,128)(2,1)S(1)} %copy-done.22), channel_id=1, source_target_pairs={{0,2},{1,3},{2,0},{3,1},{4,6},{5,7},{6,4},{7,5},{8,10},{9,11},{10,... | collective-permute-start | bytes 1327112 | tf_op jit(solution)/shard_map/ppermute | solution.py:668
  83.0 3.3 %collective-permute-done.14.came_ref = bf16[96,768]{1,0:T(8,128)(2,1)S(1)} collective-permute-done((bf16[96,768]{1,0:T(8,128)(2,1)S(1)}, bf16[96,768]{1,0:T(8,128)(2,1)S(1)}, u32[]{:S(2)}, u32[]{:S(2)}) %collective-permute-start.14) | collective-permute-done | bytes 147488 | tf_op jit(solution)/shard_map/ppermute | solution.py:642
  86.3 3.5 %shard_map.184 = bf16[192,896]{1,0:T(8,128)(2,1)S(1)} custom-call(s32[768]{0:T(1024)S(1)} %copy-done.13, bf16[192,768]{1,0:T(8,128)(2,1)S(1)} %get-tuple-element.113.query, bf16[96,768]{1,0:T(8,128)(2,1)S(1)} %constant_dynamic-slice_fusion.here_ref, bf16[96,768]{1,0:T(8,128)(2,1)S(1)} %collective-permute-done.14.came_ref, f32[120,16,128]{2,1,0:T(8,128)S(1)} %copy-done.1, ...), custom_call_target="tpu_custom_call" | custom-call | flops 1000000000 | bytes 8000000 | tf_op jit(solution)/shard_map/pallas_call | solution.py:26
  89.8 11.6 %all_to_all.16.message = bf16[8,24,896]{2,1,0:T(8,128)(2,1)S(1)} all-to-all(bf16[8,24,896]{2,1,0:T(8,128)(2,1)S(1)} %bitcast.36), channel_id=1, replica_groups=mesh['row'=4,'col'=8] {'col'}, dimensions={0} | all-to-all | bytes 688128 | tf_op jit(solution)/shard_map/all_to_all | solution.py:684
  101.4 1.0 shard_map.185.act_ref
  103.7 3.8 %collective-permute-done.16.refs_0_ = f32[24,768]{1,0:T(8,128)S(1)} collective-permute-done((f32[24,768]{1,0:T(8,128)S(1)}, f32[24,768]{1,0:T(8,128)S(1)}, u32[]{:S(2)}, u32[]{:S(2)}) %collective-permute-start.16) | collective-permute-done | bytes 73760 | tf_op jit(solution)/shard_map/ppermute | solution.py:689
  107.5 3.7 %shard_map.186 = (f32[48,768]{1,0:T(8,128)S(1)}, bf16[48,768]{1,0:T(8,128)(2,1)S(1)}) custom-call(f32[24,768]{1,0:T(8,128)S(1)} %shard_map.185.act_ref, f32[24,768]{1,0:T(8,128)S(1)} %collective-permute-done.16.refs_0_, bf16[576,768]{1,0:T(8,128)(2,1)S(1)} %copy-done.3, bf16[576,768]{1,0:T(8,128)(2,1)S(1)} %collective-permute-done.17.refs_2_, ...), custom_call_target="tpu_custom_call" | custom-call | flops 169869312 | bytes 3538944 | tf_op jit(solution)/shard_map/pallas_call | solution.py:26
  111.2 0.6 collective-permute-start.20
  111.8 3.8 %collective-permute-done.20.refs_0_ = bf16[48,768]{1,0:T(8,128)(2,1)S(1)} collective-permute-done((bf16[48,768]{1,0:T(8,128)(2,1)S(1)}, bf16[48,768]{1,0:T(8,128)(2,1)S(1)}, u32[]{:S(2)}, u32[]{:S(2)}) %collective-permute-start.20) | collective-permute-done | bytes 73760 | tf_op jit(solution)/shard_map/ppermute | solution.py:695
  115.6 0.8 shard_map.187
  116.5 0.6 collective-permute-start.22
  117.1 1.3 collective-permute-start.23
  118.3 1.3 collective-permute-done.21
  119.6 0.6 collective-permute-done.22
  120.2 1.3 %collective-permute-start.24 = (bf16[64,128]{1,0:T(8,128)(2,1)S(1)}, bf16[64,128]{1,0:T(8,128)(2,1)S(1)}, u32[]{:S(2)}, u32[]{:S(2)}) collective-permute-start(bf16[64,128]{1,0:T(8,128)(2,1)S(1)} %slice_select_fusion), channel_id=1, source_target_pairs={{0,8},{8,16},{16,24},{15,7},{23,15},{31,23}} | collective-permute-start | bytes 49160 | tf_op jit(solution)/shard_map/ppermute | solution.py:706
  121.5 4.3 %collective-permute-done.24.edge_ref = bf16[64,128]{1,0:T(8,128)(2,1)S(1)} collective-permute-done((bf16[64,128]{1,0:T(8,128)(2,1)S(1)}, bf16[64,128]{1,0:T(8,128)(2,1)S(1)}, u32[]{:S(2)}, u32[]{:S(2)}) %collective-permute-start.24) | collective-permute-done | bytes 16416 | tf_op jit(solution)/shard_map/ppermute | solution.py:706
  125.9 2.0 %shard_map.188 = f32[3,128]{1,0:T(4,128)} custom-call(bf16[256,128]{1,0:T(8,128)(2,1)S(1)} %copy-done.8, bf16[144,128]{1,0:T(8,128)(2,1)S(1)} %shard_map.172.own_ref, bf16[144,128]{1,0:T(8,128)(2,1)S(1)} %collective-permute-done.prev_ref, bf16[144,128]{1,0:T(8,128)(2,1)S(1)} %copy-done.10, bf16[192,128]{1,0:T(8,128)(2,1)S(1)} %bitcast.38, ...), custom_call_target="tpu_custom_call" | custom-call | flops 100000000 | bytes 1000000 | tf_op jit(solution)/shard_map/pallas_call | solution.py:26
  (79 shorter events, 3.6 us)
Async XLA Ops:
  0.0 0.8 copy-start.12
  2.1 11.4 %copy-start.19 = (bf16[4,128,128]{2,1,0:T(8,128)(2,1)S(1)}, bf16[4,128,128]{2,1,0:T(8,128)(2,1)}, u32[]{:S(2)}) copy-start(bf16[4,128,128]{2,1,0:T(8,128)(2,1)} %w_in.4) | copy-start | bytes 393220
  2.1 11.4 %copy-start.20 = (bf16[128,128]{1,0:T(8,128)(2,1)S(1)}, bf16[128,128]{1,0:T(8,128)(2,1)}, u32[]{:S(2)}) copy-start(bf16[128,128]{1,0:T(8,128)(2,1)} %w_out.4) | copy-start | bytes 98308
  2.6 10.7 %collective-permute-start = (bf16[144,128]{1,0:T(8,128)(2,1)S(1)}, bf16[144,128]{1,0:T(8,128)(2,1)S(1)}, u32[]{:S(2)}, u32[]{:S(2)}) collective-permute-start(bf16[144,128]{1,0:T(8,128)(2,1)S(1)} %shard_map.172.own_ref), channel_id=1, source_target_pairs={{0,1},{1,2},{2,3},{3,4},{4,5},{5,6},{6,7},{7,8},{8,9},{9,10},{10,1... | collective-permute-start | bytes 110600 | tf_op jit(solution)/shard_map/ppermute | solution.py:544
  4.6 8.8 %collective-permute-start.1 = (bf16[144,128]{1,0:T(8,128)(2,1)S(1)}, bf16[144,128]{1,0:T(8,128)(2,1)S(1)}, u32[]{:S(2)}, u32[]{:S(2)}) collective-permute-start(bf16[144,128]{1,0:T(8,128)(2,1)S(1)} %shard_map.172.own_ref), channel_id=1, source_target_pairs={{1,0},{2,1},{3,2},{4,3},{5,4},{6,5},{7,6},{8,7},{9,8},{10,9},{11,1... | collective-permute-start | bytes 110600 | tf_op jit(solution)/shard_map/ppermute | solution.py:545
  13.4 2.1 %copy-start.9 = (bf16[144,128]{1,0:T(8,128)(2,1)}, bf16[144,128]{1,0:T(8,128)(2,1)S(1)}, u32[]{:S(2)}) copy-start(bf16[144,128]{1,0:T(8,128)(2,1)S(1)} %collective-permute-done.1.next_ref) | copy-start | bytes 110596
  13.4 14.5 %collective-permute-start.2 = (bf16[288,768]{1,0:T(8,128)(2,1)}, bf16[288,768]{1,0:T(8,128)(2,1)}, u32[]{:S(2)}, u32[]{:S(2)}) collective-permute-start(bf16[288,768]{1,0:T(8,128)(2,1)} %get-tuple-element.78), channel_id=1, source_target_pairs={{0,2},{1,3},{2,0},{3,1},{4,6},{5,7},{6,4},{7,5},{8,10},{9,11},{10,... | collective-permute-start | bytes 1327112 | tf_op jit(solution)/shard_map/ppermute | solution.py:571
  16.1 11.8 %all-to-all-start = ((bf16[8,144,128]{2,1,0:T(8,128)(2,1)}), bf16[8,144,128]{2,1,0:T(8,128)(2,1)S(1)}, u32[]{:S(2)}, u32[]{:S(2)}) async-start(bf16[8,144,128]{2,1,0:T(8,128)(2,1)} %get-tuple-element.74), calls=%async_computation | async-start | bytes 589824 | tf_op jit(solution)/shard_map/all_to_all | solution.py:611
  19.6 8.4 %copy-start.17 = (bf16[192,768]{1,0:T(8,128)(2,1)S(1)}, bf16[192,768]{1,0:T(8,128)(2,1)}, u32[]{:S(2)}) copy-start(bf16[192,768]{1,0:T(8,128)(2,1)} %cond.1) | copy-start | bytes 884740
  19.6 8.3 %copy-start.18 = (bf16[128,768]{1,0:T(8,128)(2,1)S(1)}, bf16[128,768]{1,0:T(8,128)(2,1)}, u32[]{:S(2)}) copy-start(bf16[128,768]{1,0:T(8,128)(2,1)} %weight.1) | copy-start | bytes 589828
  27.9 2.8 %copy-start.21 = (bf16[2,128,16]{1,2,0:T(8,128)(2,1)S(1)}, bf16[2,128,16]{1,2,0:T(8,128)(2,1)}, u32[]{:S(2)}) copy-start(bf16[2,128,16]{1,2,0:T(8,128)(2,1)} %param.29) | copy-start | bytes 24580
  29.2 4.4 %copy-start.24 = (bf16[288,768]{1,0:T(8,128)(2,1)S(1)}, bf16[288,768]{1,0:T(8,128)(2,1)}, u32[]{:S(2)}) copy-start(bf16[288,768]{1,0:T(8,128)(2,1)} %get-tuple-element.99) | copy-start | bytes 1327108
  29.2 8.0 %copy-start.4 = (bf16[576,768]{1,0:T(8,128)(2,1)S(1)}, bf16[576,768]{1,0:T(8,128)(2,1)}, u32[]{:S(2)}) copy-start(bf16[576,768]{1,0:T(8,128)(2,1)} %get-tuple-element.101.refs_1_) | copy-start | bytes 2654212
  29.3 10.5 %collective-permute-start.3 = (bf16[96,768]{1,0:T(8,128)(2,1)S(1)}, bf16[96,768]{1,0:T(8,128)(2,1)S(1)}, u32[]{:S(2)}, u32[]{:S(2)}) collective-permute-start(bf16[96,768]{1,0:T(8,128)(2,1)S(1)} %get-tuple-element.84.here_ref), channel_id=1, source_target_pairs={{0,24},{1,25},{2,16},{3,17},{4,8},{5,9},{10,26},{11,27},{8,2},{9,3... | collective-permute-start | bytes 442376 | tf_op jit(solution)/shard_map/ppermute | solution.py:642
  33.7 21.3 %collective-permute-start.4 = (bf16[288,768]{1,0:T(8,128)(2,1)S(1)}, bf16[288,768]{1,0:T(8,128)(2,1)S(1)}, u32[]{:S(2)}, u32[]{:S(2)}) collective-permute-start(bf16[288,768]{1,0:T(8,128)(2,1)S(1)} %copy-done.24), channel_id=1, source_target_pairs={{0,2},{1,3},{2,0},{3,1},{4,6},{5,7},{6,4},{7,5},{8,10},{9,11},{10,... | collective-permute-start | bytes 1327112 | tf_op jit(solution)/shard_map/ppermute | solution.py:663
  37.3 23.2 %collective-permute-start.6 = (bf16[576,768]{1,0:T(8,128)(2,1)S(1)}, bf16[576,768]{1,0:T(8,128)(2,1)S(1)}, u32[]{:S(2)}, u32[]{:S(2)}) collective-permute-start(bf16[576,768]{1,0:T(8,128)(2,1)S(1)} %copy-done.4), channel_id=1, source_target_pairs={{0,1},{1,0},{2,3},{3,2},{4,5},{5,4},{6,7},{7,6},{8,9},{9,8},{10,11... | collective-permute-start | bytes 2654216 | tf_op jit(solution)/shard_map/ppermute | solution.py:665
  37.3 2.6 %copy-start.2 = (f32[120,16,128]{2,1,0:T(8,128)S(1)}, f32[120,16,128]{2,1,0:T(8,128)}, u32[]{:S(2)}) copy-start(f32[120,16,128]{2,1,0:T(8,128)} %get-tuple-element.85.low) | copy-start | bytes 2949124
  37.3 2.6 %copy-start.13 = (s32[768]{0:T(1024)S(1)}, s32[768]{0:T(1024)}, u32[]{:S(2)}) copy-start(s32[768]{0:T(1024)} %mask_ref.3) | copy-start | bytes 9220
  39.9 14.1 %copy-start = (bf16[2,768,768]{2,1,0:T(8,128)(2,1)S(1)}, bf16[2,768,768]{2,1,0:T(8,128)(2,1)}, u32[]{:S(2)}) copy-start(bf16[2,768,768]{2,1,0:T(8,128)(2,1)} %w_out.6) | copy-start | bytes 7077892
  53.9 1.6 %copy-start.23 = (bf16[288,768]{1,0:T(8,128)(2,1)S(1)}, bf16[288,768]{1,0:T(8,128)(2,1)}, u32[]{:S(2)}) copy-start(bf16[288,768]{1,0:T(8,128)(2,1)} %get-tuple-element.107) | copy-start | bytes 1327108
  55.0 5.5 %collective-permute-start.7 = (bf16[288,768]{1,0:T(8,128)(2,1)}, bf16[288,768]{1,0:T(8,128)(2,1)S(1)}, u32[]{:S(2)}, u32[]{:S(2)}) collective-permute-start(bf16[288,768]{1,0:T(8,128)(2,1)} %collective-permute-done.2.refs_3_), channel_id=1, source_target_pairs={{0,1},{1,0},{2,3},{3,2},{4,5},{5,4},{6,7},{7,6},{8,9},{9,8},{10,11... | collective-permute-start | bytes 1327112 | tf_op jit(solution)/shard_map/ppermute | solution.py:691
  55.1 5.4 %collective-permute-start.8 = (bf16[288,768]{1,0:T(8,128)(2,1)S(1)}, bf16[288,768]{1,0:T(8,128)(2,1)S(1)}, u32[]{:S(2)}, u32[]{:S(2)}) collective-permute-start(bf16[288,768]{1,0:T(8,128)(2,1)S(1)} %collective-permute-done.4.refs_4_), channel_id=1, source_target_pairs={{0,1},{1,0},{2,3},{3,2},{4,5},{5,4},{6,7},{7,6},{8,9},{9,8},{10,11... | collective-permute-start | bytes 1327112 | tf_op jit(solution)/shard_map/ppermute | solution.py:691
  55.6 13.6 %collective-permute-start.10 = (bf16[288,768]{1,0:T(8,128)(2,1)S(1)}, bf16[288,768]{1,0:T(8,128)(2,1)S(1)}, u32[]{:S(2)}, u32[]{:S(2)}) collective-permute-start(bf16[288,768]{1,0:T(8,128)(2,1)S(1)} %copy-done.23), channel_id=1, source_target_pairs={{0,2},{1,3},{2,0},{3,1},{4,6},{5,7},{6,4},{7,5},{8,10},{9,11},{10,... | collective-permute-start | bytes 1327112 | tf_op jit(solution)/shard_map/ppermute | solution.py:687
  56.1 4.4 %collective-permute-start.5 = (f32[24,768]{1,0:T(8,128)S(1)}, f32[24,768]{1,0:T(8,128)S(1)}, u32[]{:S(2)}, u32[]{:S(2)}) collective-permute-start(f32[24,768]{1,0:T(8,128)S(1)} %shard_map.180.act_ref), channel_id=1, source_target_pairs={{0,4},{1,5},{2,6},{3,7},{4,0},{5,1},{6,2},{7,3},{8,12},{9,13},{10,... | collective-permute-start | bytes 221192 | tf_op jit(solution)/shard_map/ppermute | solution.py:689
  64.0 4.4 %collective-permute-start.9 = (bf16[48,768]{1,0:T(8,128)(2,1)S(1)}, bf16[48,768]{1,0:T(8,128)(2,1)S(1)}, u32[]{:S(2)}, u32[]{:S(2)}) collective-permute-start(bf16[48,768]{1,0:T(8,128)(2,1)S(1)} %get-tuple-element.105), channel_id=1, source_target_pairs={{0,4},{1,5},{2,6},{3,7},{4,0},{5,1},{6,2},{7,3},{8,12},{9,13},{10,... | collective-permute-start | bytes 221192 | tf_op jit(solution)/shard_map/ppermute | solution.py:695
  69.2 4.9 %collective-permute-start.11 = (bf16[48,768]{1,0:T(8,128)(2,1)}, bf16[48,768]{1,0:T(8,128)(2,1)}, u32[]{:S(2)}, u32[]{:S(2)}) collective-permute-start(bf16[48,768]{1,0:T(8,128)(2,1)} %get-tuple-element.108), channel_id=1, source_target_pairs={{0,3},{1,2},{2,1},{3,0},{4,7},{5,6},{6,5},{7,4},{8,11},{9,10},{10,... | collective-permute-start | bytes 221192 | tf_op jit(solution)/shard_map/ppermute | solution.py:475
  69.2 6.5 %collective-permute-start.12 = (bf16[48,768]{1,0:T(8,128)(2,1)}, bf16[48,768]{1,0:T(8,128)(2,1)}, u32[]{:S(2)}, u32[]{:S(2)}) collective-permute-start(bf16[48,768]{1,0:T(8,128)(2,1)} %get-tuple-element.108), channel_id=1, source_target_pairs={{0,2},{1,3},{2,0},{3,1},{4,6},{5,7},{6,4},{7,5},{8,10},{9,11},{10,... | collective-permute-start | bytes 221192 | tf_op jit(solution)/shard_map/ppermute | solution.py:475
  70.7 5.0 %collective-permute-start.13 = (bf16[48,768]{1,0:T(8,128)(2,1)}, bf16[48,768]{1,0:T(8,128)(2,1)}, u32[]{:S(2)}, u32[]{:S(2)}) collective-permute-start(bf16[48,768]{1,0:T(8,128)(2,1)} %get-tuple-element.108), channel_id=1, source_target_pairs={{0,1},{1,0},{2,3},{3,2},{4,5},{5,4},{6,7},{7,6},{8,9},{9,8},{10,11... | collective-permute-start | bytes 221192 | tf_op jit(solution)/shard_map/ppermute | solution.py:475
  76.8 9.5 %collective-permute-start.14 = (bf16[96,768]{1,0:T(8,128)(2,1)S(1)}, bf16[96,768]{1,0:T(8,128)(2,1)S(1)}, u32[]{:S(2)}, u32[]{:S(2)}) collective-permute-start(bf16[96,768]{1,0:T(8,128)(2,1)S(1)} %constant_dynamic-slice_fusion.here_ref), channel_id=1, source_target_pairs={{0,24},{1,25},{2,16},{3,17},{4,8},{5,9},{10,26},{11,27},{8,2},{9,3... | collective-permute-start | bytes 442376 | tf_op jit(solution)/shard_map/ppermute | solution.py:642
  78.3 2.6 %copy-start.22 = (bf16[288,768]{1,0:T(8,128)(2,1)S(1)}, bf16[288,768]{1,0:T(8,128)(2,1)}, u32[]{:S(2)}) copy-start(bf16[288,768]{1,0:T(8,128)(2,1)} %get-tuple-element.121) | copy-start | bytes 1327108
  78.3 4.7 %copy-start.3 = (bf16[576,768]{1,0:T(8,128)(2,1)S(1)}, bf16[576,768]{1,0:T(8,128)(2,1)}, u32[]{:S(2)}) copy-start(bf16[576,768]{1,0:T(8,128)(2,1)} %get-tuple-element.123.refs_1_) | copy-start | bytes 2654212
  78.3 8.0 %copy-start.1 = (f32[120,16,128]{2,1,0:T(8,128)S(1)}, f32[120,16,128]{2,1,0:T(8,128)}, u32[]{:S(2)}) copy-start(f32[120,16,128]{2,1,0:T(8,128)} %get-tuple-element.115.low) | copy-start | bytes 2949124
  80.9 21.7 %collective-permute-start.15 = (bf16[288,768]{1,0:T(8,128)(2,1)S(1)}, bf16[288,768]{1,0:T(8,128)(2,1)S(1)}, u32[]{:S(2)}, u32[]{:S(2)}) collective-permute-start(bf16[288,768]{1,0:T(8,128)(2,1)S(1)} %copy-done.22), channel_id=1, source_target_pairs={{0,2},{1,3},{2,0},{3,1},{4,6},{5,7},{6,4},{7,5},{8,10},{9,11},{10,... | collective-permute-start | bytes 1327112 | tf_op jit(solution)/shard_map/ppermute | solution.py:668
  83.0 20.7 %collective-permute-start.17 = (bf16[576,768]{1,0:T(8,128)(2,1)S(1)}, bf16[576,768]{1,0:T(8,128)(2,1)S(1)}, u32[]{:S(2)}, u32[]{:S(2)}) collective-permute-start(bf16[576,768]{1,0:T(8,128)(2,1)S(1)} %copy-done.3), channel_id=1, source_target_pairs={{0,1},{1,0},{2,3},{3,2},{4,5},{5,4},{6,7},{7,6},{8,9},{9,8},{10,11... | collective-permute-start | bytes 2654216 | tf_op jit(solution)/shard_map/ppermute | solution.py:665
  102.5 13.2 %copy-start.5 = (bf16[768,128]{1,0:T(8,128)(2,1)S(1)}, bf16[768,128]{1,0:T(8,128)(2,1)}, u32[]{:S(2)}) copy-start(bf16[768,128]{1,0:T(8,128)(2,1)} %refs_1_.1) | copy-start | bytes 589828
  102.5 23.4 %copy-start.6 = (bf16[4,128,128]{2,1,0:T(8,128)(2,1)S(1)}, bf16[4,128,128]{2,1,0:T(8,128)(2,1)}, u32[]{:S(2)}) copy-start(bf16[4,128,128]{2,1,0:T(8,128)(2,1)} %w_in.7) | copy-start | bytes 393220
  102.5 23.4 %copy-start.8 = (bf16[256,128]{1,0:T(8,128)(2,1)S(1)}, bf16[256,128]{1,0:T(8,128)(2,1)}, u32[]{:S(2)}) copy-start(bf16[256,128]{1,0:T(8,128)(2,1)} %copy-done.7) | copy-start | bytes 196612
  102.5 23.4 %copy-start.10 = (bf16[144,128]{1,0:T(8,128)(2,1)S(1)}, bf16[144,128]{1,0:T(8,128)(2,1)}, u32[]{:S(2)}) copy-start(bf16[144,128]{1,0:T(8,128)(2,1)} %copy-done.9) | copy-start | bytes 110596
  102.5 23.4 %copy-start.11 = (bf16[128,128]{1,0:T(8,128)(2,1)S(1)}, bf16[128,128]{1,0:T(8,128)(2,1)}, u32[]{:S(2)}) copy-start(bf16[128,128]{1,0:T(8,128)(2,1)} %w_out.7) | copy-start | bytes 98308
  102.5 23.4 %copy-start.14 = (bf16[3,128]{1,0:T(4,128)(2,1)S(1)}, bf16[3,128]{1,0:T(4,128)(2,1)}, u32[]{:S(2)}) copy-start(bf16[3,128]{1,0:T(4,128)(2,1)} %pos.1) | copy-start | bytes 2308
  102.6 4.9 %collective-permute-start.18 = (bf16[288,768]{1,0:T(8,128)(2,1)S(1)}, bf16[288,768]{1,0:T(8,128)(2,1)S(1)}, u32[]{:S(2)}, u32[]{:S(2)}) collective-permute-start(bf16[288,768]{1,0:T(8,128)(2,1)S(1)} %collective-permute-done.10.refs_3_), channel_id=1, source_target_pairs={{0,1},{1,0},{2,3},{3,2},{4,5},{5,4},{6,7},{7,6},{8,9},{9,8},{10,11... | collective-permute-start | bytes 1327112 | tf_op jit(solution)/shard_map/ppermute | solution.py:691
  102.6 4.9 %collective-permute-start.19 = (bf16[288,768]{1,0:T(8,128)(2,1)S(1)}, bf16[288,768]{1,0:T(8,128)(2,1)S(1)}, u32[]{:S(2)}, u32[]{:S(2)}) collective-permute-start(bf16[288,768]{1,0:T(8,128)(2,1)S(1)} %collective-permute-done.15.refs_4_), channel_id=1, source_target_pairs={{0,1},{1,0},{2,3},{3,2},{4,5},{5,4},{6,7},{7,6},{8,9},{9,8},{10,11... | collective-permute-start | bytes 1327112 | tf_op jit(solution)/shard_map/ppermute | solution.py:691
  103.1 4.4 %collective-permute-start.16 = (f32[24,768]{1,0:T(8,128)S(1)}, f32[24,768]{1,0:T(8,128)S(1)}, u32[]{:S(2)}, u32[]{:S(2)}) collective-permute-start(f32[24,768]{1,0:T(8,128)S(1)} %shard_map.185.act_ref), channel_id=1, source_target_pairs={{0,4},{1,5},{2,6},{3,7},{4,0},{5,1},{6,2},{7,3},{8,12},{9,13},{10,... | collective-permute-start | bytes 221192 | tf_op jit(solution)/shard_map/ppermute | solution.py:689
  111.2 4.4 %collective-permute-start.20 = (bf16[48,768]{1,0:T(8,128)(2,1)S(1)}, bf16[48,768]{1,0:T(8,128)(2,1)S(1)}, u32[]{:S(2)}, u32[]{:S(2)}) collective-permute-start(bf16[48,768]{1,0:T(8,128)(2,1)S(1)} %get-tuple-element.127), channel_id=1, source_target_pairs={{0,4},{1,5},{2,6},{3,7},{4,0},{5,1},{6,2},{7,3},{8,12},{9,13},{10,... | collective-permute-start | bytes 221192 | tf_op jit(solution)/shard_map/ppermute | solution.py:695
  116.5 3.1 %collective-permute-start.21 = (bf16[48,128]{1,0:T(8,128)(2,1)S(1)}, bf16[48,128]{1,0:T(8,128)(2,1)S(1)}, u32[]{:S(2)}, u32[]{:S(2)}) collective-permute-start(bf16[48,128]{1,0:T(8,128)(2,1)S(1)} %get-tuple-element.128), channel_id=1, source_target_pairs={{0,3},{1,2},{2,1},{3,0},{4,7},{5,6},{6,5},{7,4},{8,11},{9,10},{10,... | collective-permute-start | bytes 36872 | tf_op jit(solution)/shard_map/ppermute | solution.py:475
  116.5 3.7 %collective-permute-start.22 = (bf16[48,128]{1,0:T(8,128)(2,1)S(1)}, bf16[48,128]{1,0:T(8,128)(2,1)S(1)}, u32[]{:S(2)}, u32[]{:S(2)}) collective-permute-start(bf16[48,128]{1,0:T(8,128)(2,1)S(1)} %get-tuple-element.128), channel_id=1, source_target_pairs={{0,2},{1,3},{2,0},{3,1},{4,6},{5,7},{6,4},{7,5},{8,10},{9,11},{10,... | collective-permute-start | bytes 36872 | tf_op jit(solution)/shard_map/ppermute | solution.py:475
  117.1 3.1 %collective-permute-start.23 = (bf16[48,128]{1,0:T(8,128)(2,1)S(1)}, bf16[48,128]{1,0:T(8,128)(2,1)S(1)}, u32[]{:S(2)}, u32[]{:S(2)}) collective-permute-start(bf16[48,128]{1,0:T(8,128)(2,1)S(1)} %get-tuple-element.128), channel_id=1, source_target_pairs={{0,1},{1,0},{2,3},{3,2},{4,5},{5,4},{6,7},{7,6},{8,9},{9,8},{10,11... | collective-permute-start | bytes 36872 | tf_op jit(solution)/shard_map/ppermute | solution.py:475
  120.2 5.6 %collective-permute-start.24 = (bf16[64,128]{1,0:T(8,128)(2,1)S(1)}, bf16[64,128]{1,0:T(8,128)(2,1)S(1)}, u32[]{:S(2)}, u32[]{:S(2)}) collective-permute-start(bf16[64,128]{1,0:T(8,128)(2,1)S(1)} %slice_select_fusion), channel_id=1, source_target_pairs={{0,8},{8,16},{16,24},{15,7},{23,15},{31,23}} | collective-permute-start | bytes 49160 | tf_op jit(solution)/shard_map/ppermute | solution.py:706
  (3 other events, 1.9 us)
